TPU v7x, 128 devices: a whole 4x4x4 slice. The times are simulated.
128 devices in a mesh: dp: 16 (over z_lo, x, core), ctx: 8 (over z_hi, y).
Axes of the slice: x: 4, y: 4, z: 4 (z_hi: 2, z_lo: 2; z = z_hi * 2 + z_lo), core: 2. Of those that a mesh axis runs over, the one named last changes fastest.
Arguments:
- layer_input: bfloat16 [16, 1024, 8192], P('dp', 'ctx')
- w_qkv: bfloat16 [8192, 1280], replicated
- d_out: bfloat16 [16, 1024, 1024], P('dp', 'ctx'), may hold values from -6 to 6
- span_order: int32 [16, 16], P('dp'), may hold values from 0 to 15, each once within a row
- doc_lengths: int32 [16, 4], P('dp'), may hold values from 1 to 512, 1024 in all within a row
Outputs:
- d_x: bfloat16 [16, 1024, 8192], P('dp', 'ctx')
- d_w: float32 [8192, 1280], P(('dp', 'ctx'))
All inputs are finite; a program needn't handle non-finite values.
Results may differ from a plain program's by a relative error of at most 0.029.
Values may be sent and summed in bfloat16 or wider, within the bound.
No kernel may reach another device: no remote copies, remote signals or barrier semaphores. Data moves between devices by JAX's collectives and lax.ppermute only.
A program may use at most 128 MiB of HBM per device.

v0:
```python
import jax
import jax.numpy as jnp
from jax import lax
from jax.sharding import PartitionSpec as P

HD = 128
HQ = 8


def place_rows(order, lengths, stored, half):
    spans = order.shape[0]
    onehot = (stored // half)[:, None] == jnp.arange(spans, dtype=jnp.int32)[None, :]
    positions = jnp.sum(jnp.where(onehot, order[None, :], 0), axis=1) * half + stored % half
    ends = jnp.cumsum(lengths)
    documents = jnp.sum((positions[:, None] >= ends[None, :]).astype(jnp.int32), axis=1)
    return (positions, documents)


def local(layer_input, w_qkv, d_out, span_order, doc_lengths):
    rows = layer_input[0]
    tokens = rows.shape[0]
    half = tokens // 2
    ctx_count = lax.axis_size("ctx")
    ctx_place = lax.axis_index("ctx")
    scale = HD ** (-0.5)
    order = span_order[0]
    lengths = doc_lengths[0]
    qkv = jnp.dot(rows, w_qkv, preferred_element_type=jnp.float32).astype(jnp.bfloat16)
    query = qkv[:, : HQ * HD].reshape(tokens, HQ, HD)
    key_value = qkv[:, HQ * HD :]
    gathered = lax.all_gather(key_value, "ctx", axis=0, tiled=True)
    key = gathered[:, :HD]
    value = gathered[:, HD:]
    local_rows = ctx_place * tokens + jnp.arange(tokens, dtype=jnp.int32)
    pos_query, doc_query = place_rows(order, lengths, local_rows, half)
    pos_key, doc_key = place_rows(
        order, lengths, jnp.arange(tokens * ctx_count, dtype=jnp.int32), half
    )
    allowed = (pos_key[None, :] <= pos_query[:, None]) & (doc_key[None, :] == doc_query[:, None])
    scores = jnp.einsum("qhd,kd->hqk", query, key, preferred_element_type=jnp.float32) * scale
    scores = jnp.where(allowed[None], scores, -1e30)
    peak = jnp.max(scores, axis=2, keepdims=True)
    expo = jnp.where(allowed[None], jnp.exp(scores - peak), 0.0)
    probs = expo / jnp.sum(expo, axis=2, keepdims=True)
    probs_low = probs.astype(jnp.bfloat16)
    grad_heads = d_out[0].reshape(tokens, HQ, HD)
    out_heads = jnp.einsum("hqk,kd->qhd", probs_low, value, preferred_element_type=jnp.float32)
    delta = jnp.sum(grad_heads.astype(jnp.float32) * out_heads, axis=2)
    grad_probs = jnp.einsum("qhd,kd->hqk", grad_heads, value, preferred_element_type=jnp.float32)
    d_scores = (probs * (grad_probs - jnp.transpose(delta)[:, :, None]) * scale).astype(
        jnp.bfloat16
    )
    d_query = jnp.einsum("hqk,kd->qhd", d_scores, key, preferred_element_type=jnp.float32).reshape(
        tokens, HQ * HD
    )
    d_key = jnp.einsum("hqk,qhd->kd", d_scores, query, preferred_element_type=jnp.float32)
    d_value = jnp.einsum("hqk,qhd->kd", probs_low, grad_heads, preferred_element_type=jnp.float32)
    owned = lax.psum_scatter(
        jnp.concatenate([d_key, d_value], axis=1).astype(jnp.bfloat16),
        "ctx",
        scatter_dimension=0,
        tiled=True,
    ).astype(jnp.float32)
    d_qkv = jnp.concatenate([d_query, owned], axis=1).astype(jnp.bfloat16)
    d_rows = lax.dot_general(
        d_qkv, w_qkv, (((1,), (1,)), ((), ())), preferred_element_type=jnp.float32
    ).astype(jnp.bfloat16)
    summed = lax.psum_scatter(
        lax.dot_general(
            rows, d_qkv, (((0,), (0,)), ((), ())), preferred_element_type=jnp.float32
        ).astype(jnp.bfloat16),
        "dp",
        scatter_dimension=0,
        tiled=True,
    )
    d_w = lax.psum_scatter(summed, "ctx", scatter_dimension=0, tiled=True).astype(jnp.float32)
    return (d_rows[None], d_w)


def solution(mesh):
    placed = (P("dp", "ctx", None), P(), P("dp", "ctx", None), P("dp", None), P("dp", None))
    return jax.shard_map(
        local,
        mesh=mesh,
        in_specs=placed,
        out_specs=(P("dp", "ctx", None), P(("dp", "ctx"), None)),
        check_vma=False,
    )
```

profile of v0, /device:TPU:0, one launch (start us, length us, event | category | flops | bytes accessed | tf_op | source)
XLA Modules:
  0.0 354.4 jit_solution(9097859853657718371)
XLA Ops:
  7.2 0.0 copy-start
  7.2 0.0 reduce-scatter.10.cloned.1.call-start
  7.2 1.5 copy-done
  8.8 0.0 copy-start.4
  8.8 0.0 copy-start.5
  8.8 0.0 copy-start.3
  8.8 8.6 %convolution_convert_fusion.2 = bf16[128,1280]{1,0:T(8,128)(2,1)S(1)} fusion(bf16[8192,1280]{1,0:T(8,128)(2,1)} %param.6, bf16[1,128,8192]{2,1,0:T(8,128)(2,1)S(1)} %copy-done), kind=kOutput, calls=%fused_computation.12 | convolution fusion | flops 2684518400 | bytes 23396352 | tf_op jit(solution)/shard_map/dot_general | solution.py:28
  17.4 0.0 copy-done.4
  17.4 0.1 select_reduce_fusion.1
  17.5 0.1 select_reduce_fusion
  17.6 0.0 copy-done.5
  17.6 0.2 reduce-window.8
  17.8 0.1 convert_reduce_fusion.1
  17.9 0.1 convert_reduce_fusion
  18.0 36.5 %all_gather.3 = bf16[1024,256]{1,0:T(8,128)(2,1)S(1)} all-gather(bf16[128,256]{1,0:T(8,128)(2,1)S(1)} %slice.16), channel_id=1, replica_groups=mesh['dp'=16,'ctx'=8] {'ctx'}, dimensions={0}, use_global_device_ids=true | all-gather | bytes 589824 | tf_op jit(solution)/shard_map/all_gather | solution.py:31
  54.5 0.2 copy.53
  54.7 0.0 copy-done.3
  54.7 0.2 copy.30
  54.9 0.3 compare_and_fusion
  55.2 3.6 %fusion.33 = (f32[8,128]{1,0:T(8,128)S(1)}, f32[8,128,1024]{1,2,0:T(8,128)}) fusion(pred[128,1024]{0,1:T(8,128)(4,1)S(1)} %compare_and_fusion, bf16[128,8,128]{0,2,1:T(8,128)(2,1)S(1)} %bitcast.88, bf16[1024,256]{1,0:T(8,128)(2,1)S(1)} %all_gather.3), kind=kOutput, calls=%fused_computation.64 | convolution fusion | flops 273679360 | bytes 4984832 | tf_op jit(solution)/shard_map/sub | solution.py:43
  58.8 2.5 fusion.12
  61.4 0.0 copy-start.2
  61.4 0.5 fusion.16
  61.9 0.8 fusion.15
  62.7 0.9 copy-done.2
  63.6 1.0 fusion.5
  64.5 0.0 copy-start.1
  64.5 1.3 copy-done.1
  65.9 0.8 fusion.14
  66.7 1.0 copy.49
  67.7 0.0 reduce-scatter.10.cloned.1.call-update
  67.7 0.0 reduce-scatter.8.cloned.1.call-start
  67.8 2.1 convolution_convert_fusion.3
  69.9 69.6 %reduce-scatter.10.cloned.1.call-done = bf16[128,256]{1,0:T(8,128)(2,1)} async-done(((bf16[1024,256]{1,0:T(8,128)(2,1)}), bf16[128,256]{1,0:T(8,128)(2,1)}) %reduce-scatter.10.cloned.1.call-update) | async-done | bytes 65552
  139.4 0.9 copy.50
  140.4 9.9 %fusion.1 = bf16[8192,1280]{0,1:T(8,128)(2,1)} fusion(bf16[1,128,8192]{2,1,0:T(8,128)(2,1)S(1)} %copy-done, bf16[128,256]{0,1:T(8,128)(2,1)S(1)} %copy.50, bf16[128,1024]{0,1:T(8,128)(2,1)S(1)} %bitcast.83), kind=kOutput, calls=%fused_computation.2 | convolution fusion | flops 2695495680 | bytes 23396352 | tf_op jit(solution)/shard_map/dot_general | solution.py:69
  150.3 0.0 reduce-scatter.8.cloned.1.call-update
  150.3 0.2 reduce-scatter.12.cloned.1.call-start
  150.6 118.5 %reduce-scatter.8.cloned.1.call-done = bf16[512,1280]{0,1:T(8,128)(2,1)} async-done(((bf16[8192,1280]{0,1:T(8,128)(2,1)}), bf16[512,1280]{0,1:T(8,128)(2,1)}) %reduce-scatter.8.cloned.1.call-update) | async-done | bytes 1310736 | tf_op jit(solution)/shard_map/reduce_scatter | solution.py:68
  269.0 2.4 copy.51
  271.5 0.0 reduce-scatter.12.cloned.1.call-update
  271.5 12.0 %fusion.2 = bf16[1,128,8192]{2,1,0:T(8,128)(2,1)} fusion(bf16[8192,1280]{1,0:T(8,128)(2,1)} %param.6, bf16[128,256]{0,1:T(8,128)(2,1)S(1)} %copy.50, bf16[128,1024]{0,1:T(8,128)(2,1)S(1)} %bitcast.84), kind=kOutput, calls=%fused_computation.4 | convolution fusion | flops 2686058496 | bytes 23396352 | tf_op jit(solution)/shard_map/dot_general | solution.py:65
  283.5 62.4 %reduce-scatter.12.cloned.1.call-done = bf16[64,1280]{1,0:T(8,128)(2,1)} async-done(((bf16[512,1280]{1,0:T(8,128)(2,1)}), bf16[64,1280]{1,0:T(8,128)(2,1)}) %reduce-scatter.12.cloned.1.call-update) | async-done | bytes 163856
  345.9 1.1 copy.52
  347.0 0.9 copy.39
  (7 shorter events, 0.1 us)
Async XLA Ops:
  7.2 1.6 copy-start
  7.2 132.3 %reduce-scatter.10.cloned.1.call-start = ((), (), s32[]{:S(2)}) async-start(), calls=%async_computation.4 | async-start | bytes 589824
  8.8 8.7 %copy-start.4 = (s32[1,16]{1,0:T(1,128)S(1)}, s32[1,16]{1,0:T(1,128)}, u32[]{:S(2)}) copy-start(s32[1,16]{1,0:T(1,128)} %param.8) | copy-start | bytes 196
  8.8 8.9 %copy-start.5 = (s32[1,4]{1,0:T(1,128)S(1)}, s32[1,4]{1,0:T(1,128)}, u32[]{:S(2)}) copy-start(s32[1,4]{1,0:T(1,128)} %param.9) | copy-start | bytes 52
  8.8 45.9 %copy-start.3 = (bf16[1,128,1024]{2,1,0:T(8,128)(2,1)S(1)}, bf16[1,128,1024]{2,1,0:T(8,128)(2,1)}, u32[]{:S(2)}) copy-start(bf16[1,128,1024]{2,1,0:T(8,128)(2,1)} %param.7) | copy-start | bytes 786436
  61.4 2.2 copy-start.2
  64.5 1.3 copy-start.1
  67.7 201.3 %reduce-scatter.8.cloned.1.call-start = ((), (), s32[]{:S(2)}) async-start(), calls=%async_computation.3 | async-start | bytes 22282240 | tf_op jit(solution)/shard_map/reduce_scatter | solution.py:68
  150.3 195.5 %reduce-scatter.12.cloned.1.call-start = ((), (), s32[]{:S(2)}) async-start(), calls=%async_computation.5 | async-start | bytes 1474560
Sparse Core Ops, SparseCore 0:
  67.9 71.5 reduce-scatter.9
  150.5 118.5 reduce-scatter.7
  273.2 72.6 reduce-scatter.11
where the time goes:
time: 355 us; the launch traced here: 354 us
  waiting for transfers between devices  250 us (70%)
  matrix products  39.3 us (11%)
  blocking collectives  36.5 us (10%)
  between operations  13.9 us (4%)
  local copies, waits for them, and re-layouts  10.5 us (3%)
    unnamed x5, waiting for transfers between devices  132 us
    reduce_scatter x1, waiting for transfers between devices, local(): lax.psum_scatter(lax.dot_general(rows, d_qkv, (((0,), (0,)), ((), ())), p...  118 us
    all_gather x1, blocking collectives, local(): gathered = lax.all_gather(key_value, 'ctx', axis=0, tiled=True)  36.5 us
    dot_general x1, matrix products, local(): lax.dot_general(d_qkv, w_qkv, (((1,), (1,)), ((), ())), preferred_element...  12 us
    unnamed x18, local copies, waits for them, and re-layouts  10.3 us
    dot_general x1, matrix products, local(): lax.dot_general(rows, d_qkv, (((0,), (0,)), ((), ())), preferred_element_...  9.93 us
    dot_general x1, matrix products, local(): jnp.dot(rows, w_qkv, preferred_element_type=jnp.float32)  8.58 us
  transfers between devices with their start and end apart: 3, of which 3 were waited for; matrix products, arithmetic and copies ran while one was open for 4% of the time, Pallas kernels for 0%

commit v1 on v0

v1 whole, which is shorter than its diff:
```python
import jax
import jax.numpy as jnp
from jax import lax
from jax.experimental import pallas as pl
from jax.experimental.pallas import tpu as pltpu
from jax.sharding import Mesh, PartitionSpec as P

HD = 128
HQ = 8
SPAN = 64
LOG2E = 1.4426950408889634
SEQ = ("zhi", "y")
OWN = ("zlo", "zhi", "y")


def nt(a, b):
    return lax.dot_general(a, b, (((1,), (1,)), ((), ())), preferred_element_type=jnp.float32)


def tn(a, b):
    return lax.dot_general(a, b, (((0,), (0,)), ((), ())), preferred_element_type=jnp.float32)


def nn(a, b):
    return jnp.dot(a, b, preferred_element_type=jnp.float32)


def attention_kernel(place_ref, order_ref, lens_ref, q_ref, do_ref, kv_ref, dq_ref, dkv_ref, bias_ref, dk_ref, dv_ref):
    scale = HD ** (-0.5)
    spans = order_ref.shape[1]
    docs = lens_ref.shape[1]
    place = place_ref[0]
    lane = lax.broadcasted_iota(jnp.int32, (1, 2 * SPAN), 1)
    pos_q = jnp.where(
        lane < SPAN,
        order_ref[0, 2 * place] * SPAN + lane,
        order_ref[0, 2 * place + 1] * SPAN + lane - SPAN,
    )
    start = jnp.zeros_like(pos_q)
    end = jnp.int32(0)
    for i in range(docs):
        end = end + lens_ref[0, i]
        start = jnp.where(pos_q >= end, end, start)
    row = lax.broadcasted_iota(jnp.int32, (SPAN, 2 * SPAN), 0)
    for s in range(spans):
        pos_k = order_ref[0, s] * SPAN + row
        allowed = (pos_k <= pos_q) & (pos_k >= start)
        bias_ref[s * SPAN : (s + 1) * SPAN, :] = jnp.where(allowed, 0.0, -jnp.inf)
    k = kv_ref[:, :HD]
    v = kv_ref[:, HD:]
    for h in range(0, HQ, 2):
        a, b, c = h * HD, (h + 1) * HD, (h + 2) * HD
        q2 = jnp.concatenate([q_ref[:, a:b], q_ref[:, b:c]], axis=0)
        d2 = jnp.concatenate([do_ref[:, a:b], do_ref[:, b:c]], axis=0)
        bias = bias_ref[...]
        s2 = nt(k, q2) + jnp.concatenate([bias, bias], axis=1)
        peak = jnp.max(s2, axis=0, keepdims=True)
        expo = jnp.exp2((s2 - peak) * (scale * LOG2E))
        inverse = 1.0 / jnp.sum(expo, axis=0, keepdims=True)
        probs = expo * inverse
        low = probs.astype(jnp.bfloat16)
        dp = nt(v, d2)
        delta = jnp.sum(low.astype(jnp.float32) * dp, axis=0, keepdims=True)
        ds = (probs * ((dp - delta) * scale)).astype(jnp.bfloat16)
        dv = nn(low, d2)
        dk = nn(ds, q2)
        if h == 0:
            dv_ref[...] = dv
            dk_ref[...] = dk
        elif h < HQ - 2:
            dv_ref[...] += dv
            dk_ref[...] += dk
        else:
            dkv_ref[:, HD:] = (dv_ref[...] + dv).astype(jnp.bfloat16)
            dkv_ref[:, :HD] = (dk_ref[...] + dk).astype(jnp.bfloat16)
        dq = tn(ds, k).astype(jnp.bfloat16)
        dq_ref[:, a:b] = dq[:HD]
        dq_ref[:, b:c] = dq[HD:]


def attention(place, order, lens, query, grad, key_value):
    tokens = query.shape[0]
    total = key_value.shape[0]
    smem = pl.BlockSpec(memory_space=pltpu.SMEM)
    vmem = pl.BlockSpec(memory_space=pltpu.VMEM)
    return pl.pallas_call(
        attention_kernel,
        out_shape=(
            jax.ShapeDtypeStruct((tokens, HQ * HD), jnp.bfloat16),
            jax.ShapeDtypeStruct((total, 2 * HD), jnp.bfloat16),
        ),
        in_specs=[smem, smem, smem, vmem, vmem, vmem],
        out_specs=(vmem, vmem),
        scratch_shapes=[
            pltpu.VMEM((total, tokens), jnp.float32),
            pltpu.VMEM((total, HD), jnp.float32),
            pltpu.VMEM((total, HD), jnp.float32),
        ],
        compiler_params=pltpu.CompilerParams(vmem_limit_bytes=24 * 1024 * 1024),
        cost_estimate=pl.CostEstimate(flops=2 * 10**9, bytes_accessed=4 * 10**6, transcendentals=10**6),
        name="attention",
    )(place, order, lens, query, grad, key_value)


def shifted(value, s):
    n = lax.axis_size("x")
    return lax.ppermute(value, "x", [(i, (i + s) % n) for i in range(n)])


def swapped(value):
    return lax.ppermute(value, "core", [(0, 1), (1, 0)])


def gather_chips(value):
    mine = jnp.concatenate([value] + [shifted(value, s) for s in range(1, lax.axis_size("x"))], axis=0)
    return mine, swapped(mine)


def local(layer_input, w_qkv, d_out, span_order, doc_lengths):
    rows = layer_input[0]
    tokens, features = rows.shape
    chips = lax.axis_size("x")
    zlos = lax.axis_size("zlo")
    at_x = lax.axis_index("x")
    at_core = lax.axis_index("core")
    seq = lax.axis_size("zhi") * lax.axis_size("y")
    place = lax.axis_index("zhi") * lax.axis_size("y") + lax.axis_index("y")
    width = features // (zlos * chips * 2)

    parts = rows.reshape(tokens, zlos, chips, 2 * width)
    pieces = []
    for s in range(chips):
        piece = lax.dynamic_index_in_dim(parts, (at_x + s) % chips, 2, keepdims=False)
        pieces.append(shifted(piece, s) if s else piece)
    pieces = jnp.stack(pieces).reshape(chips * tokens, zlos, 2, width)
    rows_own = lax.dynamic_index_in_dim(pieces, at_core, 2, keepdims=False).reshape(chips * tokens, zlos * width)
    rows_send = lax.dynamic_index_in_dim(pieces, 1 - at_core, 2, keepdims=False).reshape(chips * tokens, zlos * width)
    rows_other = swapped(rows_send)

    key_value = nn(rows, w_qkv[:, HQ * HD :]).astype(jnp.bfloat16)
    copies = jnp.broadcast_to(key_value[None], (seq, tokens, 2 * HD))
    gathered = lax.all_to_all(copies, SEQ, 0, 0, tiled=True).reshape(seq * tokens, 2 * HD)
    query = nn(rows, w_qkv[:, : HQ * HD]).astype(jnp.bfloat16)
    d_query, terms = attention(place[None], span_order, doc_lengths, query, d_out[0], gathered)
    arrived = lax.all_to_all(terms.reshape(seq, tokens, 2 * HD), SEQ, 0, 0, tiled=True)
    owned = jnp.sum(arrived.astype(jnp.float32), axis=0).astype(jnp.bfloat16)

    q_own, q_other = gather_chips(d_query)
    kv_own, kv_other = gather_chips(owned)
    grad_q = (tn(rows_own, q_own) + tn(rows_other, q_other)).astype(jnp.bfloat16)
    grad_kv = (tn(rows_own, kv_own) + tn(rows_other, kv_other)).astype(jnp.bfloat16)
    term = jnp.concatenate([grad_q, grad_kv], axis=1)
    owners = zlos * seq
    received = lax.all_to_all(term.reshape(owners, -1, term.shape[1]), OWN, 0, 0, tiled=True)
    d_w = jnp.sum(received.astype(jnp.float32), axis=0)

    d_qkv = jnp.concatenate([d_query, owned], axis=1)
    d_rows = nt(d_qkv, w_qkv).astype(jnp.bfloat16)
    return (d_rows[None], d_w)


def solution(mesh):
    fine = Mesh(mesh.devices.reshape(2, 4, 2, 2, 4), ("zlo", "x", "core", "zhi", "y"))
    dp, ctx = ("zlo", "x", "core"), ("zhi", "y")
    placed = (P(dp, ctx, None), P(), P(dp, ctx, None), P(dp, None), P(dp, None))
    return jax.shard_map(
        local,
        mesh=fine,
        in_specs=placed,
        out_specs=(P(dp, ctx, None), P(dp + ctx, None)),
        check_vma=False,
    )
```

time: 355 us -> 158 us (0.45)
  waiting for transfers between devices: 250 us -> 43.4 us
  blocking collectives: 36.5 us -> 0 us
  starting transfers between devices: 0.3 us -> 30.7 us
  local copies, waits for them, and re-layouts: 10.5 us -> 39.1 us
  between operations: 13.9 us -> 0.89 us
  matrix products: 39.3 us -> 31.8 us
  Pallas kernels: 0 us -> 6.31 us
    unnamed x5 -> x0, waiting for transfers between devices: 132 us -> none
    reduce_scatter x1 -> x0, waiting for transfers between devices: 118 us -> none  [local(): lax.psum_scatter(lax.dot_general(rows, d_qkv, (((0,), (0,)), ((), ())), p...]
    all_gather x1 -> x0, blocking collectives: 36.5 us -> none  [local(): gathered = lax.all_gather(key_value, 'ctx', axis=0, tiled=True)]
    all_to_all x0 -> x3, waiting for transfers between devices: none -> 36.3 us  [the longest x1 30.4 us: local(): lax.all_to_all(term.reshape(owners, -1, term.shape[1]), OWN, 0, 0, tiled=...]
    dynamic_slice x0 -> x8, local copies, waits for them, and re-layouts: none -> 23.7 us  [the longest x2 8.96 us: local(): lax.dynamic_index_in_dim(pieces, at_core, 2, keepdims=False)]
    all_to_all x0 -> x3, starting transfers between devices: none -> 17.6 us  [the longest x1 7.78 us: local(): lax.all_to_all(copies, SEQ, 0, 0, tiled=True).reshape(seq * tokens, 2 * HD)]
    ppermute x0 -> x12, starting transfers between devices: none -> 13.1 us  [the longest x9 13.1 us: shifted(): return lax.ppermute(value, 'x', [(i, (i + s) % n) for i in range(n)])]
    ppermute x0 -> x12, waiting for transfers between devices: none -> 7.18 us  [the longest x9 7.17 us: shifted(): return lax.ppermute(value, 'x', [(i, (i + s) % n) for i in range(n)])]
  transfers between devices with their start and end apart: 3 -> 15, of which waited for: 3 -> 7; matrix products, arithmetic and copies ran while one was open for 4% -> 37% of each run, Pallas kernels for 0% -> 4%
where the time goes in v1:
time: 158 us; the launch traced here: 156 us
  waiting for transfers between devices  43.4 us (27%)
  local copies, waits for them, and re-layouts  39.1 us (25%)
  matrix products  31.8 us (20%)
  starting transfers between devices  30.7 us (19%)
  Pallas kernels  6.31 us (4%)
  other arithmetic  3.74 us (2%)
    all_to_all x1, waiting for transfers between devices, local(): lax.all_to_all(term.reshape(owners, -1, term.shape[1]), OWN, 0, 0, tiled=...  30.4 us
    ppermute x9, starting transfers between devices, shifted(): return lax.ppermute(value, 'x', [(i, (i + s) % n) for i in range(n)])  13.1 us
    dot_general x1, matrix products, nt(): lax.dot_general(a, b, (((1,), (1,)), ((), ())), preferred_element_type=jn...  11.9 us
    dot_general x2, matrix products, nn(): return jnp.dot(a, b, preferred_element_type=jnp.float32)  11.3 us
    dynamic_slice x2, local copies, waits for them, and re-layouts, local(): lax.dynamic_index_in_dim(pieces, at_core, 2, keepdims=False)  8.96 us
    dynamic_slice x5, local copies, waits for them, and re-layouts, local(): lax.dynamic_index_in_dim(parts, (at_x + s) % chips, 2, keepdims=False)  8.87 us
    dot_general x4, matrix products, tn(): lax.dot_general(a, b, (((0,), (0,)), ((), ())), preferred_element_type=jn...  8.58 us
    all_to_all x1, starting transfers between devices, local(): lax.all_to_all(copies, SEQ, 0, 0, tiled=True).reshape(seq * tokens, 2 * HD)  7.78 us
  transfers between devices with their start and end apart: 15, of which 7 were waited for; matrix products, arithmetic and copies ran while one was open for 37% of the time, Pallas kernels for 4%

profile of v1, /device:TPU:0, one launch (start us, length us, event | category | flops | bytes accessed | tf_op | source)
XLA Modules:
  0.0 155.9 jit_solution(15296750348798900496)
XLA Ops:
  0.7 3.2 %copy.8 = bf16[1,128,8192]{1,2,0:T(8,128)(2,1)S(1)} copy(bf16[1,128,8192]{2,1,0:T(8,128)(2,1)} %param.5) | data formatting | bytes 4194304 | tf_op args[0]
  3.9 1.4 constant_dynamic-slice_fusion.5
  5.3 2.2 %copy.11 = bf16[128,2,1,1024]{3,0,2,1:T(8,128)(2,1)} copy(bf16[128,2,1,1024]{0,3,2,1:T(8,128)(2,1)} %get-tuple-element.10) | data formatting | bytes 1048576 | tf_op jit(solution)/shard_map/jit(dynamic_index_in_dim)/dynamic_slice | solution.py:133
  7.5 3.1 %collective-permute-start.1 = (bf16[128,2,1024]{2,0,1:T(8,128)(2,1)}, bf16[128,2,1024]{2,0,1:T(8,128)(2,1)}, u32[]{:S(2)}, u32[]{:S(2)}) collective-permute-start(bf16[128,2,1024]{2,0,1:T(8,128)(2,1)} %bitcast.10), channel_id=1, source_target_pairs={{0,32},{16,48},{32,0},{48,16},{1,33},{17,49},{33,1},{49,17},{2,34}... | collective-permute-start | bytes 1572872 | tf_op jit(solution)/shard_map/ppermute | solution.py:107
  10.6 2.0 %copy.12 = bf16[128,2,1,1024]{3,0,2,1:T(8,128)(2,1)} copy(bf16[128,2,1,1024]{0,3,2,1:T(8,128)(2,1)} %get-tuple-element.9) | data formatting | bytes 1048576 | tf_op jit(solution)/shard_map/jit(dynamic_index_in_dim)/dynamic_slice | solution.py:133
  12.6 1.1 collective-permute-start.2
  13.8 2.0 %copy.10 = bf16[128,2,1,1024]{3,0,2,1:T(8,128)(2,1)} copy(bf16[128,2,1,1024]{0,3,2,1:T(8,128)(2,1)} %get-tuple-element.11) | data formatting | bytes 1048576 | tf_op jit(solution)/shard_map/jit(dynamic_index_in_dim)/dynamic_slice | solution.py:133
  15.8 0.9 collective-permute-start
  16.7 3.0 %fusion.13 = bf16[128,256]{1,0:T(8,128)(2,1)S(1)} fusion(bf16[8192,1280]{1,0:T(8,128)(2,1)} %param.6, bf16[1,128,8192]{2,1,0:T(8,128)(2,1)S(1)} %copy-done.4), kind=kOutput, calls=%fused_computation.15 | convolution fusion | flops 536903680 | bytes 6356992 | tf_op jit(solution)/shard_map/dot_general | solution.py:25
  19.7 0.8 broadcast_in_dim.13
  20.5 7.8 %all-to-all-start = ((bf16[8,128,256]{2,1,0:T(8,128)(2,1)}), bf16[8,128,256]{2,1,0:T(8,128)(2,1)S(1)}, u32[]{:S(2)}, u32[]{:S(2)}) async-start(bf16[8,128,256]{2,1,0:T(8,128)(2,1)} %broadcast_in_dim.13), calls=%async_computation | async-start | bytes 1048576 | tf_op jit(solution)/shard_map/all_to_all | solution.py:142
  28.3 8.3 %fusion.8.q_ref = bf16[128,1024]{1,0:T(8,128)(2,1)S(1)} fusion(bf16[8192,1280]{1,0:T(8,128)(2,1)} %param.6, bf16[1,128,8192]{2,1,0:T(8,128)(2,1)S(1)} %copy-done.4), kind=kOutput, calls=%fused_computation.14 | convolution fusion | flops 2147614720 | bytes 19136512 | tf_op jit(solution)/shard_map/dot_general | solution.py:25
  36.6 1.2 copy.9
  37.9 1.1 all-to-all-done
  39.1 6.3 %attention.1 = (bf16[128,1024]{1,0:T(8,128)(2,1)S(1)}, bf16[1024,256]{1,0:T(8,128)(2,1)}) custom-call(s32[1]{0:T(128)} %bitcast.place_ref, s32[1,16]{1,0:T(1,128)S(1)} %copy-done.1, s32[1,4]{1,0:T(1,128)S(1)} %copy-done.2, bf16[128,1024]{1,0:T(8,128)(2,1)S(1)} %fusion.8.q_ref, bf16[128,1024]{1,0:T(8,128)(2,1)S(1)} %bitcast.39, bf16[1024,256]{1,0:T(8,128)(2,1)S(1)} %bitcast.38), custom_call_target="tpu_custom_call" | custom-call | flops 2000000000 | bytes 4000000 | tf_op jit(solution)/shard_map/attention/pallas_call | solution.py:86
  45.4 0.6 collective-permute-start.3
  46.0 1.6 %pad_maximum_fusion.1 = bf16[4,128,2,1024]{3,1,2,0:T(8,128)(2,1)S(1)} fusion(bf16[1,128,2,1024]{3,1,2,0:T(8,128)(2,1)} %bitcast.13, bf16[1,128,2,1024]{3,1,2,0:T(8,128)(2,1)} %bitcast.11, bf16[1,128,2,1024]{3,1,2,0:T(8,128)(2,1)} %bitcast.9, bf16[1,128,2,1024]{3,1,2,0:T(8,128)(2,1)S(1)} %bitcast.44), kind=kLoop, calls=%fused_computation.9 | loop fusion | flops 3145728 | bytes 4194304 | tf_op jit(solution)/shard_map/stack | solution.py:135
  47.6 1.5 copy.13
  49.1 3.3 %reshape.28 = bf16[512,2,2,512]{3,2,0,1:T(2,128)(2,1)S(1)} reshape(bf16[4,128,2,1024]{3,1,0,2:T(8,128)(2,1)} %copy.13) | data formatting | bytes 4194304 | tf_op jit(solution)/shard_map/reshape | solution.py:135
  52.4 6.3 %constant_dynamic-slice_fusion.1 = (bf16[512,2,1,512]{3,2,0,1:T(2,128)(2,1)}, bf16[512,2,1,512]{3,2,0,1:T(2,128)(2,1)}) fusion(bf16[512,2,2,512]{3,2,0,1:T(2,128)(2,1)S(1)} %reshape.28, s32[]{:T(128)S(6)} %select_n.47, s32[]{:T(128)S(6)} %select_n.48), kind=kLoop, calls=%fused_computation.25 | loop fusion | bytes 4194312 | tf_op jit(solution)/shard_map/jit(dynamic_index_in_dim)/dynamic_slice | solution.py:136
  58.8 5.8 %copy.15 = bf16[512,2,1,512]{0,3,1,2:T(8,128)(2,1)} copy(bf16[512,2,1,512]{3,2,0,1:T(2,128)(2,1)} %get-tuple-element.7) | data formatting | bytes 2097152 | tf_op jit(solution)/shard_map/jit(dynamic_index_in_dim)/dynamic_slice | solution.py:137
  64.6 3.2 %collective-permute-start.4 = (bf16[128,1024]{1,0:T(8,128)(2,1)S(1)}, bf16[128,1024]{1,0:T(8,128)(2,1)}, u32[]{:S(2)}, u32[]{:S(2)}) collective-permute-start(bf16[128,1024]{1,0:T(8,128)(2,1)S(1)} %get-tuple-element.4), channel_id=1, source_target_pairs={{0,32},{16,48},{32,0},{48,16},{1,33},{17,49},{33,1},{49,17},{2,34}... | collective-permute-start | bytes 786440 | tf_op jit(solution)/shard_map/ppermute | solution.py:107
  67.8 6.1 %all-to-all-start.1 = ((bf16[8,128,256]{2,1,0:T(8,128)(2,1)}), bf16[8,128,256]{2,1,0:T(8,128)(2,1)S(1)}, u32[]{:S(2)}, u32[]{:S(2)}) async-start(bf16[8,128,256]{2,1,0:T(8,128)(2,1)} %bitcast.4), calls=%async_computation.1 | async-start | bytes 1048576 | tf_op jit(solution)/shard_map/all_to_all | solution.py:145
  73.9 0.7 constant_dynamic-update-slice_fusion.3
  74.6 0.7 constant_dynamic-update-slice_fusion.2
  75.3 1.7 %constant_dynamic-update-slice_fusion.1 = bf16[512,1024]{1,0:T(8,128)(2,1)} fusion(bf16[512,1024]{1,0:T(8,128)(2,1)} %constant_dynamic-update-slice_fusion.2, bf16[128,1024]{1,0:T(8,128)(2,1)} %collective-permute-done.4), kind=kLoop, calls=%fused_computation.21 | loop fusion | bytes 524288
  77.0 3.4 %collective-permute-done.5 = bf16[128,1024]{1,0:T(8,128)(2,1)S(1)} collective-permute-done((bf16[128,1024]{1,0:T(8,128)(2,1)S(1)}, bf16[128,1024]{1,0:T(8,128)(2,1)S(1)}, u32[]{:S(2)}, u32[]{:S(2)}) %collective-permute-start.5) | collective-permute-done | bytes 262176 | tf_op jit(solution)/shard_map/ppermute | solution.py:107
  80.4 0.7 constant_dynamic-update-slice_fusion
  81.2 4.7 %all-to-all-done.1 = bf16[8,128,256]{2,1,0:T(8,128)(2,1)S(1)} async-done(((bf16[8,128,256]{2,1,0:T(8,128)(2,1)}), bf16[8,128,256]{2,1,0:T(8,128)(2,1)S(1)}, u32[]{:S(2)}, u32[]{:S(2)}) %all-to-all-start.1) | async-done | bytes 524320 | tf_op jit(solution)/shard_map/all_to_all | solution.py:145
  85.9 0.1 reduce_sum.21
  86.0 0.7 collective-permute-start.10
  86.6 1.4 collective-permute-start.8
  88.1 2.1 %collective-permute-start.9 = (bf16[128,256]{1,0:T(8,128)(2,1)S(1)}, bf16[128,256]{1,0:T(8,128)(2,1)S(1)}, u32[]{:S(2)}, u32[]{:S(2)}) collective-permute-start(bf16[128,256]{1,0:T(8,128)(2,1)S(1)} %reduce_sum.21), channel_id=1, source_target_pairs={{0,32},{16,48},{32,0},{48,16},{1,33},{17,49},{33,1},{49,17},{2,34}... | collective-permute-start | bytes 196616 | tf_op jit(solution)/shard_map/ppermute | solution.py:107
  90.1 0.2 collective-permute-done.10
  90.3 2.5 %collective-permute-done.8 = bf16[128,256]{1,0:T(8,128)(2,1)S(1)} collective-permute-done((bf16[128,256]{1,0:T(8,128)(2,1)S(1)}, bf16[128,256]{1,0:T(8,128)(2,1)S(1)}, u32[]{:S(2)}, u32[]{:S(2)}) %collective-permute-start.8) | collective-permute-done | bytes 65568 | tf_op jit(solution)/shard_map/ppermute | solution.py:107
  92.8 1.1 collective-permute-done.9
  93.8 0.7 pad_maximum_fusion.2
  94.6 2.6 %copy.14 = bf16[512,2,1,512]{0,3,1,2:T(8,128)(2,1)S(1)} copy(bf16[512,2,1,512]{3,2,0,1:T(2,128)(2,1)S(1)} %copy-done.3) | data formatting | bytes 2097152 | tf_op jit(solution)/shard_map/jit(dynamic_index_in_dim)/dynamic_slice | solution.py:136
  97.2 1.7 %fusion.23 = f32[1024,256]{0,1:T(8,128)S(1)} fusion(bf16[512,1024]{0,1:T(8,128)(2,1)} %collective-permute-done.6, bf16[512,256]{1,0:T(8,128)(2,1)} %collective-permute-done.11), kind=kOutput, calls=%fused_computation.32 | convolution fusion | flops 268435456 | bytes 2359296 | tf_op jit(solution)/shard_map/dot_general | solution.py:21
  99.0 1.4 fusion.7
  100.3 2.9 %fusion.22 = f32[1024,1024]{0,1:T(8,128)S(1)} fusion(bf16[512,1024]{0,1:T(8,128)(2,1)} %collective-permute-done.6, bf16[512,1024]{1,0:T(8,128)(2,1)} %collective-permute-done.7), kind=kOutput, calls=%fused_computation.31 | convolution fusion | flops 1073741824 | bytes 6291456 | tf_op jit(solution)/shard_map/dot_general | solution.py:21
  103.2 2.6 %add_convert_fusion = bf16[1024,1024]{0,1:T(8,128)(2,1)S(1)} fusion(f32[1024,1024]{0,1:T(8,128)S(1)} %fusion.22, bf16[512,1024]{0,1:T(8,128)(2,1)S(1)} %bitcast.42, bf16[512,1024]{1,0:T(8,128)(2,1)} %constant_dynamic-update-slice_fusion), kind=kOutput, calls=%fused_computation.5 | convolution fusion | flops 1075838976 | bytes 8388608 | tf_op jit(solution)/shard_map/dot_general | solution.py:21
  105.8 0.2 pad_maximum_fusion
  106.1 2.7 %copy.16 = bf16[1024,1280]{1,0:T(8,128)(2,1)} copy(bf16[1024,1280]{0,1:T(8,128)(2,1)S(1)} %pad_maximum_fusion) | data formatting | bytes 5242880 | tf_op jit(solution)/shard_map/concatenate | solution.py:152
  108.8 3.7 %all-to-all-start.2 = ((bf16[16,64,1280]{2,1,0:T(8,128)(2,1)}), bf16[16,64,1280]{2,1,0:T(8,128)(2,1)S(1)}, u32[]{:S(2)}, u32[]{:S(2)}) async-start(bf16[16,64,1280]{2,1,0:T(8,128)(2,1)} %bitcast.40), calls=%async_computation.2 | async-start | bytes 5242880 | tf_op jit(solution)/shard_map/all_to_all | solution.py:154
  112.5 11.9 %fusion.2 = bf16[1,128,8192]{2,1,0:T(8,128)(2,1)} fusion(bf16[8192,1280]{1,0:T(8,128)(2,1)} %param.6, bf16[128,256]{1,0:T(8,128)(2,1)S(1)} %reduce_sum.21, bf16[128,1024]{1,0:T(8,128)(2,1)S(1)} %get-tuple-element.4), kind=kOutput, calls=%fused_computation.3 | convolution fusion | flops 2686058496 | bytes 23396352 | tf_op jit(solution)/shard_map/dot_general | solution.py:17
  124.5 30.4 %all-to-all-done.2 = bf16[16,64,1280]{2,1,0:T(8,128)(2,1)S(1)} async-done(((bf16[16,64,1280]{2,1,0:T(8,128)(2,1)}), bf16[16,64,1280]{2,1,0:T(8,128)(2,1)S(1)}, u32[]{:S(2)}, u32[]{:S(2)}) %all-to-all-start.2) | async-done | bytes 2621472 | tf_op jit(solution)/shard_map/all_to_all | solution.py:154
  154.9 1.1 convert_reduce_fusion
  (26 shorter events, 0.1 us)
Async XLA Ops:
  5.3 11.4 %copy-start.4 = (bf16[1,128,8192]{2,1,0:T(8,128)(2,1)S(1)}, bf16[1,128,8192]{2,1,0:T(8,128)(2,1)}, u32[]{:S(2)}) copy-start(bf16[1,128,8192]{2,1,0:T(8,128)(2,1)} %param.5) | copy-start | bytes 6291460
  7.5 38.5 %collective-permute-start.1 = (bf16[128,2,1024]{2,0,1:T(8,128)(2,1)}, bf16[128,2,1024]{2,0,1:T(8,128)(2,1)}, u32[]{:S(2)}, u32[]{:S(2)}) collective-permute-start(bf16[128,2,1024]{2,0,1:T(8,128)(2,1)} %bitcast.10), channel_id=1, source_target_pairs={{0,32},{16,48},{32,0},{48,16},{1,33},{17,49},{33,1},{49,17},{2,34}... | collective-permute-start | bytes 1572872 | tf_op jit(solution)/shard_map/ppermute | solution.py:107
  12.6 33.3 %collective-permute-start.2 = (bf16[128,2,1024]{2,0,1:T(8,128)(2,1)}, bf16[128,2,1024]{2,0,1:T(8,128)(2,1)}, u32[]{:S(2)}, u32[]{:S(2)}) collective-permute-start(bf16[128,2,1024]{2,0,1:T(8,128)(2,1)} %bitcast.12), channel_id=1, source_target_pairs={{0,48},{16,0},{32,16},{48,32},{1,49},{17,1},{33,17},{49,33},{2,50}... | collective-permute-start | bytes 1572872 | tf_op jit(solution)/shard_map/ppermute | solution.py:107
  15.8 30.2 %collective-permute-start = (bf16[128,2,1024]{2,0,1:T(8,128)(2,1)}, bf16[128,2,1024]{2,0,1:T(8,128)(2,1)}, u32[]{:S(2)}, u32[]{:S(2)}) collective-permute-start(bf16[128,2,1024]{2,0,1:T(8,128)(2,1)} %bitcast.8), channel_id=1, source_target_pairs={{0,16},{16,32},{32,48},{48,0},{1,17},{17,33},{33,49},{49,1},{2,18}... | collective-permute-start | bytes 1572872 | tf_op jit(solution)/shard_map/ppermute | solution.py:107
  20.5 18.5 %all-to-all-start = ((bf16[8,128,256]{2,1,0:T(8,128)(2,1)}), bf16[8,128,256]{2,1,0:T(8,128)(2,1)S(1)}, u32[]{:S(2)}, u32[]{:S(2)}) async-start(bf16[8,128,256]{2,1,0:T(8,128)(2,1)} %broadcast_in_dim.13), calls=%async_computation | async-start | bytes 1048576 | tf_op jit(solution)/shard_map/all_to_all | solution.py:142
  28.3 10.7 %copy-start = (bf16[1,128,1024]{2,1,0:T(8,128)(2,1)S(1)}, bf16[1,128,1024]{2,1,0:T(8,128)(2,1)}, u32[]{:S(2)}) copy-start(bf16[1,128,1024]{2,1,0:T(8,128)(2,1)} %param.7) | copy-start | bytes 786436
  28.3 10.7 %copy-start.1 = (s32[1,16]{1,0:T(1,128)S(1)}, s32[1,16]{1,0:T(1,128)}, u32[]{:S(2)}) copy-start(s32[1,16]{1,0:T(1,128)} %order_ref.1) | copy-start | bytes 196
  28.3 10.7 %copy-start.2 = (s32[1,4]{1,0:T(1,128)S(1)}, s32[1,4]{1,0:T(1,128)}, u32[]{:S(2)}) copy-start(s32[1,4]{1,0:T(1,128)} %lens_ref.1) | copy-start | bytes 52
  45.4 29.2 %collective-permute-start.3 = (bf16[128,1024]{1,0:T(8,128)(2,1)S(1)}, bf16[128,1024]{1,0:T(8,128)(2,1)S(1)}, u32[]{:S(2)}, u32[]{:S(2)}) collective-permute-start(bf16[128,1024]{1,0:T(8,128)(2,1)S(1)} %get-tuple-element.4), channel_id=1, source_target_pairs={{0,16},{16,32},{32,48},{48,0},{1,17},{17,33},{33,49},{49,1},{2,18}... | collective-permute-start | bytes 786440 | tf_op jit(solution)/shard_map/ppermute | solution.py:107
  64.6 30.0 %copy-start.3 = (bf16[512,2,1,512]{3,2,0,1:T(2,128)(2,1)S(1)}, bf16[512,2,1,512]{3,2,0,1:T(2,128)(2,1)}, u32[]{:S(2)}) copy-start(bf16[512,2,1,512]{3,2,0,1:T(2,128)(2,1)} %get-tuple-element.6) | copy-start | bytes 3145732
  64.6 32.6 %collective-permute-start.6 = (bf16[512,1024]{0,1:T(8,128)(2,1)}, bf16[512,1024]{0,1:T(8,128)(2,1)}, u32[]{:S(2)}, u32[]{:S(2)}) collective-permute-start(bf16[512,1024]{0,1:T(8,128)(2,1)} %bitcast.15), channel_id=1, source_target_pairs={{0,8},{8,0},{1,9},{9,1},{2,10},{10,2},{3,11},{11,3},{4,12},{12,4},... | collective-permute-start | bytes 3145736 | tf_op jit(solution)/shard_map/ppermute | solution.py:111
  64.6 10.7 %collective-permute-start.4 = (bf16[128,1024]{1,0:T(8,128)(2,1)S(1)}, bf16[128,1024]{1,0:T(8,128)(2,1)}, u32[]{:S(2)}, u32[]{:S(2)}) collective-permute-start(bf16[128,1024]{1,0:T(8,128)(2,1)S(1)} %get-tuple-element.4), channel_id=1, source_target_pairs={{0,32},{16,48},{32,0},{48,16},{1,33},{17,49},{33,1},{49,17},{2,34}... | collective-permute-start | bytes 786440 | tf_op jit(solution)/shard_map/ppermute | solution.py:107
  67.8 12.6 %collective-permute-start.5 = (bf16[128,1024]{1,0:T(8,128)(2,1)S(1)}, bf16[128,1024]{1,0:T(8,128)(2,1)S(1)}, u32[]{:S(2)}, u32[]{:S(2)}) collective-permute-start(bf16[128,1024]{1,0:T(8,128)(2,1)S(1)} %get-tuple-element.4), channel_id=1, source_target_pairs={{0,48},{16,0},{32,16},{48,32},{1,49},{17,1},{33,17},{49,33},{2,50}... | collective-permute-start | bytes 786440 | tf_op jit(solution)/shard_map/ppermute | solution.py:107
  67.8 18.1 %all-to-all-start.1 = ((bf16[8,128,256]{2,1,0:T(8,128)(2,1)}), bf16[8,128,256]{2,1,0:T(8,128)(2,1)S(1)}, u32[]{:S(2)}, u32[]{:S(2)}) async-start(bf16[8,128,256]{2,1,0:T(8,128)(2,1)} %bitcast.4), calls=%async_computation.1 | async-start | bytes 1048576 | tf_op jit(solution)/shard_map/all_to_all | solution.py:145
  81.2 19.2 %collective-permute-start.7 = (bf16[512,1024]{1,0:T(8,128)(2,1)}, bf16[512,1024]{1,0:T(8,128)(2,1)}, u32[]{:S(2)}, u32[]{:S(2)}) collective-permute-start(bf16[512,1024]{1,0:T(8,128)(2,1)} %constant_dynamic-update-slice_fusion), channel_id=1, source_target_pairs={{0,8},{8,0},{1,9},{9,1},{2,10},{10,2},{3,11},{11,3},{4,12},{12,4},... | collective-permute-start | bytes 3145736 | tf_op jit(solution)/shard_map/ppermute | solution.py:111
  86.0 4.3 %collective-permute-start.10 = (bf16[128,256]{1,0:T(8,128)(2,1)S(1)}, bf16[128,256]{1,0:T(8,128)(2,1)S(1)}, u32[]{:S(2)}, u32[]{:S(2)}) collective-permute-start(bf16[128,256]{1,0:T(8,128)(2,1)S(1)} %reduce_sum.21), channel_id=1, source_target_pairs={{0,48},{16,0},{32,16},{48,32},{1,49},{17,1},{33,17},{49,33},{2,50}... | collective-permute-start | bytes 196616 | tf_op jit(solution)/shard_map/ppermute | solution.py:107
  86.6 6.1 %collective-permute-start.8 = (bf16[128,256]{1,0:T(8,128)(2,1)S(1)}, bf16[128,256]{1,0:T(8,128)(2,1)S(1)}, u32[]{:S(2)}, u32[]{:S(2)}) collective-permute-start(bf16[128,256]{1,0:T(8,128)(2,1)S(1)} %reduce_sum.21), channel_id=1, source_target_pairs={{0,16},{16,32},{32,48},{48,0},{1,17},{17,33},{33,49},{49,1},{2,18}... | collective-permute-start | bytes 196616 | tf_op jit(solution)/shard_map/ppermute | solution.py:107
  88.1 5.8 %collective-permute-start.9 = (bf16[128,256]{1,0:T(8,128)(2,1)S(1)}, bf16[128,256]{1,0:T(8,128)(2,1)S(1)}, u32[]{:S(2)}, u32[]{:S(2)}) collective-permute-start(bf16[128,256]{1,0:T(8,128)(2,1)S(1)} %reduce_sum.21), channel_id=1, source_target_pairs={{0,32},{16,48},{32,0},{48,16},{1,33},{17,49},{33,1},{49,17},{2,34}... | collective-permute-start | bytes 196616 | tf_op jit(solution)/shard_map/ppermute | solution.py:107
  92.8 1.8 %copy-start.5 = (bf16[128,256]{1,0:T(8,128)(2,1)}, bf16[128,256]{1,0:T(8,128)(2,1)S(1)}, u32[]{:S(2)}) copy-start(bf16[128,256]{1,0:T(8,128)(2,1)S(1)} %collective-permute-done.8) | copy-start | bytes 196612
  93.8 0.7 copy-start.6
  94.5 2.6 %collective-permute-start.11 = (bf16[512,256]{1,0:T(8,128)(2,1)}, bf16[512,256]{1,0:T(8,128)(2,1)}, u32[]{:S(2)}, u32[]{:S(2)}) collective-permute-start(bf16[512,256]{1,0:T(8,128)(2,1)} %pad_maximum_fusion.2), channel_id=1, source_target_pairs={{0,8},{8,0},{1,9},{9,1},{2,10},{10,2},{3,11},{11,3},{4,12},{12,4},... | collective-permute-start | bytes 786440 | tf_op jit(solution)/shard_map/ppermute | solution.py:111
  108.8 46.1 %all-to-all-start.2 = ((bf16[16,64,1280]{2,1,0:T(8,128)(2,1)}), bf16[16,64,1280]{2,1,0:T(8,128)(2,1)S(1)}, u32[]{:S(2)}, u32[]{:S(2)}) async-start(bf16[16,64,1280]{2,1,0:T(8,128)(2,1)} %bitcast.40), calls=%async_computation.2 | async-start | bytes 5242880 | tf_op jit(solution)/shard_map/all_to_all | solution.py:154

commit v2 on v1

v2 whole, which is shorter than its diff:
```python
import jax
import jax.numpy as jnp
from jax import lax
from jax.experimental import pallas as pl
from jax.experimental.pallas import tpu as pltpu
from jax.sharding import Mesh, PartitionSpec as P

HD = 128
HQ = 8
SPAN = 64
LOG2E = 1.4426950408889634
SEQ = ("zhi", "y")
OWN = ("zlo", "zhi", "y")


def nt(a, b):
    return lax.dot_general(a, b, (((1,), (1,)), ((), ())), preferred_element_type=jnp.float32)


def tn(a, b):
    return lax.dot_general(a, b, (((0,), (0,)), ((), ())), preferred_element_type=jnp.float32)


def nn(a, b):
    return jnp.dot(a, b, preferred_element_type=jnp.float32)


SMEM = pl.BlockSpec(memory_space=pltpu.SMEM)
VMEM = pl.BlockSpec(memory_space=pltpu.VMEM)
MIB = 1024 * 1024


def project_kernel(x_ref, w_ref, out_ref, acc_ref):
    step = pl.program_id(0)
    part = nn(x_ref[...], w_ref[...])

    @pl.when(step == 0)
    def _():
        acc_ref[...] = part

    @pl.when(step > 0)
    def _():
        acc_ref[...] += part

    @pl.when(step == pl.num_programs(0) - 1)
    def _():
        low = acc_ref[...].astype(jnp.bfloat16)
        if len(out_ref.shape) == 3:
            for i in range(out_ref.shape[0]):
                out_ref[i] = low
        else:
            out_ref[...] = low


def project(x, w, first, width, copies, depth, name):
    tokens, features = x.shape
    shape = (copies, tokens, width) if copies else (tokens, width)
    return pl.pallas_call(
        project_kernel,
        grid=(features // depth,),
        out_shape=jax.ShapeDtypeStruct(shape, jnp.bfloat16),
        in_specs=[
            pl.BlockSpec((tokens, depth), lambda i: (0, i)),
            pl.BlockSpec((depth, width), lambda i: (i, first)),
        ],
        out_specs=pl.BlockSpec(shape, lambda i: (0,) * len(shape)),
        scratch_shapes=[pltpu.VMEM((tokens, width), jnp.float32)],
        compiler_params=pltpu.CompilerParams(vmem_limit_bytes=60 * MIB),
        cost_estimate=pl.CostEstimate(
            flops=2 * tokens * features * width, bytes_accessed=2 * features * (width + tokens), transcendentals=0
        ),
        name=name,
    )(x, w)


def pack_kernel(where_ref, x_ref, *out_refs):
    chips = len(out_refs)
    features = x_ref.shape[1]
    width = features // (4 * chips)
    for s in range(chips):
        chip = lax.rem(where_ref[0] + s, chips)
        for c in range(2):
            for z in range(2):
                at = pl.multiple_of(z * (features // 2) + chip * 2 * width + c * width, width)
                out_refs[s][(2 * c + z) * width : (2 * c + z + 1) * width, :] = x_ref[:, pl.ds(at, width)].T


def pack(where, x, chips):
    tokens, features = x.shape
    shape = jax.ShapeDtypeStruct((features // chips, tokens), x.dtype)
    return pl.pallas_call(
        pack_kernel,
        out_shape=(shape,) * chips,
        in_specs=[SMEM, VMEM],
        out_specs=(VMEM,) * chips,
        compiler_params=pltpu.CompilerParams(vmem_limit_bytes=16 * MIB),
        cost_estimate=pl.CostEstimate(flops=0, bytes_accessed=4 * tokens * features, transcendentals=0),
        name="pack",
    )(where, x)


def send_kernel(where_ref, *refs):
    pieces, out_ref, sem = refs[:-2], refs[-2], refs[-1]
    half = pieces[0].shape[0] // 2
    at = pl.multiple_of((1 - where_ref[1]) * half, half)
    copies = [pltpu.make_async_copy(piece.at[pl.ds(at, half), :], out_ref.at[i], sem.at[i]) for i, piece in enumerate(pieces)]
    for copy in copies:
        copy.start()
    for copy in copies:
        copy.wait()


def send_half(where, pieces):
    rows, tokens = pieces[0].shape
    n = len(pieces)
    anywhere = pl.BlockSpec(memory_space=pl.ANY)
    return pl.pallas_call(
        send_kernel,
        out_shape=jax.ShapeDtypeStruct((n, rows // 2, tokens), pieces[0].dtype),
        in_specs=[SMEM] + [anywhere] * n,
        out_specs=anywhere,
        scratch_shapes=[pltpu.SemaphoreType.DMA((n,))],
        cost_estimate=pl.CostEstimate(flops=0, bytes_accessed=2 * n * rows * tokens, transcendentals=0),
        name="send_half",
    )(where, *pieces)


def attention_kernel(heads, last, where_ref, order_ref, lens_ref, q_ref, do_ref, kv_ref, *refs):
    if last:
        dk_in, dv_in, dq_ref, dkv_ref, bias_ref, dk_ref, dv_ref = refs
    else:
        dq_ref, dk_ref, dv_ref, bias_ref = refs
    scale = HD ** (-0.5)
    spans = order_ref.shape[1]
    docs = lens_ref.shape[1]
    place = where_ref[2]
    lane = lax.broadcasted_iota(jnp.int32, (1, 2 * SPAN), 1)
    pos_q = jnp.where(
        lane < SPAN,
        order_ref[0, 2 * place] * SPAN + lane,
        order_ref[0, 2 * place + 1] * SPAN + lane - SPAN,
    )
    start = jnp.zeros_like(pos_q)
    end = jnp.int32(0)
    for i in range(docs):
        end = end + lens_ref[0, i]
        start = jnp.where(pos_q >= end, end, start)
    row = lax.broadcasted_iota(jnp.int32, (SPAN, 2 * SPAN), 0)
    for s in range(spans):
        pos_k = order_ref[0, s] * SPAN + row
        allowed = (pos_k <= pos_q) & (pos_k >= start)
        bias_ref[s * SPAN : (s + 1) * SPAN, :] = jnp.where(allowed, 0.0, -jnp.inf)
    k = kv_ref[:, :HD]
    v = kv_ref[:, HD:]
    for h in heads:
        a, b, c = h * HD, (h + 1) * HD, (h + 2) * HD
        q2 = jnp.concatenate([q_ref[:, a:b], q_ref[:, b:c]], axis=0)
        d2 = jnp.concatenate([do_ref[:, a:b], do_ref[:, b:c]], axis=0)
        bias = bias_ref[...]
        s2 = nt(k, q2) + jnp.concatenate([bias, bias], axis=1)
        peak = jnp.max(s2, axis=0, keepdims=True)
        expo = jnp.exp2((s2 - peak) * (scale * LOG2E))
        inverse = 1.0 / jnp.sum(expo, axis=0, keepdims=True)
        probs = expo * inverse
        low = probs.astype(jnp.bfloat16)
        dp = nt(v, d2)
        delta = jnp.sum(low.astype(jnp.float32) * dp, axis=0, keepdims=True)
        ds = (probs * ((dp - delta) * scale)).astype(jnp.bfloat16)
        dq = tn(ds, k).astype(jnp.bfloat16)
        o = (h - heads[0]) * HD
        dq_ref[:, o : o + HD] = dq[:HD]
        dq_ref[:, o + HD : o + 2 * HD] = dq[HD:]
        dv = nn(low, d2)
        dk = nn(ds, q2)
        if h == heads[0] and not last:
            dv_ref[...] = dv
            dk_ref[...] = dk
        else:
            if h == heads[0]:
                dv += dv_in[...]
                dk += dk_in[...]
            else:
                dv += dv_ref[...]
                dk += dk_ref[...]
            if h == heads[-1] and last:
                dkv_ref[:, :HD] = dk.astype(jnp.bfloat16)
                dkv_ref[:, HD:] = dv.astype(jnp.bfloat16)
            else:
                dv_ref[...] = dv
                dk_ref[...] = dk


def attention(heads, where, order, lens, query, grad, key_value, carried=()):
    tokens = query.shape[0]
    total = key_value.shape[0]
    last = bool(carried)
    count = len(heads) * 2
    sums = [jax.ShapeDtypeStruct((total, HD), jnp.float32)] * 2
    outs = [jax.ShapeDtypeStruct((tokens, count * HD), jnp.bfloat16)]
    outs += [jax.ShapeDtypeStruct((total, 2 * HD), jnp.bfloat16)] if last else sums
    scratch = [pltpu.VMEM((total, tokens), jnp.float32)]
    if last:
        scratch += [pltpu.VMEM((total, HD), jnp.float32)] * 2
    work = count * tokens * total
    return pl.pallas_call(
        lambda *refs: attention_kernel(heads, last, *refs),
        out_shape=tuple(outs),
        in_specs=[SMEM, SMEM, SMEM, VMEM, VMEM, VMEM] + [VMEM] * len(carried),
        out_specs=(VMEM,) * len(outs),
        scratch_shapes=scratch,
        compiler_params=pltpu.CompilerParams(vmem_limit_bytes=24 * MIB),
        cost_estimate=pl.CostEstimate(flops=10 * work * HD, bytes_accessed=4 * 10**6, transcendentals=work),
        name="attention_last" if last else "attention_first",
    )(where, order, lens, query, grad, key_value, *carried)


def term_kernel(chips, where_ref, *refs):
    x_own, x_other = refs[:chips], refs[chips]
    g_own, g_other = refs[chips + 1 : 2 * chips + 1], refs[2 * chips + 1 : 3 * chips + 1]
    out_ref = refs[-1]
    half = x_own[0].shape[0] // 2
    at = pl.multiple_of(where_ref[1] * half, half)
    left = [x[pl.ds(at, half), :] for x in x_own] + [x_other[i] for i in range(chips)]
    right = [g[...] for g in g_own] + [g[...] for g in g_other]
    out_ref[...] = nn(jnp.concatenate(left, axis=1), jnp.concatenate(right, axis=0)).astype(out_ref.dtype)


def term(where, x_own, x_other, g_own, g_other, name):
    chips = len(x_own)
    half, tokens = x_other.shape[1:]
    width = g_own[0].shape[1]
    return pl.pallas_call(
        lambda *refs: term_kernel(chips, *refs),
        out_shape=jax.ShapeDtypeStruct((half, width), jnp.bfloat16),
        in_specs=[SMEM] + [VMEM] * (3 * chips + 1),
        out_specs=VMEM,
        compiler_params=pltpu.CompilerParams(vmem_limit_bytes=24 * MIB),
        cost_estimate=pl.CostEstimate(
            flops=4 * chips * tokens * half * width, bytes_accessed=2 * half * width, transcendentals=0
        ),
        name=name,
    )(where, *x_own, x_other, *g_own, *g_other)


def shifted(value, s):
    n = lax.axis_size("x")
    return lax.ppermute(value, "x", [(i, (i + s) % n) for i in range(n)])


def swapped(value):
    return lax.ppermute(value, "core", [(0, 1), (1, 0)])


def gather_chips(value):
    own = [value] + [shifted(value, s) for s in range(1, lax.axis_size("x"))]
    return own, [swapped(piece) for piece in own]


def after(value, *others):
    return lax.optimization_barrier((value,) + others)[0]


def to_owners(value):
    owners = lax.axis_size("zlo") * lax.axis_size("zhi") * lax.axis_size("y")
    blocks = value.reshape(owners, value.shape[0] // owners, value.shape[1])
    return lax.all_to_all(blocks, OWN, 0, 0, tiled=True)


def local(layer_input, w_qkv, d_out, span_order, doc_lengths):
    rows = layer_input[0]
    tokens = rows.shape[0]
    chips = lax.axis_size("x")
    seq = lax.axis_size("zhi") * lax.axis_size("y")
    where = jnp.stack(
        [lax.axis_index("x"), lax.axis_index("core"), lax.axis_index("zhi") * lax.axis_size("y") + lax.axis_index("y")]
    ).astype(jnp.int32)

    copies = project(rows, w_qkv, HQ // 2, 2 * HD, seq, 2048, "project_kv")
    gathered = lax.all_to_all(copies, SEQ, 0, 0, tiled=True).reshape(seq * tokens, 2 * HD)

    packed = pack(where, after(rows, copies), chips)
    pieces = [packed[0]] + [shifted(packed[s], s) for s in range(1, chips)]

    query = project(after(rows, packed[0]), w_qkv, 0, HQ * HD, 0, 1024, "project_q")
    grad = d_out[0]
    dq_a, dk_a, dv_a = attention((0, 2, 4), where, span_order, doc_lengths, query, grad, gathered)
    own_a, other_a = gather_chips(dq_a)
    sent = send_half(where, [after(piece, dq_a) for piece in pieces])
    x_other = swapped(sent)
    dq_b, terms = attention((6,), where, span_order, doc_lengths, query, after(grad, sent), gathered, (dk_a, dv_a))
    arrived = lax.all_to_all(terms.reshape(seq, tokens, 2 * HD), SEQ, 0, 0, tiled=True)

    term_a = term(where, pieces, x_other, own_a, other_a, "term_a")
    owned = jnp.sum(arrived.astype(jnp.float32), axis=0).astype(jnp.bfloat16)
    ready = after(jnp.concatenate([dq_b, owned], axis=1), term_a)
    own_b, other_b = gather_chips(ready)
    received_a = to_owners(term_a)
    term_b = term(where, pieces, x_other, own_b, other_b, "term_b")
    received_b = to_owners(after(term_b, received_a))
    d_qkv = jnp.concatenate([dq_a, own_b[0]], axis=1)
    d_rows = nt(d_qkv, w_qkv).astype(jnp.bfloat16)
    d_w = jnp.concatenate(
        [jnp.sum(received_a.astype(jnp.float32), axis=0), jnp.sum(received_b.astype(jnp.float32), axis=0)], axis=1
    )
    return (d_rows[None], d_w)


def solution(mesh):
    fine = Mesh(mesh.devices.reshape(2, 4, 2, 2, 4), ("zlo", "x", "core", "zhi", "y"))
    dp, ctx = ("zlo", "x", "core"), ("zhi", "y")
    placed = (P(dp, ctx, None), P(), P(dp, ctx, None), P(dp, None), P(dp, None))
    return jax.shard_map(
        local,
        mesh=fine,
        in_specs=placed,
        out_specs=(P(dp, ctx, None), P(dp + ctx, None)),
        check_vma=False,
    )
```

time: 158 us -> 160 us (1.013)
  Pallas kernels: 6.31 us -> 64 us
  local copies, waits for them, and re-layouts: 39.1 us -> 11.8 us
  matrix products: 31.8 us -> 12 us
  waiting for transfers between devices: 43.4 us -> 29.4 us
  starting transfers between devices: 30.7 us -> 36 us
    pallas_call x1 -> x8, Pallas kernels: 6.31 us -> 64 us  [the longest x1 33.6 us: send_half(): pl.pallas_call(send_kernel, out_shape=jax.ShapeDtypeStruct((n, rows // 2,...]
    dynamic_slice x8 -> x0, local copies, waits for them, and re-layouts: 23.7 us -> none  [the longest x2 8.96 us: local(): lax.dynamic_index_in_dim(pieces, at_core, 2, keepdims=False)]
    dot_general x6 -> x0, matrix products: 19.9 us -> none  [the longest x2 11.3 us: nn(): return jnp.dot(a, b, preferred_element_type=jnp.float32)]
    all_to_all x1 -> x2, waiting for transfers between devices: 30.4 us -> 10.6 us  [to_owners(): return lax.all_to_all(blocks, OWN, 0, 0, tiled=True)]
    unnamed x18 -> x56, local copies, waits for them, and re-layouts: 6.34 us -> 11.8 us
    ppermute x9, waiting for transfers between devices: 7.17 us -> 11.9 us  [shifted(): return lax.ppermute(value, 'x', [(i, (i + s) % n) for i in range(n)])]
    all_to_all x1 -> x2, starting transfers between devices: 3.73 us -> 8.06 us  [to_owners(): return lax.all_to_all(blocks, OWN, 0, 0, tiled=True)]
    concatenate x2 -> x0, local copies, waits for them, and re-layouts: 3.45 us -> none  [the longest x1 2.72 us: local(): term = jnp.concatenate([grad_q, grad_kv], axis=1)]
  transfers between devices with their start and end apart: 15 -> 22, of which waited for: 7 -> 13; matrix products, arithmetic and copies ran while one was open for 37% -> 9% of each run, Pallas kernels for 4% -> 16%
where the time goes in v2:
time: 160 us; the launch traced here: 158 us
  Pallas kernels  64 us (40%)
  starting transfers between devices  36 us (22%)
  waiting for transfers between devices  29.4 us (18%)
  matrix products  12 us (8%)
  local copies, waits for them, and re-layouts  11.8 us (7%)
  other arithmetic  3.73 us (2%)
    pallas_call x1, Pallas kernels, send_half(): pl.pallas_call(send_kernel, out_shape=jax.ShapeDtypeStruct((n, rows // 2,...  33.6 us
    pallas_call x2, Pallas kernels, project(): pl.pallas_call(project_kernel, grid=(features // depth,), out_shape=jax.S...  15.8 us
    ppermute x9, starting transfers between devices, shifted(): return lax.ppermute(value, 'x', [(i, (i + s) % n) for i in range(n)])  12.1 us
    dot_general x1, matrix products, nt(): lax.dot_general(a, b, (((1,), (1,)), ((), ())), preferred_element_type=jn...  12 us
    ppermute x9, waiting for transfers between devices, shifted(): return lax.ppermute(value, 'x', [(i, (i + s) % n) for i in range(n)])  11.9 us
    unnamed x56, local copies, waits for them, and re-layouts  11.8 us
    all_to_all x2, waiting for transfers between devices, to_owners(): return lax.all_to_all(blocks, OWN, 0, 0, tiled=True)  10.6 us
    all_to_all x2, starting transfers between devices, to_owners(): return lax.all_to_all(blocks, OWN, 0, 0, tiled=True)  8.06 us
  transfers between devices with their start and end apart: 22, of which 13 were waited for; matrix products, arithmetic and copies ran while one was open for 9% of the time, Pallas kernels for 16%

profile of v2, /device:TPU:0, one launch (start us, length us, event | category | flops | bytes accessed | tf_op | source)
XLA Modules:
  0.0 157.9 jit_solution(4493072634419135132)
XLA Ops:
  0.6 5.0 %project_kv.1 = bf16[8,128,256]{2,1,0:T(8,128)(2,1)} custom-call(bf16[128,8192]{1,0:T(8,128)(2,1)} %bitcast.12, bf16[8192,1280]{1,0:T(8,128)(2,1)} %w_ref.3), custom_call_target="tpu_custom_call" | custom-call | flops 536870912 | bytes 6291456 | tf_op jit(solution)/shard_map/project_kv/pallas_call | solution.py:58
  5.7 7.9 %all-to-all-start = ((bf16[8,128,256]{2,1,0:T(8,128)(2,1)}), bf16[8,128,256]{2,1,0:T(8,128)(2,1)S(1)}, u32[]{:S(2)}, u32[]{:S(2)}) async-start(bf16[8,128,256]{2,1,0:T(8,128)(2,1)} %project_kv.1), calls=%async_computation | async-start | bytes 1048576 | tf_op jit(solution)/shard_map/all_to_all | solution.py:279
  13.6 2.0 %pack.1 = (bf16[2048,128]{1,0:T(8,128)(2,1)S(1)}, bf16[2048,128]{1,0:T(8,128)(2,1)S(1)}, bf16[2048,128]{1,0:T(8,128)(2,1)}, bf16[2048,128]{1,0:T(8,128)(2,1)}) custom-call(s32[3]{0:T(128)S(1)} %pad_add_fusion.where_ref.refs_0_, bf16[128,8192]{1,0:T(8,128)(2,1)S(1)} %bitcast.14), custom_call_target="tpu_custom_call" | custom-call | bytes 4194304 | tf_op jit(solution)/shard_map/pack/pallas_call | solution.py:91
  15.6 0.8 copy-done.1
  16.4 2.8 %collective-permute-start.2 = (bf16[2048,128]{1,0:T(8,128)(2,1)}, bf16[2048,128]{1,0:T(8,128)(2,1)S(1)}, u32[]{:S(2)}, u32[]{:S(2)}) collective-permute-start(bf16[2048,128]{1,0:T(8,128)(2,1)} %get-tuple-element.29), channel_id=1, source_target_pairs={{0,48},{16,0},{32,16},{48,32},{1,49},{17,1},{33,17},{49,33},{2,50}... | collective-permute-start | bytes 1572872 | tf_op jit(solution)/shard_map/ppermute | solution.py:247
  19.2 0.8 collective-permute-start.1
  20.0 0.9 collective-permute-start
  20.9 10.7 %project_q.1.refs_3_ = bf16[128,1024]{1,0:T(8,128)(2,1)} custom-call(bf16[128,8192]{1,0:T(8,128)(2,1)} %bitcast.13, bf16[8192,1280]{1,0:T(8,128)(2,1)} %w_ref.3), custom_call_target="tpu_custom_call" | custom-call | flops 2147483648 | bytes 18874368 | tf_op jit(solution)/shard_map/project_q/pallas_call | solution.py:58
  31.7 1.1 copy-done.12
  32.8 4.7 %attention_first.1 = (bf16[128,768]{1,0:T(8,128)(2,1)S(1)}, f32[1024,128]{1,0:T(8,128)S(1)}, f32[1024,128]{1,0:T(8,128)S(1)}) custom-call(s32[3]{0:T(128)S(1)} %pad_add_fusion.where_ref.refs_0_, s32[1,16]{1,0:T(1,128)S(1)} %copy-done.26, s32[1,4]{1,0:T(1,128)S(1)} %copy-done.27, bf16[128,1024]{1,0:T(8,128)(2,1)S(1)} %copy-done.12, ...), custom_call_target="tpu_custom_call" | custom-call | flops 1006632960 | bytes 4000000 | tf_op jit(solution)/shard_map/attention_first/pallas_call | solution.py:205
  37.5 0.7 copy-done.14
  38.2 0.8 copy-done.18
  39.0 0.8 copy-done.20
  39.8 1.9 %collective-permute-done.2.refs_3_.refs_4_ = bf16[2048,128]{1,0:T(8,128)(2,1)S(1)} collective-permute-done((bf16[2048,128]{1,0:T(8,128)(2,1)}, bf16[2048,128]{1,0:T(8,128)(2,1)S(1)}, u32[]{:S(2)}, u32[]{:S(2)}) %collective-permute-start.2) | collective-permute-done | bytes 524320 | tf_op jit(solution)/shard_map/ppermute | solution.py:247
  41.7 3.6 %collective-permute-done.refs_1_.refs_2_ = bf16[2048,128]{1,0:T(8,128)(2,1)S(1)} collective-permute-done((bf16[2048,128]{1,0:T(8,128)(2,1)S(1)}, bf16[2048,128]{1,0:T(8,128)(2,1)S(1)}, u32[]{:S(2)}, u32[]{:S(2)}) %collective-permute-start) | collective-permute-done | bytes 524320 | tf_op jit(solution)/shard_map/ppermute | solution.py:247
  45.3 0.8 copy-done.7
  46.1 33.6 %send_half.1 = bf16[4,1024,128]{2,1,0:T(8,128)(2,1)} custom-call(s32[3]{0:T(128)} %copy-done.24, bf16[2048,128]{1,0:T(8,128)(2,1)} %copy-done.1, bf16[2048,128]{1,0:T(8,128)(2,1)} %copy-done.7, bf16[2048,128]{1,0:T(8,128)(2,1)} %copy-done.5, bf16[2048,128]{1,0:T(8,128)(2,1)} %copy-done.3), custom_call_target="tpu_custom_call" | custom-call | bytes 2097152 | tf_op jit(solution)/shard_map/send_half/pallas_call | solution.py:117
  79.8 1.0 collective-permute-start.6
  81.2 0.8 collective-permute-start.4
  82.1 1.0 copy-done.11
  83.1 1.0 copy-done.19
  84.2 1.0 copy-done.21
  85.2 0.9 copy-done.23
  86.1 2.1 %attention_last.1 = (bf16[128,256]{1,0:T(8,128)(2,1)S(1)}, bf16[1024,256]{1,0:T(8,128)(2,1)S(1)}) custom-call(s32[3]{0:T(128)S(1)} %copy-done.25, s32[1,16]{1,0:T(1,128)S(1)} %copy-done.26, s32[1,4]{1,0:T(1,128)S(1)} %copy-done.27, bf16[128,1024]{1,0:T(8,128)(2,1)S(1)} %copy-done.13, bf16[128,1024]{1,0:T(8,128)(2,1)S(1)} %bitcast.20, ...), custom_call_target="tpu_custom_call" | custom-call | flops 335544320 | bytes 4000000 | tf_op jit(solution)/shard_map/attention_last/pallas_call | solution.py:205
  88.2 0.8 copy-done.17
  89.1 6.9 %all-to-all-start.1 = ((bf16[8,128,256]{2,1,0:T(8,128)(2,1)}), bf16[8,128,256]{2,1,0:T(8,128)(2,1)}, u32[]{:S(2)}, u32[]{:S(2)}) async-start(bf16[8,128,256]{2,1,0:T(8,128)(2,1)} %bitcast.18), calls=%async_computation.1 | async-start | bytes 1048576 | tf_op jit(solution)/shard_map/all_to_all | solution.py:291
  96.0 0.5 collective-permute-start.10
  97.0 0.6 collective-permute-done.7.refs_10_
  98.5 0.9 copy-done.15
  99.4 4.1 %term_a.1 = bf16[1024,768]{1,0:T(8,128)(2,1)} custom-call(s32[3]{0:T(128)S(1)} %copy-done.25, bf16[2048,128]{1,0:T(8,128)(2,1)S(1)} %copy-done.2, bf16[2048,128]{1,0:T(8,128)(2,1)S(1)} %copy-done.8, bf16[2048,128]{1,0:T(8,128)(2,1)S(1)} %copy-done.6, bf16[2048,128]{1,0:T(8,128)(2,1)S(1)} %copy-done.4, ...), custom_call_target="tpu_custom_call" | custom-call | flops 1610612736 | bytes 1572864 | tf_op jit(solution)/shard_map/term_a/pallas_call | solution.py:232
  103.5 4.0 %all-to-all-done.1 = bf16[8,128,256]{2,1,0:T(8,128)(2,1)} async-done(((bf16[8,128,256]{2,1,0:T(8,128)(2,1)}), bf16[8,128,256]{2,1,0:T(8,128)(2,1)}, u32[]{:S(2)}, u32[]{:S(2)}) %all-to-all-start.1) | async-done | bytes 524320 | tf_op jit(solution)/shard_map/all_to_all | solution.py:291
  107.5 4.4 %all-to-all-start.2 = ((bf16[16,64,768]{2,1,0:T(8,128)(2,1)}), bf16[16,64,768]{2,1,0:T(8,128)(2,1)}, u32[]{:S(2)}, u32[]{:S(2)}) async-start(bf16[16,64,768]{2,1,0:T(8,128)(2,1)} %bitcast.8), calls=%async_computation.2 | async-start | bytes 3145728 | tf_op jit(solution)/shard_map/all_to_all | solution.py:266
  112.0 1.1 reduce_sum.30
  113.1 2.7 %collective-permute-start.13 = (bf16[128,512]{1,0:T(8,128)(2,1)S(1)}, bf16[128,512]{1,0:T(8,128)(2,1)S(1)}, u32[]{:S(2)}, u32[]{:S(2)}) collective-permute-start(bf16[128,512]{1,0:T(8,128)(2,1)S(1)} %pad_maximum_fusion.1.refs_6_), channel_id=1, source_target_pairs={{0,48},{16,0},{32,16},{48,32},{1,49},{17,1},{33,17},{49,33},{2,50}... | collective-permute-start | bytes 393224 | tf_op jit(solution)/shard_map/ppermute | solution.py:247
  115.8 1.6 collective-permute-start.12
  117.4 1.0 collective-permute-start.11
  118.4 2.8 %collective-permute-done.13.refs_9_ = bf16[128,512]{1,0:T(8,128)(2,1)S(1)} collective-permute-done((bf16[128,512]{1,0:T(8,128)(2,1)S(1)}, bf16[128,512]{1,0:T(8,128)(2,1)S(1)}, u32[]{:S(2)}, u32[]{:S(2)}) %collective-permute-start.13) | collective-permute-done | bytes 131104 | tf_op jit(solution)/shard_map/ppermute | solution.py:247
  121.3 2.3 %collective-permute-done.12.refs_8_ = bf16[128,512]{1,0:T(8,128)(2,1)S(1)} collective-permute-done((bf16[128,512]{1,0:T(8,128)(2,1)S(1)}, bf16[128,512]{1,0:T(8,128)(2,1)S(1)}, u32[]{:S(2)}, u32[]{:S(2)}) %collective-permute-start.12) | collective-permute-done | bytes 131104 | tf_op jit(solution)/shard_map/ppermute | solution.py:247
  123.6 1.4 collective-permute-done.11.refs_7_
  125.0 1.3 collective-permute-done.15.refs_11_
  126.3 1.8 %term_b.1 = bf16[1024,512]{1,0:T(8,128)(2,1)S(1)} custom-call(s32[3]{0:T(128)S(1)} %copy-done.25, bf16[2048,128]{1,0:T(8,128)(2,1)S(1)} %copy-done.2, bf16[2048,128]{1,0:T(8,128)(2,1)S(1)} %copy-done.8, bf16[2048,128]{1,0:T(8,128)(2,1)S(1)} %copy-done.6, bf16[2048,128]{1,0:T(8,128)(2,1)S(1)} %copy-done.4, ...), custom_call_target="tpu_custom_call" | custom-call | flops 1073741824 | bytes 1048576 | tf_op jit(solution)/shard_map/term_b/pallas_call | solution.py:232
  128.1 1.0 copy-done.9
  129.1 7.5 %all-to-all-done.2 = bf16[16,64,768]{2,1,0:T(8,128)(2,1)} async-done(((bf16[16,64,768]{2,1,0:T(8,128)(2,1)}), bf16[16,64,768]{2,1,0:T(8,128)(2,1)}, u32[]{:S(2)}, u32[]{:S(2)}) %all-to-all-start.2) | async-done | bytes 1572896 | tf_op jit(solution)/shard_map/all_to_all | solution.py:266
  136.6 3.7 %all-to-all-start.3 = ((bf16[16,64,512]{2,1,0:T(8,128)(2,1)}), bf16[16,64,512]{2,1,0:T(8,128)(2,1)S(1)}, u32[]{:S(2)}, u32[]{:S(2)}) async-start(bf16[16,64,512]{2,1,0:T(8,128)(2,1)} %bitcast.15), calls=%async_computation.3 | async-start | bytes 2097152 | tf_op jit(solution)/shard_map/all_to_all | solution.py:266
  140.3 12.0 %fusion = bf16[1,128,8192]{2,1,0:T(8,128)(2,1)} fusion(bf16[8192,1280]{1,0:T(8,128)(2,1)} %w_ref.3, bf16[128,512]{1,0:T(8,128)(2,1)S(1)} %pad_maximum_fusion.1.refs_6_, bf16[128,768]{1,0:T(8,128)(2,1)S(1)} %copy-done.16), kind=kOutput, calls=%fused_computation.1 | convolution fusion | flops 2686058496 | bytes 23396352 | tf_op jit(solution)/shard_map/dot_general | solution.py:17
  152.3 1.6 %convert_reduce_fusion = f32[64,768]{1,0:T(8,128)S(1)} fusion(bf16[16,64,768]{2,1,0:T(8,128)(2,1)} %all-to-all-done.2), kind=kLoop, calls=%fused_computation.2 | loop fusion | flops 1523712 | bytes 1769472 | tf_op jit(solution)/shard_map/reduce_sum | solution.py:303
  153.9 3.1 %all-to-all-done.3 = bf16[16,64,512]{2,1,0:T(8,128)(2,1)S(1)} async-done(((bf16[16,64,512]{2,1,0:T(8,128)(2,1)}), bf16[16,64,512]{2,1,0:T(8,128)(2,1)S(1)}, u32[]{:S(2)}, u32[]{:S(2)}) %all-to-all-start.3) | async-done | bytes 1048608 | tf_op jit(solution)/shard_map/all_to_all | solution.py:266
  157.2 0.7 pad_maximum_fusion
  (67 shorter events, 2.2 us)
Async XLA Ops:
  0.6 13.0 %copy-start = (bf16[1,128,8192]{2,1,0:T(8,128)(2,1)S(1)}, bf16[1,128,8192]{2,1,0:T(8,128)(2,1)}, u32[]{:S(2)}) copy-start(bf16[1,128,8192]{2,1,0:T(8,128)(2,1)} %param.5) | copy-start | bytes 6291460
  5.7 26.0 %all-to-all-start = ((bf16[8,128,256]{2,1,0:T(8,128)(2,1)}), bf16[8,128,256]{2,1,0:T(8,128)(2,1)S(1)}, u32[]{:S(2)}, u32[]{:S(2)}) async-start(bf16[8,128,256]{2,1,0:T(8,128)(2,1)} %project_kv.1), calls=%async_computation | async-start | bytes 1048576 | tf_op jit(solution)/shard_map/all_to_all | solution.py:279
  13.6 18.0 %copy-start.24 = (s32[3]{0:T(128)}, s32[3]{0:T(128)S(1)}, u32[]{:S(2)}) copy-start(s32[3]{0:T(128)S(1)} %pad_add_fusion.where_ref.refs_0_) | copy-start | bytes 40
  15.6 0.8 copy-start.1
  16.4 25.2 %collective-permute-start.2 = (bf16[2048,128]{1,0:T(8,128)(2,1)}, bf16[2048,128]{1,0:T(8,128)(2,1)S(1)}, u32[]{:S(2)}, u32[]{:S(2)}) collective-permute-start(bf16[2048,128]{1,0:T(8,128)(2,1)} %get-tuple-element.29), channel_id=1, source_target_pairs={{0,48},{16,0},{32,16},{48,32},{1,49},{17,1},{33,17},{49,33},{2,50}... | collective-permute-start | bytes 1572872 | tf_op jit(solution)/shard_map/ppermute | solution.py:247
  19.2 22.5 %collective-permute-start.1 = (bf16[2048,128]{1,0:T(8,128)(2,1)}, bf16[2048,128]{1,0:T(8,128)(2,1)S(1)}, u32[]{:S(2)}, u32[]{:S(2)}) collective-permute-start(bf16[2048,128]{1,0:T(8,128)(2,1)} %get-tuple-element.27), channel_id=1, source_target_pairs={{0,32},{16,48},{32,0},{48,16},{1,33},{17,49},{33,1},{49,17},{2,34}... | collective-permute-start | bytes 1572872 | tf_op jit(solution)/shard_map/ppermute | solution.py:247
  20.0 25.3 %collective-permute-start = (bf16[2048,128]{1,0:T(8,128)(2,1)S(1)}, bf16[2048,128]{1,0:T(8,128)(2,1)S(1)}, u32[]{:S(2)}, u32[]{:S(2)}) collective-permute-start(bf16[2048,128]{1,0:T(8,128)(2,1)S(1)} %get-tuple-element.25), channel_id=1, source_target_pairs={{0,16},{16,32},{32,48},{48,0},{1,17},{17,33},{33,49},{49,1},{2,18}... | collective-permute-start | bytes 1572872 | tf_op jit(solution)/shard_map/ppermute | solution.py:247
  20.9 10.8 %copy-start.22 = (bf16[1,128,1024]{2,1,0:T(8,128)(2,1)S(1)}, bf16[1,128,1024]{2,1,0:T(8,128)(2,1)}, u32[]{:S(2)}) copy-start(bf16[1,128,1024]{2,1,0:T(8,128)(2,1)} %param.7) | copy-start | bytes 786436
  20.9 10.8 %copy-start.26 = (s32[1,16]{1,0:T(1,128)S(1)}, s32[1,16]{1,0:T(1,128)}, u32[]{:S(2)}) copy-start(s32[1,16]{1,0:T(1,128)} %refs_1_.3) | copy-start | bytes 196
  20.9 10.8 %copy-start.27 = (s32[1,4]{1,0:T(1,128)S(1)}, s32[1,4]{1,0:T(1,128)}, u32[]{:S(2)}) copy-start(s32[1,4]{1,0:T(1,128)} %refs_2_.3) | copy-start | bytes 52
  31.6 13.6 %copy-start.10 = (bf16[8,128,256]{2,1,0:T(8,128)(2,1)}, bf16[8,128,256]{2,1,0:T(8,128)(2,1)S(1)}, u32[]{:S(2)}) copy-start(bf16[8,128,256]{2,1,0:T(8,128)(2,1)S(1)} %all-to-all-done) | copy-start | bytes 1572868
  31.7 1.1 copy-start.12
  39.0 0.8 copy-start.20
  39.8 42.3 %copy-start.13 = (bf16[128,1024]{1,0:T(8,128)(2,1)S(1)}, bf16[128,1024]{1,0:T(8,128)(2,1)}, u32[]{:S(2)}) copy-start(bf16[128,1024]{1,0:T(8,128)(2,1)} %project_q.1.refs_3_) | copy-start | bytes 786436
  39.8 42.3 %copy-start.25 = (s32[3]{0:T(128)S(1)}, s32[3]{0:T(128)}, u32[]{:S(2)}) copy-start(s32[3]{0:T(128)} %copy-done.24) | copy-start | bytes 40
  41.7 3.6 %copy-start.3 = (bf16[2048,128]{1,0:T(8,128)(2,1)}, bf16[2048,128]{1,0:T(8,128)(2,1)S(1)}, u32[]{:S(2)}) copy-start(bf16[2048,128]{1,0:T(8,128)(2,1)S(1)} %collective-permute-done.2.refs_3_.refs_4_) | copy-start | bytes 1572868
  41.7 3.6 %copy-start.5 = (bf16[2048,128]{1,0:T(8,128)(2,1)}, bf16[2048,128]{1,0:T(8,128)(2,1)S(1)}, u32[]{:S(2)}) copy-start(bf16[2048,128]{1,0:T(8,128)(2,1)S(1)} %collective-permute-done.1.refs_2_.refs_3_) | copy-start | bytes 1572868
  45.2 0.8 copy-start.7
  79.6 18.9 %copy-start.2 = (bf16[2048,128]{1,0:T(8,128)(2,1)S(1)}, bf16[2048,128]{1,0:T(8,128)(2,1)}, u32[]{:S(2)}) copy-start(bf16[2048,128]{1,0:T(8,128)(2,1)} %copy-done.1) | copy-start | bytes 1572868
  79.6 18.9 %copy-start.4 = (bf16[2048,128]{1,0:T(8,128)(2,1)S(1)}, bf16[2048,128]{1,0:T(8,128)(2,1)}, u32[]{:S(2)}) copy-start(bf16[2048,128]{1,0:T(8,128)(2,1)} %copy-done.3) | copy-start | bytes 1572868
  79.7 18.8 %copy-start.6 = (bf16[2048,128]{1,0:T(8,128)(2,1)S(1)}, bf16[2048,128]{1,0:T(8,128)(2,1)}, u32[]{:S(2)}) copy-start(bf16[2048,128]{1,0:T(8,128)(2,1)} %copy-done.5) | copy-start | bytes 1572868
  79.7 18.8 %copy-start.8 = (bf16[2048,128]{1,0:T(8,128)(2,1)S(1)}, bf16[2048,128]{1,0:T(8,128)(2,1)}, u32[]{:S(2)}) copy-start(bf16[2048,128]{1,0:T(8,128)(2,1)} %copy-done.7) | copy-start | bytes 1572868
  79.7 18.8 %collective-permute-start.3 = (bf16[4,1024,128]{2,1,0:T(8,128)(2,1)}, bf16[4,1024,128]{2,1,0:T(8,128)(2,1)S(1)}, u32[]{:S(2)}, u32[]{:S(2)}) collective-permute-start(bf16[4,1024,128]{2,1,0:T(8,128)(2,1)} %send_half.1), channel_id=1, source_target_pairs={{0,8},{8,0},{1,9},{9,1},{2,10},{10,2},{3,11},{11,3},{4,12},{12,4},... | collective-permute-start | bytes 3145736 | tf_op jit(solution)/shard_map/ppermute | solution.py:251
  79.8 16.2 %collective-permute-start.6 = (bf16[128,768]{1,0:T(8,128)(2,1)}, bf16[128,768]{1,0:T(8,128)(2,1)}, u32[]{:S(2)}, u32[]{:S(2)}) collective-permute-start(bf16[128,768]{1,0:T(8,128)(2,1)} %copy-done.14), channel_id=1, source_target_pairs={{0,48},{16,0},{32,16},{48,32},{1,49},{17,1},{33,17},{49,33},{2,50}... | collective-permute-start | bytes 589832 | tf_op jit(solution)/shard_map/ppermute | solution.py:247
  80.8 15.7 %collective-permute-start.5 = (bf16[128,768]{1,0:T(8,128)(2,1)}, bf16[128,768]{1,0:T(8,128)(2,1)}, u32[]{:S(2)}, u32[]{:S(2)}) collective-permute-start(bf16[128,768]{1,0:T(8,128)(2,1)} %copy-done.14), channel_id=1, source_target_pairs={{0,32},{16,48},{32,0},{48,16},{1,33},{17,49},{33,1},{49,17},{2,34}... | collective-permute-start | bytes 589832 | tf_op jit(solution)/shard_map/ppermute | solution.py:247
  81.2 15.4 %collective-permute-start.4 = (bf16[128,768]{1,0:T(8,128)(2,1)}, bf16[128,768]{1,0:T(8,128)(2,1)}, u32[]{:S(2)}, u32[]{:S(2)}) collective-permute-start(bf16[128,768]{1,0:T(8,128)(2,1)} %copy-done.14), channel_id=1, source_target_pairs={{0,16},{16,32},{32,48},{48,0},{1,17},{17,33},{33,49},{49,1},{2,18}... | collective-permute-start | bytes 589832 | tf_op jit(solution)/shard_map/ppermute | solution.py:247
  82.1 1.0 copy-start.11
  83.1 1.0 copy-start.19
  84.1 1.0 copy-start.21
  85.2 0.9 copy-start.23
  88.2 0.8 copy-start.17
  89.1 18.5 %all-to-all-start.1 = ((bf16[8,128,256]{2,1,0:T(8,128)(2,1)}), bf16[8,128,256]{2,1,0:T(8,128)(2,1)}, u32[]{:S(2)}, u32[]{:S(2)}) async-start(bf16[8,128,256]{2,1,0:T(8,128)(2,1)} %bitcast.18), calls=%async_computation.1 | async-start | bytes 1048576 | tf_op jit(solution)/shard_map/all_to_all | solution.py:291
  96.0 1.7 %collective-permute-start.7 = (bf16[128,768]{1,0:T(8,128)(2,1)}, bf16[128,768]{1,0:T(8,128)(2,1)S(1)}, u32[]{:S(2)}, u32[]{:S(2)}) collective-permute-start(bf16[128,768]{1,0:T(8,128)(2,1)} %copy-done.14), channel_id=1, source_target_pairs={{0,8},{8,0},{1,9},{9,1},{2,10},{10,2},{3,11},{11,3},{4,12},{12,4},... | collective-permute-start | bytes 589832 | tf_op jit(solution)/shard_map/ppermute | solution.py:251
  96.0 1.9 %collective-permute-start.10 = (bf16[128,768]{1,0:T(8,128)(2,1)}, bf16[128,768]{1,0:T(8,128)(2,1)S(1)}, u32[]{:S(2)}, u32[]{:S(2)}) collective-permute-start(bf16[128,768]{1,0:T(8,128)(2,1)} %collective-permute-done.6.refs_9_), channel_id=1, source_target_pairs={{0,8},{8,0},{1,9},{9,1},{2,10},{10,2},{3,11},{11,3},{4,12},{12,4},... | collective-permute-start | bytes 589832 | tf_op jit(solution)/shard_map/ppermute | solution.py:251
  96.5 1.7 %collective-permute-start.9 = (bf16[128,768]{1,0:T(8,128)(2,1)}, bf16[128,768]{1,0:T(8,128)(2,1)S(1)}, u32[]{:S(2)}, u32[]{:S(2)}) collective-permute-start(bf16[128,768]{1,0:T(8,128)(2,1)} %collective-permute-done.5.refs_8_), channel_id=1, source_target_pairs={{0,8},{8,0},{1,9},{9,1},{2,10},{10,2},{3,11},{11,3},{4,12},{12,4},... | collective-permute-start | bytes 589832 | tf_op jit(solution)/shard_map/ppermute | solution.py:251
  96.6 1.9 %collective-permute-start.8 = (bf16[128,768]{1,0:T(8,128)(2,1)}, bf16[128,768]{1,0:T(8,128)(2,1)S(1)}, u32[]{:S(2)}, u32[]{:S(2)}) collective-permute-start(bf16[128,768]{1,0:T(8,128)(2,1)} %collective-permute-done.4.refs_7_), channel_id=1, source_target_pairs={{0,8},{8,0},{1,9},{9,1},{2,10},{10,2},{3,11},{11,3},{4,12},{12,4},... | collective-permute-start | bytes 589832 | tf_op jit(solution)/shard_map/ppermute | solution.py:251
  98.5 0.9 copy-start.15
  107.5 29.1 %all-to-all-start.2 = ((bf16[16,64,768]{2,1,0:T(8,128)(2,1)}), bf16[16,64,768]{2,1,0:T(8,128)(2,1)}, u32[]{:S(2)}, u32[]{:S(2)}) async-start(bf16[16,64,768]{2,1,0:T(8,128)(2,1)} %bitcast.8), calls=%async_computation.2 | async-start | bytes 3145728 | tf_op jit(solution)/shard_map/all_to_all | solution.py:266
  113.1 8.2 %collective-permute-start.13 = (bf16[128,512]{1,0:T(8,128)(2,1)S(1)}, bf16[128,512]{1,0:T(8,128)(2,1)S(1)}, u32[]{:S(2)}, u32[]{:S(2)}) collective-permute-start(bf16[128,512]{1,0:T(8,128)(2,1)S(1)} %pad_maximum_fusion.1.refs_6_), channel_id=1, source_target_pairs={{0,48},{16,0},{32,16},{48,32},{1,49},{17,1},{33,17},{49,33},{2,50}... | collective-permute-start | bytes 393224 | tf_op jit(solution)/shard_map/ppermute | solution.py:247
  115.8 7.7 %collective-permute-start.12 = (bf16[128,512]{1,0:T(8,128)(2,1)S(1)}, bf16[128,512]{1,0:T(8,128)(2,1)S(1)}, u32[]{:S(2)}, u32[]{:S(2)}) collective-permute-start(bf16[128,512]{1,0:T(8,128)(2,1)S(1)} %pad_maximum_fusion.1.refs_6_), channel_id=1, source_target_pairs={{0,32},{16,48},{32,0},{48,16},{1,33},{17,49},{33,1},{49,17},{2,34}... | collective-permute-start | bytes 393224 | tf_op jit(solution)/shard_map/ppermute | solution.py:247
  117.4 7.6 %collective-permute-start.11 = (bf16[128,512]{1,0:T(8,128)(2,1)S(1)}, bf16[128,512]{1,0:T(8,128)(2,1)S(1)}, u32[]{:S(2)}, u32[]{:S(2)}) collective-permute-start(bf16[128,512]{1,0:T(8,128)(2,1)S(1)} %pad_maximum_fusion.1.refs_6_), channel_id=1, source_target_pairs={{0,16},{16,32},{32,48},{48,0},{1,17},{17,33},{33,49},{49,1},{2,18}... | collective-permute-start | bytes 393224 | tf_op jit(solution)/shard_map/ppermute | solution.py:247
  118.4 6.5 %collective-permute-start.14 = (bf16[128,512]{1,0:T(8,128)(2,1)S(1)}, bf16[128,512]{1,0:T(8,128)(2,1)S(1)}, u32[]{:S(2)}, u32[]{:S(2)}) collective-permute-start(bf16[128,512]{1,0:T(8,128)(2,1)S(1)} %pad_maximum_fusion.1.refs_6_), channel_id=1, source_target_pairs={{0,8},{8,0},{1,9},{9,1},{2,10},{10,2},{3,11},{11,3},{4,12},{12,4},... | collective-permute-start | bytes 393224 | tf_op jit(solution)/shard_map/ppermute | solution.py:251
  121.3 3.7 %collective-permute-start.17 = (bf16[128,512]{1,0:T(8,128)(2,1)S(1)}, bf16[128,512]{1,0:T(8,128)(2,1)S(1)}, u32[]{:S(2)}, u32[]{:S(2)}) collective-permute-start(bf16[128,512]{1,0:T(8,128)(2,1)S(1)} %collective-permute-done.13.refs_9_), channel_id=1, source_target_pairs={{0,8},{8,0},{1,9},{9,1},{2,10},{10,2},{3,11},{11,3},{4,12},{12,4},... | collective-permute-start | bytes 393224 | tf_op jit(solution)/shard_map/ppermute | solution.py:251
  123.6 1.4 collective-permute-start.16
  125.0 1.3 collective-permute-start.15
  128.1 1.0 copy-start.9
  129.1 11.2 %copy-start.16 = (bf16[128,768]{1,0:T(8,128)(2,1)S(1)}, bf16[128,768]{1,0:T(8,128)(2,1)}, u32[]{:S(2)}) copy-start(bf16[128,768]{1,0:T(8,128)(2,1)} %copy-done.14) | copy-start | bytes 589828
  136.6 20.4 %all-to-all-start.3 = ((bf16[16,64,512]{2,1,0:T(8,128)(2,1)}), bf16[16,64,512]{2,1,0:T(8,128)(2,1)S(1)}, u32[]{:S(2)}, u32[]{:S(2)}) async-start(bf16[16,64,512]{2,1,0:T(8,128)(2,1)} %bitcast.15), calls=%async_computation.3 | async-start | bytes 2097152 | tf_op jit(solution)/shard_map/all_to_all | solution.py:266
  (2 other events, 1.5 us)

commit v3 on v1

v3 whole, which is shorter than its diff:
```python
import jax
import jax.numpy as jnp
from jax import lax
from jax.experimental import pallas as pl
from jax.experimental.pallas import tpu as pltpu
from jax.sharding import Mesh, PartitionSpec as P

HD = 128
HQ = 8
SPAN = 64
LOG2E = 1.4426950408889634
SEQ = ("zhi", "y")
OWN = ("zlo", "zhi", "y")


def nt(a, b):
    return lax.dot_general(a, b, (((1,), (1,)), ((), ())), preferred_element_type=jnp.float32)


def tn(a, b):
    return lax.dot_general(a, b, (((0,), (0,)), ((), ())), preferred_element_type=jnp.float32)


def nn(a, b):
    return jnp.dot(a, b, preferred_element_type=jnp.float32)


SMEM = pl.BlockSpec(memory_space=pltpu.SMEM)
VMEM = pl.BlockSpec(memory_space=pltpu.VMEM)
MIB = 1024 * 1024


def first_kernel(chips, where_ref, x_ref, w_ref, kv_ref, *refs):
    out_refs, acc_ref = refs[:chips], refs[chips]
    step = pl.program_id(0)
    depth = w_ref.shape[0]
    part = nn(x_ref[:, pl.ds(pl.multiple_of(step * depth, depth), depth)], w_ref[...])

    features = x_ref.shape[1]
    width = features // (4 * chips)
    for s in range(chips):
        chip = lax.rem(where_ref[0] + s, chips)
        for z in range(2):
            at = pl.multiple_of(z * (features // 2) + chip * 2 * width + step * width, width)
            out_refs[s][z * width : (z + 1) * width, :] = x_ref[:, pl.ds(at, width)].T

    @pl.when(step == 0)
    def _():
        acc_ref[...] = part

    @pl.when(step > 0)
    def _():
        acc_ref[...] += part

    @pl.when(step == pl.num_programs(0) - 1)
    def _():
        low = acc_ref[...].astype(jnp.bfloat16)
        for i in range(kv_ref.shape[0]):
            kv_ref[i] = low


def first(where, x, w, copies, chips):
    tokens, features = x.shape
    width = 2 * HD
    depth = features // 2
    pieces = jax.ShapeDtypeStruct((features // chips, tokens), x.dtype)
    return pl.pallas_call(
        lambda *refs: first_kernel(chips, *refs),
        grid=(features // depth,),
        out_shape=(jax.ShapeDtypeStruct((copies, tokens, width), jnp.bfloat16),) + (pieces,) * chips,
        in_specs=[
            SMEM,
            pl.BlockSpec((tokens, features), lambda i: (0, 0)),
            pl.BlockSpec((depth, width), lambda i: (i, HQ // 2)),
        ],
        out_specs=(pl.BlockSpec((copies, tokens, width), lambda i: (0, 0, 0)),)
        + (pl.BlockSpec((features // chips // 2, tokens), lambda i: (i, 0)),) * chips,
        scratch_shapes=[pltpu.VMEM((tokens, width), jnp.float32)],
        compiler_params=pltpu.CompilerParams(vmem_limit_bytes=50 * MIB),
        cost_estimate=pl.CostEstimate(flops=2 * tokens * features * width, bytes_accessed=10 * MIB, transcendentals=0),
        name="first",
    )(where, x, w)


def query_kernel(x_ref, w_ref, out_ref):
    out_ref[...] = nn(x_ref[...], w_ref[...]).astype(jnp.bfloat16)


def project_query(x, w):
    tokens, features = x.shape
    width = 2 * HD
    return pl.pallas_call(
        query_kernel,
        grid=(HQ // 2,),
        out_shape=jax.ShapeDtypeStruct((tokens, HQ * HD), jnp.bfloat16),
        in_specs=[pl.BlockSpec((tokens, features), lambda i: (0, 0)), pl.BlockSpec((features, width), lambda i: (0, i))],
        out_specs=pl.BlockSpec((tokens, width), lambda i: (0, i)),
        compiler_params=pltpu.CompilerParams(vmem_limit_bytes=44 * MIB),
        cost_estimate=pl.CostEstimate(flops=2 * tokens * features * HQ * HD, bytes_accessed=20 * MIB, transcendentals=0),
        name="project_query",
    )(x, w)


def send_kernel(where_ref, *refs):
    pieces, out_ref = refs[:-1], refs[-1]
    half = pieces[0].shape[0] // 2
    at = pl.multiple_of((1 - where_ref[1]) * half, half)
    for i, piece in enumerate(pieces):
        out_ref[i] = piece[pl.ds(at, half), :]


def send_half(where, pieces):
    rows, tokens = pieces[0].shape
    n = len(pieces)
    return pl.pallas_call(
        send_kernel,
        out_shape=jax.ShapeDtypeStruct((n, rows // 2, tokens), pieces[0].dtype),
        in_specs=[SMEM] + [VMEM] * n,
        out_specs=VMEM,
        compiler_params=pltpu.CompilerParams(vmem_limit_bytes=8 * MIB),
        cost_estimate=pl.CostEstimate(flops=0, bytes_accessed=MIB, transcendentals=0),
        name="send_half",
    )(where, *pieces)


def join_kernel(where_ref, *refs):
    pieces, other, out_ref = refs[:-2], refs[-2], refs[-1]
    half, tokens = other.shape[1:]
    n = len(pieces)
    at = pl.multiple_of(where_ref[1] * half, half)
    for i in range(n):
        out_ref[:, i * tokens : (i + 1) * tokens] = pieces[i][pl.ds(at, half), :]
        out_ref[:, (n + i) * tokens : (n + i + 1) * tokens] = other[i]


def join(where, pieces, other):
    n, half, tokens = other.shape
    return pl.pallas_call(
        join_kernel,
        out_shape=jax.ShapeDtypeStruct((half, 2 * n * tokens), other.dtype),
        in_specs=[SMEM] + [VMEM] * (n + 1),
        out_specs=VMEM,
        compiler_params=pltpu.CompilerParams(vmem_limit_bytes=8 * MIB),
        cost_estimate=pl.CostEstimate(flops=0, bytes_accessed=MIB, transcendentals=0),
        name="join",
    )(where, *pieces, other)


def attention_kernel(where_ref, order_ref, lens_ref, q_ref, do_ref, kv_ref, dq_ref, dkv_ref, bias_ref, dk_ref, dv_ref):
    scale = HD ** (-0.5)
    spans = order_ref.shape[1]
    docs = lens_ref.shape[1]
    place = where_ref[2]
    lane = lax.broadcasted_iota(jnp.int32, (1, 2 * SPAN), 1)
    pos_q = jnp.where(
        lane < SPAN,
        order_ref[0, 2 * place] * SPAN + lane,
        order_ref[0, 2 * place + 1] * SPAN + lane - SPAN,
    )
    start = jnp.zeros_like(pos_q)
    end = jnp.int32(0)
    for i in range(docs):
        end = end + lens_ref[0, i]
        start = jnp.where(pos_q >= end, end, start)
    row = lax.broadcasted_iota(jnp.int32, (SPAN, 2 * SPAN), 0)
    for s in range(spans):
        pos_k = order_ref[0, s] * SPAN + row
        allowed = (pos_k <= pos_q) & (pos_k >= start)
        bias_ref[s * SPAN : (s + 1) * SPAN, :] = jnp.where(allowed, 0.0, -jnp.inf)
    k = kv_ref[:, :HD]
    v = kv_ref[:, HD:]
    for h in range(0, HQ, 2):
        a, b, c = h * HD, (h + 1) * HD, (h + 2) * HD
        q2 = jnp.concatenate([q_ref[:, a:b], q_ref[:, b:c]], axis=0)
        d2 = jnp.concatenate([do_ref[:, a:b], do_ref[:, b:c]], axis=0)
        bias = bias_ref[...]
        s2 = nt(k, q2) + jnp.concatenate([bias, bias], axis=1)
        peak = jnp.max(s2, axis=0, keepdims=True)
        expo = jnp.exp2((s2 - peak) * (scale * LOG2E))
        inverse = 1.0 / jnp.sum(expo, axis=0, keepdims=True)
        probs = expo * inverse
        low = probs.astype(jnp.bfloat16)
        dp = nt(v, d2)
        delta = jnp.sum(low.astype(jnp.float32) * dp, axis=0, keepdims=True)
        ds = (probs * ((dp - delta) * scale)).astype(jnp.bfloat16)
        dq = tn(ds, k).astype(jnp.bfloat16)
        dq_ref[:, a:b] = dq[:HD]
        dq_ref[:, b:c] = dq[HD:]
        dv = nn(low, d2)
        dk = nn(ds, q2)
        if h > 0:
            dv += dv_ref[...]
            dk += dk_ref[...]
        if h < HQ - 2:
            dv_ref[...] = dv
            dk_ref[...] = dk
        else:
            dkv_ref[:, :HD] = dk.astype(jnp.bfloat16)
            dkv_ref[:, HD:] = dv.astype(jnp.bfloat16)


def attention(where, order, lens, query, grad, key_value):
    tokens = query.shape[0]
    total = key_value.shape[0]
    work = HQ * tokens * total
    return pl.pallas_call(
        attention_kernel,
        out_shape=(
            jax.ShapeDtypeStruct((tokens, HQ * HD), jnp.bfloat16),
            jax.ShapeDtypeStruct((total, 2 * HD), jnp.bfloat16),
        ),
        in_specs=[SMEM, SMEM, SMEM, VMEM, VMEM, VMEM],
        out_specs=(VMEM, VMEM),
        scratch_shapes=[
            pltpu.VMEM((total, tokens), jnp.float32),
            pltpu.VMEM((total, HD), jnp.float32),
            pltpu.VMEM((total, HD), jnp.float32),
        ],
        compiler_params=pltpu.CompilerParams(vmem_limit_bytes=24 * MIB),
        cost_estimate=pl.CostEstimate(flops=10 * work * HD, bytes_accessed=4 * 10**6, transcendentals=work),
        name="attention",
    )(where, order, lens, query, grad, key_value)


def term_kernel(x_ref, *refs):
    pieces, out_ref = refs[:-1], refs[-1]
    step = 2 * HD
    for at in range(0, out_ref.shape[1], step):
        right = jnp.concatenate([g[:, at : at + step] for g in pieces], axis=0)
        out_ref[:, at : at + step] = nn(x_ref[...], right).astype(out_ref.dtype)


def term(joined, pieces, name):
    half, depth = joined.shape
    width = pieces[0].shape[1]
    return pl.pallas_call(
        term_kernel,
        out_shape=jax.ShapeDtypeStruct((half, width), jnp.bfloat16),
        in_specs=[VMEM] * (1 + len(pieces)),
        out_specs=VMEM,
        compiler_params=pltpu.CompilerParams(vmem_limit_bytes=16 * MIB),
        cost_estimate=pl.CostEstimate(flops=2 * depth * half * width, bytes_accessed=2 * half * width, transcendentals=0),
        name=name,
    )(joined, *pieces)


def last_kernel(x_ref, done_ref, *refs):
    pieces, out_ref = refs[:-1], refs[-1]
    width = done_ref.shape[1]
    right = jnp.concatenate([g[...] for g in pieces], axis=0)
    out_ref[:, width:] = nn(x_ref[...], right).astype(out_ref.dtype)
    out_ref[:, :width] = done_ref[...]


def last(joined, done, pieces):
    half, depth = joined.shape
    width = pieces[0].shape[1]
    return pl.pallas_call(
        last_kernel,
        out_shape=jax.ShapeDtypeStruct((half, done.shape[1] + width), jnp.bfloat16),
        in_specs=[VMEM] * (2 + len(pieces)),
        out_specs=VMEM,
        compiler_params=pltpu.CompilerParams(vmem_limit_bytes=16 * MIB),
        cost_estimate=pl.CostEstimate(flops=2 * depth * half * width, bytes_accessed=2 * half * width, transcendentals=0),
        name="term_kv",
    )(joined, done, *pieces)


def shifted(value, s):
    n = lax.axis_size("x")
    return lax.ppermute(value, "x", [(i, (i + s) % n) for i in range(n)])


def swapped(value):
    return lax.ppermute(value, "core", [(0, 1), (1, 0)])


def gather_chips(value):
    own = [value] + [shifted(value, s) for s in range(1, lax.axis_size("x"))]
    return own, [swapped(piece) for piece in own]


def after(value, *others):
    return lax.optimization_barrier((value,) + others)[0]


def to_owners(value):
    owners = lax.axis_size("zlo") * lax.axis_size("zhi") * lax.axis_size("y")
    blocks = value.reshape(owners, value.shape[0] // owners, value.shape[1])
    return lax.all_to_all(blocks, OWN, 0, 0, tiled=True)


def local(layer_input, w_qkv, d_out, span_order, doc_lengths):
    rows = layer_input[0]
    tokens = rows.shape[0]
    chips = lax.axis_size("x")
    seq = lax.axis_size("zhi") * lax.axis_size("y")
    where = jnp.stack(
        [lax.axis_index("x"), lax.axis_index("core"), lax.axis_index("zhi") * lax.axis_size("y") + lax.axis_index("y")]
    ).astype(jnp.int32)

    copies, *packed = first(where, rows, w_qkv, seq, chips)
    gathered = lax.all_to_all(copies, SEQ, 0, 0, tiled=True).reshape(seq * tokens, 2 * HD)
    pieces = [packed[0]] + [shifted(packed[s], s) for s in range(1, chips)]
    query = project_query(after(rows, packed[0]), w_qkv)
    d_query, terms = attention(where, span_order, doc_lengths, query, d_out[0], gathered)
    own_q, other_q = gather_chips(d_query)
    arrived = lax.all_to_all(terms.reshape(seq, tokens, 2 * HD), SEQ, 0, 0, tiled=True)

    pieces = [after(piece, terms) for piece in pieces]
    x_other = swapped(send_half(where, pieces))
    joined = join(where, pieces, x_other)
    term_q = term(joined, own_q + other_q, "term_q")
    owned = jnp.sum(arrived.astype(jnp.float32), axis=0).astype(jnp.bfloat16)
    own_kv, other_kv = gather_chips(owned)
    received = to_owners(last(joined, term_q, own_kv + other_kv))
    d_qkv = jnp.concatenate([d_query, owned], axis=1)
    d_rows = nt(d_qkv, w_qkv).astype(jnp.bfloat16)
    d_w = jnp.sum(received.astype(jnp.float32), axis=0)
    return (d_rows[None], d_w)


def solution(mesh):
    fine = Mesh(mesh.devices.reshape(2, 4, 2, 2, 4), ("zlo", "x", "core", "zhi", "y"))
    dp, ctx = ("zlo", "x", "core"), ("zhi", "y")
    placed = (P(dp, ctx, None), P(), P(dp, ctx, None), P(dp, None), P(dp, None))
    return jax.shard_map(
        local,
        mesh=fine,
        in_specs=placed,
        out_specs=(P(dp, ctx, None), P(dp + ctx, None)),
        check_vma=False,
    )
```

time: 158 us -> 136 us (0.86)
  local copies, waits for them, and re-layouts: 39.1 us -> 5.03 us
  Pallas kernels: 6.31 us -> 27.7 us
  matrix products: 31.8 us -> 11.9 us
  starting transfers between devices: 30.7 us -> 37.3 us
  waiting for transfers between devices: 43.4 us -> 48.4 us
    dynamic_slice x8 -> x0, local copies, waits for them, and re-layouts: 23.7 us -> none  [the longest x2 8.96 us: local(): lax.dynamic_index_in_dim(pieces, at_core, 2, keepdims=False)]
    pallas_call x0 -> x6, Pallas kernels: none -> 21.1 us  [the longest x1 7.5 us: project_query(): pl.pallas_call(query_kernel, grid=(HQ // 2,), out_shape=jax.ShapeDtypeStr...]
    dot_general x6 -> x0, matrix products: 19.9 us -> none  [the longest x2 11.3 us: nn(): return jnp.dot(a, b, preferred_element_type=jnp.float32)]
    ppermute x9, waiting for transfers between devices: 7.17 us -> 18.3 us  [shifted(): return lax.ppermute(value, 'x', [(i, (i + s) % n) for i in range(n)])]
    all_to_all x1, waiting for transfers between devices: 4.7 us -> 0.01 us  [local(): lax.all_to_all(terms.reshape(seq, tokens, 2 * HD), SEQ, 0, 0, tiled=True)]
    all_to_all x1, starting transfers between devices: 3.73 us -> 7.24 us  [to_owners(): return lax.all_to_all(blocks, OWN, 0, 0, tiled=True)]
    concatenate x2 -> x0, local copies, waits for them, and re-layouts: 3.45 us -> none  [the longest x1 2.72 us: local(): term = jnp.concatenate([grad_q, grad_kv], axis=1)]
    reshape x1 -> x0, local copies, waits for them, and re-layouts: 3.31 us -> none  [local(): pieces = jnp.stack(pieces).reshape(chips * tokens, zlos, 2, width)]
  transfers between devices with their start and end apart: 15 -> 21, of which waited for: 7 -> 5; matrix products, arithmetic and copies ran while one was open for 37% -> 10% of each run, Pallas kernels for 4% -> 14%
where the time goes in v3:
time: 136 us; the launch traced here: 135 us
  waiting for transfers between devices  48.4 us (36%)
  starting transfers between devices  37.3 us (27%)
  Pallas kernels  27.7 us (20%)
  matrix products  11.9 us (9%)
  local copies, waits for them, and re-layouts  5.03 us (4%)
  other arithmetic  4.04 us (3%)
    all_to_all x1, waiting for transfers between devices, to_owners(): return lax.all_to_all(blocks, OWN, 0, 0, tiled=True)  30.1 us
    ppermute x9, waiting for transfers between devices, shifted(): return lax.ppermute(value, 'x', [(i, (i + s) % n) for i in range(n)])  18.3 us
    ppermute x9, starting transfers between devices, shifted(): return lax.ppermute(value, 'x', [(i, (i + s) % n) for i in range(n)])  13.6 us
    dot_general x1, matrix products, nt(): lax.dot_general(a, b, (((1,), (1,)), ((), ())), preferred_element_type=jn...  11.9 us
    all_to_all x1, starting transfers between devices, local(): lax.all_to_all(copies, SEQ, 0, 0, tiled=True).reshape(seq * tokens, 2 * HD)  7.87 us
    pallas_call x1, Pallas kernels, project_query(): pl.pallas_call(query_kernel, grid=(HQ // 2,), out_shape=jax.ShapeDtypeStr...  7.5 us
    all_to_all x1, starting transfers between devices, to_owners(): return lax.all_to_all(blocks, OWN, 0, 0, tiled=True)  7.24 us
    all_to_all x1, starting transfers between devices, local(): lax.all_to_all(terms.reshape(seq, tokens, 2 * HD), SEQ, 0, 0, tiled=True)  6.93 us
  transfers between devices with their start and end apart: 21, of which 5 were waited for; matrix products, arithmetic and copies ran while one was open for 10% of the time, Pallas kernels for 14%

profile of v3, /device:TPU:0, one launch (start us, length us, event | category | flops | bytes accessed | tf_op | source)
XLA Modules:
  0.0 135.3 jit_solution(9541631510718506022)
XLA Ops:
  0.6 0.1 pad_add_fusion.refs_0_.where_ref
  0.7 4.5 %first.1 = (bf16[8,128,256]{2,1,0:T(8,128)(2,1)}, bf16[2048,128]{1,0:T(8,128)(2,1)S(1)}, bf16[2048,128]{1,0:T(8,128)(2,1)S(1)}, bf16[2048,128]{1,0:T(8,128)(2,1)S(1)}, bf16[2048,128]{1,0:T(8,128)(2,1)S(1)}) custom-call(s32[3]{0:T(128)S(1)} %pad_add_fusion.refs_0_.where_ref, bf16[128,8192]{1,0:T(8,128)(2,1)} %bitcast.11, bf16[8192,1280]{1,0:T(8,128)(2,1)} %w_ref.1), custom_call_target="tpu_custom_call" | custom-call | flops 536870912 | bytes 10485760 | tf_op jit(solution)/shard_map/first/pallas_call | solution.py:67
  5.2 0.8 copy-done.4
  6.0 0.8 copy-done.5
  6.8 0.8 copy-done.6
  7.6 7.9 %all-to-all-start = ((bf16[8,128,256]{2,1,0:T(8,128)(2,1)}), bf16[8,128,256]{2,1,0:T(8,128)(2,1)}, u32[]{:S(2)}, u32[]{:S(2)}) async-start(bf16[8,128,256]{2,1,0:T(8,128)(2,1)} %get-tuple-element.16), calls=%async_computation | async-start | bytes 1048576 | tf_op jit(solution)/shard_map/all_to_all | solution.py:303
  15.5 3.0 %collective-permute-start.1 = (bf16[2048,128]{1,0:T(8,128)(2,1)}, bf16[2048,128]{1,0:T(8,128)(2,1)S(1)}, u32[]{:S(2)}, u32[]{:S(2)}) collective-permute-start(bf16[2048,128]{1,0:T(8,128)(2,1)} %copy-done.6), channel_id=1, source_target_pairs={{0,32},{16,48},{32,0},{48,16},{1,33},{17,49},{33,1},{49,17},{2,34}... | collective-permute-start | bytes 1572872 | tf_op jit(solution)/shard_map/ppermute | solution.py:271
  18.5 1.1 collective-permute-start.2
  19.6 0.9 collective-permute-start
  20.5 7.5 %project_query.1.q_ref = bf16[128,1024]{1,0:T(8,128)(2,1)S(1)} custom-call(bf16[128,8192]{1,0:T(8,128)(2,1)S(1)} %bitcast.12, bf16[8192,1280]{1,0:T(8,128)(2,1)} %w_ref.1), custom_call_target="tpu_custom_call" | custom-call | flops 2147483648 | bytes 20971520 | tf_op jit(solution)/shard_map/project_query/pallas_call | solution.py:92
  28.1 0.0 copy-start.2
  28.1 0.7 copy-done.2
  28.8 0.9 copy-done.3
  29.7 0.9 copy-done.7
  30.7 6.6 %attention.1 = (bf16[128,1024]{1,0:T(8,128)(2,1)S(1)}, bf16[1024,256]{1,0:T(8,128)(2,1)S(1)}) custom-call(s32[3]{0:T(128)S(1)} %pad_add_fusion.refs_0_.where_ref, s32[1,16]{1,0:T(1,128)S(1)} %copy-done.8, s32[1,4]{1,0:T(1,128)S(1)} %copy-done.9, bf16[128,1024]{1,0:T(8,128)(2,1)S(1)} %copy-done.3, bf16[128,1024]{1,0:T(8,128)(2,1)S(1)} %bitcast.14, ...), custom_call_target="tpu_custom_call" | custom-call | flops 1342177280 | bytes 4000000 | tf_op jit(solution)/shard_map/attention/pallas_call | solution.py:206
  37.2 0.0 copy-start.1
  37.3 4.8 %collective-permute-done.2.refs_3_ = bf16[2048,128]{1,0:T(8,128)(2,1)} collective-permute-done((bf16[2048,128]{1,0:T(8,128)(2,1)}, bf16[2048,128]{1,0:T(8,128)(2,1)}, u32[]{:S(2)}, u32[]{:S(2)}) %collective-permute-start.2) | collective-permute-done | bytes 524320 | tf_op jit(solution)/shard_map/ppermute | solution.py:271
  42.0 0.0 collective-permute-done.refs_1_
  42.1 1.3 send_half.1
  43.3 0.1 collective-permute-start.3
  43.4 2.7 %collective-permute-start.6 = (bf16[128,1024]{1,0:T(8,128)(2,1)S(1)}, bf16[128,1024]{1,0:T(8,128)(2,1)}, u32[]{:S(2)}, u32[]{:S(2)}) collective-permute-start(bf16[128,1024]{1,0:T(8,128)(2,1)S(1)} %get-tuple-element.17.refs_0_), channel_id=1, source_target_pairs={{0,48},{16,0},{32,16},{48,32},{1,49},{17,1},{33,17},{49,33},{2,50}... | collective-permute-start | bytes 786440 | tf_op jit(solution)/shard_map/ppermute | solution.py:271
  46.1 6.9 %all-to-all-start.1 = ((bf16[8,128,256]{2,1,0:T(8,128)(2,1)}), bf16[8,128,256]{2,1,0:T(8,128)(2,1)}, u32[]{:S(2)}, u32[]{:S(2)}) async-start(bf16[8,128,256]{2,1,0:T(8,128)(2,1)} %bitcast.13), calls=%async_computation.1 | async-start | bytes 1048576 | tf_op jit(solution)/shard_map/all_to_all | solution.py:308
  53.1 0.0 collective-permute-start.4
  53.1 2.3 %collective-permute-start.5 = (bf16[128,1024]{1,0:T(8,128)(2,1)S(1)}, bf16[128,1024]{1,0:T(8,128)(2,1)}, u32[]{:S(2)}, u32[]{:S(2)}) collective-permute-start(bf16[128,1024]{1,0:T(8,128)(2,1)S(1)} %get-tuple-element.17.refs_0_), channel_id=1, source_target_pairs={{0,32},{16,48},{32,0},{48,16},{1,33},{17,49},{33,1},{49,17},{2,34}... | collective-permute-start | bytes 786440 | tf_op jit(solution)/shard_map/ppermute | solution.py:271
  55.4 0.5 collective-permute-start.10
  55.9 12.2 %collective-permute-done.4.refs_1_ = bf16[128,1024]{1,0:T(8,128)(2,1)} collective-permute-done((bf16[128,1024]{1,0:T(8,128)(2,1)S(1)}, bf16[128,1024]{1,0:T(8,128)(2,1)}, u32[]{:S(2)}, u32[]{:S(2)}) %collective-permute-start.4) | collective-permute-done | bytes 262176 | tf_op jit(solution)/shard_map/ppermute | solution.py:271
  68.1 0.5 collective-permute-start.9
  68.6 0.0 all-to-all-done.1
  68.6 1.1 reduce_sum.21.refs_0_
  69.7 0.0 collective-permute-done.7.refs_4_
  69.7 0.1 collective-permute-start.11
  69.8 0.0 collective-permute-done.10.refs_7_
  69.8 0.9 collective-permute-start.12
  70.8 0.0 collective-permute-done.3.refs_4_
  70.8 2.6 %collective-permute-start.13 = (bf16[128,256]{1,0:T(8,128)(2,1)S(1)}, bf16[128,256]{1,0:T(8,128)(2,1)S(1)}, u32[]{:S(2)}, u32[]{:S(2)}) collective-permute-start(bf16[128,256]{1,0:T(8,128)(2,1)S(1)} %reduce_sum.21.refs_0_), channel_id=1, source_target_pairs={{0,48},{16,0},{32,16},{48,32},{1,49},{17,1},{33,17},{49,33},{2,50}... | collective-permute-start | bytes 196616 | tf_op jit(solution)/shard_map/ppermute | solution.py:271
  73.3 1.8 %join.1.x_ref = bf16[1024,1024]{1,0:T(8,128)(2,1)S(1)} custom-call(s32[3]{0:T(128)S(1)} %pad_add_fusion.refs_0_.where_ref, bf16[2048,128]{1,0:T(8,128)(2,1)S(1)} %get-tuple-element.19.refs_0_, bf16[2048,128]{1,0:T(8,128)(2,1)} %collective-permute-done.refs_1_, bf16[2048,128]{1,0:T(8,128)(2,1)S(1)} %collective-permute-done.1.refs_2_, ...), custom_call_target="tpu_custom_call" | custom-call | bytes 1048576 | tf_op jit(solution)/shard_map/join/pallas_call | solution.py:138
  75.1 0.0 collective-permute-done.8.refs_5_
  75.1 0.1 collective-permute-start.14
  75.2 1.2 collective-permute-done.11.refs_1_
  76.4 0.5 collective-permute-start.16
  76.9 0.1 collective-permute-done.13.refs_3_
  77.0 0.0 collective-permute-start.17
  77.0 3.7 %term_q.1.done_ref = bf16[1024,1024]{1,0:T(8,128)(2,1)S(1)} custom-call(bf16[1024,1024]{1,0:T(8,128)(2,1)S(1)} %join.1.x_ref, bf16[128,1024]{1,0:T(8,128)(2,1)S(1)} %get-tuple-element.17.refs_0_, bf16[128,1024]{1,0:T(8,128)(2,1)} %collective-permute-done.4.refs_1_, bf16[128,1024]{1,0:T(8,128)(2,1)} %collective-permute-done.5.refs_2_, ...), custom_call_target="tpu_custom_call" | custom-call | flops 2147483648 | bytes 2097152 | tf_op jit(solution)/shard_map/term_q/pallas_call | solution.py:236
  80.8 2.3 %term_kv.1 = bf16[1024,1280]{1,0:T(8,128)(2,1)} custom-call(bf16[1024,1024]{1,0:T(8,128)(2,1)S(1)} %join.1.x_ref, bf16[1024,1024]{1,0:T(8,128)(2,1)S(1)} %term_q.1.done_ref, bf16[128,256]{1,0:T(8,128)(2,1)S(1)} %reduce_sum.21.refs_0_, bf16[128,256]{1,0:T(8,128)(2,1)S(1)} %collective-permute-done.11.refs_1_, ...), custom_call_target="tpu_custom_call" | custom-call | flops 536870912 | bytes 524288 | tf_op jit(solution)/shard_map/term_kv/pallas_call | solution.py:258
  83.2 7.2 %all-to-all-start.2 = ((bf16[16,64,1280]{2,1,0:T(8,128)(2,1)}), bf16[16,64,1280]{2,1,0:T(8,128)(2,1)}, u32[]{:S(2)}, u32[]{:S(2)}) async-start(bf16[16,64,1280]{2,1,0:T(8,128)(2,1)} %bitcast.8), calls=%async_computation.2 | async-start | bytes 5242880 | tf_op jit(solution)/shard_map/all_to_all | solution.py:290
  90.4 11.9 %fusion = bf16[1,128,8192]{2,1,0:T(8,128)(2,1)} fusion(bf16[8192,1280]{1,0:T(8,128)(2,1)} %w_ref.1, bf16[128,256]{1,0:T(8,128)(2,1)S(1)} %reduce_sum.21.refs_0_, bf16[128,1024]{1,0:T(8,128)(2,1)S(1)} %get-tuple-element.17.refs_0_), kind=kOutput, calls=%fused_computation.1 | convolution fusion | flops 2686058496 | bytes 23396352 | tf_op jit(solution)/shard_map/dot_general | solution.py:17
  102.4 30.1 %all-to-all-done.2 = bf16[16,64,1280]{2,1,0:T(8,128)(2,1)} async-done(((bf16[16,64,1280]{2,1,0:T(8,128)(2,1)}), bf16[16,64,1280]{2,1,0:T(8,128)(2,1)}, u32[]{:S(2)}, u32[]{:S(2)}) %all-to-all-start.2) | async-done | bytes 2621472 | tf_op jit(solution)/shard_map/all_to_all | solution.py:290
  132.4 2.8 %convert_reduce_fusion = f32[64,1280]{1,0:T(8,128)} fusion(bf16[16,64,1280]{2,1,0:T(8,128)(2,1)} %all-to-all-done.2), kind=kLoop, calls=%fused_computation.2 | loop fusion | flops 2539520 | bytes 2949120 | tf_op jit(solution)/shard_map/reduce_sum | solution.py:319
  (25 shorter events, 0.1 us)
Async XLA Ops:
  0.7 19.8 %copy-start = (bf16[1,128,8192]{2,1,0:T(8,128)(2,1)S(1)}, bf16[1,128,8192]{2,1,0:T(8,128)(2,1)}, u32[]{:S(2)}) copy-start(bf16[1,128,8192]{2,1,0:T(8,128)(2,1)} %param.5) | copy-start | bytes 6291460
  5.2 0.8 copy-start.4
  6.0 0.8 copy-start.5
  6.8 0.8 copy-start.6
  7.6 21.1 %all-to-all-start = ((bf16[8,128,256]{2,1,0:T(8,128)(2,1)}), bf16[8,128,256]{2,1,0:T(8,128)(2,1)}, u32[]{:S(2)}, u32[]{:S(2)}) async-start(bf16[8,128,256]{2,1,0:T(8,128)(2,1)} %get-tuple-element.16), calls=%async_computation | async-start | bytes 1048576 | tf_op jit(solution)/shard_map/all_to_all | solution.py:303
  15.5 21.8 %collective-permute-start.1 = (bf16[2048,128]{1,0:T(8,128)(2,1)}, bf16[2048,128]{1,0:T(8,128)(2,1)S(1)}, u32[]{:S(2)}, u32[]{:S(2)}) collective-permute-start(bf16[2048,128]{1,0:T(8,128)(2,1)} %copy-done.6), channel_id=1, source_target_pairs={{0,32},{16,48},{32,0},{48,16},{1,33},{17,49},{33,1},{49,17},{2,34}... | collective-permute-start | bytes 1572872 | tf_op jit(solution)/shard_map/ppermute | solution.py:271
  18.5 23.5 %collective-permute-start.2 = (bf16[2048,128]{1,0:T(8,128)(2,1)}, bf16[2048,128]{1,0:T(8,128)(2,1)}, u32[]{:S(2)}, u32[]{:S(2)}) collective-permute-start(bf16[2048,128]{1,0:T(8,128)(2,1)} %copy-done.5), channel_id=1, source_target_pairs={{0,48},{16,0},{32,16},{48,32},{1,49},{17,1},{33,17},{49,33},{2,50}... | collective-permute-start | bytes 1572872 | tf_op jit(solution)/shard_map/ppermute | solution.py:271
  19.6 22.4 %collective-permute-start = (bf16[2048,128]{1,0:T(8,128)(2,1)}, bf16[2048,128]{1,0:T(8,128)(2,1)}, u32[]{:S(2)}, u32[]{:S(2)}) collective-permute-start(bf16[2048,128]{1,0:T(8,128)(2,1)} %copy-done.4), channel_id=1, source_target_pairs={{0,16},{16,32},{32,48},{48,0},{1,17},{17,33},{33,49},{49,1},{2,18}... | collective-permute-start | bytes 1572872 | tf_op jit(solution)/shard_map/ppermute | solution.py:271
  20.5 8.2 %copy-start.8 = (s32[1,16]{1,0:T(1,128)S(1)}, s32[1,16]{1,0:T(1,128)}, u32[]{:S(2)}) copy-start(s32[1,16]{1,0:T(1,128)} %order_ref.1) | copy-start | bytes 196
  20.5 8.2 %copy-start.9 = (s32[1,4]{1,0:T(1,128)S(1)}, s32[1,4]{1,0:T(1,128)}, u32[]{:S(2)}) copy-start(s32[1,4]{1,0:T(1,128)} %lens_ref.1) | copy-start | bytes 52
  28.1 0.7 copy-start.2
  28.8 1.0 copy-start.3
  29.7 0.9 copy-start.7
  37.2 8.9 %copy-start.1 = (bf16[1024,256]{1,0:T(8,128)(2,1)}, bf16[1024,256]{1,0:T(8,128)(2,1)S(1)}, u32[]{:S(2)}) copy-start(bf16[1024,256]{1,0:T(8,128)(2,1)S(1)} %get-tuple-element.18) | copy-start | bytes 1572868
  43.3 27.4 %collective-permute-start.3 = (bf16[4,1024,128]{2,1,0:T(8,128)(2,1)S(1)}, bf16[4,1024,128]{2,1,0:T(8,128)(2,1)S(1)}, u32[]{:S(2)}, u32[]{:S(2)}) collective-permute-start(bf16[4,1024,128]{2,1,0:T(8,128)(2,1)S(1)} %send_half.1), channel_id=1, source_target_pairs={{0,8},{8,0},{1,9},{9,1},{2,10},{10,2},{3,11},{11,3},{4,12},{12,4},... | collective-permute-start | bytes 3145736 | tf_op jit(solution)/shard_map/ppermute | solution.py:275
  43.4 11.9 %collective-permute-start.6 = (bf16[128,1024]{1,0:T(8,128)(2,1)S(1)}, bf16[128,1024]{1,0:T(8,128)(2,1)}, u32[]{:S(2)}, u32[]{:S(2)}) collective-permute-start(bf16[128,1024]{1,0:T(8,128)(2,1)S(1)} %get-tuple-element.17.refs_0_), channel_id=1, source_target_pairs={{0,48},{16,0},{32,16},{48,32},{1,49},{17,1},{33,17},{49,33},{2,50}... | collective-permute-start | bytes 786440 | tf_op jit(solution)/shard_map/ppermute | solution.py:271
  46.1 22.5 %all-to-all-start.1 = ((bf16[8,128,256]{2,1,0:T(8,128)(2,1)}), bf16[8,128,256]{2,1,0:T(8,128)(2,1)}, u32[]{:S(2)}, u32[]{:S(2)}) async-start(bf16[8,128,256]{2,1,0:T(8,128)(2,1)} %bitcast.13), calls=%async_computation.1 | async-start | bytes 1048576 | tf_op jit(solution)/shard_map/all_to_all | solution.py:308
  53.1 15.0 %collective-permute-start.4 = (bf16[128,1024]{1,0:T(8,128)(2,1)S(1)}, bf16[128,1024]{1,0:T(8,128)(2,1)}, u32[]{:S(2)}, u32[]{:S(2)}) collective-permute-start(bf16[128,1024]{1,0:T(8,128)(2,1)S(1)} %get-tuple-element.17.refs_0_), channel_id=1, source_target_pairs={{0,16},{16,32},{32,48},{48,0},{1,17},{17,33},{33,49},{49,1},{2,18}... | collective-permute-start | bytes 786440 | tf_op jit(solution)/shard_map/ppermute | solution.py:271
  53.1 15.0 %collective-permute-start.5 = (bf16[128,1024]{1,0:T(8,128)(2,1)S(1)}, bf16[128,1024]{1,0:T(8,128)(2,1)}, u32[]{:S(2)}, u32[]{:S(2)}) collective-permute-start(bf16[128,1024]{1,0:T(8,128)(2,1)S(1)} %get-tuple-element.17.refs_0_), channel_id=1, source_target_pairs={{0,32},{16,48},{32,0},{48,16},{1,33},{17,49},{33,1},{49,17},{2,34}... | collective-permute-start | bytes 786440 | tf_op jit(solution)/shard_map/ppermute | solution.py:271
  55.4 14.4 %collective-permute-start.7 = (bf16[128,1024]{1,0:T(8,128)(2,1)S(1)}, bf16[128,1024]{1,0:T(8,128)(2,1)}, u32[]{:S(2)}, u32[]{:S(2)}) collective-permute-start(bf16[128,1024]{1,0:T(8,128)(2,1)S(1)} %get-tuple-element.17.refs_0_), channel_id=1, source_target_pairs={{0,8},{8,0},{1,9},{9,1},{2,10},{10,2},{3,11},{11,3},{4,12},{12,4},... | collective-permute-start | bytes 786440 | tf_op jit(solution)/shard_map/ppermute | solution.py:275
  55.4 14.5 %collective-permute-start.10 = (bf16[128,1024]{1,0:T(8,128)(2,1)}, bf16[128,1024]{1,0:T(8,128)(2,1)}, u32[]{:S(2)}, u32[]{:S(2)}) collective-permute-start(bf16[128,1024]{1,0:T(8,128)(2,1)} %collective-permute-done.6.refs_3_), channel_id=1, source_target_pairs={{0,8},{8,0},{1,9},{9,1},{2,10},{10,2},{3,11},{11,3},{4,12},{12,4},... | collective-permute-start | bytes 786440 | tf_op jit(solution)/shard_map/ppermute | solution.py:275
  68.1 7.0 %collective-permute-start.8 = (bf16[128,1024]{1,0:T(8,128)(2,1)}, bf16[128,1024]{1,0:T(8,128)(2,1)}, u32[]{:S(2)}, u32[]{:S(2)}) collective-permute-start(bf16[128,1024]{1,0:T(8,128)(2,1)} %collective-permute-done.4.refs_1_), channel_id=1, source_target_pairs={{0,8},{8,0},{1,9},{9,1},{2,10},{10,2},{3,11},{11,3},{4,12},{12,4},... | collective-permute-start | bytes 786440 | tf_op jit(solution)/shard_map/ppermute | solution.py:275
  68.1 8.9 %collective-permute-start.9 = (bf16[128,1024]{1,0:T(8,128)(2,1)}, bf16[128,1024]{1,0:T(8,128)(2,1)}, u32[]{:S(2)}, u32[]{:S(2)}) collective-permute-start(bf16[128,1024]{1,0:T(8,128)(2,1)} %collective-permute-done.5.refs_2_), channel_id=1, source_target_pairs={{0,8},{8,0},{1,9},{9,1},{2,10},{10,2},{3,11},{11,3},{4,12},{12,4},... | collective-permute-start | bytes 786440 | tf_op jit(solution)/shard_map/ppermute | solution.py:275
  69.7 6.7 %collective-permute-start.11 = (bf16[128,256]{1,0:T(8,128)(2,1)S(1)}, bf16[128,256]{1,0:T(8,128)(2,1)S(1)}, u32[]{:S(2)}, u32[]{:S(2)}) collective-permute-start(bf16[128,256]{1,0:T(8,128)(2,1)S(1)} %reduce_sum.21.refs_0_), channel_id=1, source_target_pairs={{0,16},{16,32},{32,48},{48,0},{1,17},{17,33},{33,49},{49,1},{2,18}... | collective-permute-start | bytes 196616 | tf_op jit(solution)/shard_map/ppermute | solution.py:271
  69.8 6.6 %collective-permute-start.12 = (bf16[128,256]{1,0:T(8,128)(2,1)S(1)}, bf16[128,256]{1,0:T(8,128)(2,1)S(1)}, u32[]{:S(2)}, u32[]{:S(2)}) collective-permute-start(bf16[128,256]{1,0:T(8,128)(2,1)S(1)} %reduce_sum.21.refs_0_), channel_id=1, source_target_pairs={{0,32},{16,48},{32,0},{48,16},{1,33},{17,49},{33,1},{49,17},{2,34}... | collective-permute-start | bytes 196616 | tf_op jit(solution)/shard_map/ppermute | solution.py:271
  70.8 6.3 %collective-permute-start.13 = (bf16[128,256]{1,0:T(8,128)(2,1)S(1)}, bf16[128,256]{1,0:T(8,128)(2,1)S(1)}, u32[]{:S(2)}, u32[]{:S(2)}) collective-permute-start(bf16[128,256]{1,0:T(8,128)(2,1)S(1)} %reduce_sum.21.refs_0_), channel_id=1, source_target_pairs={{0,48},{16,0},{32,16},{48,32},{1,49},{17,1},{33,17},{49,33},{2,50}... | collective-permute-start | bytes 196616 | tf_op jit(solution)/shard_map/ppermute | solution.py:271
  75.1 5.7 %collective-permute-start.14 = (bf16[128,256]{1,0:T(8,128)(2,1)S(1)}, bf16[128,256]{1,0:T(8,128)(2,1)S(1)}, u32[]{:S(2)}, u32[]{:S(2)}) collective-permute-start(bf16[128,256]{1,0:T(8,128)(2,1)S(1)} %reduce_sum.21.refs_0_), channel_id=1, source_target_pairs={{0,8},{8,0},{1,9},{9,1},{2,10},{10,2},{3,11},{11,3},{4,12},{12,4},... | collective-permute-start | bytes 196616 | tf_op jit(solution)/shard_map/ppermute | solution.py:275
  76.4 4.4 %collective-permute-start.15 = (bf16[128,256]{1,0:T(8,128)(2,1)S(1)}, bf16[128,256]{1,0:T(8,128)(2,1)S(1)}, u32[]{:S(2)}, u32[]{:S(2)}) collective-permute-start(bf16[128,256]{1,0:T(8,128)(2,1)S(1)} %collective-permute-done.11.refs_1_), channel_id=1, source_target_pairs={{0,8},{8,0},{1,9},{9,1},{2,10},{10,2},{3,11},{11,3},{4,12},{12,4},... | collective-permute-start | bytes 196616 | tf_op jit(solution)/shard_map/ppermute | solution.py:275
  76.4 4.4 %collective-permute-start.16 = (bf16[128,256]{1,0:T(8,128)(2,1)S(1)}, bf16[128,256]{1,0:T(8,128)(2,1)S(1)}, u32[]{:S(2)}, u32[]{:S(2)}) collective-permute-start(bf16[128,256]{1,0:T(8,128)(2,1)S(1)} %collective-permute-done.12.refs_2_), channel_id=1, source_target_pairs={{0,8},{8,0},{1,9},{9,1},{2,10},{10,2},{3,11},{11,3},{4,12},{12,4},... | collective-permute-start | bytes 196616 | tf_op jit(solution)/shard_map/ppermute | solution.py:275
  77.0 3.8 %collective-permute-start.17 = (bf16[128,256]{1,0:T(8,128)(2,1)S(1)}, bf16[128,256]{1,0:T(8,128)(2,1)S(1)}, u32[]{:S(2)}, u32[]{:S(2)}) collective-permute-start(bf16[128,256]{1,0:T(8,128)(2,1)S(1)} %collective-permute-done.13.refs_3_), channel_id=1, source_target_pairs={{0,8},{8,0},{1,9},{9,1},{2,10},{10,2},{3,11},{11,3},{4,12},{12,4},... | collective-permute-start | bytes 196616 | tf_op jit(solution)/shard_map/ppermute | solution.py:275
  83.2 49.3 %all-to-all-start.2 = ((bf16[16,64,1280]{2,1,0:T(8,128)(2,1)}), bf16[16,64,1280]{2,1,0:T(8,128)(2,1)}, u32[]{:S(2)}, u32[]{:S(2)}) async-start(bf16[16,64,1280]{2,1,0:T(8,128)(2,1)} %bitcast.8), calls=%async_computation.2 | async-start | bytes 5242880 | tf_op jit(solution)/shard_map/all_to_all | solution.py:290

commit v4 on v3

v4 whole, which is shorter than its diff:
```python
import jax
import jax.numpy as jnp
from jax import lax
from jax.experimental import pallas as pl
from jax.experimental.pallas import tpu as pltpu
from jax.sharding import Mesh, PartitionSpec as P

HD = 128
HQ = 8
SPAN = 64
LOG2E = 1.4426950408889634
FIRST = 768
SEQ = ("zhi", "y")
DEPTH = ("zlo", "zhi")


def nt(a, b):
    return lax.dot_general(a, b, (((1,), (1,)), ((), ())), preferred_element_type=jnp.float32)


def tn(a, b):
    return lax.dot_general(a, b, (((0,), (0,)), ((), ())), preferred_element_type=jnp.float32)


def nn(a, b):
    return jnp.dot(a, b, preferred_element_type=jnp.float32)


SMEM = pl.BlockSpec(memory_space=pltpu.SMEM)
VMEM = pl.BlockSpec(memory_space=pltpu.VMEM)
MIB = 1024 * 1024
SMALL = pl.CostEstimate(flops=1, bytes_accessed=1, transcendentals=0)


def whole(value):
    return pl.BlockSpec(value.shape, lambda i: (0,) * value.ndim)


def pack_kernel(where_ref, x_ref, *out_refs):
    chips = len(out_refs)
    step = pl.program_id(0)
    features = x_ref.shape[1]
    width = features // (4 * chips)
    for s in range(chips):
        chip = lax.rem(where_ref[0] + s, chips)
        for z in range(2):
            at = pl.multiple_of(z * (features // 2) + chip * 2 * width + step * width, width)
            out_refs[s][z * width : (z + 1) * width, :] = x_ref[:, pl.ds(at, width)].T


def pack(where, x, chips):
    tokens, features = x.shape
    return pl.pallas_call(
        pack_kernel,
        grid=(2,),
        out_shape=(pltpu.HBM((features // chips, tokens), x.dtype),) * chips,
        in_specs=[SMEM, whole(x)],
        out_specs=(pl.BlockSpec((features // chips // 2, tokens), lambda i: (i, 0)),) * chips,
        compiler_params=pltpu.CompilerParams(vmem_limit_bytes=60 * MIB),
        cost_estimate=SMALL,
        name="pack",
    )(where, x)


def kv_kernel(x_ref, w_ref, kv_ref, acc_ref):
    step = pl.program_id(0)
    part = nn(x_ref[...], w_ref[...])

    @pl.when(step == 0)
    def _():
        acc_ref[...] = part

    @pl.when(step > 0)
    def _():
        acc_ref[...] += part

    @pl.when(step == pl.num_programs(0) - 1)
    def _():
        low = acc_ref[...].astype(jnp.bfloat16)
        for i in range(kv_ref.shape[0]):
            kv_ref[i] = low


def project_kv(x, w, copies):
    tokens, features = x.shape
    width = 2 * HD
    depth = features // 2
    return pl.pallas_call(
        kv_kernel,
        grid=(features // depth,),
        out_shape=pltpu.HBM((copies, tokens, width), jnp.bfloat16),
        in_specs=[
            pl.BlockSpec((tokens, depth), lambda i: (0, i)),
            pl.BlockSpec((depth, width), lambda i: (i, HQ // 2)),
        ],
        out_specs=pl.BlockSpec((copies, tokens, width), lambda i: (0, 0, 0)),
        scratch_shapes=[pltpu.VMEM((tokens, width), jnp.float32)],
        compiler_params=pltpu.CompilerParams(vmem_limit_bytes=60 * MIB),
        cost_estimate=SMALL,
        name="project_kv",
    )(x, w)


def query_kernel(x_ref, w_ref, out_ref):
    out_ref[...] = nn(x_ref[...], w_ref[...]).astype(jnp.bfloat16)


def project_query(x, w):
    tokens, features = x.shape
    width = 2 * HD
    return pl.pallas_call(
        query_kernel,
        grid=(HQ // 2,),
        out_shape=pltpu.HBM((tokens, HQ * HD), jnp.bfloat16),
        in_specs=[pl.BlockSpec((tokens, features), lambda i: (0, 0)), pl.BlockSpec((features, width), lambda i: (0, i))],
        out_specs=pl.BlockSpec((tokens, width), lambda i: (0, i)),
        compiler_params=pltpu.CompilerParams(vmem_limit_bytes=60 * MIB),
        cost_estimate=SMALL,
        name="project_query",
    )(x, w)


def halves_kernel(where_ref, *refs):
    pieces, own_ref, send_ref = refs[:-2], refs[-2], refs[-1]
    half, tokens = own_ref.shape[0], pieces[0].shape[1]
    own = pl.multiple_of(where_ref[1] * half, half)
    send = pl.multiple_of((1 - where_ref[1]) * half, half)
    for i, piece in enumerate(pieces):
        own_ref[:, i * tokens : (i + 1) * tokens] = piece[pl.ds(own, half), :]
        send_ref[:, i * tokens : (i + 1) * tokens] = piece[pl.ds(send, half), :]


def halves(where, pieces):
    rows, tokens = pieces[0].shape
    shape = (rows // 2, len(pieces) * tokens)
    return pl.pallas_call(
        halves_kernel,
        grid=(1,),
        out_shape=(pltpu.HBM(shape, jnp.bfloat16),) * 2,
        in_specs=[SMEM] + [whole(piece) for piece in pieces],
        out_specs=(pl.BlockSpec(shape, lambda i: (0, 0)),) * 2,
        compiler_params=pltpu.CompilerParams(vmem_limit_bytes=20 * MIB),
        cost_estimate=SMALL,
        name="halves",
    )(where, *pieces)


def attention_kernel(where_ref, order_ref, lens_ref, q_ref, do_ref, kv_ref, dq_ref, dkv_ref, bias_ref, dk_ref, dv_ref):
    scale = HD ** (-0.5)
    spans = order_ref.shape[1]
    docs = lens_ref.shape[1]
    place = where_ref[2]
    lane = lax.broadcasted_iota(jnp.int32, (1, 2 * SPAN), 1)
    pos_q = jnp.where(
        lane < SPAN,
        order_ref[0, 2 * place] * SPAN + lane,
        order_ref[0, 2 * place + 1] * SPAN + lane - SPAN,
    )
    start = jnp.zeros_like(pos_q)
    end = jnp.int32(0)
    for i in range(docs):
        end = end + lens_ref[0, i]
        start = jnp.where(pos_q >= end, end, start)
    row = lax.broadcasted_iota(jnp.int32, (SPAN, 2 * SPAN), 0)
    for s in range(spans):
        pos_k = order_ref[0, s] * SPAN + row
        allowed = (pos_k <= pos_q) & (pos_k >= start)
        bias_ref[s * SPAN : (s + 1) * SPAN, :] = jnp.where(allowed, 0.0, -jnp.inf)
    k = kv_ref[:, :HD]
    v = kv_ref[:, HD:]
    for h in range(0, HQ, 2):
        a, b, c = h * HD, (h + 1) * HD, (h + 2) * HD
        q2 = jnp.concatenate([q_ref[:, a:b], q_ref[:, b:c]], axis=0)
        d2 = jnp.concatenate([do_ref[:, a:b], do_ref[:, b:c]], axis=0)
        bias = bias_ref[...]
        s2 = nt(k, q2) + jnp.concatenate([bias, bias], axis=1)
        peak = jnp.max(s2, axis=0, keepdims=True)
        expo = jnp.exp2((s2 - peak) * (scale * LOG2E))
        inverse = 1.0 / jnp.sum(expo, axis=0, keepdims=True)
        probs = expo * inverse
        low = probs.astype(jnp.bfloat16)
        dp = nt(v, d2)
        delta = jnp.sum(low.astype(jnp.float32) * dp, axis=0, keepdims=True)
        ds = (probs * ((dp - delta) * scale)).astype(jnp.bfloat16)
        dq = tn(ds, k).astype(jnp.bfloat16)
        dq_ref[:, a:b] = dq[:HD]
        dq_ref[:, b:c] = dq[HD:]
        dv = nn(low, d2)
        dk = nn(ds, q2)
        if h > 0:
            dv += dv_ref[...]
            dk += dk_ref[...]
        if h < HQ - 2:
            dv_ref[...] = dv
            dk_ref[...] = dk
        else:
            dkv_ref[:, :HD] = dk.astype(jnp.bfloat16)
            dkv_ref[:, HD:] = dv.astype(jnp.bfloat16)


def attention(where, order, lens, query, grad, key_value):
    tokens = query.shape[0]
    total = key_value.shape[0]
    work = HQ * tokens * total
    return pl.pallas_call(
        attention_kernel,
        out_shape=(
            pltpu.HBM((tokens, HQ * HD), jnp.bfloat16),
            pltpu.HBM((total, 2 * HD), jnp.bfloat16),
        ),
        grid=(1,),
        in_specs=[SMEM, SMEM, SMEM] + [whole(v) for v in (query, grad, key_value)],
        out_specs=(whole(query), whole(key_value)),
        scratch_shapes=[
            pltpu.VMEM((total, tokens), jnp.float32),
            pltpu.VMEM((total, HD), jnp.float32),
            pltpu.VMEM((total, HD), jnp.float32),
        ],
        compiler_params=pltpu.CompilerParams(vmem_limit_bytes=24 * MIB),
        cost_estimate=SMALL,
        name="attention",
    )(where, order, lens, query, grad, key_value)


def both(x_own, x_other, pieces, at, width):
    n = len(pieces) // 2
    near = jnp.concatenate([g[:, pl.ds(at, width)] for g in pieces[:n]], axis=0)
    far = jnp.concatenate([g[:, pl.ds(at, width)] for g in pieces[n:]], axis=0)
    return nn(x_own, near) + nn(x_other, far)


def term_query_kernel(own_ref, other_ref, *refs):
    pieces, out_ref, done_ref = refs[:-2], refs[-2], refs[-1]
    step = pl.program_id(0)
    width = out_ref.shape[2]
    at = pl.multiple_of(step * width, width)
    part = both(own_ref[...], other_ref[...], pieces, at, width).astype(out_ref.dtype)
    blocks = out_ref.shape[0]
    rows = own_ref.shape[0] // (blocks * blocks)

    @pl.when(step < FIRST // (2 * HD))
    def _():
        for i in range(blocks):
            for y in range(blocks):
                here = (i * blocks + y) * rows
                out_ref[y, i * rows : (i + 1) * rows, :] = part[here : here + rows]

    @pl.when(step >= FIRST // (2 * HD))
    def _():
        done_ref[...] = part


def term_query(own, other, pieces, blocks):
    half, depth = own.shape
    width = pieces[0].shape[1]
    step = 2 * HD
    first = FIRST // step
    return pl.pallas_call(
        term_query_kernel,
        grid=(width // step,),
        out_shape=(
            pltpu.HBM((blocks, half // blocks, FIRST), jnp.bfloat16),
            pltpu.HBM((half, width - FIRST), jnp.bfloat16),
        ),
        in_specs=[whole(own), whole(other)] + [VMEM] * len(pieces),
        out_specs=(
            pl.BlockSpec((blocks, half // blocks, step), lambda j: (0, 0, jnp.minimum(j, first - 1))),
            pl.BlockSpec((half, step), lambda j: (0, jnp.maximum(j - first, 0))),
        ),
        compiler_params=pltpu.CompilerParams(vmem_limit_bytes=20 * MIB),
        cost_estimate=SMALL,
        name="term_query",
    )(own, other, *pieces)


def ring_block(where_ref, s):
    place = lax.rem(where_ref[3] + s, 4)
    return 2 * lax.rem(place, 2) + place // 2


def term_second_kernel(where_ref, own_ref, other_ref, done_ref, *refs):
    pieces, outs = refs[:-4], refs[-4:]
    rows = outs[0].shape[0]
    done = done_ref.shape[1]
    for s in range(4):
        at = pl.multiple_of(ring_block(where_ref, s) * rows, rows)
        outs[s][:, :done] = done_ref[pl.ds(at, rows), :]
        part = both(own_ref[pl.ds(at, rows), :], other_ref[pl.ds(at, rows), :], pieces, 0, pieces[0].shape[1])
        outs[s][:, done:] = part.astype(outs[s].dtype)


def term_second(where, own, other, done, pieces):
    half, depth = own.shape
    width = pieces[0].shape[1]
    out = pltpu.HBM((half // 4, done.shape[1] + width), jnp.bfloat16)
    return pl.pallas_call(
        term_second_kernel,
        grid=(1,),
        out_shape=(out,) * 4,
        in_specs=[SMEM] + [whole(value) for value in (own, other, done)] + [VMEM] * len(pieces),
        out_specs=(pl.BlockSpec(out.shape, lambda i: (0, 0)),) * 4,
        compiler_params=pltpu.CompilerParams(vmem_limit_bytes=20 * MIB),
        cost_estimate=SMALL,
        name="term_second",
    )(where, own, other, done, *pieces)


def middle_kernel(along_z, where_ref, *refs):
    parts, outs = refs[:-4], refs[-4:]
    rows = outs[0].shape[0]
    for s in range(4):
        block = ring_block(where_ref, s) if along_z else lax.rem(where_ref[4] + s, 4)
        at = pl.multiple_of(block * rows, rows)
        total = sum(part[pl.ds(at, rows), :].astype(jnp.float32) for part in parts)
        outs[s][...] = total.astype(outs[s].dtype)


def middle_stacked_kernel(where_ref, stack_ref, *outs):
    middle_kernel(True, where_ref, *[stack_ref.at[i] for i in range(stack_ref.shape[0])], *outs)


def middle(where, parts, along_z):
    stacked = len(parts) == 1
    rows, width = parts[0].shape[-2:]
    return pl.pallas_call(
        middle_stacked_kernel if stacked else lambda *refs: middle_kernel(along_z, *refs),
        grid=(1,),
        out_shape=(pltpu.HBM((rows // 4, width), jnp.float32),) + (pltpu.HBM((rows // 4, width), jnp.bfloat16),) * 3,
        in_specs=[SMEM] + [whole(part) for part in parts],
        out_specs=(pl.BlockSpec((rows // 4, width), lambda i: (0, 0)),) * 4,
        compiler_params=pltpu.CompilerParams(vmem_limit_bytes=14 * MIB),
        cost_estimate=SMALL,
        name="middle_z" if along_z else "middle_y",
    )(where, *parts)


def final_kernel(*refs):
    out_ref = refs[-1]
    out_ref[:, :FIRST] = sum(part[...].astype(jnp.float32) for part in refs[:4])
    out_ref[:, FIRST:] = sum(part[...].astype(jnp.float32) for part in refs[4:8])


def final(parts):
    rows = parts[0].shape[0]
    width = FIRST + parts[4].shape[1]
    return pl.pallas_call(
        final_kernel,
        out_shape=jax.ShapeDtypeStruct((rows, width), jnp.float32),
        in_specs=[VMEM] * 8,
        out_specs=VMEM,
        compiler_params=pltpu.CompilerParams(vmem_limit_bytes=8 * MIB),
        cost_estimate=SMALL,
        name="final",
    )(*parts)


def shifted(value, s):
    n = lax.axis_size("x")
    return lax.ppermute(value, "x", [(i, (i + s) % n) for i in range(n)])


def swapped(value):
    return lax.ppermute(value, "core", [(0, 1), (1, 0)])


def gather_chips(value):
    own = [value] + [shifted(value, s) for s in range(1, lax.axis_size("x"))]
    return own, [swapped(piece) for piece in own]


def after(value, *others):
    return lax.optimization_barrier((value,) + others)[0]


def ring_index(place):
    return 2 * (place % 2) + place // 2


def shifted_z(value, s):
    return lax.ppermute(value, DEPTH, [(ring_index(i), ring_index((i + s) % 4)) for i in range(4)])


def shifted_y(value, s):
    return lax.ppermute(value, "y", [(i, (i + s) % 4) for i in range(4)])


def local(layer_input, w_qkv, d_out, span_order, doc_lengths):
    rows = layer_input[0]
    tokens = rows.shape[0]
    chips = lax.axis_size("x")
    seq = lax.axis_size("zhi") * lax.axis_size("y")
    at_zlo, at_zhi, at_y = lax.axis_index("zlo"), lax.axis_index("zhi"), lax.axis_index("y")
    where = jnp.stack(
        [lax.axis_index("x"), lax.axis_index("core"), at_zhi * lax.axis_size("y") + at_y, at_zhi * 2 + at_zlo, at_y]
    ).astype(jnp.int32)

    packed = pack(where, rows, chips)
    rows = after(rows, packed[0])
    copies = project_kv(rows, w_qkv, seq)
    gathered = lax.all_to_all(copies, SEQ, 0, 0, tiled=True).reshape(seq * tokens, 2 * HD)
    pieces = [packed[0]] + [shifted(packed[s], s) for s in range(1, chips)]
    query = project_query(after(rows, copies), w_qkv)
    d_query, terms = attention(where, span_order, doc_lengths, query, d_out[0], gathered)
    own_q, other_q = gather_chips(d_query)
    arrived = lax.all_to_all(terms.reshape(seq, tokens, 2 * HD), SEQ, 0, 0, tiled=True)
    pieces = [after(piece, terms) for piece in pieces]
    x_own, x_send = halves(where, pieces)
    x_other = swapped(x_send)

    stacked, done = term_query(x_own, x_other, own_q + other_q, lax.axis_size("y"))
    group_y = lax.all_to_all(stacked, "y", 0, 0, tiled=True)
    owned = jnp.sum(arrived.astype(jnp.float32), axis=0).astype(jnp.bfloat16)
    own_kv, other_kv = gather_chips(owned)
    parts = term_second(where, x_own, x_other, done, own_kv + other_kv)
    d_qkv = jnp.concatenate([d_query, owned], axis=1)
    d_rows = nt(d_qkv, w_qkv).astype(jnp.bfloat16)
    group_z = [parts[0]] + [after(shifted_z(parts[s], s), d_rows) for s in range(1, 4)]

    sums_z = middle(where, [group_y], True)
    sums_y = middle(where, group_z, False)
    last = [sums_z[0]] + [shifted_z(sums_z[s], s) for s in range(1, 4)]
    last += [sums_y[0]] + [shifted_y(sums_y[s], s) for s in range(1, 4)]
    d_w = final(last)
    return (d_rows[None], d_w)


def solution(mesh):
    fine = Mesh(mesh.devices.reshape(2, 4, 2, 2, 4), ("zlo", "x", "core", "zhi", "y"))
    dp, ctx = ("zlo", "x", "core"), ("zhi", "y")
    placed = (P(dp, ctx, None), P(), P(dp, ctx, None), P(dp, None), P(dp, None))
    return jax.shard_map(
        local,
        mesh=fine,
        in_specs=placed,
        out_specs=(P(dp, ctx, None), P(dp + ctx, None)),
        check_vma=False,
    )
```

time: 136 us -> 136 us (level)
  waiting for transfers between devices: 48.4 us -> 30.1 us
  starting transfers between devices: 37.3 us -> 46.8 us
  Pallas kernels: 27.7 us -> 36.5 us
  local copies, waits for them, and re-layouts: 5.03 us -> 8.23 us
  other arithmetic: 4.04 us -> 1.12 us
    all_to_all x1, waiting for transfers between devices: 30.1 us -> 0.01 us  [local(): group_y = lax.all_to_all(stacked, 'y', 0, 0, tiled=True)]
    ppermute x0 -> x9, starting transfers between devices: none -> 15.4 us  [the longest x6 9.3 us: shifted_z(): lax.ppermute(value, DEPTH, [(ring_index(i), ring_index((i + s) % 4)) for...]
    pallas_call x7 -> x10, Pallas kernels: 27.7 us -> 36.5 us  [the longest x1 8.72 us: project_query(): pl.pallas_call(query_kernel, grid=(HQ // 2,), out_shape=pltpu.HBM((tokens...]
    ppermute x9, waiting for transfers between devices: 18.3 us -> 25 us  [shifted(): return lax.ppermute(value, 'x', [(i, (i + s) % n) for i in range(n)])]
    ppermute x0 -> x9, waiting for transfers between devices: none -> 3.06 us  [the longest x3 3.05 us: shifted_y(): return lax.ppermute(value, 'y', [(i, (i + s) % 4) for i in range(4)])]
    reduce_sum x1 -> x0, other arithmetic: 2.85 us -> none  [local(): d_w = jnp.sum(received.astype(jnp.float32), axis=0)]
    all_to_all x1, starting transfers between devices: 7.24 us -> 4.56 us  [local(): group_y = lax.all_to_all(stacked, 'y', 0, 0, tiled=True)]
    unnamed x20 -> x32, local copies, waits for them, and re-layouts: 5.03 us -> 7.62 us
  transfers between devices with their start and end apart: 21 -> 30, of which waited for: 5 -> 9; matrix products, arithmetic and copies ran while one was open for 10% -> 10% of each run, Pallas kernels for 14% -> 22%
where the time goes in v4:
time: 136 us; the launch traced here: 135 us
  starting transfers between devices  46.8 us (34%)
  Pallas kernels  36.5 us (27%)
  waiting for transfers between devices  30.1 us (22%)
  matrix products  11.9 us (9%)
  local copies, waits for them, and re-layouts  8.23 us (6%)
    ppermute x9, waiting for transfers between devices, shifted(): return lax.ppermute(value, 'x', [(i, (i + s) % n) for i in range(n)])  25 us
    ppermute x9, starting transfers between devices, shifted(): return lax.ppermute(value, 'x', [(i, (i + s) % n) for i in range(n)])  12.6 us
    dot_general x1, matrix products, nt(): lax.dot_general(a, b, (((1,), (1,)), ((), ())), preferred_element_type=jn...  11.9 us
    ppermute x6, starting transfers between devices, shifted_z(): lax.ppermute(value, DEPTH, [(ring_index(i), ring_index((i + s) % 4)) for...  9.3 us
    pallas_call x1, Pallas kernels, project_query(): pl.pallas_call(query_kernel, grid=(HQ // 2,), out_shape=pltpu.HBM((tokens...  8.72 us
    all_to_all x1, starting transfers between devices, local(): lax.all_to_all(copies, SEQ, 0, 0, tiled=True).reshape(seq * tokens, 2 * HD)  7.78 us
    unnamed x32, local copies, waits for them, and re-layouts  7.62 us
    pallas_call x1, Pallas kernels, attention(): pl.pallas_call(attention_kernel, out_shape=(pltpu.HBM((tokens, HQ * HD),...  6.88 us
  transfers between devices with their start and end apart: 30, of which 9 were waited for; matrix products, arithmetic and copies ran while one was open for 10% of the time, Pallas kernels for 22%

profile of v4, /device:TPU:0, one launch (start us, length us, event | category | flops | bytes accessed | tf_op | source)
XLA Modules:
  0.0 135.4 jit_solution(17527517450798034492)
XLA Ops:
  0.6 0.6 stack.23.where_ref.refs_0_
  1.2 3.2 %pack.1 = (bf16[2048,128]{1,0:T(8,128)(2,1)}, bf16[2048,128]{1,0:T(8,128)(2,1)}, bf16[2048,128]{1,0:T(8,128)(2,1)}, bf16[2048,128]{1,0:T(8,128)(2,1)}) custom-call(s32[5]{0:T(128)} %stack.23.where_ref.refs_0_, bf16[128,8192]{1,0:T(8,128)(2,1)} %bitcast.13), custom_call_target="tpu_custom_call" | custom-call | flops 1 | bytes 1 | tf_op jit(solution)/shard_map/pack/pallas_call | solution.py:53
  4.4 1.6 %collective-permute-start = (bf16[2048,128]{1,0:T(8,128)(2,1)}, bf16[2048,128]{1,0:T(8,128)(2,1)S(1)}, u32[]{:S(2)}, u32[]{:S(2)}) collective-permute-start(bf16[2048,128]{1,0:T(8,128)(2,1)} %get-tuple-element.39), channel_id=1, source_target_pairs={{0,16},{16,32},{32,48},{48,0},{1,17},{17,33},{33,49},{49,1},{2,18}... | collective-permute-start | bytes 1572872 | tf_op jit(solution)/shard_map/ppermute | solution.py:359
  6.0 2.7 %collective-permute-start.1 = (bf16[2048,128]{1,0:T(8,128)(2,1)}, bf16[2048,128]{1,0:T(8,128)(2,1)S(1)}, u32[]{:S(2)}, u32[]{:S(2)}) collective-permute-start(bf16[2048,128]{1,0:T(8,128)(2,1)} %get-tuple-element.41), channel_id=1, source_target_pairs={{0,32},{16,48},{32,0},{48,16},{1,33},{17,49},{33,1},{49,17},{2,34}... | collective-permute-start | bytes 1572872 | tf_op jit(solution)/shard_map/ppermute | solution.py:359
  8.8 1.4 %collective-permute-start.2 = (bf16[2048,128]{1,0:T(8,128)(2,1)}, bf16[2048,128]{1,0:T(8,128)(2,1)S(1)}, u32[]{:S(2)}, u32[]{:S(2)}) collective-permute-start(bf16[2048,128]{1,0:T(8,128)(2,1)} %get-tuple-element.43), channel_id=1, source_target_pairs={{0,48},{16,0},{32,16},{48,32},{1,49},{17,1},{33,17},{49,33},{2,50}... | collective-permute-start | bytes 1572872 | tf_op jit(solution)/shard_map/ppermute | solution.py:359
  10.2 4.2 %project_kv.1 = bf16[8,128,256]{2,1,0:T(8,128)(2,1)} custom-call(bf16[128,8192]{1,0:T(8,128)(2,1)} %bitcast.14, bf16[8192,1280]{1,0:T(8,128)(2,1)} %w_ref.3), custom_call_target="tpu_custom_call" | custom-call | flops 1 | bytes 1 | tf_op jit(solution)/shard_map/project_kv/pallas_call | solution.py:88
  14.4 7.8 %all-to-all-start = ((bf16[8,128,256]{2,1,0:T(8,128)(2,1)}), bf16[8,128,256]{2,1,0:T(8,128)(2,1)S(1)}, u32[]{:S(2)}, u32[]{:S(2)}) async-start(bf16[8,128,256]{2,1,0:T(8,128)(2,1)} %project_kv.1), calls=%async_computation | async-start | bytes 1048576 | tf_op jit(solution)/shard_map/all_to_all | solution.py:400
  22.2 8.7 %project_query.1.q_ref = bf16[128,1024]{1,0:T(8,128)(2,1)} custom-call(bf16[128,8192]{1,0:T(8,128)(2,1)} %bitcast.15, bf16[8192,1280]{1,0:T(8,128)(2,1)} %w_ref.3), custom_call_target="tpu_custom_call" | custom-call | flops 1 | bytes 1 | tf_op jit(solution)/shard_map/project_query/pallas_call | solution.py:111
  30.9 2.0 %all-to-all-done = bf16[8,128,256]{2,1,0:T(8,128)(2,1)S(1)} async-done(((bf16[8,128,256]{2,1,0:T(8,128)(2,1)}), bf16[8,128,256]{2,1,0:T(8,128)(2,1)S(1)}, u32[]{:S(2)}, u32[]{:S(2)}) %all-to-all-start) | async-done | bytes 524320 | tf_op jit(solution)/shard_map/all_to_all | solution.py:400
  32.9 0.9 copy-done.6
  33.9 6.9 %attention.1 = (bf16[128,1024]{1,0:T(8,128)(2,1)}, bf16[1024,256]{1,0:T(8,128)(2,1)}) custom-call(s32[5]{0:T(128)S(1)} %copy-done.13, s32[1,16]{1,0:T(1,128)S(1)} %copy-done.14, s32[1,4]{1,0:T(1,128)S(1)} %copy-done.15, bf16[128,1024]{1,0:T(8,128)(2,1)S(1)} %copy-done.6, bf16[128,1024]{1,0:T(8,128)(2,1)S(1)} %bitcast.12, bf16[1024,256]{1,0:T(8,128)(2,1)S(1)} %bitcast.11), custom_call_target="tpu_custom_call" | custom-call | flops 1 | bytes 1 | tf_op jit(solution)/shard_map/attention/pallas_call | solution.py:205
  40.8 2.2 %halves.1 = (bf16[1024,512]{1,0:T(8,128)(2,1)}, bf16[1024,512]{1,0:T(8,128)(2,1)}) custom-call(s32[5]{0:T(128)S(1)} %copy-done.13, bf16[2048,128]{1,0:T(8,128)(2,1)S(1)} %copy-done.7, bf16[2048,128]{1,0:T(8,128)(2,1)S(1)} %collective-permute-done.refs_1_, bf16[2048,128]{1,0:T(8,128)(2,1)S(1)} %collective-permute-done.1.refs_2_, ...), custom_call_target="tpu_custom_call" | custom-call | flops 1 | bytes 1 | tf_op jit(solution)/shard_map/halves/pallas_call | solution.py:136
  43.0 5.4 %all-to-all-start.1 = ((bf16[8,128,256]{2,1,0:T(8,128)(2,1)}), bf16[8,128,256]{2,1,0:T(8,128)(2,1)}, u32[]{:S(2)}, u32[]{:S(2)}) async-start(bf16[8,128,256]{2,1,0:T(8,128)(2,1)} %bitcast.17), calls=%async_computation.1 | async-start | bytes 1048576 | tf_op jit(solution)/shard_map/all_to_all | solution.py:405
  48.4 2.7 %collective-permute-start.5 = (bf16[128,1024]{1,0:T(8,128)(2,1)}, bf16[128,1024]{1,0:T(8,128)(2,1)S(1)}, u32[]{:S(2)}, u32[]{:S(2)}) collective-permute-start(bf16[128,1024]{1,0:T(8,128)(2,1)} %get-tuple-element.36.refs_0_), channel_id=1, source_target_pairs={{0,32},{16,48},{32,0},{48,16},{1,33},{17,49},{33,1},{49,17},{2,34}... | collective-permute-start | bytes 786440 | tf_op jit(solution)/shard_map/ppermute | solution.py:359
  51.0 6.7 %collective-permute-done.6.refs_3_ = bf16[128,1024]{1,0:T(8,128)(2,1)S(1)} collective-permute-done((bf16[128,1024]{1,0:T(8,128)(2,1)}, bf16[128,1024]{1,0:T(8,128)(2,1)S(1)}, u32[]{:S(2)}, u32[]{:S(2)}) %collective-permute-start.6) | collective-permute-done | bytes 262176 | tf_op jit(solution)/shard_map/ppermute | solution.py:359
  57.7 1.6 %collective-permute-done.5.refs_2_ = bf16[128,1024]{1,0:T(8,128)(2,1)S(1)} collective-permute-done((bf16[128,1024]{1,0:T(8,128)(2,1)}, bf16[128,1024]{1,0:T(8,128)(2,1)S(1)}, u32[]{:S(2)}, u32[]{:S(2)}) %collective-permute-start.5) | collective-permute-done | bytes 262176 | tf_op jit(solution)/shard_map/ppermute | solution.py:359
  59.4 4.9 %collective-permute-done.4.refs_1_ = bf16[128,1024]{1,0:T(8,128)(2,1)S(1)} collective-permute-done((bf16[128,1024]{1,0:T(8,128)(2,1)}, bf16[128,1024]{1,0:T(8,128)(2,1)S(1)}, u32[]{:S(2)}, u32[]{:S(2)}) %collective-permute-start.4) | collective-permute-done | bytes 262176 | tf_op jit(solution)/shard_map/ppermute | solution.py:359
  64.3 1.1 reduce_sum.12.refs_0_
  65.4 1.6 %collective-permute-start.16 = (bf16[128,256]{1,0:T(8,128)(2,1)S(1)}, bf16[128,256]{1,0:T(8,128)(2,1)S(1)}, u32[]{:S(2)}, u32[]{:S(2)}) collective-permute-start(bf16[128,256]{1,0:T(8,128)(2,1)S(1)} %reduce_sum.12.refs_0_), channel_id=1, source_target_pairs={{0,48},{16,0},{32,16},{48,32},{1,49},{17,1},{33,17},{49,33},{2,50}... | collective-permute-start | bytes 196616 | tf_op jit(solution)/shard_map/ppermute | solution.py:359
  67.0 2.9 %collective-permute-done.16.refs_3_ = bf16[128,256]{1,0:T(8,128)(2,1)S(1)} collective-permute-done((bf16[128,256]{1,0:T(8,128)(2,1)S(1)}, bf16[128,256]{1,0:T(8,128)(2,1)S(1)}, u32[]{:S(2)}, u32[]{:S(2)}) %collective-permute-start.16) | collective-permute-done | bytes 65568 | tf_op jit(solution)/shard_map/ppermute | solution.py:359
  69.9 1.7 %collective-permute-start.15 = (bf16[128,256]{1,0:T(8,128)(2,1)S(1)}, bf16[128,256]{1,0:T(8,128)(2,1)}, u32[]{:S(2)}, u32[]{:S(2)}) collective-permute-start(bf16[128,256]{1,0:T(8,128)(2,1)S(1)} %reduce_sum.12.refs_0_), channel_id=1, source_target_pairs={{0,32},{16,48},{32,0},{48,16},{1,33},{17,49},{33,1},{49,17},{2,34}... | collective-permute-start | bytes 196616 | tf_op jit(solution)/shard_map/ppermute | solution.py:359
  71.7 4.1 %collective-permute-done.15.refs_2_ = bf16[128,256]{1,0:T(8,128)(2,1)} collective-permute-done((bf16[128,256]{1,0:T(8,128)(2,1)S(1)}, bf16[128,256]{1,0:T(8,128)(2,1)}, u32[]{:S(2)}, u32[]{:S(2)}) %collective-permute-start.15) | collective-permute-done | bytes 65568 | tf_op jit(solution)/shard_map/ppermute | solution.py:359
  75.8 0.8 collective-permute-start.14
  76.7 4.7 %collective-permute-done.14.refs_1_ = bf16[128,256]{1,0:T(8,128)(2,1)} collective-permute-done((bf16[128,256]{1,0:T(8,128)(2,1)S(1)}, bf16[128,256]{1,0:T(8,128)(2,1)}, u32[]{:S(2)}, u32[]{:S(2)}) %collective-permute-start.14) | collective-permute-done | bytes 65568 | tf_op jit(solution)/shard_map/ppermute | solution.py:359
  82.4 1.6 %copy-done = bf16[1024,512]{1,0:T(8,128)(2,1)S(1)} copy-done((bf16[1024,512]{1,0:T(8,128)(2,1)S(1)}, bf16[1024,512]{1,0:T(8,128)(2,1)}, u32[]{:S(2)}) %copy-start) | copy-done | bytes 1048600
  84.1 0.9 copy-done.4
  85.0 5.2 %term_query.1 = (bf16[4,256,768]{2,1,0:T(8,128)(2,1)}, bf16[1024,256]{1,0:T(8,128)(2,1)}) custom-call(bf16[1024,512]{1,0:T(8,128)(2,1)S(1)} %copy-done, bf16[1024,512]{1,0:T(8,128)(2,1)S(1)} %collective-permute-done.3.other_ref, bf16[128,1024]{1,0:T(8,128)(2,1)S(1)} %copy-done.4, bf16[128,1024]{1,0:T(8,128)(2,1)S(1)} %collective-permute-done.4.refs_1_, ...), custom_call_target="tpu_custom_call" | custom-call | flops 1 | bytes 1 | tf_op jit(solution)/shard_map/term_query/pallas_call | solution.py:258
  90.2 4.6 %all-to-all-start.2 = ((bf16[4,256,768]{2,1,0:T(8,128)(2,1)}), bf16[4,256,768]{2,1,0:T(8,128)(2,1)S(1)}, u32[]{:S(2)}, u32[]{:S(2)}) async-start(bf16[4,256,768]{2,1,0:T(8,128)(2,1)} %get-tuple-element.47), calls=%async_computation.2 | async-start | bytes 3145728 | tf_op jit(solution)/shard_map/all_to_all | solution.py:411
  94.8 1.2 copy-done.3
  96.0 1.0 copy-done.8
  97.1 2.6 %term_second.1 = (bf16[256,512]{1,0:T(8,128)(2,1)}, bf16[256,512]{1,0:T(8,128)(2,1)}, bf16[256,512]{1,0:T(8,128)(2,1)}, bf16[256,512]{1,0:T(8,128)(2,1)}) custom-call(s32[5]{0:T(128)S(1)} %copy-done.13, bf16[1024,512]{1,0:T(8,128)(2,1)S(1)} %copy-done.1, bf16[1024,512]{1,0:T(8,128)(2,1)S(1)} %copy-done.3, bf16[1024,256]{1,0:T(8,128)(2,1)S(1)} %copy-done.8, ...), custom_call_target="tpu_custom_call" | custom-call | flops 1 | bytes 1 | tf_op jit(solution)/shard_map/term_second/pallas_call | solution.py:296
  99.6 1.0 collective-permute-start.21
  100.7 3.6 %collective-permute-start.22 = (bf16[256,512]{1,0:T(8,128)(2,1)}, bf16[256,512]{1,0:T(8,128)(2,1)S(1)}, u32[]{:S(2)}, u32[]{:S(2)}) collective-permute-start(bf16[256,512]{1,0:T(8,128)(2,1)} %get-tuple-element.56), channel_id=1, source_target_pairs={{0,4},{64,68},{4,0},{68,64},{1,5},{65,69},{5,1},{69,65},{2,6},{66,... | collective-permute-start | bytes 786440 | tf_op jit(solution)/shard_map/ppermute | solution.py:380
  104.2 1.0 collective-permute-start.23
  105.3 11.9 %convolution_convert_fusion = bf16[128,8192]{1,0:T(8,128)(2,1)} fusion(bf16[8192,1280]{1,0:T(8,128)(2,1)} %w_ref.3, bf16[128,256]{1,0:T(8,128)(2,1)S(1)} %reduce_sum.12.refs_0_, bf16[128,1024]{1,0:T(8,128)(2,1)S(1)} %copy-done.5), kind=kOutput, calls=%fused_computation | convolution fusion | flops 2686058496 | bytes 23396352 | tf_op jit(solution)/shard_map/dot_general | solution.py:18
  117.2 1.3 middle_y.1
  118.5 2.0 %collective-permute-start.24 = (bf16[64,512]{1,0:T(8,128)(2,1)}, bf16[64,512]{1,0:T(8,128)(2,1)S(1)}, u32[]{:S(2)}, u32[]{:S(2)}) collective-permute-start(bf16[64,512]{1,0:T(8,128)(2,1)} %get-tuple-element.61), channel_id=1, source_target_pairs={{0,1},{1,2},{2,3},{3,0},{4,5},{5,6},{6,7},{7,4},{8,9},{9,10},{10,1... | collective-permute-start | bytes 196616 | tf_op jit(solution)/shard_map/ppermute | solution.py:384
  120.5 1.4 %middle_z.1 = (f32[64,768]{1,0:T(8,128)}, bf16[64,768]{1,0:T(8,128)(2,1)}, bf16[64,768]{1,0:T(8,128)(2,1)}, bf16[64,768]{1,0:T(8,128)(2,1)}) custom-call(s32[5]{0:T(128)S(1)} %copy-done.13, bf16[4,256,768]{2,1,0:T(8,128)(2,1)S(1)} %all-to-all-done.2.stack_ref), custom_call_target="tpu_custom_call" | custom-call | flops 1 | bytes 1 | tf_op jit(solution)/shard_map/middle_z/pallas_call | solution.py:325
  122.0 1.0 collective-permute-start.11
  123.0 1.1 collective-permute-start.12
  124.1 1.6 %collective-permute-start.13 = (bf16[64,768]{1,0:T(8,128)(2,1)}, bf16[64,768]{1,0:T(8,128)(2,1)S(1)}, u32[]{:S(2)}, u32[]{:S(2)}) collective-permute-start(bf16[64,768]{1,0:T(8,128)(2,1)} %get-tuple-element.51), channel_id=1, source_target_pairs={{0,68},{64,0},{4,64},{68,4},{1,69},{65,1},{5,65},{69,5},{2,70},{66... | collective-permute-start | bytes 294920 | tf_op jit(solution)/shard_map/ppermute | solution.py:380
  125.7 2.7 %collective-permute-start.25 = (bf16[64,512]{1,0:T(8,128)(2,1)}, bf16[64,512]{1,0:T(8,128)(2,1)S(1)}, u32[]{:S(2)}, u32[]{:S(2)}) collective-permute-start(bf16[64,512]{1,0:T(8,128)(2,1)} %get-tuple-element.62), channel_id=1, source_target_pairs={{0,2},{1,3},{2,0},{3,1},{4,6},{5,7},{6,4},{7,5},{8,10},{9,11},{10,... | collective-permute-start | bytes 196616 | tf_op jit(solution)/shard_map/ppermute | solution.py:384
  128.3 1.4 %collective-permute-start.26 = (bf16[64,512]{1,0:T(8,128)(2,1)}, bf16[64,512]{1,0:T(8,128)(2,1)S(1)}, u32[]{:S(2)}, u32[]{:S(2)}) collective-permute-start(bf16[64,512]{1,0:T(8,128)(2,1)} %get-tuple-element.63), channel_id=1, source_target_pairs={{0,3},{1,0},{2,1},{3,2},{4,7},{5,4},{6,5},{7,6},{8,11},{9,8},{10,9... | collective-permute-start | bytes 196616 | tf_op jit(solution)/shard_map/ppermute | solution.py:384
  129.8 1.9 %collective-permute-done.25.refs_6_ = bf16[64,512]{1,0:T(8,128)(2,1)S(1)} collective-permute-done((bf16[64,512]{1,0:T(8,128)(2,1)}, bf16[64,512]{1,0:T(8,128)(2,1)S(1)}, u32[]{:S(2)}, u32[]{:S(2)}) %collective-permute-start.25) | collective-permute-done | bytes 65568 | tf_op jit(solution)/shard_map/ppermute | solution.py:384
  131.6 1.2 collective-permute-done.26.refs_7_
  132.8 0.9 copy-done.11
  133.8 0.9 copy-done.12
  134.7 0.8 final.1
  (57 shorter events, 1.2 us)
Async XLA Ops:
  4.4 36.3 %collective-permute-start = (bf16[2048,128]{1,0:T(8,128)(2,1)}, bf16[2048,128]{1,0:T(8,128)(2,1)S(1)}, u32[]{:S(2)}, u32[]{:S(2)}) collective-permute-start(bf16[2048,128]{1,0:T(8,128)(2,1)} %get-tuple-element.39), channel_id=1, source_target_pairs={{0,16},{16,32},{32,48},{48,0},{1,17},{17,33},{33,49},{49,1},{2,18}... | collective-permute-start | bytes 1572872 | tf_op jit(solution)/shard_map/ppermute | solution.py:359
  6.0 34.7 %collective-permute-start.1 = (bf16[2048,128]{1,0:T(8,128)(2,1)}, bf16[2048,128]{1,0:T(8,128)(2,1)S(1)}, u32[]{:S(2)}, u32[]{:S(2)}) collective-permute-start(bf16[2048,128]{1,0:T(8,128)(2,1)} %get-tuple-element.41), channel_id=1, source_target_pairs={{0,32},{16,48},{32,0},{48,16},{1,33},{17,49},{33,1},{49,17},{2,34}... | collective-permute-start | bytes 1572872 | tf_op jit(solution)/shard_map/ppermute | solution.py:359
  8.8 32.0 %collective-permute-start.2 = (bf16[2048,128]{1,0:T(8,128)(2,1)}, bf16[2048,128]{1,0:T(8,128)(2,1)S(1)}, u32[]{:S(2)}, u32[]{:S(2)}) collective-permute-start(bf16[2048,128]{1,0:T(8,128)(2,1)} %get-tuple-element.43), channel_id=1, source_target_pairs={{0,48},{16,0},{32,16},{48,32},{1,49},{17,1},{33,17},{49,33},{2,50}... | collective-permute-start | bytes 1572872 | tf_op jit(solution)/shard_map/ppermute | solution.py:359
  14.4 18.5 %all-to-all-start = ((bf16[8,128,256]{2,1,0:T(8,128)(2,1)}), bf16[8,128,256]{2,1,0:T(8,128)(2,1)S(1)}, u32[]{:S(2)}, u32[]{:S(2)}) async-start(bf16[8,128,256]{2,1,0:T(8,128)(2,1)} %project_kv.1), calls=%async_computation | async-start | bytes 1048576 | tf_op jit(solution)/shard_map/all_to_all | solution.py:400
  22.1 10.7 %copy-start.9 = (bf16[1,128,1024]{2,1,0:T(8,128)(2,1)S(1)}, bf16[1,128,1024]{2,1,0:T(8,128)(2,1)}, u32[]{:S(2)}) copy-start(bf16[1,128,1024]{2,1,0:T(8,128)(2,1)} %param.7) | copy-start | bytes 786436
  22.1 10.7 %copy-start.13 = (s32[5]{0:T(128)S(1)}, s32[5]{0:T(128)}, u32[]{:S(2)}) copy-start(s32[5]{0:T(128)} %stack.23.where_ref.refs_0_) | copy-start | bytes 64
  22.2 10.7 %copy-start.14 = (s32[1,16]{1,0:T(1,128)S(1)}, s32[1,16]{1,0:T(1,128)}, u32[]{:S(2)}) copy-start(s32[1,16]{1,0:T(1,128)} %order_ref.1) | copy-start | bytes 196
  22.2 10.7 %copy-start.15 = (s32[1,4]{1,0:T(1,128)S(1)}, s32[1,4]{1,0:T(1,128)}, u32[]{:S(2)}) copy-start(s32[1,4]{1,0:T(1,128)} %lens_ref.1) | copy-start | bytes 52
  22.2 18.6 %copy-start.7 = (bf16[2048,128]{1,0:T(8,128)(2,1)S(1)}, bf16[2048,128]{1,0:T(8,128)(2,1)}, u32[]{:S(2)}) copy-start(bf16[2048,128]{1,0:T(8,128)(2,1)} %get-tuple-element.38.refs_0_) | copy-start | bytes 1572868
  32.9 1.0 copy-start.6
  43.0 39.4 %collective-permute-start.3 = (bf16[1024,512]{1,0:T(8,128)(2,1)}, bf16[1024,512]{1,0:T(8,128)(2,1)S(1)}, u32[]{:S(2)}, u32[]{:S(2)}) collective-permute-start(bf16[1024,512]{1,0:T(8,128)(2,1)} %get-tuple-element.46), channel_id=1, source_target_pairs={{0,8},{8,0},{1,9},{9,1},{2,10},{10,2},{3,11},{11,3},{4,12},{12,4},... | collective-permute-start | bytes 3145736 | tf_op jit(solution)/shard_map/ppermute | solution.py:363
  43.0 51.8 %copy-start.1 = (bf16[1024,512]{1,0:T(8,128)(2,1)S(1)}, bf16[1024,512]{1,0:T(8,128)(2,1)}, u32[]{:S(2)}) copy-start(bf16[1024,512]{1,0:T(8,128)(2,1)} %get-tuple-element.45.own_ref) | copy-start | bytes 3145732
  43.0 21.2 %all-to-all-start.1 = ((bf16[8,128,256]{2,1,0:T(8,128)(2,1)}), bf16[8,128,256]{2,1,0:T(8,128)(2,1)}, u32[]{:S(2)}, u32[]{:S(2)}) async-start(bf16[8,128,256]{2,1,0:T(8,128)(2,1)} %bitcast.17), calls=%async_computation.1 | async-start | bytes 1048576 | tf_op jit(solution)/shard_map/all_to_all | solution.py:405
  48.4 9.4 %collective-permute-start.6 = (bf16[128,1024]{1,0:T(8,128)(2,1)}, bf16[128,1024]{1,0:T(8,128)(2,1)S(1)}, u32[]{:S(2)}, u32[]{:S(2)}) collective-permute-start(bf16[128,1024]{1,0:T(8,128)(2,1)} %get-tuple-element.36.refs_0_), channel_id=1, source_target_pairs={{0,48},{16,0},{32,16},{48,32},{1,49},{17,1},{33,17},{49,33},{2,50}... | collective-permute-start | bytes 786440 | tf_op jit(solution)/shard_map/ppermute | solution.py:359
  48.4 11.0 %collective-permute-start.5 = (bf16[128,1024]{1,0:T(8,128)(2,1)}, bf16[128,1024]{1,0:T(8,128)(2,1)S(1)}, u32[]{:S(2)}, u32[]{:S(2)}) collective-permute-start(bf16[128,1024]{1,0:T(8,128)(2,1)} %get-tuple-element.36.refs_0_), channel_id=1, source_target_pairs={{0,32},{16,48},{32,0},{48,16},{1,33},{17,49},{33,1},{49,17},{2,34}... | collective-permute-start | bytes 786440 | tf_op jit(solution)/shard_map/ppermute | solution.py:359
  51.0 13.2 %collective-permute-start.4 = (bf16[128,1024]{1,0:T(8,128)(2,1)}, bf16[128,1024]{1,0:T(8,128)(2,1)S(1)}, u32[]{:S(2)}, u32[]{:S(2)}) collective-permute-start(bf16[128,1024]{1,0:T(8,128)(2,1)} %get-tuple-element.36.refs_0_), channel_id=1, source_target_pairs={{0,16},{16,32},{32,48},{48,0},{1,17},{17,33},{33,49},{49,1},{2,18}... | collective-permute-start | bytes 786440 | tf_op jit(solution)/shard_map/ppermute | solution.py:359
  51.0 14.3 %collective-permute-start.7 = (bf16[128,1024]{1,0:T(8,128)(2,1)}, bf16[128,1024]{1,0:T(8,128)(2,1)S(1)}, u32[]{:S(2)}, u32[]{:S(2)}) collective-permute-start(bf16[128,1024]{1,0:T(8,128)(2,1)} %get-tuple-element.36.refs_0_), channel_id=1, source_target_pairs={{0,8},{8,0},{1,9},{9,1},{2,10},{10,2},{3,11},{11,3},{4,12},{12,4},... | collective-permute-start | bytes 786440 | tf_op jit(solution)/shard_map/ppermute | solution.py:363
  57.7 23.7 %collective-permute-start.10 = (bf16[128,1024]{1,0:T(8,128)(2,1)S(1)}, bf16[128,1024]{1,0:T(8,128)(2,1)S(1)}, u32[]{:S(2)}, u32[]{:S(2)}) collective-permute-start(bf16[128,1024]{1,0:T(8,128)(2,1)S(1)} %collective-permute-done.6.refs_3_), channel_id=1, source_target_pairs={{0,8},{8,0},{1,9},{9,1},{2,10},{10,2},{3,11},{11,3},{4,12},{12,4},... | collective-permute-start | bytes 786440 | tf_op jit(solution)/shard_map/ppermute | solution.py:363
  59.4 22.6 %collective-permute-start.9 = (bf16[128,1024]{1,0:T(8,128)(2,1)S(1)}, bf16[128,1024]{1,0:T(8,128)(2,1)}, u32[]{:S(2)}, u32[]{:S(2)}) collective-permute-start(bf16[128,1024]{1,0:T(8,128)(2,1)S(1)} %collective-permute-done.5.refs_2_), channel_id=1, source_target_pairs={{0,8},{8,0},{1,9},{9,1},{2,10},{10,2},{3,11},{11,3},{4,12},{12,4},... | collective-permute-start | bytes 786440 | tf_op jit(solution)/shard_map/ppermute | solution.py:363
  64.2 17.8 %collective-permute-start.8 = (bf16[128,1024]{1,0:T(8,128)(2,1)S(1)}, bf16[128,1024]{1,0:T(8,128)(2,1)}, u32[]{:S(2)}, u32[]{:S(2)}) collective-permute-start(bf16[128,1024]{1,0:T(8,128)(2,1)S(1)} %collective-permute-done.4.refs_1_), channel_id=1, source_target_pairs={{0,8},{8,0},{1,9},{9,1},{2,10},{10,2},{3,11},{11,3},{4,12},{12,4},... | collective-permute-start | bytes 786440 | tf_op jit(solution)/shard_map/ppermute | solution.py:363
  65.4 4.6 %collective-permute-start.16 = (bf16[128,256]{1,0:T(8,128)(2,1)S(1)}, bf16[128,256]{1,0:T(8,128)(2,1)S(1)}, u32[]{:S(2)}, u32[]{:S(2)}) collective-permute-start(bf16[128,256]{1,0:T(8,128)(2,1)S(1)} %reduce_sum.12.refs_0_), channel_id=1, source_target_pairs={{0,48},{16,0},{32,16},{48,32},{1,49},{17,1},{33,17},{49,33},{2,50}... | collective-permute-start | bytes 196616 | tf_op jit(solution)/shard_map/ppermute | solution.py:359
  69.9 5.9 %collective-permute-start.15 = (bf16[128,256]{1,0:T(8,128)(2,1)S(1)}, bf16[128,256]{1,0:T(8,128)(2,1)}, u32[]{:S(2)}, u32[]{:S(2)}) collective-permute-start(bf16[128,256]{1,0:T(8,128)(2,1)S(1)} %reduce_sum.12.refs_0_), channel_id=1, source_target_pairs={{0,32},{16,48},{32,0},{48,16},{1,33},{17,49},{33,1},{49,17},{2,34}... | collective-permute-start | bytes 196616 | tf_op jit(solution)/shard_map/ppermute | solution.py:359
  75.8 5.6 %collective-permute-start.14 = (bf16[128,256]{1,0:T(8,128)(2,1)S(1)}, bf16[128,256]{1,0:T(8,128)(2,1)}, u32[]{:S(2)}, u32[]{:S(2)}) collective-permute-start(bf16[128,256]{1,0:T(8,128)(2,1)S(1)} %reduce_sum.12.refs_0_), channel_id=1, source_target_pairs={{0,16},{16,32},{32,48},{48,0},{1,17},{17,33},{33,49},{49,1},{2,18}... | collective-permute-start | bytes 196616 | tf_op jit(solution)/shard_map/ppermute | solution.py:359
  81.4 13.4 %collective-permute-start.17 = (bf16[128,256]{1,0:T(8,128)(2,1)S(1)}, bf16[128,256]{1,0:T(8,128)(2,1)}, u32[]{:S(2)}, u32[]{:S(2)}) collective-permute-start(bf16[128,256]{1,0:T(8,128)(2,1)S(1)} %reduce_sum.12.refs_0_), channel_id=1, source_target_pairs={{0,8},{8,0},{1,9},{9,1},{2,10},{10,2},{3,11},{11,3},{4,12},{12,4},... | collective-permute-start | bytes 196616 | tf_op jit(solution)/shard_map/ppermute | solution.py:363
  81.4 13.4 %collective-permute-start.20 = (bf16[128,256]{1,0:T(8,128)(2,1)S(1)}, bf16[128,256]{1,0:T(8,128)(2,1)}, u32[]{:S(2)}, u32[]{:S(2)}) collective-permute-start(bf16[128,256]{1,0:T(8,128)(2,1)S(1)} %collective-permute-done.16.refs_3_), channel_id=1, source_target_pairs={{0,8},{8,0},{1,9},{9,1},{2,10},{10,2},{3,11},{11,3},{4,12},{12,4},... | collective-permute-start | bytes 196616 | tf_op jit(solution)/shard_map/ppermute | solution.py:363
  81.9 12.9 %collective-permute-start.19 = (bf16[128,256]{1,0:T(8,128)(2,1)}, bf16[128,256]{1,0:T(8,128)(2,1)}, u32[]{:S(2)}, u32[]{:S(2)}) collective-permute-start(bf16[128,256]{1,0:T(8,128)(2,1)} %collective-permute-done.15.refs_2_), channel_id=1, source_target_pairs={{0,8},{8,0},{1,9},{9,1},{2,10},{10,2},{3,11},{11,3},{4,12},{12,4},... | collective-permute-start | bytes 196616 | tf_op jit(solution)/shard_map/ppermute | solution.py:363
  82.0 12.8 %collective-permute-start.18 = (bf16[128,256]{1,0:T(8,128)(2,1)}, bf16[128,256]{1,0:T(8,128)(2,1)}, u32[]{:S(2)}, u32[]{:S(2)}) collective-permute-start(bf16[128,256]{1,0:T(8,128)(2,1)} %collective-permute-done.14.refs_1_), channel_id=1, source_target_pairs={{0,8},{8,0},{1,9},{9,1},{2,10},{10,2},{3,11},{11,3},{4,12},{12,4},... | collective-permute-start | bytes 196616 | tf_op jit(solution)/shard_map/ppermute | solution.py:363
  82.4 7.8 %copy-start.2 = (bf16[1024,512]{1,0:T(8,128)(2,1)}, bf16[1024,512]{1,0:T(8,128)(2,1)S(1)}, u32[]{:S(2)}) copy-start(bf16[1024,512]{1,0:T(8,128)(2,1)S(1)} %collective-permute-done.3.other_ref) | copy-start | bytes 3145732
  82.4 1.6 %copy-start = (bf16[1024,512]{1,0:T(8,128)(2,1)S(1)}, bf16[1024,512]{1,0:T(8,128)(2,1)}, u32[]{:S(2)}) copy-start(bf16[1024,512]{1,0:T(8,128)(2,1)} %get-tuple-element.45.own_ref) | copy-start | bytes 3145732
  84.0 0.9 copy-start.4
  90.2 15.0 %copy-start.5 = (bf16[128,1024]{1,0:T(8,128)(2,1)S(1)}, bf16[128,1024]{1,0:T(8,128)(2,1)}, u32[]{:S(2)}) copy-start(bf16[128,1024]{1,0:T(8,128)(2,1)} %get-tuple-element.36.refs_0_) | copy-start | bytes 786436
  90.2 30.3 %all-to-all-start.2 = ((bf16[4,256,768]{2,1,0:T(8,128)(2,1)}), bf16[4,256,768]{2,1,0:T(8,128)(2,1)S(1)}, u32[]{:S(2)}, u32[]{:S(2)}) async-start(bf16[4,256,768]{2,1,0:T(8,128)(2,1)} %get-tuple-element.47), calls=%async_computation.2 | async-start | bytes 3145728 | tf_op jit(solution)/shard_map/all_to_all | solution.py:411
  94.8 1.2 copy-start.3
  96.0 1.0 copy-start.8
  99.6 17.6 %collective-permute-start.21 = (bf16[256,512]{1,0:T(8,128)(2,1)}, bf16[256,512]{1,0:T(8,128)(2,1)S(1)}, u32[]{:S(2)}, u32[]{:S(2)}) collective-permute-start(bf16[256,512]{1,0:T(8,128)(2,1)} %get-tuple-element.54), channel_id=1, source_target_pairs={{0,64},{64,4},{4,68},{68,0},{1,65},{65,5},{5,69},{69,1},{2,66},{66... | collective-permute-start | bytes 786440 | tf_op jit(solution)/shard_map/ppermute | solution.py:380
  100.7 16.5 %collective-permute-start.22 = (bf16[256,512]{1,0:T(8,128)(2,1)}, bf16[256,512]{1,0:T(8,128)(2,1)S(1)}, u32[]{:S(2)}, u32[]{:S(2)}) collective-permute-start(bf16[256,512]{1,0:T(8,128)(2,1)} %get-tuple-element.56), channel_id=1, source_target_pairs={{0,4},{64,68},{4,0},{68,64},{1,5},{65,69},{5,1},{69,65},{2,6},{66,... | collective-permute-start | bytes 786440 | tf_op jit(solution)/shard_map/ppermute | solution.py:380
  104.2 13.0 %copy-start.10 = (bf16[256,512]{1,0:T(8,128)(2,1)S(1)}, bf16[256,512]{1,0:T(8,128)(2,1)}, u32[]{:S(2)}) copy-start(bf16[256,512]{1,0:T(8,128)(2,1)} %get-tuple-element.53.refs_1_) | copy-start | bytes 786436
  104.2 12.9 %collective-permute-start.23 = (bf16[256,512]{1,0:T(8,128)(2,1)}, bf16[256,512]{1,0:T(8,128)(2,1)S(1)}, u32[]{:S(2)}, u32[]{:S(2)}) collective-permute-start(bf16[256,512]{1,0:T(8,128)(2,1)} %get-tuple-element.58), channel_id=1, source_target_pairs={{0,68},{64,0},{4,64},{68,4},{1,69},{65,1},{5,65},{69,5},{2,70},{66... | collective-permute-start | bytes 786440 | tf_op jit(solution)/shard_map/ppermute | solution.py:380
  118.5 9.8 %collective-permute-start.24 = (bf16[64,512]{1,0:T(8,128)(2,1)}, bf16[64,512]{1,0:T(8,128)(2,1)S(1)}, u32[]{:S(2)}, u32[]{:S(2)}) collective-permute-start(bf16[64,512]{1,0:T(8,128)(2,1)} %get-tuple-element.61), channel_id=1, source_target_pairs={{0,1},{1,2},{2,3},{3,0},{4,5},{5,6},{6,7},{7,4},{8,9},{9,10},{10,1... | collective-permute-start | bytes 196616 | tf_op jit(solution)/shard_map/ppermute | solution.py:384
  122.0 10.9 %collective-permute-start.11 = (bf16[64,768]{1,0:T(8,128)(2,1)}, bf16[64,768]{1,0:T(8,128)(2,1)S(1)}, u32[]{:S(2)}, u32[]{:S(2)}) collective-permute-start(bf16[64,768]{1,0:T(8,128)(2,1)} %get-tuple-element.49), channel_id=1, source_target_pairs={{0,64},{64,4},{4,68},{68,0},{1,65},{65,5},{5,69},{69,1},{2,66},{66... | collective-permute-start | bytes 294920 | tf_op jit(solution)/shard_map/ppermute | solution.py:380
  123.0 9.8 %collective-permute-start.12 = (bf16[64,768]{1,0:T(8,128)(2,1)}, bf16[64,768]{1,0:T(8,128)(2,1)S(1)}, u32[]{:S(2)}, u32[]{:S(2)}) collective-permute-start(bf16[64,768]{1,0:T(8,128)(2,1)} %get-tuple-element.50), channel_id=1, source_target_pairs={{0,4},{64,68},{4,0},{68,64},{1,5},{65,69},{5,1},{69,65},{2,6},{66,... | collective-permute-start | bytes 294920 | tf_op jit(solution)/shard_map/ppermute | solution.py:380
  124.1 8.7 %collective-permute-start.13 = (bf16[64,768]{1,0:T(8,128)(2,1)}, bf16[64,768]{1,0:T(8,128)(2,1)S(1)}, u32[]{:S(2)}, u32[]{:S(2)}) collective-permute-start(bf16[64,768]{1,0:T(8,128)(2,1)} %get-tuple-element.51), channel_id=1, source_target_pairs={{0,68},{64,0},{4,64},{68,4},{1,69},{65,1},{5,65},{69,5},{2,70},{66... | collective-permute-start | bytes 294920 | tf_op jit(solution)/shard_map/ppermute | solution.py:380
  125.7 6.0 %collective-permute-start.25 = (bf16[64,512]{1,0:T(8,128)(2,1)}, bf16[64,512]{1,0:T(8,128)(2,1)S(1)}, u32[]{:S(2)}, u32[]{:S(2)}) collective-permute-start(bf16[64,512]{1,0:T(8,128)(2,1)} %get-tuple-element.62), channel_id=1, source_target_pairs={{0,2},{1,3},{2,0},{3,1},{4,6},{5,7},{6,4},{7,5},{8,10},{9,11},{10,... | collective-permute-start | bytes 196616 | tf_op jit(solution)/shard_map/ppermute | solution.py:384
  128.3 4.5 %collective-permute-start.26 = (bf16[64,512]{1,0:T(8,128)(2,1)}, bf16[64,512]{1,0:T(8,128)(2,1)S(1)}, u32[]{:S(2)}, u32[]{:S(2)}) collective-permute-start(bf16[64,512]{1,0:T(8,128)(2,1)} %get-tuple-element.63), channel_id=1, source_target_pairs={{0,3},{1,0},{2,1},{3,2},{4,7},{5,4},{6,5},{7,6},{8,11},{9,8},{10,9... | collective-permute-start | bytes 196616 | tf_op jit(solution)/shard_map/ppermute | solution.py:384
  132.8 0.9 copy-start.11
  133.8 0.9 copy-start.12

commit v5 on v4

--- a/solution.py
+++ b/solution.py
@@ -111,17 +111,16 @@
     return pl.pallas_call(
         query_kernel,
         grid=(HQ // 2,),
-        out_shape=pltpu.HBM((tokens, HQ * HD), jnp.bfloat16),
+        out_shape=jax.ShapeDtypeStruct((tokens, HQ * HD), jnp.bfloat16),
         in_specs=[pl.BlockSpec((tokens, features), lambda i: (0, 0)), pl.BlockSpec((features, width), lambda i: (0, i))],
         out_specs=pl.BlockSpec((tokens, width), lambda i: (0, i)),
-        compiler_params=pltpu.CompilerParams(vmem_limit_bytes=60 * MIB),
+        compiler_params=pltpu.CompilerParams(vmem_limit_bytes=44 * MIB),
         cost_estimate=SMALL,
         name="project_query",
     )(x, w)
 
 
-def halves_kernel(where_ref, *refs):
-    pieces, own_ref, send_ref = refs[:-2], refs[-2], refs[-1]
+def halves(where_ref, pieces, own_ref, send_ref):
     half, tokens = own_ref.shape[0], pieces[0].shape[1]
     own = pl.multiple_of(where_ref[1] * half, half)
     send = pl.multiple_of((1 - where_ref[1]) * half, half)
@@ -130,22 +129,9 @@
         send_ref[:, i * tokens : (i + 1) * tokens] = piece[pl.ds(send, half), :]
 
 
-def halves(where, pieces):
-    rows, tokens = pieces[0].shape
-    shape = (rows // 2, len(pieces) * tokens)
-    return pl.pallas_call(
-        halves_kernel,
-        grid=(1,),
-        out_shape=(pltpu.HBM(shape, jnp.bfloat16),) * 2,
-        in_specs=[SMEM] + [whole(piece) for piece in pieces],
-        out_specs=(pl.BlockSpec(shape, lambda i: (0, 0)),) * 2,
-        compiler_params=pltpu.CompilerParams(vmem_limit_bytes=20 * MIB),
-        cost_estimate=SMALL,
-        name="halves",
-    )(where, *pieces)
-
-
-def attention_kernel(where_ref, order_ref, lens_ref, q_ref, do_ref, kv_ref, dq_ref, dkv_ref, bias_ref, dk_ref, dv_ref):
+def attention_kernel(where_ref, order_ref, lens_ref, q_ref, do_ref, kv_ref, *refs):
+    pieces, (dq_ref, dkv_ref, own_ref, send_ref, bias_ref, dk_ref, dv_ref) = refs[:-7], refs[-7:]
+    halves(where_ref, pieces, own_ref, send_ref)
     scale = HD ** (-0.5)
     spans = order_ref.shape[1]
     docs = lens_ref.shape[1]
@@ -198,28 +184,31 @@
             dkv_ref[:, HD:] = dv.astype(jnp.bfloat16)
 
 
-def attention(where, order, lens, query, grad, key_value):
+def attention(where, order, lens, query, grad, key_value, pieces):
+    rows, width = pieces[0].shape
+    half = jax.ShapeDtypeStruct((rows // 2, width * len(pieces)), jnp.bfloat16)
     tokens = query.shape[0]
     total = key_value.shape[0]
-    work = HQ * tokens * total
     return pl.pallas_call(
         attention_kernel,
         out_shape=(
             pltpu.HBM((tokens, HQ * HD), jnp.bfloat16),
             pltpu.HBM((total, 2 * HD), jnp.bfloat16),
+            pltpu.HBM(half.shape, half.dtype),
+            pltpu.HBM(half.shape, half.dtype),
         ),
         grid=(1,),
-        in_specs=[SMEM, SMEM, SMEM] + [whole(v) for v in (query, grad, key_value)],
-        out_specs=(whole(query), whole(key_value)),
+        in_specs=[SMEM] * 3 + [VMEM] * (3 + len(pieces)),
+        out_specs=(whole(query), whole(key_value), whole(half), whole(half)),
         scratch_shapes=[
             pltpu.VMEM((total, tokens), jnp.float32),
             pltpu.VMEM((total, HD), jnp.float32),
             pltpu.VMEM((total, HD), jnp.float32),
         ],
-        compiler_params=pltpu.CompilerParams(vmem_limit_bytes=24 * MIB),
+        compiler_params=pltpu.CompilerParams(vmem_limit_bytes=30 * MIB),
         cost_estimate=SMALL,
         name="attention",
-    )(where, order, lens, query, grad, key_value)
+    )(where, order, lens, query, grad, key_value, *pieces)
 
 
 def both(x_own, x_other, pieces, at, width):
@@ -262,7 +251,7 @@
             pltpu.HBM((blocks, half // blocks, FIRST), jnp.bfloat16),
             pltpu.HBM((half, width - FIRST), jnp.bfloat16),
         ),
-        in_specs=[whole(own), whole(other)] + [VMEM] * len(pieces),
+        in_specs=[VMEM] * (2 + len(pieces)),
         out_specs=(
             pl.BlockSpec((blocks, half // blocks, step), lambda j: (0, 0, jnp.minimum(j, first - 1))),
             pl.BlockSpec((half, step), lambda j: (0, jnp.maximum(j - first, 0))),
@@ -297,7 +286,7 @@
         term_second_kernel,
         grid=(1,),
         out_shape=(out,) * 4,
-        in_specs=[SMEM] + [whole(value) for value in (own, other, done)] + [VMEM] * len(pieces),
+        in_specs=[SMEM] + [VMEM] * (3 + len(pieces)),
         out_specs=(pl.BlockSpec(out.shape, lambda i: (0, 0)),) * 4,
         compiler_params=pltpu.CompilerParams(vmem_limit_bytes=20 * MIB),
         cost_estimate=SMALL,
@@ -325,9 +314,9 @@
     return pl.pallas_call(
         middle_stacked_kernel if stacked else lambda *refs: middle_kernel(along_z, *refs),
         grid=(1,),
-        out_shape=(pltpu.HBM((rows // 4, width), jnp.float32),) + (pltpu.HBM((rows // 4, width), jnp.bfloat16),) * 3,
-        in_specs=[SMEM] + [whole(part) for part in parts],
-        out_specs=(pl.BlockSpec((rows // 4, width), lambda i: (0, 0)),) * 4,
+        out_shape=(jax.ShapeDtypeStruct((rows // 4, width), jnp.float32),) + (pltpu.HBM((rows // 4, width), jnp.bfloat16),) * 3,
+        in_specs=[SMEM] + [VMEM] * len(parts),
+        out_specs=(VMEM,) + (pl.BlockSpec((rows // 4, width), lambda i: (0, 0)),) * 3,
         compiler_params=pltpu.CompilerParams(vmem_limit_bytes=14 * MIB),
         cost_estimate=SMALL,
         name="middle_z" if along_z else "middle_y",
@@ -363,12 +352,14 @@
     return lax.ppermute(value, "core", [(0, 1), (1, 0)])
 
 
-def gather_chips(value):
+def gather_chips(value, *others):
     own = [value] + [shifted(value, s) for s in range(1, lax.axis_size("x"))]
-    return own, [swapped(piece) for piece in own]
+    return own, [swapped(after(piece, *others)) for piece in own]
 
 
 def after(value, *others):
+    if not others:
+        return value
     return lax.optimization_barrier((value,) + others)[0]
 
 
@@ -400,17 +391,15 @@
     gathered = lax.all_to_all(copies, SEQ, 0, 0, tiled=True).reshape(seq * tokens, 2 * HD)
     pieces = [packed[0]] + [shifted(packed[s], s) for s in range(1, chips)]
     query = project_query(after(rows, copies), w_qkv)
-    d_query, terms = attention(where, span_order, doc_lengths, query, d_out[0], gathered)
+    d_query, terms, x_own, x_send = attention(where, span_order, doc_lengths, query, d_out[0], gathered, pieces)
     own_q, other_q = gather_chips(d_query)
-    arrived = lax.all_to_all(terms.reshape(seq, tokens, 2 * HD), SEQ, 0, 0, tiled=True)
-    pieces = [after(piece, terms) for piece in pieces]
-    x_own, x_send = halves(where, pieces)
+    arrived = lax.all_to_all(after(terms, other_q[0]).reshape(seq, tokens, 2 * HD), SEQ, 0, 0, tiled=True)
     x_other = swapped(x_send)
 
     stacked, done = term_query(x_own, x_other, own_q + other_q, lax.axis_size("y"))
     group_y = lax.all_to_all(stacked, "y", 0, 0, tiled=True)
     owned = jnp.sum(arrived.astype(jnp.float32), axis=0).astype(jnp.bfloat16)
-    own_kv, other_kv = gather_chips(owned)
+    own_kv, other_kv = gather_chips(after(owned, *other_q), done)
     parts = term_second(where, x_own, x_other, done, own_kv + other_kv)
     d_qkv = jnp.concatenate([d_query, owned], axis=1)
     d_rows = nt(d_qkv, w_qkv).astype(jnp.bfloat16)

time: 136 us -> 122 us (0.90)
  waiting for transfers between devices: 30.1 us -> 17.7 us
  Pallas kernels: 36.5 us -> 34.5 us
  local copies, waits for them, and re-layouts: 8.23 us -> 6.41 us
  starting transfers between devices: 46.8 us -> 48.4 us
    ppermute x9, waiting for transfers between devices: 25 us -> 4.42 us  [shifted(): return lax.ppermute(value, 'x', [(i, (i + s) % n) for i in range(n)])]
    all_to_all x1, waiting for transfers between devices: 0.01 us -> 6.01 us  [local(): lax.all_to_all(after(terms, other_q[0]).reshape(seq, tokens, 2 * HD), SEQ...]
    pallas_call x2 -> x1, Pallas kernels: 11 us -> 7.43 us  [project_query(): pl.pallas_call(query_kernel, grid=(HQ // 2,), out_shape=jax.ShapeDtypeStr...]
    all_to_all x1, starting transfers between devices: 5.35 us -> 7.92 us  [local(): lax.all_to_all(after(terms, other_q[0]).reshape(seq, tokens, 2 * HD), SEQ...]
    unnamed x32 -> x28, local copies, waits for them, and re-layouts: 7.62 us -> 5.79 us
    pallas_call x1, Pallas kernels: 6.88 us -> 8.42 us  [attention(): pl.pallas_call(attention_kernel, out_shape=(pltpu.HBM((tokens, HQ * HD),...]
  transfers between devices with their start and end apart: 30 -> 30, of which waited for: 9 -> 6; matrix products, arithmetic and copies ran while one was open for 10% -> 11% of each run, Pallas kernels for 22% -> 18%
where the time goes in v5:
time: 122 us; the launch traced here: 121 us
  starting transfers between devices  48.4 us (40%)
  Pallas kernels  34.5 us (28%)
  waiting for transfers between devices  17.7 us (15%)
  matrix products  12 us (10%)
  local copies, waits for them, and re-layouts  6.41 us (5%)
    ppermute x9, starting transfers between devices, shifted(): return lax.ppermute(value, 'x', [(i, (i + s) % n) for i in range(n)])  13.1 us
    dot_general x1, matrix products, nt(): lax.dot_general(a, b, (((1,), (1,)), ((), ())), preferred_element_type=jn...  12 us
    pallas_call x1, Pallas kernels, attention(): pl.pallas_call(attention_kernel, out_shape=(pltpu.HBM((tokens, HQ * HD),...  8.42 us
    ppermute x6, starting transfers between devices, shifted_z(): lax.ppermute(value, DEPTH, [(ring_index(i), ring_index((i + s) % 4)) for...  8.04 us
    all_to_all x1, starting transfers between devices, local(): lax.all_to_all(after(terms, other_q[0]).reshape(seq, tokens, 2 * HD), SEQ...  7.92 us
    all_to_all x1, starting transfers between devices, local(): lax.all_to_all(copies, SEQ, 0, 0, tiled=True).reshape(seq * tokens, 2 * HD)  7.78 us
    pallas_call x1, Pallas kernels, project_query(): pl.pallas_call(query_kernel, grid=(HQ // 2,), out_shape=jax.ShapeDtypeStr...  7.43 us
    all_to_all x1, waiting for transfers between devices, local(): lax.all_to_all(after(terms, other_q[0]).reshape(seq, tokens, 2 * HD), SEQ...  6.01 us
  transfers between devices with their start and end apart: 30, of which 6 were waited for; matrix products, arithmetic and copies ran while one was open for 11% of the time, Pallas kernels for 18%

profile of v5, /device:TPU:0, one launch (start us, length us, event | category | flops | bytes accessed | tf_op | source)
XLA Modules:
  0.0 121.0 jit_solution(15992055154573082723)
XLA Ops:
  0.6 0.6 stack.23.where_ref.refs_0_
  1.3 3.2 %pack.1 = (bf16[2048,128]{1,0:T(8,128)(2,1)}, bf16[2048,128]{1,0:T(8,128)(2,1)}, bf16[2048,128]{1,0:T(8,128)(2,1)}, bf16[2048,128]{1,0:T(8,128)(2,1)}) custom-call(s32[5]{0:T(128)} %stack.23.where_ref.refs_0_, bf16[128,8192]{1,0:T(8,128)(2,1)} %bitcast.11), custom_call_target="tpu_custom_call" | custom-call | flops 1 | bytes 1 | tf_op jit(solution)/shard_map/pack/pallas_call | solution.py:53
  4.4 1.6 %collective-permute-start = (bf16[2048,128]{1,0:T(8,128)(2,1)}, bf16[2048,128]{1,0:T(8,128)(2,1)}, u32[]{:S(2)}, u32[]{:S(2)}) collective-permute-start(bf16[2048,128]{1,0:T(8,128)(2,1)} %get-tuple-element.38), channel_id=1, source_target_pairs={{0,16},{16,32},{32,48},{48,0},{1,17},{17,33},{33,49},{49,1},{2,18}... | collective-permute-start | bytes 1572872 | tf_op jit(solution)/shard_map/ppermute | solution.py:348
  6.0 2.7 %collective-permute-start.1 = (bf16[2048,128]{1,0:T(8,128)(2,1)}, bf16[2048,128]{1,0:T(8,128)(2,1)}, u32[]{:S(2)}, u32[]{:S(2)}) collective-permute-start(bf16[2048,128]{1,0:T(8,128)(2,1)} %get-tuple-element.39), channel_id=1, source_target_pairs={{0,32},{16,48},{32,0},{48,16},{1,33},{17,49},{33,1},{49,17},{2,34}... | collective-permute-start | bytes 1572872 | tf_op jit(solution)/shard_map/ppermute | solution.py:348
  8.7 1.4 %collective-permute-start.2 = (bf16[2048,128]{1,0:T(8,128)(2,1)}, bf16[2048,128]{1,0:T(8,128)(2,1)}, u32[]{:S(2)}, u32[]{:S(2)}) collective-permute-start(bf16[2048,128]{1,0:T(8,128)(2,1)} %get-tuple-element.40), channel_id=1, source_target_pairs={{0,48},{16,0},{32,16},{48,32},{1,49},{17,1},{33,17},{49,33},{2,50}... | collective-permute-start | bytes 1572872 | tf_op jit(solution)/shard_map/ppermute | solution.py:348
  10.2 4.3 %project_kv.1 = bf16[8,128,256]{2,1,0:T(8,128)(2,1)} custom-call(bf16[128,8192]{1,0:T(8,128)(2,1)} %bitcast.12, bf16[8192,1280]{1,0:T(8,128)(2,1)} %w_ref.3), custom_call_target="tpu_custom_call" | custom-call | flops 1 | bytes 1 | tf_op jit(solution)/shard_map/project_kv/pallas_call | solution.py:88
  14.5 7.8 %all-to-all-start = ((bf16[8,128,256]{2,1,0:T(8,128)(2,1)}), bf16[8,128,256]{2,1,0:T(8,128)(2,1)S(1)}, u32[]{:S(2)}, u32[]{:S(2)}) async-start(bf16[8,128,256]{2,1,0:T(8,128)(2,1)} %project_kv.1), calls=%async_computation | async-start | bytes 1048576 | tf_op jit(solution)/shard_map/all_to_all | solution.py:391
  22.3 7.4 %project_query.1.q_ref = bf16[128,1024]{1,0:T(8,128)(2,1)S(1)} custom-call(bf16[128,8192]{1,0:T(8,128)(2,1)S(1)} %bitcast.13, bf16[8192,1280]{1,0:T(8,128)(2,1)} %w_ref.3), custom_call_target="tpu_custom_call" | custom-call | flops 1 | bytes 1 | tf_op jit(solution)/shard_map/project_query/pallas_call | solution.py:111
  29.8 3.3 %all-to-all-done = bf16[8,128,256]{2,1,0:T(8,128)(2,1)S(1)} async-done(((bf16[8,128,256]{2,1,0:T(8,128)(2,1)}), bf16[8,128,256]{2,1,0:T(8,128)(2,1)S(1)}, u32[]{:S(2)}, u32[]{:S(2)}) %all-to-all-start) | async-done | bytes 524320 | tf_op jit(solution)/shard_map/all_to_all | solution.py:391
  33.1 0.9 copy-done.9
  34.0 8.4 %attention.1 = (bf16[128,1024]{1,0:T(8,128)(2,1)}, bf16[1024,256]{1,0:T(8,128)(2,1)}, bf16[1024,512]{1,0:T(8,128)(2,1)}, bf16[1024,512]{1,0:T(8,128)(2,1)}) custom-call(s32[5]{0:T(128)S(1)} %copy-done.11, s32[1,16]{1,0:T(1,128)S(1)} %copy-done.12, s32[1,4]{1,0:T(1,128)S(1)} %copy-done.13, bf16[128,1024]{1,0:T(8,128)(2,1)S(1)} %project_query.1.q_ref, ...), custom_call_target="tpu_custom_call" | custom-call | flops 1 | bytes 1 | tf_op jit(solution)/shard_map/attention/pallas_call | solution.py:192
  42.4 0.5 collective-permute-start.3
  42.9 1.0 collective-permute-start.7
  43.9 1.0 collective-permute-start.5
  45.0 1.5 %collective-permute-start.6 = (bf16[128,1024]{1,0:T(8,128)(2,1)}, bf16[128,1024]{1,0:T(8,128)(2,1)S(1)}, u32[]{:S(2)}, u32[]{:S(2)}) collective-permute-start(bf16[128,1024]{1,0:T(8,128)(2,1)} %get-tuple-element.41.refs_0_), channel_id=1, source_target_pairs={{0,32},{16,48},{32,0},{48,16},{1,33},{17,49},{33,1},{49,17},{2,34}... | collective-permute-start | bytes 786440 | tf_op jit(solution)/shard_map/ppermute | solution.py:348
  46.5 7.9 %all-to-all-start.1 = ((bf16[8,128,256]{2,1,0:T(8,128)(2,1)}), bf16[8,128,256]{2,1,0:T(8,128)(2,1)}, u32[]{:S(2)}, u32[]{:S(2)}) async-start(bf16[8,128,256]{2,1,0:T(8,128)(2,1)} %bitcast.17), calls=%async_computation.1 | async-start | bytes 1048576 | tf_op jit(solution)/shard_map/all_to_all | solution.py:396
  54.5 0.1 collective-permute-start.10
  54.5 4.4 %collective-permute-done.5.refs_1_ = bf16[128,1024]{1,0:T(8,128)(2,1)S(1)} collective-permute-done((bf16[128,1024]{1,0:T(8,128)(2,1)}, bf16[128,1024]{1,0:T(8,128)(2,1)S(1)}, u32[]{:S(2)}, u32[]{:S(2)}) %collective-permute-start.5) | collective-permute-done | bytes 262176 | tf_op jit(solution)/shard_map/ppermute | solution.py:348
  58.9 0.5 collective-permute-start.9
  59.5 6.0 %all-to-all-done.1 = bf16[8,128,256]{2,1,0:T(8,128)(2,1)} async-done(((bf16[8,128,256]{2,1,0:T(8,128)(2,1)}), bf16[8,128,256]{2,1,0:T(8,128)(2,1)}, u32[]{:S(2)}, u32[]{:S(2)}) %all-to-all-start.1) | async-done | bytes 524320 | tf_op jit(solution)/shard_map/all_to_all | solution.py:396
  65.5 1.1 reduce_sum.12.refs_0_
  66.6 1.4 %collective-permute-start.16 = (bf16[128,256]{1,0:T(8,128)(2,1)S(1)}, bf16[128,256]{1,0:T(8,128)(2,1)S(1)}, u32[]{:S(2)}, u32[]{:S(2)}) collective-permute-start(bf16[128,256]{1,0:T(8,128)(2,1)S(1)} %reduce_sum.12.refs_0_), channel_id=1, source_target_pairs={{0,48},{16,0},{32,16},{48,32},{1,49},{17,1},{33,17},{49,33},{2,50}... | collective-permute-start | bytes 196616 | tf_op jit(solution)/shard_map/ppermute | solution.py:348
  68.0 2.4 %collective-permute-start.15 = (bf16[128,256]{1,0:T(8,128)(2,1)S(1)}, bf16[128,256]{1,0:T(8,128)(2,1)}, u32[]{:S(2)}, u32[]{:S(2)}) collective-permute-start(bf16[128,256]{1,0:T(8,128)(2,1)S(1)} %reduce_sum.12.refs_0_), channel_id=1, source_target_pairs={{0,32},{16,48},{32,0},{48,16},{1,33},{17,49},{33,1},{49,17},{2,34}... | collective-permute-start | bytes 196616 | tf_op jit(solution)/shard_map/ppermute | solution.py:348
  70.5 1.6 %copy-done.1 = bf16[1024,512]{1,0:T(8,128)(2,1)S(1)} copy-done((bf16[1024,512]{1,0:T(8,128)(2,1)S(1)}, bf16[1024,512]{1,0:T(8,128)(2,1)}, u32[]{:S(2)}) %copy-start.1) | copy-done | bytes 1048600
  72.1 0.9 copy-done.5
  73.0 5.2 %term_query.1 = (bf16[4,256,768]{2,1,0:T(8,128)(2,1)}, bf16[1024,256]{1,0:T(8,128)(2,1)}) custom-call(bf16[1024,512]{1,0:T(8,128)(2,1)S(1)} %copy-done.1, bf16[1024,512]{1,0:T(8,128)(2,1)S(1)} %collective-permute-done.4.other_ref, bf16[128,1024]{1,0:T(8,128)(2,1)S(1)} %copy-done.5, bf16[128,1024]{1,0:T(8,128)(2,1)S(1)} %collective-permute-done.5.refs_1_, ...), custom_call_target="tpu_custom_call" | custom-call | flops 1 | bytes 1 | tf_op jit(solution)/shard_map/term_query/pallas_call | solution.py:247
  78.3 0.5 collective-permute-start.19
  78.8 0.1 collective-permute-start.18
  78.9 0.4 collective-permute-start.17
  79.3 3.6 %all-to-all-start.2 = ((bf16[4,256,768]{2,1,0:T(8,128)(2,1)}), bf16[4,256,768]{2,1,0:T(8,128)(2,1)S(1)}, u32[]{:S(2)}, u32[]{:S(2)}) async-start(bf16[4,256,768]{2,1,0:T(8,128)(2,1)} %get-tuple-element.46), calls=%async_computation.2 | async-start | bytes 3145728 | tf_op jit(solution)/shard_map/all_to_all | solution.py:400
  83.0 1.2 %copy-done.4 = bf16[1024,512]{1,0:T(8,128)(2,1)S(1)} copy-done((bf16[1024,512]{1,0:T(8,128)(2,1)S(1)}, bf16[1024,512]{1,0:T(8,128)(2,1)}, u32[]{:S(2)}) %copy-start.4) | copy-done | bytes 1048600
  84.2 1.0 copy-done.8
  85.2 2.4 %term_second.1 = (bf16[256,512]{1,0:T(8,128)(2,1)}, bf16[256,512]{1,0:T(8,128)(2,1)}, bf16[256,512]{1,0:T(8,128)(2,1)}, bf16[256,512]{1,0:T(8,128)(2,1)}) custom-call(s32[5]{0:T(128)S(1)} %copy-done.11, bf16[1024,512]{1,0:T(8,128)(2,1)S(1)} %copy-done.2, bf16[1024,512]{1,0:T(8,128)(2,1)S(1)} %copy-done.4, bf16[1024,256]{1,0:T(8,128)(2,1)S(1)} %copy-done.8, ...), custom_call_target="tpu_custom_call" | custom-call | flops 1 | bytes 1 | tf_op jit(solution)/shard_map/term_second/pallas_call | solution.py:285
  87.7 0.7 collective-permute-start.23
  88.4 2.4 %collective-permute-start.22 = (bf16[256,512]{1,0:T(8,128)(2,1)}, bf16[256,512]{1,0:T(8,128)(2,1)S(1)}, u32[]{:S(2)}, u32[]{:S(2)}) collective-permute-start(bf16[256,512]{1,0:T(8,128)(2,1)} %get-tuple-element.60), channel_id=1, source_target_pairs={{0,4},{64,68},{4,0},{68,64},{1,5},{65,69},{5,1},{69,65},{2,6},{66,... | collective-permute-start | bytes 786440 | tf_op jit(solution)/shard_map/ppermute | solution.py:371
  90.8 12.0 %convolution_convert_fusion = bf16[128,8192]{1,0:T(8,128)(2,1)} fusion(bf16[8192,1280]{1,0:T(8,128)(2,1)} %w_ref.3, bf16[128,256]{1,0:T(8,128)(2,1)S(1)} %reduce_sum.12.refs_0_, bf16[128,1024]{1,0:T(8,128)(2,1)S(1)} %copy-done.6), kind=kOutput, calls=%fused_computation | convolution fusion | flops 2686058496 | bytes 23396352 | tf_op jit(solution)/shard_map/dot_general | solution.py:18
  102.8 1.0 collective-permute-done.21.refs_2_
  103.8 1.3 %middle_y.1 = (f32[64,512]{1,0:T(8,128)S(1)}, bf16[64,512]{1,0:T(8,128)(2,1)}, bf16[64,512]{1,0:T(8,128)(2,1)}, bf16[64,512]{1,0:T(8,128)(2,1)}) custom-call(s32[5]{0:T(128)S(1)} %copy-done.11, bf16[256,512]{1,0:T(8,128)(2,1)S(1)} %copy-done.10, bf16[256,512]{1,0:T(8,128)(2,1)S(1)} %collective-permute-done.21.refs_2_, ...), custom_call_target="tpu_custom_call" | custom-call | flops 1 | bytes 1 | tf_op jit(solution)/shard_map/middle_y/pallas_call | solution.py:314
  105.1 1.7 %collective-permute-start.24 = (bf16[64,512]{1,0:T(8,128)(2,1)}, bf16[64,512]{1,0:T(8,128)(2,1)S(1)}, u32[]{:S(2)}, u32[]{:S(2)}) collective-permute-start(bf16[64,512]{1,0:T(8,128)(2,1)} %get-tuple-element.65), channel_id=1, source_target_pairs={{0,1},{1,2},{2,3},{3,0},{4,5},{5,6},{6,7},{7,4},{8,9},{9,10},{10,1... | collective-permute-start | bytes 196616 | tf_op jit(solution)/shard_map/ppermute | solution.py:375
  106.7 1.4 %middle_z.1 = (f32[64,768]{1,0:T(8,128)S(1)}, bf16[64,768]{1,0:T(8,128)(2,1)}, bf16[64,768]{1,0:T(8,128)(2,1)}, bf16[64,768]{1,0:T(8,128)(2,1)}) custom-call(s32[5]{0:T(128)S(1)} %copy-done.11, bf16[4,256,768]{2,1,0:T(8,128)(2,1)S(1)} %all-to-all-done.2.stack_ref), custom_call_target="tpu_custom_call" | custom-call | flops 1 | bytes 1 | tf_op jit(solution)/shard_map/middle_z/pallas_call | solution.py:314
  108.1 0.9 collective-permute-start.11
  109.0 3.0 %collective-permute-start.12 = (bf16[64,768]{1,0:T(8,128)(2,1)}, bf16[64,768]{1,0:T(8,128)(2,1)S(1)}, u32[]{:S(2)}, u32[]{:S(2)}) collective-permute-start(bf16[64,768]{1,0:T(8,128)(2,1)} %get-tuple-element.49), channel_id=1, source_target_pairs={{0,4},{64,68},{4,0},{68,64},{1,5},{65,69},{5,1},{69,65},{2,6},{66,... | collective-permute-start | bytes 294920 | tf_op jit(solution)/shard_map/ppermute | solution.py:371
  112.0 1.0 collective-permute-start.13
  113.1 2.7 %collective-permute-start.25 = (bf16[64,512]{1,0:T(8,128)(2,1)}, bf16[64,512]{1,0:T(8,128)(2,1)S(1)}, u32[]{:S(2)}, u32[]{:S(2)}) collective-permute-start(bf16[64,512]{1,0:T(8,128)(2,1)} %get-tuple-element.66), channel_id=1, source_target_pairs={{0,2},{1,3},{2,0},{3,1},{4,6},{5,7},{6,4},{7,5},{8,10},{9,11},{10,... | collective-permute-start | bytes 196616 | tf_op jit(solution)/shard_map/ppermute | solution.py:375
  115.7 1.5 %collective-permute-start.26 = (bf16[64,512]{1,0:T(8,128)(2,1)}, bf16[64,512]{1,0:T(8,128)(2,1)S(1)}, u32[]{:S(2)}, u32[]{:S(2)}) collective-permute-start(bf16[64,512]{1,0:T(8,128)(2,1)} %get-tuple-element.67), channel_id=1, source_target_pairs={{0,3},{1,0},{2,1},{3,2},{4,7},{5,4},{6,5},{7,6},{8,11},{9,8},{10,9... | collective-permute-start | bytes 196616 | tf_op jit(solution)/shard_map/ppermute | solution.py:375
  117.2 1.8 %collective-permute-done.25.refs_6_ = bf16[64,512]{1,0:T(8,128)(2,1)S(1)} collective-permute-done((bf16[64,512]{1,0:T(8,128)(2,1)}, bf16[64,512]{1,0:T(8,128)(2,1)S(1)}, u32[]{:S(2)}, u32[]{:S(2)}) %collective-permute-start.25) | collective-permute-done | bytes 65568 | tf_op jit(solution)/shard_map/ppermute | solution.py:375
  119.0 1.2 collective-permute-done.26.refs_7_
  120.2 0.8 final.1
  (52 shorter events, 0.2 us)
Async XLA Ops:
  4.4 28.6 %collective-permute-start = (bf16[2048,128]{1,0:T(8,128)(2,1)}, bf16[2048,128]{1,0:T(8,128)(2,1)}, u32[]{:S(2)}, u32[]{:S(2)}) collective-permute-start(bf16[2048,128]{1,0:T(8,128)(2,1)} %get-tuple-element.38), channel_id=1, source_target_pairs={{0,16},{16,32},{32,48},{48,0},{1,17},{17,33},{33,49},{49,1},{2,18}... | collective-permute-start | bytes 1572872 | tf_op jit(solution)/shard_map/ppermute | solution.py:348
  6.0 27.0 %collective-permute-start.1 = (bf16[2048,128]{1,0:T(8,128)(2,1)}, bf16[2048,128]{1,0:T(8,128)(2,1)}, u32[]{:S(2)}, u32[]{:S(2)}) collective-permute-start(bf16[2048,128]{1,0:T(8,128)(2,1)} %get-tuple-element.39), channel_id=1, source_target_pairs={{0,32},{16,48},{32,0},{48,16},{1,33},{17,49},{33,1},{49,17},{2,34}... | collective-permute-start | bytes 1572872 | tf_op jit(solution)/shard_map/ppermute | solution.py:348
  8.7 24.3 %collective-permute-start.2 = (bf16[2048,128]{1,0:T(8,128)(2,1)}, bf16[2048,128]{1,0:T(8,128)(2,1)}, u32[]{:S(2)}, u32[]{:S(2)}) collective-permute-start(bf16[2048,128]{1,0:T(8,128)(2,1)} %get-tuple-element.40), channel_id=1, source_target_pairs={{0,48},{16,0},{32,16},{48,32},{1,49},{17,1},{33,17},{49,33},{2,50}... | collective-permute-start | bytes 1572872 | tf_op jit(solution)/shard_map/ppermute | solution.py:348
  10.2 12.1 %copy-start = (bf16[1,128,8192]{2,1,0:T(8,128)(2,1)S(1)}, bf16[1,128,8192]{2,1,0:T(8,128)(2,1)}, u32[]{:S(2)}) copy-start(bf16[1,128,8192]{2,1,0:T(8,128)(2,1)} %param.5) | copy-start | bytes 6291460
  14.5 18.5 %all-to-all-start = ((bf16[8,128,256]{2,1,0:T(8,128)(2,1)}), bf16[8,128,256]{2,1,0:T(8,128)(2,1)S(1)}, u32[]{:S(2)}, u32[]{:S(2)}) async-start(bf16[8,128,256]{2,1,0:T(8,128)(2,1)} %project_kv.1), calls=%async_computation | async-start | bytes 1048576 | tf_op jit(solution)/shard_map/all_to_all | solution.py:391
  22.3 10.8 %copy-start.7 = (bf16[2048,128]{1,0:T(8,128)(2,1)S(1)}, bf16[2048,128]{1,0:T(8,128)(2,1)}, u32[]{:S(2)}) copy-start(bf16[2048,128]{1,0:T(8,128)(2,1)} %get-tuple-element.35.refs_0_) | copy-start | bytes 1572868
  22.3 10.8 %copy-start.11 = (s32[5]{0:T(128)S(1)}, s32[5]{0:T(128)}, u32[]{:S(2)}) copy-start(s32[5]{0:T(128)} %stack.23.where_ref.refs_0_) | copy-start | bytes 64
  22.3 10.8 %copy-start.12 = (s32[1,16]{1,0:T(1,128)S(1)}, s32[1,16]{1,0:T(1,128)}, u32[]{:S(2)}) copy-start(s32[1,16]{1,0:T(1,128)} %order_ref.1) | copy-start | bytes 196
  22.3 10.8 %copy-start.13 = (s32[1,4]{1,0:T(1,128)S(1)}, s32[1,4]{1,0:T(1,128)}, u32[]{:S(2)}) copy-start(s32[1,4]{1,0:T(1,128)} %lens_ref.1) | copy-start | bytes 52
  33.1 1.0 copy-start.9
  42.4 28.0 %collective-permute-start.4 = (bf16[1024,512]{1,0:T(8,128)(2,1)}, bf16[1024,512]{1,0:T(8,128)(2,1)S(1)}, u32[]{:S(2)}, u32[]{:S(2)}) collective-permute-start(bf16[1024,512]{1,0:T(8,128)(2,1)} %get-tuple-element.45), channel_id=1, source_target_pairs={{0,8},{8,0},{1,9},{9,1},{2,10},{10,2},{3,11},{11,3},{4,12},{12,4},... | collective-permute-start | bytes 3145736 | tf_op jit(solution)/shard_map/ppermute | solution.py:352
  42.4 4.1 %collective-permute-start.3 = (bf16[128,1024]{1,0:T(8,128)(2,1)}, bf16[128,1024]{1,0:T(8,128)(2,1)S(1)}, u32[]{:S(2)}, u32[]{:S(2)}) collective-permute-start(bf16[128,1024]{1,0:T(8,128)(2,1)} %get-tuple-element.41.refs_0_), channel_id=1, source_target_pairs={{0,8},{8,0},{1,9},{9,1},{2,10},{10,2},{3,11},{11,3},{4,12},{12,4},... | collective-permute-start | bytes 786440 | tf_op jit(solution)/shard_map/ppermute | solution.py:352
  42.9 11.5 %collective-permute-start.7 = (bf16[128,1024]{1,0:T(8,128)(2,1)}, bf16[128,1024]{1,0:T(8,128)(2,1)S(1)}, u32[]{:S(2)}, u32[]{:S(2)}) collective-permute-start(bf16[128,1024]{1,0:T(8,128)(2,1)} %get-tuple-element.41.refs_0_), channel_id=1, source_target_pairs={{0,48},{16,0},{32,16},{48,32},{1,49},{17,1},{33,17},{49,33},{2,50}... | collective-permute-start | bytes 786440 | tf_op jit(solution)/shard_map/ppermute | solution.py:348
  43.9 15.0 %collective-permute-start.5 = (bf16[128,1024]{1,0:T(8,128)(2,1)}, bf16[128,1024]{1,0:T(8,128)(2,1)S(1)}, u32[]{:S(2)}, u32[]{:S(2)}) collective-permute-start(bf16[128,1024]{1,0:T(8,128)(2,1)} %get-tuple-element.41.refs_0_), channel_id=1, source_target_pairs={{0,16},{16,32},{32,48},{48,0},{1,17},{17,33},{33,49},{49,1},{2,18}... | collective-permute-start | bytes 786440 | tf_op jit(solution)/shard_map/ppermute | solution.py:348
  45.0 14.0 %collective-permute-start.6 = (bf16[128,1024]{1,0:T(8,128)(2,1)}, bf16[128,1024]{1,0:T(8,128)(2,1)S(1)}, u32[]{:S(2)}, u32[]{:S(2)}) collective-permute-start(bf16[128,1024]{1,0:T(8,128)(2,1)} %get-tuple-element.41.refs_0_), channel_id=1, source_target_pairs={{0,32},{16,48},{32,0},{48,16},{1,33},{17,49},{33,1},{49,17},{2,34}... | collective-permute-start | bytes 786440 | tf_op jit(solution)/shard_map/ppermute | solution.py:348
  46.5 36.4 %copy-start.2 = (bf16[1024,512]{1,0:T(8,128)(2,1)S(1)}, bf16[1024,512]{1,0:T(8,128)(2,1)}, u32[]{:S(2)}) copy-start(bf16[1024,512]{1,0:T(8,128)(2,1)} %get-tuple-element.44.own_ref) | copy-start | bytes 3145732
  46.5 18.9 %all-to-all-start.1 = ((bf16[8,128,256]{2,1,0:T(8,128)(2,1)}), bf16[8,128,256]{2,1,0:T(8,128)(2,1)}, u32[]{:S(2)}, u32[]{:S(2)}) async-start(bf16[8,128,256]{2,1,0:T(8,128)(2,1)} %bitcast.17), calls=%async_computation.1 | async-start | bytes 1048576 | tf_op jit(solution)/shard_map/all_to_all | solution.py:396
  54.5 12.1 %collective-permute-start.10 = (bf16[128,1024]{1,0:T(8,128)(2,1)S(1)}, bf16[128,1024]{1,0:T(8,128)(2,1)S(1)}, u32[]{:S(2)}, u32[]{:S(2)}) collective-permute-start(bf16[128,1024]{1,0:T(8,128)(2,1)S(1)} %collective-permute-done.7.refs_3_), channel_id=1, source_target_pairs={{0,8},{8,0},{1,9},{9,1},{2,10},{10,2},{3,11},{11,3},{4,12},{12,4},... | collective-permute-start | bytes 786440 | tf_op jit(solution)/shard_map/ppermute | solution.py:352
  58.9 7.7 %collective-permute-start.8 = (bf16[128,1024]{1,0:T(8,128)(2,1)S(1)}, bf16[128,1024]{1,0:T(8,128)(2,1)}, u32[]{:S(2)}, u32[]{:S(2)}) collective-permute-start(bf16[128,1024]{1,0:T(8,128)(2,1)S(1)} %collective-permute-done.5.refs_1_), channel_id=1, source_target_pairs={{0,8},{8,0},{1,9},{9,1},{2,10},{10,2},{3,11},{11,3},{4,12},{12,4},... | collective-permute-start | bytes 786440 | tf_op jit(solution)/shard_map/ppermute | solution.py:352
  58.9 7.7 %collective-permute-start.9 = (bf16[128,1024]{1,0:T(8,128)(2,1)S(1)}, bf16[128,1024]{1,0:T(8,128)(2,1)}, u32[]{:S(2)}, u32[]{:S(2)}) collective-permute-start(bf16[128,1024]{1,0:T(8,128)(2,1)S(1)} %collective-permute-done.6.refs_2_), channel_id=1, source_target_pairs={{0,8},{8,0},{1,9},{9,1},{2,10},{10,2},{3,11},{11,3},{4,12},{12,4},... | collective-permute-start | bytes 786440 | tf_op jit(solution)/shard_map/ppermute | solution.py:352
  66.6 11.6 %collective-permute-start.16 = (bf16[128,256]{1,0:T(8,128)(2,1)S(1)}, bf16[128,256]{1,0:T(8,128)(2,1)S(1)}, u32[]{:S(2)}, u32[]{:S(2)}) collective-permute-start(bf16[128,256]{1,0:T(8,128)(2,1)S(1)} %reduce_sum.12.refs_0_), channel_id=1, source_target_pairs={{0,48},{16,0},{32,16},{48,32},{1,49},{17,1},{33,17},{49,33},{2,50}... | collective-permute-start | bytes 196616 | tf_op jit(solution)/shard_map/ppermute | solution.py:348
  68.0 10.3 %collective-permute-start.15 = (bf16[128,256]{1,0:T(8,128)(2,1)S(1)}, bf16[128,256]{1,0:T(8,128)(2,1)}, u32[]{:S(2)}, u32[]{:S(2)}) collective-permute-start(bf16[128,256]{1,0:T(8,128)(2,1)S(1)} %reduce_sum.12.refs_0_), channel_id=1, source_target_pairs={{0,32},{16,48},{32,0},{48,16},{1,33},{17,49},{33,1},{49,17},{2,34}... | collective-permute-start | bytes 196616 | tf_op jit(solution)/shard_map/ppermute | solution.py:348
  70.4 8.4 %collective-permute-start.14 = (bf16[128,256]{1,0:T(8,128)(2,1)S(1)}, bf16[128,256]{1,0:T(8,128)(2,1)}, u32[]{:S(2)}, u32[]{:S(2)}) collective-permute-start(bf16[128,256]{1,0:T(8,128)(2,1)S(1)} %reduce_sum.12.refs_0_), channel_id=1, source_target_pairs={{0,16},{16,32},{32,48},{48,0},{1,17},{17,33},{33,49},{49,1},{2,18}... | collective-permute-start | bytes 196616 | tf_op jit(solution)/shard_map/ppermute | solution.py:348
  70.4 8.9 %copy-start.3 = (bf16[1024,512]{1,0:T(8,128)(2,1)}, bf16[1024,512]{1,0:T(8,128)(2,1)S(1)}, u32[]{:S(2)}) copy-start(bf16[1024,512]{1,0:T(8,128)(2,1)S(1)} %collective-permute-done.4.other_ref) | copy-start | bytes 3145732
  70.5 1.6 %copy-start.1 = (bf16[1024,512]{1,0:T(8,128)(2,1)S(1)}, bf16[1024,512]{1,0:T(8,128)(2,1)}, u32[]{:S(2)}) copy-start(bf16[1024,512]{1,0:T(8,128)(2,1)} %get-tuple-element.44.own_ref) | copy-start | bytes 3145732
  72.1 0.9 copy-start.5
  78.2 12.5 %copy-start.6 = (bf16[128,1024]{1,0:T(8,128)(2,1)S(1)}, bf16[128,1024]{1,0:T(8,128)(2,1)}, u32[]{:S(2)}) copy-start(bf16[128,1024]{1,0:T(8,128)(2,1)} %get-tuple-element.41.refs_0_) | copy-start | bytes 786436
  78.2 4.7 %collective-permute-start.20 = (bf16[128,256]{1,0:T(8,128)(2,1)S(1)}, bf16[128,256]{1,0:T(8,128)(2,1)S(1)}, u32[]{:S(2)}, u32[]{:S(2)}) collective-permute-start(bf16[128,256]{1,0:T(8,128)(2,1)S(1)} %collective-permute-done.16.refs_3_), channel_id=1, source_target_pairs={{0,8},{8,0},{1,9},{9,1},{2,10},{10,2},{3,11},{11,3},{4,12},{12,4},... | collective-permute-start | bytes 196616 | tf_op jit(solution)/shard_map/ppermute | solution.py:352
  78.3 4.6 %collective-permute-start.19 = (bf16[128,256]{1,0:T(8,128)(2,1)}, bf16[128,256]{1,0:T(8,128)(2,1)S(1)}, u32[]{:S(2)}, u32[]{:S(2)}) collective-permute-start(bf16[128,256]{1,0:T(8,128)(2,1)} %collective-permute-done.15.refs_2_), channel_id=1, source_target_pairs={{0,8},{8,0},{1,9},{9,1},{2,10},{10,2},{3,11},{11,3},{4,12},{12,4},... | collective-permute-start | bytes 196616 | tf_op jit(solution)/shard_map/ppermute | solution.py:352
  78.8 4.1 %collective-permute-start.18 = (bf16[128,256]{1,0:T(8,128)(2,1)}, bf16[128,256]{1,0:T(8,128)(2,1)S(1)}, u32[]{:S(2)}, u32[]{:S(2)}) collective-permute-start(bf16[128,256]{1,0:T(8,128)(2,1)} %collective-permute-done.14.refs_1_), channel_id=1, source_target_pairs={{0,8},{8,0},{1,9},{9,1},{2,10},{10,2},{3,11},{11,3},{4,12},{12,4},... | collective-permute-start | bytes 196616 | tf_op jit(solution)/shard_map/ppermute | solution.py:352
  78.9 4.0 %collective-permute-start.17 = (bf16[128,256]{1,0:T(8,128)(2,1)S(1)}, bf16[128,256]{1,0:T(8,128)(2,1)S(1)}, u32[]{:S(2)}, u32[]{:S(2)}) collective-permute-start(bf16[128,256]{1,0:T(8,128)(2,1)S(1)} %reduce_sum.12.refs_0_), channel_id=1, source_target_pairs={{0,8},{8,0},{1,9},{9,1},{2,10},{10,2},{3,11},{11,3},{4,12},{12,4},... | collective-permute-start | bytes 196616 | tf_op jit(solution)/shard_map/ppermute | solution.py:352
  79.3 27.4 %all-to-all-start.2 = ((bf16[4,256,768]{2,1,0:T(8,128)(2,1)}), bf16[4,256,768]{2,1,0:T(8,128)(2,1)S(1)}, u32[]{:S(2)}, u32[]{:S(2)}) async-start(bf16[4,256,768]{2,1,0:T(8,128)(2,1)} %get-tuple-element.46), calls=%async_computation.2 | async-start | bytes 3145728 | tf_op jit(solution)/shard_map/all_to_all | solution.py:400
  83.0 1.2 %copy-start.4 = (bf16[1024,512]{1,0:T(8,128)(2,1)S(1)}, bf16[1024,512]{1,0:T(8,128)(2,1)}, u32[]{:S(2)}) copy-start(bf16[1024,512]{1,0:T(8,128)(2,1)} %copy-done.3) | copy-start | bytes 3145732
  84.2 1.0 copy-start.8
  87.7 15.1 %collective-permute-start.23 = (bf16[256,512]{1,0:T(8,128)(2,1)}, bf16[256,512]{1,0:T(8,128)(2,1)S(1)}, u32[]{:S(2)}, u32[]{:S(2)}) collective-permute-start(bf16[256,512]{1,0:T(8,128)(2,1)} %get-tuple-element.62), channel_id=1, source_target_pairs={{0,68},{64,0},{4,64},{68,4},{1,69},{65,1},{5,65},{69,5},{2,70},{66... | collective-permute-start | bytes 786440 | tf_op jit(solution)/shard_map/ppermute | solution.py:371
  88.4 14.4 %collective-permute-start.22 = (bf16[256,512]{1,0:T(8,128)(2,1)}, bf16[256,512]{1,0:T(8,128)(2,1)S(1)}, u32[]{:S(2)}, u32[]{:S(2)}) collective-permute-start(bf16[256,512]{1,0:T(8,128)(2,1)} %get-tuple-element.60), channel_id=1, source_target_pairs={{0,4},{64,68},{4,0},{68,64},{1,5},{65,69},{5,1},{69,65},{2,6},{66,... | collective-permute-start | bytes 786440 | tf_op jit(solution)/shard_map/ppermute | solution.py:371
  90.8 13.0 %copy-start.10 = (bf16[256,512]{1,0:T(8,128)(2,1)S(1)}, bf16[256,512]{1,0:T(8,128)(2,1)}, u32[]{:S(2)}) copy-start(bf16[256,512]{1,0:T(8,128)(2,1)} %get-tuple-element.57.refs_1_) | copy-start | bytes 786436
  90.8 13.0 %collective-permute-start.21 = (bf16[256,512]{1,0:T(8,128)(2,1)}, bf16[256,512]{1,0:T(8,128)(2,1)S(1)}, u32[]{:S(2)}, u32[]{:S(2)}) collective-permute-start(bf16[256,512]{1,0:T(8,128)(2,1)} %get-tuple-element.58), channel_id=1, source_target_pairs={{0,64},{64,4},{4,68},{68,0},{1,65},{65,5},{5,69},{69,1},{2,66},{66... | collective-permute-start | bytes 786440 | tf_op jit(solution)/shard_map/ppermute | solution.py:371
  105.1 10.7 %collective-permute-start.24 = (bf16[64,512]{1,0:T(8,128)(2,1)}, bf16[64,512]{1,0:T(8,128)(2,1)S(1)}, u32[]{:S(2)}, u32[]{:S(2)}) collective-permute-start(bf16[64,512]{1,0:T(8,128)(2,1)} %get-tuple-element.65), channel_id=1, source_target_pairs={{0,1},{1,2},{2,3},{3,0},{4,5},{5,6},{6,7},{7,4},{8,9},{9,10},{10,1... | collective-permute-start | bytes 196616 | tf_op jit(solution)/shard_map/ppermute | solution.py:375
  108.1 12.1 %collective-permute-start.11 = (bf16[64,768]{1,0:T(8,128)(2,1)}, bf16[64,768]{1,0:T(8,128)(2,1)S(1)}, u32[]{:S(2)}, u32[]{:S(2)}) collective-permute-start(bf16[64,768]{1,0:T(8,128)(2,1)} %get-tuple-element.48), channel_id=1, source_target_pairs={{0,64},{64,4},{4,68},{68,0},{1,65},{65,5},{5,69},{69,1},{2,66},{66... | collective-permute-start | bytes 294920 | tf_op jit(solution)/shard_map/ppermute | solution.py:371
  109.0 11.2 %collective-permute-start.12 = (bf16[64,768]{1,0:T(8,128)(2,1)}, bf16[64,768]{1,0:T(8,128)(2,1)S(1)}, u32[]{:S(2)}, u32[]{:S(2)}) collective-permute-start(bf16[64,768]{1,0:T(8,128)(2,1)} %get-tuple-element.49), channel_id=1, source_target_pairs={{0,4},{64,68},{4,0},{68,64},{1,5},{65,69},{5,1},{69,65},{2,6},{66,... | collective-permute-start | bytes 294920 | tf_op jit(solution)/shard_map/ppermute | solution.py:371
  112.0 8.2 %collective-permute-start.13 = (bf16[64,768]{1,0:T(8,128)(2,1)}, bf16[64,768]{1,0:T(8,128)(2,1)S(1)}, u32[]{:S(2)}, u32[]{:S(2)}) collective-permute-start(bf16[64,768]{1,0:T(8,128)(2,1)} %get-tuple-element.50), channel_id=1, source_target_pairs={{0,68},{64,0},{4,64},{68,4},{1,69},{65,1},{5,65},{69,5},{2,70},{66... | collective-permute-start | bytes 294920 | tf_op jit(solution)/shard_map/ppermute | solution.py:371
  113.1 6.0 %collective-permute-start.25 = (bf16[64,512]{1,0:T(8,128)(2,1)}, bf16[64,512]{1,0:T(8,128)(2,1)S(1)}, u32[]{:S(2)}, u32[]{:S(2)}) collective-permute-start(bf16[64,512]{1,0:T(8,128)(2,1)} %get-tuple-element.66), channel_id=1, source_target_pairs={{0,2},{1,3},{2,0},{3,1},{4,6},{5,7},{6,4},{7,5},{8,10},{9,11},{10,... | collective-permute-start | bytes 196616 | tf_op jit(solution)/shard_map/ppermute | solution.py:375
  115.7 4.5 %collective-permute-start.26 = (bf16[64,512]{1,0:T(8,128)(2,1)}, bf16[64,512]{1,0:T(8,128)(2,1)S(1)}, u32[]{:S(2)}, u32[]{:S(2)}) collective-permute-start(bf16[64,512]{1,0:T(8,128)(2,1)} %get-tuple-element.67), channel_id=1, source_target_pairs={{0,3},{1,0},{2,1},{3,2},{4,7},{5,4},{6,5},{7,6},{8,11},{9,8},{10,9... | collective-permute-start | bytes 196616 | tf_op jit(solution)/shard_map/ppermute | solution.py:375

commit v6 on v4

--- a/solution.py
+++ b/solution.py
@@ -111,10 +111,10 @@
     return pl.pallas_call(
         query_kernel,
         grid=(HQ // 2,),
-        out_shape=pltpu.HBM((tokens, HQ * HD), jnp.bfloat16),
+        out_shape=jax.ShapeDtypeStruct((tokens, HQ * HD), jnp.bfloat16),
         in_specs=[pl.BlockSpec((tokens, features), lambda i: (0, 0)), pl.BlockSpec((features, width), lambda i: (0, i))],
         out_specs=pl.BlockSpec((tokens, width), lambda i: (0, i)),
-        compiler_params=pltpu.CompilerParams(vmem_limit_bytes=60 * MIB),
+        compiler_params=pltpu.CompilerParams(vmem_limit_bytes=44 * MIB),
         cost_estimate=SMALL,
         name="project_query",
     )(x, w)
@@ -132,12 +132,13 @@
 
 def halves(where, pieces):
     rows, tokens = pieces[0].shape
-    shape = (rows // 2, len(pieces) * tokens)
+    n = len(pieces)
+    shape = (rows // 2, n * tokens)
     return pl.pallas_call(
         halves_kernel,
         grid=(1,),
         out_shape=(pltpu.HBM(shape, jnp.bfloat16),) * 2,
-        in_specs=[SMEM] + [whole(piece) for piece in pieces],
+        in_specs=[SMEM] + [VMEM] * n,
         out_specs=(pl.BlockSpec(shape, lambda i: (0, 0)),) * 2,
         compiler_params=pltpu.CompilerParams(vmem_limit_bytes=20 * MIB),
         cost_estimate=SMALL,
@@ -145,7 +146,8 @@
     )(where, *pieces)
 
 
-def attention_kernel(where_ref, order_ref, lens_ref, q_ref, do_ref, kv_ref, dq_ref, dkv_ref, bias_ref, dk_ref, dv_ref):
+def attention_kernel(where_ref, order_ref, lens_ref, q_ref, do_ref, kv_ref, *refs):
+    dq_ref, dkv_ref, bias_ref, dk_ref, dv_ref = refs
     scale = HD ** (-0.5)
     spans = order_ref.shape[1]
     docs = lens_ref.shape[1]
@@ -201,7 +203,6 @@
 def attention(where, order, lens, query, grad, key_value):
     tokens = query.shape[0]
     total = key_value.shape[0]
-    work = HQ * tokens * total
     return pl.pallas_call(
         attention_kernel,
         out_shape=(
@@ -209,34 +210,29 @@
             pltpu.HBM((total, 2 * HD), jnp.bfloat16),
         ),
         grid=(1,),
-        in_specs=[SMEM, SMEM, SMEM] + [whole(v) for v in (query, grad, key_value)],
+        in_specs=[SMEM] * 3 + [VMEM] * 3,
         out_specs=(whole(query), whole(key_value)),
         scratch_shapes=[
             pltpu.VMEM((total, tokens), jnp.float32),
             pltpu.VMEM((total, HD), jnp.float32),
             pltpu.VMEM((total, HD), jnp.float32),
         ],
-        compiler_params=pltpu.CompilerParams(vmem_limit_bytes=24 * MIB),
+        compiler_params=pltpu.CompilerParams(vmem_limit_bytes=30 * MIB),
         cost_estimate=SMALL,
         name="attention",
     )(where, order, lens, query, grad, key_value)
 
 
-def both(x_own, x_other, pieces, at, width):
-    n = len(pieces) // 2
-    near = jnp.concatenate([g[:, pl.ds(at, width)] for g in pieces[:n]], axis=0)
-    far = jnp.concatenate([g[:, pl.ds(at, width)] for g in pieces[n:]], axis=0)
-    return nn(x_own, near) + nn(x_other, far)
-
-
-def term_query_kernel(own_ref, other_ref, *refs):
-    pieces, out_ref, done_ref = refs[:-2], refs[-2], refs[-1]
+def term_query_kernel(*refs):
+    parts, pieces, out_ref, done_ref = refs[:2], refs[2:-2], refs[-2], refs[-1]
     step = pl.program_id(0)
     width = out_ref.shape[2]
     at = pl.multiple_of(step * width, width)
-    part = both(own_ref[...], other_ref[...], pieces, at, width).astype(out_ref.dtype)
+    left = jnp.concatenate([part[...] for part in parts], axis=1)
+    right = jnp.concatenate([g[:, pl.ds(at, width)] for g in pieces], axis=0)
+    part = nn(left, right).astype(out_ref.dtype)
     blocks = out_ref.shape[0]
-    rows = own_ref.shape[0] // (blocks * blocks)
+    rows = left.shape[0] // (blocks * blocks)
 
     @pl.when(step < FIRST // (2 * HD))
     def _():
@@ -250,8 +246,8 @@
         done_ref[...] = part
 
 
-def term_query(own, other, pieces, blocks):
-    half, depth = own.shape
+def term_query(parts, pieces, blocks):
+    half = parts[0].shape[0]
     width = pieces[0].shape[1]
     step = 2 * HD
     first = FIRST // step
@@ -262,7 +258,7 @@
             pltpu.HBM((blocks, half // blocks, FIRST), jnp.bfloat16),
             pltpu.HBM((half, width - FIRST), jnp.bfloat16),
         ),
-        in_specs=[whole(own), whole(other)] + [VMEM] * len(pieces),
+        in_specs=[VMEM] * (len(parts) + len(pieces)),
         out_specs=(
             pl.BlockSpec((blocks, half // blocks, step), lambda j: (0, 0, jnp.minimum(j, first - 1))),
             pl.BlockSpec((half, step), lambda j: (0, jnp.maximum(j - first, 0))),
@@ -270,7 +266,7 @@
         compiler_params=pltpu.CompilerParams(vmem_limit_bytes=20 * MIB),
         cost_estimate=SMALL,
         name="term_query",
-    )(own, other, *pieces)
+    )(*parts, *pieces)
 
 
 def ring_block(where_ref, s):
@@ -278,80 +274,97 @@
     return 2 * lax.rem(place, 2) + place // 2
 
 
-def term_second_kernel(where_ref, own_ref, other_ref, done_ref, *refs):
-    pieces, outs = refs[:-4], refs[-4:]
+def term_second_kernel(where_ref, *refs):
+    parts, done_ref, pieces, outs = refs[:2], refs[2], refs[3:-4], refs[-4:]
     rows = outs[0].shape[0]
     done = done_ref.shape[1]
+    right = jnp.concatenate([g[...] for g in pieces], axis=0)
     for s in range(4):
         at = pl.multiple_of(ring_block(where_ref, s) * rows, rows)
+        left = jnp.concatenate([part[pl.ds(at, rows), :] for part in parts], axis=1)
         outs[s][:, :done] = done_ref[pl.ds(at, rows), :]
-        part = both(own_ref[pl.ds(at, rows), :], other_ref[pl.ds(at, rows), :], pieces, 0, pieces[0].shape[1])
-        outs[s][:, done:] = part.astype(outs[s].dtype)
-
-
-def term_second(where, own, other, done, pieces):
-    half, depth = own.shape
+        outs[s][:, done:] = nn(left, right).astype(outs[s].dtype)
+
+
+def term_second(where, parts, done, pieces):
+    half = parts[0].shape[0]
     width = pieces[0].shape[1]
     out = pltpu.HBM((half // 4, done.shape[1] + width), jnp.bfloat16)
     return pl.pallas_call(
         term_second_kernel,
         grid=(1,),
         out_shape=(out,) * 4,
-        in_specs=[SMEM] + [whole(value) for value in (own, other, done)] + [VMEM] * len(pieces),
+        in_specs=[SMEM] + [VMEM] * (1 + len(parts) + len(pieces)),
         out_specs=(pl.BlockSpec(out.shape, lambda i: (0, 0)),) * 4,
-        compiler_params=pltpu.CompilerParams(vmem_limit_bytes=20 * MIB),
+        compiler_params=pltpu.CompilerParams(vmem_limit_bytes=60 * MIB),
         cost_estimate=SMALL,
         name="term_second",
-    )(where, own, other, done, *pieces)
-
-
-def middle_kernel(along_z, where_ref, *refs):
+    )(where, *parts, done, *pieces)
+
+
+def middle_z_kernel(stack_ref, out_ref):
+    rows = out_ref.shape[1]
+    for i in range(out_ref.shape[0]):
+        parts = [stack_ref[j, i * rows : (i + 1) * rows, :].astype(jnp.float32) for j in range(stack_ref.shape[0])]
+        out_ref[i] = sum(parts).astype(out_ref.dtype)
+
+
+def middle_z(stack):
+    blocks, rows, width = stack.shape
+    out = pltpu.HBM((blocks, rows // blocks, width), jnp.bfloat16)
+    return pl.pallas_call(
+        middle_z_kernel,
+        grid=(1,),
+        out_shape=out,
+        in_specs=[VMEM],
+        out_specs=pl.BlockSpec(out.shape, lambda i: (0, 0, 0)),
+        compiler_params=pltpu.CompilerParams(vmem_limit_bytes=14 * MIB),
+        cost_estimate=SMALL,
+        name="middle_z",
+    )(stack)
+
+
+def middle_y_kernel(where_ref, *refs):
     parts, outs = refs[:-4], refs[-4:]
     rows = outs[0].shape[0]
     for s in range(4):
-        block = ring_block(where_ref, s) if along_z else lax.rem(where_ref[4] + s, 4)
-        at = pl.multiple_of(block * rows, rows)
+        at = pl.multiple_of(lax.rem(where_ref[4] + s, 4) * rows, rows)
         total = sum(part[pl.ds(at, rows), :].astype(jnp.float32) for part in parts)
         outs[s][...] = total.astype(outs[s].dtype)
 
 
-def middle_stacked_kernel(where_ref, stack_ref, *outs):
-    middle_kernel(True, where_ref, *[stack_ref.at[i] for i in range(stack_ref.shape[0])], *outs)
-
-
-def middle(where, parts, along_z):
-    stacked = len(parts) == 1
-    rows, width = parts[0].shape[-2:]
-    return pl.pallas_call(
-        middle_stacked_kernel if stacked else lambda *refs: middle_kernel(along_z, *refs),
+def middle_y(where, parts):
+    rows, width = parts[0].shape
+    return pl.pallas_call(
+        middle_y_kernel,
         grid=(1,),
-        out_shape=(pltpu.HBM((rows // 4, width), jnp.float32),) + (pltpu.HBM((rows // 4, width), jnp.bfloat16),) * 3,
-        in_specs=[SMEM] + [whole(part) for part in parts],
-        out_specs=(pl.BlockSpec((rows // 4, width), lambda i: (0, 0)),) * 4,
+        out_shape=(jax.ShapeDtypeStruct((rows // 4, width), jnp.float32),) + (pltpu.HBM((rows // 4, width), jnp.bfloat16),) * 3,
+        in_specs=[SMEM] + [VMEM] * len(parts),
+        out_specs=(VMEM,) + (pl.BlockSpec((rows // 4, width), lambda i: (0, 0)),) * 3,
         compiler_params=pltpu.CompilerParams(vmem_limit_bytes=14 * MIB),
         cost_estimate=SMALL,
-        name="middle_z" if along_z else "middle_y",
+        name="middle_y",
     )(where, *parts)
 
 
-def final_kernel(*refs):
-    out_ref = refs[-1]
-    out_ref[:, :FIRST] = sum(part[...].astype(jnp.float32) for part in refs[:4])
-    out_ref[:, FIRST:] = sum(part[...].astype(jnp.float32) for part in refs[4:8])
-
-
-def final(parts):
-    rows = parts[0].shape[0]
-    width = FIRST + parts[4].shape[1]
+def final_kernel(stack_ref, *refs):
+    parts, out_ref = refs[:-1], refs[-1]
+    out_ref[:, :FIRST] = sum(stack_ref[i].astype(jnp.float32) for i in range(stack_ref.shape[0]))
+    out_ref[:, FIRST:] = sum(part[...].astype(jnp.float32) for part in parts)
+
+
+def final(stack, parts):
+    rows = stack.shape[1]
+    width = FIRST + parts[0].shape[1]
     return pl.pallas_call(
         final_kernel,
         out_shape=jax.ShapeDtypeStruct((rows, width), jnp.float32),
-        in_specs=[VMEM] * 8,
+        in_specs=[VMEM] * 5,
         out_specs=VMEM,
         compiler_params=pltpu.CompilerParams(vmem_limit_bytes=8 * MIB),
         cost_estimate=SMALL,
         name="final",
-    )(*parts)
+    )(stack, *parts)
 
 
 def shifted(value, s):
@@ -363,12 +376,14 @@
     return lax.ppermute(value, "core", [(0, 1), (1, 0)])
 
 
-def gather_chips(value):
+def gather_chips(value, *others):
     own = [value] + [shifted(value, s) for s in range(1, lax.axis_size("x"))]
-    return own, [swapped(piece) for piece in own]
+    return own, [swapped(after(piece, *others)) for piece in own]
 
 
 def after(value, *others):
+    if not others:
+        return value
     return lax.optimization_barrier((value,) + others)[0]
 
 
@@ -402,25 +417,21 @@
     query = project_query(after(rows, copies), w_qkv)
     d_query, terms = attention(where, span_order, doc_lengths, query, d_out[0], gathered)
     own_q, other_q = gather_chips(d_query)
-    arrived = lax.all_to_all(terms.reshape(seq, tokens, 2 * HD), SEQ, 0, 0, tiled=True)
-    pieces = [after(piece, terms) for piece in pieces]
-    x_own, x_send = halves(where, pieces)
-    x_other = swapped(x_send)
-
-    stacked, done = term_query(x_own, x_other, own_q + other_q, lax.axis_size("y"))
+    arrived = lax.all_to_all(after(terms, other_q[0]).reshape(seq, tokens, 2 * HD), SEQ, 0, 0, tiled=True)
+    x_own, x_send = halves(where, [after(piece, terms) for piece in pieces])
+    columns = [x_own, swapped(x_send)]
+
+    stacked, done = term_query(columns, own_q + other_q, lax.axis_size("y"))
     group_y = lax.all_to_all(stacked, "y", 0, 0, tiled=True)
     owned = jnp.sum(arrived.astype(jnp.float32), axis=0).astype(jnp.bfloat16)
-    own_kv, other_kv = gather_chips(owned)
-    parts = term_second(where, x_own, x_other, done, own_kv + other_kv)
-    d_qkv = jnp.concatenate([d_query, owned], axis=1)
+    own_kv, other_kv = gather_chips(after(owned, done))
+    parts = term_second(where, columns, done, own_kv + other_kv)
+    second_z = lax.all_to_all(middle_z(group_y), DEPTH, 0, 0, tiled=True)
+    d_qkv = after(jnp.concatenate([d_query, owned], axis=1), group_y)
     d_rows = nt(d_qkv, w_qkv).astype(jnp.bfloat16)
     group_z = [parts[0]] + [after(shifted_z(parts[s], s), d_rows) for s in range(1, 4)]
-
-    sums_z = middle(where, [group_y], True)
-    sums_y = middle(where, group_z, False)
-    last = [sums_z[0]] + [shifted_z(sums_z[s], s) for s in range(1, 4)]
-    last += [sums_y[0]] + [shifted_y(sums_y[s], s) for s in range(1, 4)]
-    d_w = final(last)
+    sums = middle_y(where, group_z)
+    d_w = final(second_z, [sums[0]] + [shifted_y(sums[s], s) for s in range(1, 4)])
     return (d_rows[None], d_w)
 
 

time: 136 us -> 120 us (0.88)
  starting transfers between devices: 46.8 us -> 38.3 us
  local copies, waits for them, and re-layouts: 8.23 us -> 4.8 us
  waiting for transfers between devices: 30.1 us -> 27.5 us
    ppermute x9, waiting for transfers between devices: 25 us -> 14 us  [shifted(): return lax.ppermute(value, 'x', [(i, (i + s) % n) for i in range(n)])]
    ppermute x6 -> x3, starting transfers between devices: 9.3 us -> 3.77 us  [shifted_z(): lax.ppermute(value, DEPTH, [(ring_index(i), ring_index((i + s) % 4)) for...]
    all_to_all x1, waiting for transfers between devices: 0.01 us -> 3.46 us  [local(): group_y = lax.all_to_all(stacked, 'y', 0, 0, tiled=True)]
    unnamed x32 -> x40, local copies, waits for them, and re-layouts: 7.62 us -> 4.18 us
    ppermute x3, starting transfers between devices: 6.12 us -> 3.24 us  [shifted_y(): return lax.ppermute(value, 'y', [(i, (i + s) % 4) for i in range(4)])]
    ppermute x9, waiting for transfers between devices: 0.02 us -> 2.76 us  [swapped(): return lax.ppermute(value, 'core', [(0, 1), (1, 0)])]
    all_to_all x1 -> x2, starting transfers between devices: 5.35 us -> 7.57 us  [the longest x1 4.11 us: local(): lax.all_to_all(after(terms, other_q[0]).reshape(seq, tokens, 2 * HD), SEQ...]
    pallas_call x3, Pallas kernels: 11.4 us -> 9.67 us  [the longest x1 7.44 us: project_query(): pl.pallas_call(query_kernel, grid=(HQ // 2,), out_shape=jax.ShapeDtypeStr...]
  transfers between devices with their start and end apart: 30 -> 28, of which waited for: 9 -> 15; matrix products, arithmetic and copies ran while one was open for 10% -> 11% of each run, Pallas kernels for 22% -> 24%
where the time goes in v6:
time: 120 us; the launch traced here: 119 us
  starting transfers between devices  38.3 us (32%)
  Pallas kernels  35.3 us (29%)
  waiting for transfers between devices  27.5 us (23%)
  matrix products  12.5 us (10%)
  local copies, waits for them, and re-layouts  4.8 us (4%)
    ppermute x9, waiting for transfers between devices, shifted(): return lax.ppermute(value, 'x', [(i, (i + s) % n) for i in range(n)])  14 us
    dot_general x1, matrix products, nt(): lax.dot_general(a, b, (((1,), (1,)), ((), ())), preferred_element_type=jn...  12.5 us
    ppermute x9, starting transfers between devices, shifted(): return lax.ppermute(value, 'x', [(i, (i + s) % n) for i in range(n)])  11.6 us
    all_to_all x1, starting transfers between devices, local(): lax.all_to_all(copies, SEQ, 0, 0, tiled=True).reshape(seq * tokens, 2 * HD)  7.78 us
    pallas_call x1, Pallas kernels, project_query(): pl.pallas_call(query_kernel, grid=(HQ // 2,), out_shape=jax.ShapeDtypeStr...  7.44 us
    pallas_call x1, Pallas kernels, attention(): pl.pallas_call(attention_kernel, out_shape=(pltpu.HBM((tokens, HQ * HD),...  6.84 us
    pallas_call x1, Pallas kernels, project_kv(): pl.pallas_call(kv_kernel, grid=(features // depth,), out_shape=pltpu.HBM(...  4.31 us
    unnamed x40, local copies, waits for them, and re-layouts  4.18 us
  transfers between devices with their start and end apart: 28, of which 15 were waited for; matrix products, arithmetic and copies ran while one was open for 11% of the time, Pallas kernels for 24%

profile of v6, /device:TPU:0, one launch (start us, length us, event | category | flops | bytes accessed | tf_op | source)
XLA Modules:
  0.0 119.4 jit_solution(10834341051207034969)
XLA Ops:
  0.6 0.6 stack.23.where_ref
  1.3 3.2 %pack.1 = (bf16[2048,128]{1,0:T(8,128)(2,1)}, bf16[2048,128]{1,0:T(8,128)(2,1)}, bf16[2048,128]{1,0:T(8,128)(2,1)}, bf16[2048,128]{1,0:T(8,128)(2,1)}) custom-call(s32[5]{0:T(128)} %stack.23.where_ref, bf16[128,8192]{1,0:T(8,128)(2,1)} %bitcast.12), custom_call_target="tpu_custom_call" | custom-call | flops 1 | bytes 1 | tf_op jit(solution)/shard_map/pack/pallas_call | solution.py:53
  4.5 1.6 %collective-permute-start.1 = (bf16[2048,128]{1,0:T(8,128)(2,1)}, bf16[2048,128]{1,0:T(8,128)(2,1)}, u32[]{:S(2)}, u32[]{:S(2)}) collective-permute-start(bf16[2048,128]{1,0:T(8,128)(2,1)} %get-tuple-element.39), channel_id=1, source_target_pairs={{0,16},{16,32},{32,48},{48,0},{1,17},{17,33},{33,49},{49,1},{2,18}... | collective-permute-start | bytes 1572872 | tf_op jit(solution)/shard_map/ppermute | solution.py:372
  6.1 2.7 %collective-permute-start.2 = (bf16[2048,128]{1,0:T(8,128)(2,1)}, bf16[2048,128]{1,0:T(8,128)(2,1)}, u32[]{:S(2)}, u32[]{:S(2)}) collective-permute-start(bf16[2048,128]{1,0:T(8,128)(2,1)} %get-tuple-element.41), channel_id=1, source_target_pairs={{0,32},{16,48},{32,0},{48,16},{1,33},{17,49},{33,1},{49,17},{2,34}... | collective-permute-start | bytes 1572872 | tf_op jit(solution)/shard_map/ppermute | solution.py:372
  8.8 1.4 %collective-permute-start.3 = (bf16[2048,128]{1,0:T(8,128)(2,1)}, bf16[2048,128]{1,0:T(8,128)(2,1)}, u32[]{:S(2)}, u32[]{:S(2)}) collective-permute-start(bf16[2048,128]{1,0:T(8,128)(2,1)} %get-tuple-element.43), channel_id=1, source_target_pairs={{0,48},{16,0},{32,16},{48,32},{1,49},{17,1},{33,17},{49,33},{2,50}... | collective-permute-start | bytes 1572872 | tf_op jit(solution)/shard_map/ppermute | solution.py:372
  10.2 4.3 %project_kv.1 = bf16[8,128,256]{2,1,0:T(8,128)(2,1)} custom-call(bf16[128,8192]{1,0:T(8,128)(2,1)} %bitcast.13, bf16[8192,1280]{1,0:T(8,128)(2,1)} %w_ref.3), custom_call_target="tpu_custom_call" | custom-call | flops 1 | bytes 1 | tf_op jit(solution)/shard_map/project_kv/pallas_call | solution.py:88
  14.5 7.8 %all-to-all-start = ((bf16[8,128,256]{2,1,0:T(8,128)(2,1)}), bf16[8,128,256]{2,1,0:T(8,128)(2,1)S(1)}, u32[]{:S(2)}, u32[]{:S(2)}) async-start(bf16[8,128,256]{2,1,0:T(8,128)(2,1)} %project_kv.1), calls=%async_computation | async-start | bytes 1048576 | tf_op jit(solution)/shard_map/all_to_all | solution.py:415
  22.4 7.4 %project_query.1.q_ref = bf16[128,1024]{1,0:T(8,128)(2,1)S(1)} custom-call(bf16[128,8192]{1,0:T(8,128)(2,1)S(1)} %bitcast.14, bf16[8192,1280]{1,0:T(8,128)(2,1)} %w_ref.3), custom_call_target="tpu_custom_call" | custom-call | flops 1 | bytes 1 | tf_op jit(solution)/shard_map/project_query/pallas_call | solution.py:111
  29.8 3.3 %all-to-all-done = bf16[8,128,256]{2,1,0:T(8,128)(2,1)S(1)} async-done(((bf16[8,128,256]{2,1,0:T(8,128)(2,1)}), bf16[8,128,256]{2,1,0:T(8,128)(2,1)S(1)}, u32[]{:S(2)}, u32[]{:S(2)}) %all-to-all-start) | async-done | bytes 524320 | tf_op jit(solution)/shard_map/all_to_all | solution.py:415
  33.1 0.9 copy-done.6
  34.0 6.8 %attention.1 = (bf16[128,1024]{1,0:T(8,128)(2,1)}, bf16[1024,256]{1,0:T(8,128)(2,1)}) custom-call(s32[5]{0:T(128)S(1)} %copy-done.8, s32[1,16]{1,0:T(1,128)S(1)} %copy-done.10, s32[1,4]{1,0:T(1,128)S(1)} %copy-done.11, bf16[128,1024]{1,0:T(8,128)(2,1)S(1)} %project_query.1.q_ref, bf16[128,1024]{1,0:T(8,128)(2,1)S(1)} %bitcast.16, bf16[1024,256]{1,0:T(8,128)(2,1)S(1)} %bitcast.15), custom_call_target="tpu_custom_call" | custom-call | flops 1 | bytes 1 | tf_op jit(solution)/shard_map/attention/pallas_call | solution.py:206
  40.9 3.0 %halves.1 = (bf16[1024,512]{1,0:T(8,128)(2,1)}, bf16[1024,512]{1,0:T(8,128)(2,1)}) custom-call(s32[5]{0:T(128)S(1)} %copy-done.8, bf16[2048,128]{1,0:T(8,128)(2,1)S(1)} %copy-done.5, bf16[2048,128]{1,0:T(8,128)(2,1)} %collective-permute-done.1.refs_1_, bf16[2048,128]{1,0:T(8,128)(2,1)} %collective-permute-done.2.refs_2_, ...), custom_call_target="tpu_custom_call" | custom-call | flops 1 | bytes 1 | tf_op jit(solution)/shard_map/halves/pallas_call | solution.py:137
  43.9 0.5 collective-permute-start
  44.5 0.3 collective-permute-start.7
  44.7 2.4 %collective-permute-start.6 = (bf16[128,1024]{1,0:T(8,128)(2,1)}, bf16[128,1024]{1,0:T(8,128)(2,1)S(1)}, u32[]{:S(2)}, u32[]{:S(2)}) collective-permute-start(bf16[128,1024]{1,0:T(8,128)(2,1)} %get-tuple-element.35.refs_2_), channel_id=1, source_target_pairs={{0,32},{16,48},{32,0},{48,16},{1,33},{17,49},{33,1},{49,17},{2,34}... | collective-permute-start | bytes 786440 | tf_op jit(solution)/shard_map/ppermute | solution.py:372
  47.2 4.1 %all-to-all-start.1 = ((bf16[8,128,256]{2,1,0:T(8,128)(2,1)}), bf16[8,128,256]{2,1,0:T(8,128)(2,1)S(1)}, u32[]{:S(2)}, u32[]{:S(2)}) async-start(bf16[8,128,256]{2,1,0:T(8,128)(2,1)} %bitcast.18), calls=%async_computation.1 | async-start | bytes 1048576 | tf_op jit(solution)/shard_map/all_to_all | solution.py:420
  51.3 2.5 %collective-permute-done.7.refs_5_ = bf16[128,1024]{1,0:T(8,128)(2,1)S(1)} collective-permute-done((bf16[128,1024]{1,0:T(8,128)(2,1)}, bf16[128,1024]{1,0:T(8,128)(2,1)S(1)}, u32[]{:S(2)}, u32[]{:S(2)}) %collective-permute-start.7) | collective-permute-done | bytes 262176 | tf_op jit(solution)/shard_map/ppermute | solution.py:372
  53.8 1.9 %collective-permute-done.6.refs_4_ = bf16[128,1024]{1,0:T(8,128)(2,1)S(1)} collective-permute-done((bf16[128,1024]{1,0:T(8,128)(2,1)}, bf16[128,1024]{1,0:T(8,128)(2,1)S(1)}, u32[]{:S(2)}, u32[]{:S(2)}) %collective-permute-start.6) | collective-permute-done | bytes 262176 | tf_op jit(solution)/shard_map/ppermute | solution.py:372
  55.7 4.3 %collective-permute-done.5.refs_3_ = bf16[128,1024]{1,0:T(8,128)(2,1)S(1)} collective-permute-done((bf16[128,1024]{1,0:T(8,128)(2,1)}, bf16[128,1024]{1,0:T(8,128)(2,1)S(1)}, u32[]{:S(2)}, u32[]{:S(2)}) %collective-permute-start.5) | collective-permute-done | bytes 262176 | tf_op jit(solution)/shard_map/ppermute | solution.py:372
  60.0 1.5 %collective-permute-done.8.refs_7_ = bf16[128,1024]{1,0:T(8,128)(2,1)S(1)} collective-permute-done((bf16[128,1024]{1,0:T(8,128)(2,1)S(1)}, bf16[128,1024]{1,0:T(8,128)(2,1)S(1)}, u32[]{:S(2)}, u32[]{:S(2)}) %collective-permute-start.8) | collective-permute-done | bytes 262176 | tf_op jit(solution)/shard_map/ppermute | solution.py:376
  61.5 1.6 %copy-done.1 = bf16[1024,512]{1,0:T(8,128)(2,1)S(1)} copy-done((bf16[1024,512]{1,0:T(8,128)(2,1)S(1)}, bf16[1024,512]{1,0:T(8,128)(2,1)}, u32[]{:S(2)}) %copy-start.1) | copy-done | bytes 1048600
  63.2 0.9 copy-done.3
  64.1 4.1 %term_query.1 = (bf16[4,256,768]{2,1,0:T(8,128)(2,1)}, bf16[1024,256]{1,0:T(8,128)(2,1)}) custom-call(bf16[1024,512]{1,0:T(8,128)(2,1)S(1)} %copy-done.1, bf16[1024,512]{1,0:T(8,128)(2,1)S(1)} %collective-permute-done.4.refs_1_, bf16[128,1024]{1,0:T(8,128)(2,1)S(1)} %copy-done.3, bf16[128,1024]{1,0:T(8,128)(2,1)S(1)} %collective-permute-done.5.refs_3_, ...), custom_call_target="tpu_custom_call" | custom-call | flops 1 | bytes 1 | tf_op jit(solution)/shard_map/term_query/pallas_call | solution.py:254
  68.2 3.7 %all-to-all-start.2 = ((bf16[4,256,768]{2,1,0:T(8,128)(2,1)}), bf16[4,256,768]{2,1,0:T(8,128)(2,1)S(1)}, u32[]{:S(2)}, u32[]{:S(2)}) async-start(bf16[4,256,768]{2,1,0:T(8,128)(2,1)} %get-tuple-element.47), calls=%async_computation.2 | async-start | bytes 3145728 | tf_op jit(solution)/shard_map/all_to_all | solution.py:425
  72.1 1.6 %collective-permute-start.13 = (bf16[128,256]{1,0:T(8,128)(2,1)S(1)}, bf16[128,256]{1,0:T(8,128)(2,1)S(1)}, u32[]{:S(2)}, u32[]{:S(2)}) collective-permute-start(bf16[128,256]{1,0:T(8,128)(2,1)S(1)} %reduce_sum.12.refs_3_), channel_id=1, source_target_pairs={{0,48},{16,0},{32,16},{48,32},{1,49},{17,1},{33,17},{49,33},{2,50}... | collective-permute-start | bytes 196616 | tf_op jit(solution)/shard_map/ppermute | solution.py:372
  73.7 1.4 %collective-permute-start.12 = (bf16[128,256]{1,0:T(8,128)(2,1)S(1)}, bf16[128,256]{1,0:T(8,128)(2,1)S(1)}, u32[]{:S(2)}, u32[]{:S(2)}) collective-permute-start(bf16[128,256]{1,0:T(8,128)(2,1)S(1)} %reduce_sum.12.refs_3_), channel_id=1, source_target_pairs={{0,32},{16,48},{32,0},{48,16},{1,33},{17,49},{33,1},{49,17},{2,34}... | collective-permute-start | bytes 196616 | tf_op jit(solution)/shard_map/ppermute | solution.py:372
  75.3 1.8 %collective-permute-done.13.refs_6_ = bf16[128,256]{1,0:T(8,128)(2,1)S(1)} collective-permute-done((bf16[128,256]{1,0:T(8,128)(2,1)S(1)}, bf16[128,256]{1,0:T(8,128)(2,1)S(1)}, u32[]{:S(2)}, u32[]{:S(2)}) %collective-permute-start.13) | collective-permute-done | bytes 65568 | tf_op jit(solution)/shard_map/ppermute | solution.py:372
  77.1 2.8 %collective-permute-done.12.refs_5_ = bf16[128,256]{1,0:T(8,128)(2,1)S(1)} collective-permute-done((bf16[128,256]{1,0:T(8,128)(2,1)S(1)}, bf16[128,256]{1,0:T(8,128)(2,1)S(1)}, u32[]{:S(2)}, u32[]{:S(2)}) %collective-permute-start.12) | collective-permute-done | bytes 65568 | tf_op jit(solution)/shard_map/ppermute | solution.py:372
  79.9 0.7 collective-permute-done.11.refs_4_
  80.7 0.5 collective-permute-done.16.refs_9_
  81.2 0.7 collective-permute-done.15.refs_8_
  81.9 0.6 copy-done.19
  82.6 3.3 %term_second.1 = (bf16[256,512]{1,0:T(8,128)(2,1)}, bf16[256,512]{1,0:T(8,128)(2,1)}, bf16[256,512]{1,0:T(8,128)(2,1)}, bf16[256,512]{1,0:T(8,128)(2,1)}) custom-call(s32[5]{0:T(128)} %stack.23.where_ref, bf16[1024,512]{1,0:T(8,128)(2,1)} %get-tuple-element.45.refs_0_, bf16[1024,512]{1,0:T(8,128)(2,1)} %copy-done.2, ...), custom_call_target="tpu_custom_call" | custom-call | flops 1 | bytes 1 | tf_op jit(solution)/shard_map/term_second/pallas_call | solution.py:293
  85.8 1.0 collective-permute-start.18
  86.9 1.4 %collective-permute-start.19 = (bf16[256,512]{1,0:T(8,128)(2,1)}, bf16[256,512]{1,0:T(8,128)(2,1)S(1)}, u32[]{:S(2)}, u32[]{:S(2)}) collective-permute-start(bf16[256,512]{1,0:T(8,128)(2,1)} %get-tuple-element.54), channel_id=1, source_target_pairs={{0,4},{64,68},{4,0},{68,64},{1,5},{65,69},{5,1},{69,65},{2,6},{66,... | collective-permute-start | bytes 786440 | tf_op jit(solution)/shard_map/ppermute | solution.py:395
  88.2 1.4 %collective-permute-start.20 = (bf16[256,512]{1,0:T(8,128)(2,1)}, bf16[256,512]{1,0:T(8,128)(2,1)S(1)}, u32[]{:S(2)}, u32[]{:S(2)}) collective-permute-start(bf16[256,512]{1,0:T(8,128)(2,1)} %get-tuple-element.56), channel_id=1, source_target_pairs={{0,68},{64,0},{4,64},{68,4},{1,69},{65,1},{5,65},{69,5},{2,70},{66... | collective-permute-start | bytes 786440 | tf_op jit(solution)/shard_map/ppermute | solution.py:395
  89.6 3.5 %all-to-all-done.2.stack_ref = bf16[4,256,768]{2,1,0:T(8,128)(2,1)S(1)} async-done(((bf16[4,256,768]{2,1,0:T(8,128)(2,1)}), bf16[4,256,768]{2,1,0:T(8,128)(2,1)S(1)}, u32[]{:S(2)}, u32[]{:S(2)}) %all-to-all-start.2) | async-done | bytes 1572896 | tf_op jit(solution)/shard_map/all_to_all | solution.py:425
  93.1 1.0 middle_z.1
  94.0 3.5 %all-to-all-start.3 = ((bf16[4,64,768]{2,1,0:T(8,128)(2,1)}), bf16[4,64,768]{2,1,0:T(8,128)(2,1)S(1)}, u32[]{:S(2)}, u32[]{:S(2)}) async-start(bf16[4,64,768]{2,1,0:T(8,128)(2,1)} %middle_z.1), calls=%async_computation.3 | async-start | bytes 786432 | tf_op jit(solution)/shard_map/all_to_all | solution.py:429
  97.5 12.5 %convolution_convert_fusion = bf16[128,8192]{1,0:T(8,128)(2,1)} fusion(bf16[128,1280]{1,0:T(8,128)(2,1)S(1)} %pad_maximum_fusion, bf16[8192,1280]{1,0:T(8,128)(2,1)} %w_ref.3), kind=kOutput, calls=%fused_computation | convolution fusion | flops 2685403136 | bytes 23396352 | tf_op jit(solution)/shard_map/dot_general | solution.py:18
  110.1 1.3 %middle_y.1 = (f32[64,512]{1,0:T(8,128)S(1)}, bf16[64,512]{1,0:T(8,128)(2,1)}, bf16[64,512]{1,0:T(8,128)(2,1)}, bf16[64,512]{1,0:T(8,128)(2,1)}) custom-call(s32[5]{0:T(128)S(1)} %copy-done.9, bf16[256,512]{1,0:T(8,128)(2,1)S(1)} %copy-done.7, bf16[256,512]{1,0:T(8,128)(2,1)S(1)} %collective-permute-done.18.refs_1_, ...), custom_call_target="tpu_custom_call" | custom-call | flops 1 | bytes 1 | tf_op jit(solution)/shard_map/middle_y/pallas_call | solution.py:338
  111.3 0.6 collective-permute-start.21
  111.9 2.1 %collective-permute-start.22 = (bf16[64,512]{1,0:T(8,128)(2,1)}, bf16[64,512]{1,0:T(8,128)(2,1)S(1)}, u32[]{:S(2)}, u32[]{:S(2)}) collective-permute-start(bf16[64,512]{1,0:T(8,128)(2,1)} %get-tuple-element.60), channel_id=1, source_target_pairs={{0,2},{1,3},{2,0},{3,1},{4,6},{5,7},{6,4},{7,5},{8,10},{9,11},{10,... | collective-permute-start | bytes 196616 | tf_op jit(solution)/shard_map/ppermute | solution.py:399
  114.0 0.6 collective-permute-start.23
  114.6 2.4 %collective-permute-done.21.refs_1_ = bf16[64,512]{1,0:T(8,128)(2,1)S(1)} collective-permute-done((bf16[64,512]{1,0:T(8,128)(2,1)}, bf16[64,512]{1,0:T(8,128)(2,1)S(1)}, u32[]{:S(2)}, u32[]{:S(2)}) %collective-permute-start.21) | collective-permute-done | bytes 65568 | tf_op jit(solution)/shard_map/ppermute | solution.py:399
  117.0 0.9 collective-permute-done.22.refs_2_
  117.9 0.7 collective-permute-done.23.refs_3_
  118.6 0.8 final.1
  (62 shorter events, 0.5 us)
Async XLA Ops:
  4.5 36.4 %collective-permute-start.1 = (bf16[2048,128]{1,0:T(8,128)(2,1)}, bf16[2048,128]{1,0:T(8,128)(2,1)}, u32[]{:S(2)}, u32[]{:S(2)}) collective-permute-start(bf16[2048,128]{1,0:T(8,128)(2,1)} %get-tuple-element.39), channel_id=1, source_target_pairs={{0,16},{16,32},{32,48},{48,0},{1,17},{17,33},{33,49},{49,1},{2,18}... | collective-permute-start | bytes 1572872 | tf_op jit(solution)/shard_map/ppermute | solution.py:372
  6.1 34.8 %collective-permute-start.2 = (bf16[2048,128]{1,0:T(8,128)(2,1)}, bf16[2048,128]{1,0:T(8,128)(2,1)}, u32[]{:S(2)}, u32[]{:S(2)}) collective-permute-start(bf16[2048,128]{1,0:T(8,128)(2,1)} %get-tuple-element.41), channel_id=1, source_target_pairs={{0,32},{16,48},{32,0},{48,16},{1,33},{17,49},{33,1},{49,17},{2,34}... | collective-permute-start | bytes 1572872 | tf_op jit(solution)/shard_map/ppermute | solution.py:372
  8.8 32.1 %collective-permute-start.3 = (bf16[2048,128]{1,0:T(8,128)(2,1)}, bf16[2048,128]{1,0:T(8,128)(2,1)}, u32[]{:S(2)}, u32[]{:S(2)}) collective-permute-start(bf16[2048,128]{1,0:T(8,128)(2,1)} %get-tuple-element.43), channel_id=1, source_target_pairs={{0,48},{16,0},{32,16},{48,32},{1,49},{17,1},{33,17},{49,33},{2,50}... | collective-permute-start | bytes 1572872 | tf_op jit(solution)/shard_map/ppermute | solution.py:372
  10.2 12.1 %copy-start = (bf16[1,128,8192]{2,1,0:T(8,128)(2,1)S(1)}, bf16[1,128,8192]{2,1,0:T(8,128)(2,1)}, u32[]{:S(2)}) copy-start(bf16[1,128,8192]{2,1,0:T(8,128)(2,1)} %param.5) | copy-start | bytes 6291460
  14.5 18.5 %all-to-all-start = ((bf16[8,128,256]{2,1,0:T(8,128)(2,1)}), bf16[8,128,256]{2,1,0:T(8,128)(2,1)S(1)}, u32[]{:S(2)}, u32[]{:S(2)}) async-start(bf16[8,128,256]{2,1,0:T(8,128)(2,1)} %project_kv.1), calls=%async_computation | async-start | bytes 1048576 | tf_op jit(solution)/shard_map/all_to_all | solution.py:415
  22.3 10.7 %copy-start.8 = (s32[5]{0:T(128)S(1)}, s32[5]{0:T(128)}, u32[]{:S(2)}) copy-start(s32[5]{0:T(128)} %stack.23.where_ref) | copy-start | bytes 64
  22.3 10.7 %copy-start.10 = (s32[1,16]{1,0:T(1,128)S(1)}, s32[1,16]{1,0:T(1,128)}, u32[]{:S(2)}) copy-start(s32[1,16]{1,0:T(1,128)} %order_ref.1) | copy-start | bytes 196
  22.3 10.7 %copy-start.11 = (s32[1,4]{1,0:T(1,128)S(1)}, s32[1,4]{1,0:T(1,128)}, u32[]{:S(2)}) copy-start(s32[1,4]{1,0:T(1,128)} %lens_ref.1) | copy-start | bytes 52
  22.4 18.5 %copy-start.5 = (bf16[2048,128]{1,0:T(8,128)(2,1)S(1)}, bf16[2048,128]{1,0:T(8,128)(2,1)}, u32[]{:S(2)}) copy-start(bf16[2048,128]{1,0:T(8,128)(2,1)} %get-tuple-element.38.refs_0_) | copy-start | bytes 1572868
  33.1 1.0 copy-start.6
  43.9 17.6 %collective-permute-start.4 = (bf16[1024,512]{1,0:T(8,128)(2,1)}, bf16[1024,512]{1,0:T(8,128)(2,1)S(1)}, u32[]{:S(2)}, u32[]{:S(2)}) collective-permute-start(bf16[1024,512]{1,0:T(8,128)(2,1)} %get-tuple-element.46), channel_id=1, source_target_pairs={{0,8},{8,0},{1,9},{9,1},{2,10},{10,2},{3,11},{11,3},{4,12},{12,4},... | collective-permute-start | bytes 3145736 | tf_op jit(solution)/shard_map/ppermute | solution.py:376
  43.9 3.2 %collective-permute-start = (bf16[128,1024]{1,0:T(8,128)(2,1)}, bf16[128,1024]{1,0:T(8,128)(2,1)S(1)}, u32[]{:S(2)}, u32[]{:S(2)}) collective-permute-start(bf16[128,1024]{1,0:T(8,128)(2,1)} %get-tuple-element.35.refs_2_), channel_id=1, source_target_pairs={{0,8},{8,0},{1,9},{9,1},{2,10},{10,2},{3,11},{11,3},{4,12},{12,4},... | collective-permute-start | bytes 786440 | tf_op jit(solution)/shard_map/ppermute | solution.py:376
  44.5 9.4 %collective-permute-start.7 = (bf16[128,1024]{1,0:T(8,128)(2,1)}, bf16[128,1024]{1,0:T(8,128)(2,1)S(1)}, u32[]{:S(2)}, u32[]{:S(2)}) collective-permute-start(bf16[128,1024]{1,0:T(8,128)(2,1)} %get-tuple-element.35.refs_2_), channel_id=1, source_target_pairs={{0,48},{16,0},{32,16},{48,32},{1,49},{17,1},{33,17},{49,33},{2,50}... | collective-permute-start | bytes 786440 | tf_op jit(solution)/shard_map/ppermute | solution.py:372
  44.7 11.0 %collective-permute-start.6 = (bf16[128,1024]{1,0:T(8,128)(2,1)}, bf16[128,1024]{1,0:T(8,128)(2,1)S(1)}, u32[]{:S(2)}, u32[]{:S(2)}) collective-permute-start(bf16[128,1024]{1,0:T(8,128)(2,1)} %get-tuple-element.35.refs_2_), channel_id=1, source_target_pairs={{0,32},{16,48},{32,0},{48,16},{1,33},{17,49},{33,1},{49,17},{2,34}... | collective-permute-start | bytes 786440 | tf_op jit(solution)/shard_map/ppermute | solution.py:372
  47.1 12.9 %collective-permute-start.5 = (bf16[128,1024]{1,0:T(8,128)(2,1)}, bf16[128,1024]{1,0:T(8,128)(2,1)S(1)}, u32[]{:S(2)}, u32[]{:S(2)}) collective-permute-start(bf16[128,1024]{1,0:T(8,128)(2,1)} %get-tuple-element.35.refs_2_), channel_id=1, source_target_pairs={{0,16},{16,32},{32,48},{48,0},{1,17},{17,33},{33,49},{49,1},{2,18}... | collective-permute-start | bytes 786440 | tf_op jit(solution)/shard_map/ppermute | solution.py:372
  47.2 33.4 %copy-start.4 = (bf16[128,1024]{1,0:T(8,128)(2,1)S(1)}, bf16[128,1024]{1,0:T(8,128)(2,1)}, u32[]{:S(2)}) copy-start(bf16[128,1024]{1,0:T(8,128)(2,1)} %get-tuple-element.35.refs_2_) | copy-start | bytes 786436
  47.2 21.1 %all-to-all-start.1 = ((bf16[8,128,256]{2,1,0:T(8,128)(2,1)}), bf16[8,128,256]{2,1,0:T(8,128)(2,1)S(1)}, u32[]{:S(2)}, u32[]{:S(2)}) async-start(bf16[8,128,256]{2,1,0:T(8,128)(2,1)} %bitcast.18), calls=%async_computation.1 | async-start | bytes 1048576 | tf_op jit(solution)/shard_map/all_to_all | solution.py:420
  53.8 6.2 %collective-permute-start.10 = (bf16[128,1024]{1,0:T(8,128)(2,1)S(1)}, bf16[128,1024]{1,0:T(8,128)(2,1)S(1)}, u32[]{:S(2)}, u32[]{:S(2)}) collective-permute-start(bf16[128,1024]{1,0:T(8,128)(2,1)S(1)} %collective-permute-done.7.refs_5_), channel_id=1, source_target_pairs={{0,8},{8,0},{1,9},{9,1},{2,10},{10,2},{3,11},{11,3},{4,12},{12,4},... | collective-permute-start | bytes 786440 | tf_op jit(solution)/shard_map/ppermute | solution.py:376
  55.7 4.3 %collective-permute-start.9 = (bf16[128,1024]{1,0:T(8,128)(2,1)S(1)}, bf16[128,1024]{1,0:T(8,128)(2,1)S(1)}, u32[]{:S(2)}, u32[]{:S(2)}) collective-permute-start(bf16[128,1024]{1,0:T(8,128)(2,1)S(1)} %collective-permute-done.6.refs_4_), channel_id=1, source_target_pairs={{0,8},{8,0},{1,9},{9,1},{2,10},{10,2},{3,11},{11,3},{4,12},{12,4},... | collective-permute-start | bytes 786440 | tf_op jit(solution)/shard_map/ppermute | solution.py:376
  60.0 1.5 %collective-permute-start.8 = (bf16[128,1024]{1,0:T(8,128)(2,1)S(1)}, bf16[128,1024]{1,0:T(8,128)(2,1)S(1)}, u32[]{:S(2)}, u32[]{:S(2)}) collective-permute-start(bf16[128,1024]{1,0:T(8,128)(2,1)S(1)} %collective-permute-done.5.refs_3_), channel_id=1, source_target_pairs={{0,8},{8,0},{1,9},{9,1},{2,10},{10,2},{3,11},{11,3},{4,12},{12,4},... | collective-permute-start | bytes 786440 | tf_op jit(solution)/shard_map/ppermute | solution.py:376
  61.5 19.1 %copy-start.2 = (bf16[1024,512]{1,0:T(8,128)(2,1)}, bf16[1024,512]{1,0:T(8,128)(2,1)S(1)}, u32[]{:S(2)}) copy-start(bf16[1024,512]{1,0:T(8,128)(2,1)S(1)} %collective-permute-done.4.refs_1_) | copy-start | bytes 3145732
  61.5 1.6 %copy-start.1 = (bf16[1024,512]{1,0:T(8,128)(2,1)S(1)}, bf16[1024,512]{1,0:T(8,128)(2,1)}, u32[]{:S(2)}) copy-start(bf16[1024,512]{1,0:T(8,128)(2,1)} %get-tuple-element.45.refs_0_) | copy-start | bytes 3145732
  63.1 0.9 copy-start.3
  68.2 24.8 %all-to-all-start.2 = ((bf16[4,256,768]{2,1,0:T(8,128)(2,1)}), bf16[4,256,768]{2,1,0:T(8,128)(2,1)S(1)}, u32[]{:S(2)}, u32[]{:S(2)}) async-start(bf16[4,256,768]{2,1,0:T(8,128)(2,1)} %get-tuple-element.47), calls=%async_computation.2 | async-start | bytes 3145728 | tf_op jit(solution)/shard_map/all_to_all | solution.py:425
  72.1 9.8 %copy-start.12 = (bf16[128,256]{1,0:T(8,128)(2,1)}, bf16[128,256]{1,0:T(8,128)(2,1)S(1)}, u32[]{:S(2)}) copy-start(bf16[128,256]{1,0:T(8,128)(2,1)S(1)} %reduce_sum.12.refs_3_) | copy-start | bytes 196612
  72.1 5.0 %collective-permute-start.13 = (bf16[128,256]{1,0:T(8,128)(2,1)S(1)}, bf16[128,256]{1,0:T(8,128)(2,1)S(1)}, u32[]{:S(2)}, u32[]{:S(2)}) collective-permute-start(bf16[128,256]{1,0:T(8,128)(2,1)S(1)} %reduce_sum.12.refs_3_), channel_id=1, source_target_pairs={{0,48},{16,0},{32,16},{48,32},{1,49},{17,1},{33,17},{49,33},{2,50}... | collective-permute-start | bytes 196616 | tf_op jit(solution)/shard_map/ppermute | solution.py:372
  73.7 6.2 %collective-permute-start.12 = (bf16[128,256]{1,0:T(8,128)(2,1)S(1)}, bf16[128,256]{1,0:T(8,128)(2,1)S(1)}, u32[]{:S(2)}, u32[]{:S(2)}) collective-permute-start(bf16[128,256]{1,0:T(8,128)(2,1)S(1)} %reduce_sum.12.refs_3_), channel_id=1, source_target_pairs={{0,32},{16,48},{32,0},{48,16},{1,33},{17,49},{33,1},{49,17},{2,34}... | collective-permute-start | bytes 196616 | tf_op jit(solution)/shard_map/ppermute | solution.py:372
  75.1 5.5 %collective-permute-start.11 = (bf16[128,256]{1,0:T(8,128)(2,1)S(1)}, bf16[128,256]{1,0:T(8,128)(2,1)S(1)}, u32[]{:S(2)}, u32[]{:S(2)}) collective-permute-start(bf16[128,256]{1,0:T(8,128)(2,1)S(1)} %reduce_sum.12.refs_3_), channel_id=1, source_target_pairs={{0,16},{16,32},{32,48},{48,0},{1,17},{17,33},{33,49},{49,1},{2,18}... | collective-permute-start | bytes 196616 | tf_op jit(solution)/shard_map/ppermute | solution.py:372
  75.3 5.4 %collective-permute-start.14 = (bf16[128,256]{1,0:T(8,128)(2,1)S(1)}, bf16[128,256]{1,0:T(8,128)(2,1)S(1)}, u32[]{:S(2)}, u32[]{:S(2)}) collective-permute-start(bf16[128,256]{1,0:T(8,128)(2,1)S(1)} %reduce_sum.12.refs_3_), channel_id=1, source_target_pairs={{0,8},{8,0},{1,9},{9,1},{2,10},{10,2},{3,11},{11,3},{4,12},{12,4},... | collective-permute-start | bytes 196616 | tf_op jit(solution)/shard_map/ppermute | solution.py:376
  77.1 4.8 %copy-start.13 = (bf16[128,256]{1,0:T(8,128)(2,1)}, bf16[128,256]{1,0:T(8,128)(2,1)S(1)}, u32[]{:S(2)}) copy-start(bf16[128,256]{1,0:T(8,128)(2,1)S(1)} %collective-permute-done.13.refs_6_) | copy-start | bytes 196612
  77.1 3.6 %collective-permute-start.17 = (bf16[128,256]{1,0:T(8,128)(2,1)S(1)}, bf16[128,256]{1,0:T(8,128)(2,1)S(1)}, u32[]{:S(2)}, u32[]{:S(2)}) collective-permute-start(bf16[128,256]{1,0:T(8,128)(2,1)S(1)} %collective-permute-done.13.refs_6_), channel_id=1, source_target_pairs={{0,8},{8,0},{1,9},{9,1},{2,10},{10,2},{3,11},{11,3},{4,12},{12,4},... | collective-permute-start | bytes 196616 | tf_op jit(solution)/shard_map/ppermute | solution.py:376
  79.9 2.0 %copy-start.14 = (bf16[128,256]{1,0:T(8,128)(2,1)}, bf16[128,256]{1,0:T(8,128)(2,1)S(1)}, u32[]{:S(2)}) copy-start(bf16[128,256]{1,0:T(8,128)(2,1)S(1)} %collective-permute-done.12.refs_5_) | copy-start | bytes 196612
  79.9 1.3 %collective-permute-start.16 = (bf16[128,256]{1,0:T(8,128)(2,1)S(1)}, bf16[128,256]{1,0:T(8,128)(2,1)S(1)}, u32[]{:S(2)}, u32[]{:S(2)}) collective-permute-start(bf16[128,256]{1,0:T(8,128)(2,1)S(1)} %collective-permute-done.12.refs_5_), channel_id=1, source_target_pairs={{0,8},{8,0},{1,9},{9,1},{2,10},{10,2},{3,11},{11,3},{4,12},{12,4},... | collective-permute-start | bytes 196616 | tf_op jit(solution)/shard_map/ppermute | solution.py:376
  80.6 1.3 %copy-start.15 = (bf16[128,256]{1,0:T(8,128)(2,1)}, bf16[128,256]{1,0:T(8,128)(2,1)S(1)}, u32[]{:S(2)}) copy-start(bf16[128,256]{1,0:T(8,128)(2,1)S(1)} %collective-permute-done.11.refs_4_) | copy-start | bytes 196612
  80.6 1.3 %collective-permute-start.15 = (bf16[128,256]{1,0:T(8,128)(2,1)S(1)}, bf16[128,256]{1,0:T(8,128)(2,1)S(1)}, u32[]{:S(2)}, u32[]{:S(2)}) collective-permute-start(bf16[128,256]{1,0:T(8,128)(2,1)S(1)} %collective-permute-done.11.refs_4_), channel_id=1, source_target_pairs={{0,8},{8,0},{1,9},{9,1},{2,10},{10,2},{3,11},{11,3},{4,12},{12,4},... | collective-permute-start | bytes 196616 | tf_op jit(solution)/shard_map/ppermute | solution.py:376
  80.7 1.2 %copy-start.16 = (bf16[128,256]{1,0:T(8,128)(2,1)}, bf16[128,256]{1,0:T(8,128)(2,1)S(1)}, u32[]{:S(2)}) copy-start(bf16[128,256]{1,0:T(8,128)(2,1)S(1)} %collective-permute-done.14.refs_7_) | copy-start | bytes 196612
  80.7 1.2 %copy-start.17 = (bf16[128,256]{1,0:T(8,128)(2,1)}, bf16[128,256]{1,0:T(8,128)(2,1)S(1)}, u32[]{:S(2)}) copy-start(bf16[128,256]{1,0:T(8,128)(2,1)S(1)} %collective-permute-done.17.refs_10_) | copy-start | bytes 196612
  81.2 0.7 copy-start.18
  81.9 0.6 copy-start.19
  85.8 24.2 %collective-permute-start.18 = (bf16[256,512]{1,0:T(8,128)(2,1)}, bf16[256,512]{1,0:T(8,128)(2,1)S(1)}, u32[]{:S(2)}, u32[]{:S(2)}) collective-permute-start(bf16[256,512]{1,0:T(8,128)(2,1)} %get-tuple-element.52), channel_id=1, source_target_pairs={{0,64},{64,4},{4,68},{68,0},{1,65},{65,5},{5,69},{69,1},{2,66},{66... | collective-permute-start | bytes 786440 | tf_op jit(solution)/shard_map/ppermute | solution.py:395
  86.9 23.2 %collective-permute-start.19 = (bf16[256,512]{1,0:T(8,128)(2,1)}, bf16[256,512]{1,0:T(8,128)(2,1)S(1)}, u32[]{:S(2)}, u32[]{:S(2)}) collective-permute-start(bf16[256,512]{1,0:T(8,128)(2,1)} %get-tuple-element.54), channel_id=1, source_target_pairs={{0,4},{64,68},{4,0},{68,64},{1,5},{65,69},{5,1},{69,65},{2,6},{66,... | collective-permute-start | bytes 786440 | tf_op jit(solution)/shard_map/ppermute | solution.py:395
  88.2 21.8 %collective-permute-start.20 = (bf16[256,512]{1,0:T(8,128)(2,1)}, bf16[256,512]{1,0:T(8,128)(2,1)S(1)}, u32[]{:S(2)}, u32[]{:S(2)}) collective-permute-start(bf16[256,512]{1,0:T(8,128)(2,1)} %get-tuple-element.56), channel_id=1, source_target_pairs={{0,68},{64,0},{4,64},{68,4},{1,69},{65,1},{5,65},{69,5},{2,70},{66... | collective-permute-start | bytes 786440 | tf_op jit(solution)/shard_map/ppermute | solution.py:395
  94.0 24.6 %all-to-all-start.3 = ((bf16[4,64,768]{2,1,0:T(8,128)(2,1)}), bf16[4,64,768]{2,1,0:T(8,128)(2,1)S(1)}, u32[]{:S(2)}, u32[]{:S(2)}) async-start(bf16[4,64,768]{2,1,0:T(8,128)(2,1)} %middle_z.1), calls=%async_computation.3 | async-start | bytes 786432 | tf_op jit(solution)/shard_map/all_to_all | solution.py:429
  97.5 12.5 %copy-start.7 = (bf16[256,512]{1,0:T(8,128)(2,1)S(1)}, bf16[256,512]{1,0:T(8,128)(2,1)}, u32[]{:S(2)}) copy-start(bf16[256,512]{1,0:T(8,128)(2,1)} %get-tuple-element.51.refs_0_) | copy-start | bytes 786436
  97.5 12.5 %copy-start.9 = (s32[5]{0:T(128)S(1)}, s32[5]{0:T(128)}, u32[]{:S(2)}) copy-start(s32[5]{0:T(128)} %stack.23.where_ref) | copy-start | bytes 64
  111.3 5.7 %collective-permute-start.21 = (bf16[64,512]{1,0:T(8,128)(2,1)}, bf16[64,512]{1,0:T(8,128)(2,1)S(1)}, u32[]{:S(2)}, u32[]{:S(2)}) collective-permute-start(bf16[64,512]{1,0:T(8,128)(2,1)} %get-tuple-element.59), channel_id=1, source_target_pairs={{0,1},{1,2},{2,3},{3,0},{4,5},{5,6},{6,7},{7,4},{8,9},{9,10},{10,1... | collective-permute-start | bytes 196616 | tf_op jit(solution)/shard_map/ppermute | solution.py:399
  111.9 6.0 %collective-permute-start.22 = (bf16[64,512]{1,0:T(8,128)(2,1)}, bf16[64,512]{1,0:T(8,128)(2,1)S(1)}, u32[]{:S(2)}, u32[]{:S(2)}) collective-permute-start(bf16[64,512]{1,0:T(8,128)(2,1)} %get-tuple-element.60), channel_id=1, source_target_pairs={{0,2},{1,3},{2,0},{3,1},{4,6},{5,7},{6,4},{7,5},{8,10},{9,11},{10,... | collective-permute-start | bytes 196616 | tf_op jit(solution)/shard_map/ppermute | solution.py:399
  114.0 4.6 %collective-permute-start.23 = (bf16[64,512]{1,0:T(8,128)(2,1)}, bf16[64,512]{1,0:T(8,128)(2,1)S(1)}, u32[]{:S(2)}, u32[]{:S(2)}) collective-permute-start(bf16[64,512]{1,0:T(8,128)(2,1)} %get-tuple-element.61), channel_id=1, source_target_pairs={{0,3},{1,0},{2,1},{3,2},{4,7},{5,4},{6,5},{7,6},{8,11},{9,8},{10,9... | collective-permute-start | bytes 196616 | tf_op jit(solution)/shard_map/ppermute | solution.py:399

commit v7 on v6

--- a/solution.py
+++ b/solution.py
@@ -9,7 +9,6 @@
 HQ = 8
 SPAN = 64
 LOG2E = 1.4426950408889634
-FIRST = 768
 SEQ = ("zhi", "y")
 DEPTH = ("zlo", "zhi")
 
@@ -36,69 +35,68 @@
     return pl.BlockSpec(value.shape, lambda i: (0,) * value.ndim)
 
 
-def pack_kernel(where_ref, x_ref, *out_refs):
-    chips = len(out_refs)
-    step = pl.program_id(0)
+def first_kernel(where_ref, x_hbm, w_hbm, kv_hbm, *refs):
+    chips = len(refs) - 7
+    out_hbm = refs[:chips]
+    x_ref, w_ref, piece_ref, kv_ref, in_sem, piece_sem, kv_sem = refs[chips:]
     features = x_ref.shape[1]
     width = features // (4 * chips)
+    chunks = in_sem.shape[0] - 1
+    depth = features // chunks
+    load_x = pltpu.make_async_copy(x_hbm, x_ref, in_sem.at[chunks])
+    load_x.start()
+    loads = []
+    for i in range(chunks):
+        rows = pl.ds(i * depth, depth)
+        loads.append(pltpu.make_async_copy(w_hbm.at[rows, pl.ds(HQ * HD, 2 * HD)], w_ref.at[rows, :], in_sem.at[i]))
+        loads[i].start()
+    load_x.wait()
+    stores = []
     for s in range(chips):
         chip = lax.rem(where_ref[0] + s, chips)
-        for z in range(2):
-            at = pl.multiple_of(z * (features // 2) + chip * 2 * width + step * width, width)
-            out_refs[s][z * width : (z + 1) * width, :] = x_ref[:, pl.ds(at, width)].T
-
-
-def pack(where, x, chips):
-    tokens, features = x.shape
-    return pl.pallas_call(
-        pack_kernel,
-        grid=(2,),
-        out_shape=(pltpu.HBM((features // chips, tokens), x.dtype),) * chips,
-        in_specs=[SMEM, whole(x)],
-        out_specs=(pl.BlockSpec((features // chips // 2, tokens), lambda i: (i, 0)),) * chips,
-        compiler_params=pltpu.CompilerParams(vmem_limit_bytes=60 * MIB),
-        cost_estimate=SMALL,
-        name="pack",
-    )(where, x)
-
-
-def kv_kernel(x_ref, w_ref, kv_ref, acc_ref):
-    step = pl.program_id(0)
-    part = nn(x_ref[...], w_ref[...])
-
-    @pl.when(step == 0)
-    def _():
-        acc_ref[...] = part
-
-    @pl.when(step > 0)
-    def _():
-        acc_ref[...] += part
-
-    @pl.when(step == pl.num_programs(0) - 1)
-    def _():
-        low = acc_ref[...].astype(jnp.bfloat16)
-        for i in range(kv_ref.shape[0]):
-            kv_ref[i] = low
-
-
-def project_kv(x, w, copies):
+        for c in range(2):
+            for z in range(2):
+                at = pl.multiple_of(z * (features // 2) + chip * 2 * width + c * width, width)
+                piece_ref[s, (2 * c + z) * width : (2 * c + z + 1) * width, :] = x_ref[:, pl.ds(at, width)].T
+        stores.append(pltpu.make_async_copy(piece_ref.at[s], out_hbm[s], piece_sem.at[s]))
+        stores[s].start()
+    total = None
+    for i in range(chunks):
+        loads[i].wait()
+        part = nn(x_ref[:, i * depth : (i + 1) * depth], w_ref[i * depth : (i + 1) * depth, :])
+        total = part if total is None else total + part
+    kv_ref[...] = total.astype(jnp.bfloat16)
+    copies = kv_hbm.shape[0]
+    for i in range(copies):
+        stores.append(pltpu.make_async_copy(kv_ref, kv_hbm.at[i], kv_sem.at[i]))
+        stores[-1].start()
+    for store in stores:
+        store.wait()
+
+
+def first(where, x, w, copies, chips):
     tokens, features = x.shape
     width = 2 * HD
-    depth = features // 2
-    return pl.pallas_call(
-        kv_kernel,
-        grid=(features // depth,),
-        out_shape=pltpu.HBM((copies, tokens, width), jnp.bfloat16),
-        in_specs=[
-            pl.BlockSpec((tokens, depth), lambda i: (0, i)),
-            pl.BlockSpec((depth, width), lambda i: (i, HQ // 2)),
+    anywhere = pl.BlockSpec(memory_space=pltpu.HBM)
+    return pl.pallas_call(
+        first_kernel,
+        out_shape=(pltpu.HBM((copies, tokens, width), jnp.bfloat16),)
+        + (pltpu.HBM((features // chips, tokens), x.dtype),) * chips,
+        in_specs=[SMEM, anywhere, anywhere],
+        out_specs=(anywhere,) * (chips + 1),
+        scratch_shapes=[
+            pltpu.VMEM((tokens, features), x.dtype),
+            pltpu.VMEM((features, width), x.dtype),
+            pltpu.VMEM((chips, features // chips, tokens), x.dtype),
+            pltpu.VMEM((tokens, width), jnp.bfloat16),
+            pltpu.SemaphoreType.DMA((5,)),
+            pltpu.SemaphoreType.DMA((chips,)),
+            pltpu.SemaphoreType.DMA((copies,)),
         ],
-        out_specs=pl.BlockSpec((copies, tokens, width), lambda i: (0, 0, 0)),
-        scratch_shapes=[pltpu.VMEM((tokens, width), jnp.float32)],
         compiler_params=pltpu.CompilerParams(vmem_limit_bytes=60 * MIB),
         cost_estimate=SMALL,
-        name="project_kv",
-    )(x, w)
+        name="first",
+    )(where, x, w)
 
 
 def query_kernel(x_ref, w_ref, out_ref):
@@ -140,7 +138,7 @@
         out_shape=(pltpu.HBM(shape, jnp.bfloat16),) * 2,
         in_specs=[SMEM] + [VMEM] * n,
         out_specs=(pl.BlockSpec(shape, lambda i: (0, 0)),) * 2,
-        compiler_params=pltpu.CompilerParams(vmem_limit_bytes=20 * MIB),
+        compiler_params=pltpu.CompilerParams(vmem_limit_bytes=60 * MIB),
         cost_estimate=SMALL,
         name="halves",
     )(where, *pieces)
@@ -224,7 +222,7 @@
 
 
 def term_query_kernel(*refs):
-    parts, pieces, out_ref, done_ref = refs[:2], refs[2:-2], refs[-2], refs[-1]
+    parts, pieces, out_ref = refs[:2], refs[2:-1], refs[-1]
     step = pl.program_id(0)
     width = out_ref.shape[2]
     at = pl.multiple_of(step * width, width)
@@ -233,36 +231,22 @@
     part = nn(left, right).astype(out_ref.dtype)
     blocks = out_ref.shape[0]
     rows = left.shape[0] // (blocks * blocks)
-
-    @pl.when(step < FIRST // (2 * HD))
-    def _():
-        for i in range(blocks):
-            for y in range(blocks):
-                here = (i * blocks + y) * rows
-                out_ref[y, i * rows : (i + 1) * rows, :] = part[here : here + rows]
-
-    @pl.when(step >= FIRST // (2 * HD))
-    def _():
-        done_ref[...] = part
+    for i in range(blocks):
+        for y in range(blocks):
+            here = (i * blocks + y) * rows
+            out_ref[y, i * rows : (i + 1) * rows, :] = part[here : here + rows]
 
 
 def term_query(parts, pieces, blocks):
     half = parts[0].shape[0]
     width = pieces[0].shape[1]
     step = 2 * HD
-    first = FIRST // step
     return pl.pallas_call(
         term_query_kernel,
         grid=(width // step,),
-        out_shape=(
-            pltpu.HBM((blocks, half // blocks, FIRST), jnp.bfloat16),
-            pltpu.HBM((half, width - FIRST), jnp.bfloat16),
-        ),
+        out_shape=pltpu.HBM((blocks, half // blocks, width), jnp.bfloat16),
         in_specs=[VMEM] * (len(parts) + len(pieces)),
-        out_specs=(
-            pl.BlockSpec((blocks, half // blocks, step), lambda j: (0, 0, jnp.minimum(j, first - 1))),
-            pl.BlockSpec((half, step), lambda j: (0, jnp.maximum(j - first, 0))),
-        ),
+        out_specs=pl.BlockSpec((blocks, half // blocks, step), lambda j: (0, 0, j)),
         compiler_params=pltpu.CompilerParams(vmem_limit_bytes=20 * MIB),
         cost_estimate=SMALL,
         name="term_query",
@@ -275,31 +259,29 @@
 
 
 def term_second_kernel(where_ref, *refs):
-    parts, done_ref, pieces, outs = refs[:2], refs[2], refs[3:-4], refs[-4:]
+    parts, pieces, outs = refs[:2], refs[2:-4], refs[-4:]
     rows = outs[0].shape[0]
-    done = done_ref.shape[1]
     right = jnp.concatenate([g[...] for g in pieces], axis=0)
     for s in range(4):
         at = pl.multiple_of(ring_block(where_ref, s) * rows, rows)
         left = jnp.concatenate([part[pl.ds(at, rows), :] for part in parts], axis=1)
-        outs[s][:, :done] = done_ref[pl.ds(at, rows), :]
-        outs[s][:, done:] = nn(left, right).astype(outs[s].dtype)
-
-
-def term_second(where, parts, done, pieces):
+        outs[s][...] = nn(left, right).astype(outs[s].dtype)
+
+
+def term_second(where, parts, pieces):
     half = parts[0].shape[0]
     width = pieces[0].shape[1]
-    out = pltpu.HBM((half // 4, done.shape[1] + width), jnp.bfloat16)
+    out = pltpu.HBM((half // 4, width), jnp.bfloat16)
     return pl.pallas_call(
         term_second_kernel,
         grid=(1,),
         out_shape=(out,) * 4,
-        in_specs=[SMEM] + [VMEM] * (1 + len(parts) + len(pieces)),
+        in_specs=[SMEM] + [VMEM] * (len(parts) + len(pieces)),
         out_specs=(pl.BlockSpec(out.shape, lambda i: (0, 0)),) * 4,
         compiler_params=pltpu.CompilerParams(vmem_limit_bytes=60 * MIB),
         cost_estimate=SMALL,
         name="term_second",
-    )(where, *parts, done, *pieces)
+    )(where, *parts, *pieces)
 
 
 def middle_z_kernel(stack_ref, out_ref):
@@ -349,13 +331,14 @@
 
 def final_kernel(stack_ref, *refs):
     parts, out_ref = refs[:-1], refs[-1]
-    out_ref[:, :FIRST] = sum(stack_ref[i].astype(jnp.float32) for i in range(stack_ref.shape[0]))
-    out_ref[:, FIRST:] = sum(part[...].astype(jnp.float32) for part in parts)
+    first = stack_ref.shape[2]
+    out_ref[:, :first] = sum(stack_ref[i].astype(jnp.float32) for i in range(stack_ref.shape[0]))
+    out_ref[:, first:] = sum(part[...].astype(jnp.float32) for part in parts)
 
 
 def final(stack, parts):
     rows = stack.shape[1]
-    width = FIRST + parts[0].shape[1]
+    width = stack.shape[2] + parts[0].shape[1]
     return pl.pallas_call(
         final_kernel,
         out_shape=jax.ShapeDtypeStruct((rows, width), jnp.float32),
@@ -409,9 +392,7 @@
         [lax.axis_index("x"), lax.axis_index("core"), at_zhi * lax.axis_size("y") + at_y, at_zhi * 2 + at_zlo, at_y]
     ).astype(jnp.int32)
 
-    packed = pack(where, rows, chips)
-    rows = after(rows, packed[0])
-    copies = project_kv(rows, w_qkv, seq)
+    copies, *packed = first(where, rows, w_qkv, seq, chips)
     gathered = lax.all_to_all(copies, SEQ, 0, 0, tiled=True).reshape(seq * tokens, 2 * HD)
     pieces = [packed[0]] + [shifted(packed[s], s) for s in range(1, chips)]
     query = project_query(after(rows, copies), w_qkv)
@@ -421,16 +402,16 @@
     x_own, x_send = halves(where, [after(piece, terms) for piece in pieces])
     columns = [x_own, swapped(x_send)]
 
-    stacked, done = term_query(columns, own_q + other_q, lax.axis_size("y"))
+    stacked = term_query(columns, own_q + other_q, lax.axis_size("y"))
     group_y = lax.all_to_all(stacked, "y", 0, 0, tiled=True)
     owned = jnp.sum(arrived.astype(jnp.float32), axis=0).astype(jnp.bfloat16)
-    own_kv, other_kv = gather_chips(after(owned, done))
-    parts = term_second(where, columns, done, own_kv + other_kv)
-    second_z = lax.all_to_all(middle_z(group_y), DEPTH, 0, 0, tiled=True)
-    d_qkv = after(jnp.concatenate([d_query, owned], axis=1), group_y)
+    own_kv, other_kv = gather_chips(after(owned, stacked))
+    parts = term_second(where, columns, own_kv + other_kv)
+    d_qkv = after(jnp.concatenate([d_query, owned], axis=1), parts[0])
     d_rows = nt(d_qkv, w_qkv).astype(jnp.bfloat16)
     group_z = [parts[0]] + [after(shifted_z(parts[s], s), d_rows) for s in range(1, 4)]
     sums = middle_y(where, group_z)
+    second_z = lax.all_to_all(middle_z(after(group_y, sums[1])), DEPTH, 0, 0, tiled=True)
     d_w = final(second_z, [sums[0]] + [shifted_y(sums[s], s) for s in range(1, 4)])
     return (d_rows[None], d_w)
 

time: 120 us -> 116 us (0.967)
  waiting for transfers between devices: 27.5 us -> 22 us
  starting transfers between devices: 38.3 us -> 41.7 us
  Pallas kernels: 35.3 us -> 33 us
    ppermute x9, waiting for transfers between devices: 14 us -> 8.72 us  [shifted(): return lax.ppermute(value, 'x', [(i, (i + s) % n) for i in range(n)])]
    all_to_all x1, waiting for transfers between devices: 0.01 us -> 3.54 us  [local(): lax.all_to_all(after(terms, other_q[0]).reshape(seq, tokens, 2 * HD), SEQ...]
    all_to_all x1, waiting for transfers between devices: 3.46 us -> 0.54 us  [local(): group_y = lax.all_to_all(stacked, 'y', 0, 0, tiled=True)]
    pallas_call x3 -> x2, Pallas kernels: 11.7 us -> 9.4 us  [the longest x1 5.54 us: first(): pl.pallas_call(first_kernel, out_shape=(pltpu.HBM((copies, tokens, width)...]
    all_to_all x1, starting transfers between devices: 4.11 us -> 5.46 us  [local(): lax.all_to_all(after(terms, other_q[0]).reshape(seq, tokens, 2 * HD), SEQ...]
    ppermute x9, waiting for transfers between devices: 2.76 us -> 1.47 us  [swapped(): return lax.ppermute(value, 'core', [(0, 1), (1, 0)])]
    unnamed x40 -> x34, local copies, waits for them, and re-layouts: 4.18 us -> 3.22 us
  transfers between devices with their start and end apart: 28 -> 28, of which waited for: 15 -> 14; matrix products, arithmetic and copies ran while one was open for 11% -> 11% of each run, Pallas kernels for 24% -> 16%
where the time goes in v7:
time: 116 us; the launch traced here: 114 us
  starting transfers between devices  41.7 us (36%)
  Pallas kernels  33 us (28%)
  waiting for transfers between devices  22 us (19%)
  matrix products  12.8 us (11%)
  local copies, waits for them, and re-layouts  3.9 us (3%)
    dot_general x1, matrix products, nt(): lax.dot_general(a, b, (((1,), (1,)), ((), ())), preferred_element_type=jn...  12.8 us
    ppermute x9, starting transfers between devices, shifted(): return lax.ppermute(value, 'x', [(i, (i + s) % n) for i in range(n)])  12.2 us
    ppermute x9, waiting for transfers between devices, shifted(): return lax.ppermute(value, 'x', [(i, (i + s) % n) for i in range(n)])  8.72 us
    all_to_all x1, starting transfers between devices, local(): lax.all_to_all(copies, SEQ, 0, 0, tiled=True).reshape(seq * tokens, 2 * HD)  7.79 us
    pallas_call x1, Pallas kernels, project_query(): pl.pallas_call(query_kernel, grid=(HQ // 2,), out_shape=jax.ShapeDtypeStr...  7.42 us
    pallas_call x1, Pallas kernels, attention(): pl.pallas_call(attention_kernel, out_shape=(pltpu.HBM((tokens, HQ * HD),...  6.86 us
    pallas_call x1, Pallas kernels, first(): pl.pallas_call(first_kernel, out_shape=(pltpu.HBM((copies, tokens, width)...  5.54 us
    all_to_all x1, starting transfers between devices, local(): lax.all_to_all(after(terms, other_q[0]).reshape(seq, tokens, 2 * HD), SEQ...  5.46 us
  transfers between devices with their start and end apart: 28, of which 14 were waited for; matrix products, arithmetic and copies ran while one was open for 11% of the time, Pallas kernels for 16%

profile of v7, /device:TPU:0, one launch (start us, length us, event | category | flops | bytes accessed | tf_op | source)
XLA Modules:
  0.0 114.4 jit_solution(9912923777817791628)
XLA Ops:
  0.6 0.7 stack.23.where_ref
  1.3 5.5 %first.1 = (bf16[8,128,256]{2,1,0:T(8,128)(2,1)}, bf16[2048,128]{1,0:T(8,128)(2,1)}, bf16[2048,128]{1,0:T(8,128)(2,1)}, bf16[2048,128]{1,0:T(8,128)(2,1)}, bf16[2048,128]{1,0:T(8,128)(2,1)}) custom-call(s32[5]{0:T(128)} %stack.23.where_ref, bf16[128,8192]{1,0:T(8,128)(2,1)} %bitcast.12, bf16[8192,1280]{1,0:T(8,128)(2,1)} %w_ref.1), custom_call_target="tpu_custom_call" | custom-call | flops 1 | bytes 1 | tf_op jit(solution)/shard_map/first/pallas_call | solution.py:81
  6.9 1.6 %collective-permute-start.1 = (bf16[2048,128]{1,0:T(8,128)(2,1)}, bf16[2048,128]{1,0:T(8,128)(2,1)}, u32[]{:S(2)}, u32[]{:S(2)}) collective-permute-start(bf16[2048,128]{1,0:T(8,128)(2,1)} %get-tuple-element.38), channel_id=1, source_target_pairs={{0,16},{16,32},{32,48},{48,0},{1,17},{17,33},{33,49},{49,1},{2,18}... | collective-permute-start | bytes 1572872 | tf_op jit(solution)/shard_map/ppermute | solution.py:355
  8.5 2.7 %collective-permute-start.2 = (bf16[2048,128]{1,0:T(8,128)(2,1)}, bf16[2048,128]{1,0:T(8,128)(2,1)}, u32[]{:S(2)}, u32[]{:S(2)}) collective-permute-start(bf16[2048,128]{1,0:T(8,128)(2,1)} %get-tuple-element.40), channel_id=1, source_target_pairs={{0,32},{16,48},{32,0},{48,16},{1,33},{17,49},{33,1},{49,17},{2,34}... | collective-permute-start | bytes 1572872 | tf_op jit(solution)/shard_map/ppermute | solution.py:355
  11.2 1.4 %collective-permute-start.3 = (bf16[2048,128]{1,0:T(8,128)(2,1)}, bf16[2048,128]{1,0:T(8,128)(2,1)}, u32[]{:S(2)}, u32[]{:S(2)}) collective-permute-start(bf16[2048,128]{1,0:T(8,128)(2,1)} %get-tuple-element.42), channel_id=1, source_target_pairs={{0,48},{16,0},{32,16},{48,32},{1,49},{17,1},{33,17},{49,33},{2,50}... | collective-permute-start | bytes 1572872 | tf_op jit(solution)/shard_map/ppermute | solution.py:355
  12.7 7.8 %all-to-all-start = ((bf16[8,128,256]{2,1,0:T(8,128)(2,1)}), bf16[8,128,256]{2,1,0:T(8,128)(2,1)S(1)}, u32[]{:S(2)}, u32[]{:S(2)}) async-start(bf16[8,128,256]{2,1,0:T(8,128)(2,1)} %get-tuple-element.31), calls=%async_computation | async-start | bytes 1048576 | tf_op jit(solution)/shard_map/all_to_all | solution.py:396
  20.5 7.4 %project_query.1.q_ref = bf16[128,1024]{1,0:T(8,128)(2,1)S(1)} custom-call(bf16[128,8192]{1,0:T(8,128)(2,1)S(1)} %bitcast.13, bf16[8192,1280]{1,0:T(8,128)(2,1)} %w_ref.1), custom_call_target="tpu_custom_call" | custom-call | flops 1 | bytes 1 | tf_op jit(solution)/shard_map/project_query/pallas_call | solution.py:109
  27.9 3.3 %all-to-all-done = bf16[8,128,256]{2,1,0:T(8,128)(2,1)S(1)} async-done(((bf16[8,128,256]{2,1,0:T(8,128)(2,1)}), bf16[8,128,256]{2,1,0:T(8,128)(2,1)S(1)}, u32[]{:S(2)}, u32[]{:S(2)}) %all-to-all-start) | async-done | bytes 524320 | tf_op jit(solution)/shard_map/all_to_all | solution.py:396
  31.2 6.9 %attention.1 = (bf16[128,1024]{1,0:T(8,128)(2,1)}, bf16[1024,256]{1,0:T(8,128)(2,1)}) custom-call(s32[5]{0:T(128)S(1)} %copy-done.7, s32[1,16]{1,0:T(1,128)S(1)} %copy-done.9, s32[1,4]{1,0:T(1,128)S(1)} %copy-done.10, bf16[128,1024]{1,0:T(8,128)(2,1)S(1)} %project_query.1.q_ref, bf16[128,1024]{1,0:T(8,128)(2,1)S(1)} %bitcast.15, bf16[1024,256]{1,0:T(8,128)(2,1)S(1)} %bitcast.14), custom_call_target="tpu_custom_call" | custom-call | flops 1 | bytes 1 | tf_op jit(solution)/shard_map/attention/pallas_call | solution.py:204
  38.1 3.2 %halves.1 = (bf16[1024,512]{1,0:T(8,128)(2,1)}, bf16[1024,512]{1,0:T(8,128)(2,1)}) custom-call(s32[5]{0:T(128)} %stack.23.where_ref, bf16[2048,128]{1,0:T(8,128)(2,1)} %get-tuple-element.37.refs_0_, bf16[2048,128]{1,0:T(8,128)(2,1)} %collective-permute-done.1.refs_1_, bf16[2048,128]{1,0:T(8,128)(2,1)} %collective-permute-done.2.refs_2_, ...), custom_call_target="tpu_custom_call" | custom-call | flops 1 | bytes 1 | tf_op jit(solution)/shard_map/halves/pallas_call | solution.py:135
  41.3 0.5 collective-permute-start
  41.8 0.3 collective-permute-start.7
  42.1 2.4 %collective-permute-start.6 = (bf16[128,1024]{1,0:T(8,128)(2,1)}, bf16[128,1024]{1,0:T(8,128)(2,1)S(1)}, u32[]{:S(2)}, u32[]{:S(2)}) collective-permute-start(bf16[128,1024]{1,0:T(8,128)(2,1)} %get-tuple-element.33.refs_2_), channel_id=1, source_target_pairs={{0,32},{16,48},{32,0},{48,16},{1,33},{17,49},{33,1},{49,17},{2,34}... | collective-permute-start | bytes 786440 | tf_op jit(solution)/shard_map/ppermute | solution.py:355
  44.5 0.1 collective-permute-done.refs_6_
  44.6 5.5 %all-to-all-start.1 = ((bf16[8,128,256]{2,1,0:T(8,128)(2,1)}), bf16[8,128,256]{2,1,0:T(8,128)(2,1)S(1)}, u32[]{:S(2)}, u32[]{:S(2)}) async-start(bf16[8,128,256]{2,1,0:T(8,128)(2,1)} %bitcast.17), calls=%async_computation.1 | async-start | bytes 1048576 | tf_op jit(solution)/shard_map/all_to_all | solution.py:401
  50.0 1.2 %collective-permute-done.7.refs_5_ = bf16[128,1024]{1,0:T(8,128)(2,1)S(1)} collective-permute-done((bf16[128,1024]{1,0:T(8,128)(2,1)}, bf16[128,1024]{1,0:T(8,128)(2,1)S(1)}, u32[]{:S(2)}, u32[]{:S(2)}) %collective-permute-start.7) | collective-permute-done | bytes 262176 | tf_op jit(solution)/shard_map/ppermute | solution.py:355
  51.2 1.9 %collective-permute-done.6.refs_4_ = bf16[128,1024]{1,0:T(8,128)(2,1)S(1)} collective-permute-done((bf16[128,1024]{1,0:T(8,128)(2,1)}, bf16[128,1024]{1,0:T(8,128)(2,1)S(1)}, u32[]{:S(2)}, u32[]{:S(2)}) %collective-permute-start.6) | collective-permute-done | bytes 262176 | tf_op jit(solution)/shard_map/ppermute | solution.py:355
  53.1 4.3 %collective-permute-done.5.refs_3_ = bf16[128,1024]{1,0:T(8,128)(2,1)S(1)} collective-permute-done((bf16[128,1024]{1,0:T(8,128)(2,1)}, bf16[128,1024]{1,0:T(8,128)(2,1)S(1)}, u32[]{:S(2)}, u32[]{:S(2)}) %collective-permute-start.5) | collective-permute-done | bytes 262176 | tf_op jit(solution)/shard_map/ppermute | solution.py:355
  57.4 3.5 %all-to-all-done.1 = bf16[8,128,256]{2,1,0:T(8,128)(2,1)S(1)} async-done(((bf16[8,128,256]{2,1,0:T(8,128)(2,1)}), bf16[8,128,256]{2,1,0:T(8,128)(2,1)S(1)}, u32[]{:S(2)}, u32[]{:S(2)}) %all-to-all-start.1) | async-done | bytes 524320 | tf_op jit(solution)/shard_map/all_to_all | solution.py:401
  61.1 1.6 %copy-done.1 = bf16[1024,512]{1,0:T(8,128)(2,1)S(1)} copy-done((bf16[1024,512]{1,0:T(8,128)(2,1)S(1)}, bf16[1024,512]{1,0:T(8,128)(2,1)}, u32[]{:S(2)}) %copy-start.1) | copy-done | bytes 1048600
  62.7 0.9 copy-done.3
  63.6 3.9 %term_query.1 = bf16[4,256,1024]{2,1,0:T(8,128)(2,1)} custom-call(bf16[1024,512]{1,0:T(8,128)(2,1)S(1)} %copy-done.1, bf16[1024,512]{1,0:T(8,128)(2,1)S(1)} %collective-permute-done.4.refs_1_, bf16[128,1024]{1,0:T(8,128)(2,1)S(1)} %copy-done.3, bf16[128,1024]{1,0:T(8,128)(2,1)S(1)} %collective-permute-done.5.refs_3_, ...), custom_call_target="tpu_custom_call" | custom-call | flops 1 | bytes 1 | tf_op jit(solution)/shard_map/term_query/pallas_call | solution.py:244
  67.5 2.6 %collective-permute-start.13 = (bf16[128,256]{1,0:T(8,128)(2,1)S(1)}, bf16[128,256]{1,0:T(8,128)(2,1)S(1)}, u32[]{:S(2)}, u32[]{:S(2)}) collective-permute-start(bf16[128,256]{1,0:T(8,128)(2,1)S(1)} %reduce_sum.12.refs_2_), channel_id=1, source_target_pairs={{0,48},{16,0},{32,16},{48,32},{1,49},{17,1},{33,17},{49,33},{2,50}... | collective-permute-start | bytes 196616 | tf_op jit(solution)/shard_map/ppermute | solution.py:355
  70.1 1.2 %collective-permute-start.12 = (bf16[128,256]{1,0:T(8,128)(2,1)S(1)}, bf16[128,256]{1,0:T(8,128)(2,1)}, u32[]{:S(2)}, u32[]{:S(2)}) collective-permute-start(bf16[128,256]{1,0:T(8,128)(2,1)S(1)} %reduce_sum.12.refs_2_), channel_id=1, source_target_pairs={{0,32},{16,48},{32,0},{48,16},{1,33},{17,49},{33,1},{49,17},{2,34}... | collective-permute-start | bytes 196616 | tf_op jit(solution)/shard_map/ppermute | solution.py:355
  71.3 3.6 %all-to-all-start.2 = ((bf16[4,256,1024]{2,1,0:T(8,128)(2,1)}), bf16[4,256,1024]{2,1,0:T(8,128)(2,1)S(1)}, u32[]{:S(2)}, u32[]{:S(2)}) async-start(bf16[4,256,1024]{2,1,0:T(8,128)(2,1)} %term_query.1), calls=%async_computation.2 | async-start | bytes 4194304 | tf_op jit(solution)/shard_map/all_to_all | solution.py:406
  74.9 0.1 collective-permute-start.14
  75.0 0.5 collective-permute-start.17
  75.5 0.5 collective-permute-done.12.refs_4_
  75.9 0.9 collective-permute-done.11.refs_3_
  76.9 0.5 collective-permute-done.16.refs_8_
  77.4 0.9 collective-permute-done.15.refs_7_
  78.3 0.6 copy-done.16
  78.9 3.0 %term_second.1 = (bf16[256,256]{1,0:T(8,128)(2,1)}, bf16[256,256]{1,0:T(8,128)(2,1)}, bf16[256,256]{1,0:T(8,128)(2,1)}, bf16[256,256]{1,0:T(8,128)(2,1)}) custom-call(s32[5]{0:T(128)} %stack.23.where_ref, bf16[1024,512]{1,0:T(8,128)(2,1)} %get-tuple-element.44.refs_0_, bf16[1024,512]{1,0:T(8,128)(2,1)} %copy-done.2, bf16[128,256]{1,0:T(8,128)(2,1)} %copy-done.11, ...), custom_call_target="tpu_custom_call" | custom-call | flops 1 | bytes 1 | tf_op jit(solution)/shard_map/term_second/pallas_call | solution.py:275
  82.0 1.0 collective-permute-start.18
  83.0 1.2 %collective-permute-start.19 = (bf16[256,256]{1,0:T(8,128)(2,1)}, bf16[256,256]{1,0:T(8,128)(2,1)S(1)}, u32[]{:S(2)}, u32[]{:S(2)}) collective-permute-start(bf16[256,256]{1,0:T(8,128)(2,1)} %get-tuple-element.51), channel_id=1, source_target_pairs={{0,4},{64,68},{4,0},{68,64},{1,5},{65,69},{5,1},{69,65},{2,6},{66,... | collective-permute-start | bytes 393224 | tf_op jit(solution)/shard_map/ppermute | solution.py:378
  84.2 1.6 %collective-permute-start.20 = (bf16[256,256]{1,0:T(8,128)(2,1)}, bf16[256,256]{1,0:T(8,128)(2,1)S(1)}, u32[]{:S(2)}, u32[]{:S(2)}) collective-permute-start(bf16[256,256]{1,0:T(8,128)(2,1)} %get-tuple-element.53), channel_id=1, source_target_pairs={{0,68},{64,0},{4,64},{68,4},{1,69},{65,1},{5,65},{69,5},{2,70},{66... | collective-permute-start | bytes 393224 | tf_op jit(solution)/shard_map/ppermute | solution.py:378
  85.7 12.8 %convolution_convert_fusion = bf16[128,8192]{1,0:T(8,128)(2,1)} fusion(bf16[128,1280]{1,0:T(8,128)(2,1)S(1)} %pad_maximum_fusion, bf16[8192,1280]{1,0:T(8,128)(2,1)} %w_ref.1), kind=kOutput, calls=%fused_computation | convolution fusion | flops 2685403136 | bytes 23396352 | tf_op jit(solution)/shard_map/dot_general | solution.py:17
  98.5 1.2 %middle_y.1 = (f32[64,256]{1,0:T(8,128)S(1)}, bf16[64,256]{1,0:T(8,128)(2,1)}, bf16[64,256]{1,0:T(8,128)(2,1)}, bf16[64,256]{1,0:T(8,128)(2,1)}) custom-call(s32[5]{0:T(128)S(1)} %copy-done.8, bf16[256,256]{1,0:T(8,128)(2,1)S(1)} %copy-done.6, bf16[256,256]{1,0:T(8,128)(2,1)S(1)} %collective-permute-done.18.refs_1_, ...), custom_call_target="tpu_custom_call" | custom-call | flops 1 | bytes 1 | tf_op jit(solution)/shard_map/middle_y/pallas_call | solution.py:320
  99.8 0.5 all-to-all-done.2.stack_ref
  100.3 1.1 middle_z.1
  101.3 3.5 %all-to-all-start.3 = ((bf16[4,64,1024]{2,1,0:T(8,128)(2,1)}), bf16[4,64,1024]{2,1,0:T(8,128)(2,1)S(1)}, u32[]{:S(2)}, u32[]{:S(2)}) async-start(bf16[4,64,1024]{2,1,0:T(8,128)(2,1)} %middle_z.1), calls=%async_computation.3 | async-start | bytes 1048576 | tf_op jit(solution)/shard_map/all_to_all | solution.py:414
  104.8 2.3 %collective-permute-start.22 = (bf16[64,256]{1,0:T(8,128)(2,1)}, bf16[64,256]{1,0:T(8,128)(2,1)S(1)}, u32[]{:S(2)}, u32[]{:S(2)}) collective-permute-start(bf16[64,256]{1,0:T(8,128)(2,1)} %get-tuple-element.58), channel_id=1, source_target_pairs={{0,2},{1,3},{2,0},{3,1},{4,6},{5,7},{6,4},{7,5},{8,10},{9,11},{10,... | collective-permute-start | bytes 98312 | tf_op jit(solution)/shard_map/ppermute | solution.py:382
  107.1 1.2 %collective-permute-start.23 = (bf16[64,256]{1,0:T(8,128)(2,1)}, bf16[64,256]{1,0:T(8,128)(2,1)S(1)}, u32[]{:S(2)}, u32[]{:S(2)}) collective-permute-start(bf16[64,256]{1,0:T(8,128)(2,1)} %get-tuple-element.59), channel_id=1, source_target_pairs={{0,3},{1,0},{2,1},{3,2},{4,7},{5,4},{6,5},{7,6},{8,11},{9,8},{10,9... | collective-permute-start | bytes 98312 | tf_op jit(solution)/shard_map/ppermute | solution.py:382
  108.3 0.9 collective-permute-start.21
  109.2 1.4 %collective-permute-done.22.refs_2_ = bf16[64,256]{1,0:T(8,128)(2,1)S(1)} collective-permute-done((bf16[64,256]{1,0:T(8,128)(2,1)}, bf16[64,256]{1,0:T(8,128)(2,1)S(1)}, u32[]{:S(2)}, u32[]{:S(2)}) %collective-permute-start.22) | collective-permute-done | bytes 32800 | tf_op jit(solution)/shard_map/ppermute | solution.py:382
  110.5 0.7 collective-permute-done.23.refs_3_
  111.2 2.4 %collective-permute-done.21.refs_1_ = bf16[64,256]{1,0:T(8,128)(2,1)S(1)} collective-permute-done((bf16[64,256]{1,0:T(8,128)(2,1)}, bf16[64,256]{1,0:T(8,128)(2,1)S(1)}, u32[]{:S(2)}, u32[]{:S(2)}) %collective-permute-start.21) | collective-permute-done | bytes 32800 | tf_op jit(solution)/shard_map/ppermute | solution.py:382
  113.6 0.8 final.1
  (55 shorter events, 0.2 us)
Async XLA Ops:
  1.3 19.1 %copy-start = (bf16[1,128,8192]{2,1,0:T(8,128)(2,1)S(1)}, bf16[1,128,8192]{2,1,0:T(8,128)(2,1)}, u32[]{:S(2)}) copy-start(bf16[1,128,8192]{2,1,0:T(8,128)(2,1)} %param.5) | copy-start | bytes 6291460
  6.9 31.2 %collective-permute-start.1 = (bf16[2048,128]{1,0:T(8,128)(2,1)}, bf16[2048,128]{1,0:T(8,128)(2,1)}, u32[]{:S(2)}, u32[]{:S(2)}) collective-permute-start(bf16[2048,128]{1,0:T(8,128)(2,1)} %get-tuple-element.38), channel_id=1, source_target_pairs={{0,16},{16,32},{32,48},{48,0},{1,17},{17,33},{33,49},{49,1},{2,18}... | collective-permute-start | bytes 1572872 | tf_op jit(solution)/shard_map/ppermute | solution.py:355
  8.5 29.6 %collective-permute-start.2 = (bf16[2048,128]{1,0:T(8,128)(2,1)}, bf16[2048,128]{1,0:T(8,128)(2,1)}, u32[]{:S(2)}, u32[]{:S(2)}) collective-permute-start(bf16[2048,128]{1,0:T(8,128)(2,1)} %get-tuple-element.40), channel_id=1, source_target_pairs={{0,32},{16,48},{32,0},{48,16},{1,33},{17,49},{33,1},{49,17},{2,34}... | collective-permute-start | bytes 1572872 | tf_op jit(solution)/shard_map/ppermute | solution.py:355
  11.2 26.9 %collective-permute-start.3 = (bf16[2048,128]{1,0:T(8,128)(2,1)}, bf16[2048,128]{1,0:T(8,128)(2,1)}, u32[]{:S(2)}, u32[]{:S(2)}) collective-permute-start(bf16[2048,128]{1,0:T(8,128)(2,1)} %get-tuple-element.42), channel_id=1, source_target_pairs={{0,48},{16,0},{32,16},{48,32},{1,49},{17,1},{33,17},{49,33},{2,50}... | collective-permute-start | bytes 1572872 | tf_op jit(solution)/shard_map/ppermute | solution.py:355
  12.7 18.5 %all-to-all-start = ((bf16[8,128,256]{2,1,0:T(8,128)(2,1)}), bf16[8,128,256]{2,1,0:T(8,128)(2,1)S(1)}, u32[]{:S(2)}, u32[]{:S(2)}) async-start(bf16[8,128,256]{2,1,0:T(8,128)(2,1)} %get-tuple-element.31), calls=%async_computation | async-start | bytes 1048576 | tf_op jit(solution)/shard_map/all_to_all | solution.py:396
  20.5 10.7 %copy-start.5 = (bf16[1,128,1024]{2,1,0:T(8,128)(2,1)S(1)}, bf16[1,128,1024]{2,1,0:T(8,128)(2,1)}, u32[]{:S(2)}) copy-start(bf16[1,128,1024]{2,1,0:T(8,128)(2,1)} %param.7) | copy-start | bytes 786436
  20.5 10.7 %copy-start.7 = (s32[5]{0:T(128)S(1)}, s32[5]{0:T(128)}, u32[]{:S(2)}) copy-start(s32[5]{0:T(128)} %stack.23.where_ref) | copy-start | bytes 64
  20.5 10.7 %copy-start.9 = (s32[1,16]{1,0:T(1,128)S(1)}, s32[1,16]{1,0:T(1,128)}, u32[]{:S(2)}) copy-start(s32[1,16]{1,0:T(1,128)} %order_ref.1) | copy-start | bytes 196
  20.5 10.7 %copy-start.10 = (s32[1,4]{1,0:T(1,128)S(1)}, s32[1,4]{1,0:T(1,128)}, u32[]{:S(2)}) copy-start(s32[1,4]{1,0:T(1,128)} %lens_ref.1) | copy-start | bytes 52
  41.3 19.7 %collective-permute-start.4 = (bf16[1024,512]{1,0:T(8,128)(2,1)}, bf16[1024,512]{1,0:T(8,128)(2,1)S(1)}, u32[]{:S(2)}, u32[]{:S(2)}) collective-permute-start(bf16[1024,512]{1,0:T(8,128)(2,1)} %get-tuple-element.45), channel_id=1, source_target_pairs={{0,8},{8,0},{1,9},{9,1},{2,10},{10,2},{3,11},{11,3},{4,12},{12,4},... | collective-permute-start | bytes 3145736 | tf_op jit(solution)/shard_map/ppermute | solution.py:359
  41.3 3.2 %collective-permute-start = (bf16[128,1024]{1,0:T(8,128)(2,1)}, bf16[128,1024]{1,0:T(8,128)(2,1)S(1)}, u32[]{:S(2)}, u32[]{:S(2)}) collective-permute-start(bf16[128,1024]{1,0:T(8,128)(2,1)} %get-tuple-element.33.refs_2_), channel_id=1, source_target_pairs={{0,8},{8,0},{1,9},{9,1},{2,10},{10,2},{3,11},{11,3},{4,12},{12,4},... | collective-permute-start | bytes 786440 | tf_op jit(solution)/shard_map/ppermute | solution.py:359
  41.8 9.4 %collective-permute-start.7 = (bf16[128,1024]{1,0:T(8,128)(2,1)}, bf16[128,1024]{1,0:T(8,128)(2,1)S(1)}, u32[]{:S(2)}, u32[]{:S(2)}) collective-permute-start(bf16[128,1024]{1,0:T(8,128)(2,1)} %get-tuple-element.33.refs_2_), channel_id=1, source_target_pairs={{0,48},{16,0},{32,16},{48,32},{1,49},{17,1},{33,17},{49,33},{2,50}... | collective-permute-start | bytes 786440 | tf_op jit(solution)/shard_map/ppermute | solution.py:355
  42.1 11.0 %collective-permute-start.6 = (bf16[128,1024]{1,0:T(8,128)(2,1)}, bf16[128,1024]{1,0:T(8,128)(2,1)S(1)}, u32[]{:S(2)}, u32[]{:S(2)}) collective-permute-start(bf16[128,1024]{1,0:T(8,128)(2,1)} %get-tuple-element.33.refs_2_), channel_id=1, source_target_pairs={{0,32},{16,48},{32,0},{48,16},{1,33},{17,49},{33,1},{49,17},{2,34}... | collective-permute-start | bytes 786440 | tf_op jit(solution)/shard_map/ppermute | solution.py:355
  44.5 12.9 %collective-permute-start.5 = (bf16[128,1024]{1,0:T(8,128)(2,1)}, bf16[128,1024]{1,0:T(8,128)(2,1)S(1)}, u32[]{:S(2)}, u32[]{:S(2)}) collective-permute-start(bf16[128,1024]{1,0:T(8,128)(2,1)} %get-tuple-element.33.refs_2_), channel_id=1, source_target_pairs={{0,16},{16,32},{32,48},{48,0},{1,17},{17,33},{33,49},{49,1},{2,18}... | collective-permute-start | bytes 786440 | tf_op jit(solution)/shard_map/ppermute | solution.py:355
  44.6 16.4 %all-to-all-start.1 = ((bf16[8,128,256]{2,1,0:T(8,128)(2,1)}), bf16[8,128,256]{2,1,0:T(8,128)(2,1)S(1)}, u32[]{:S(2)}, u32[]{:S(2)}) async-start(bf16[8,128,256]{2,1,0:T(8,128)(2,1)} %bitcast.17), calls=%async_computation.1 | async-start | bytes 1048576 | tf_op jit(solution)/shard_map/all_to_all | solution.py:401
  51.2 9.8 %collective-permute-start.10 = (bf16[128,1024]{1,0:T(8,128)(2,1)S(1)}, bf16[128,1024]{1,0:T(8,128)(2,1)S(1)}, u32[]{:S(2)}, u32[]{:S(2)}) collective-permute-start(bf16[128,1024]{1,0:T(8,128)(2,1)S(1)} %collective-permute-done.7.refs_5_), channel_id=1, source_target_pairs={{0,8},{8,0},{1,9},{9,1},{2,10},{10,2},{3,11},{11,3},{4,12},{12,4},... | collective-permute-start | bytes 786440 | tf_op jit(solution)/shard_map/ppermute | solution.py:359
  53.1 8.0 %collective-permute-start.9 = (bf16[128,1024]{1,0:T(8,128)(2,1)S(1)}, bf16[128,1024]{1,0:T(8,128)(2,1)S(1)}, u32[]{:S(2)}, u32[]{:S(2)}) collective-permute-start(bf16[128,1024]{1,0:T(8,128)(2,1)S(1)} %collective-permute-done.6.refs_4_), channel_id=1, source_target_pairs={{0,8},{8,0},{1,9},{9,1},{2,10},{10,2},{3,11},{11,3},{4,12},{12,4},... | collective-permute-start | bytes 786440 | tf_op jit(solution)/shard_map/ppermute | solution.py:359
  57.4 3.7 %collective-permute-start.8 = (bf16[128,1024]{1,0:T(8,128)(2,1)S(1)}, bf16[128,1024]{1,0:T(8,128)(2,1)S(1)}, u32[]{:S(2)}, u32[]{:S(2)}) collective-permute-start(bf16[128,1024]{1,0:T(8,128)(2,1)S(1)} %collective-permute-done.5.refs_3_), channel_id=1, source_target_pairs={{0,8},{8,0},{1,9},{9,1},{2,10},{10,2},{3,11},{11,3},{4,12},{12,4},... | collective-permute-start | bytes 786440 | tf_op jit(solution)/shard_map/ppermute | solution.py:359
  61.0 15.8 %copy-start.11 = (bf16[128,256]{1,0:T(8,128)(2,1)}, bf16[128,256]{1,0:T(8,128)(2,1)S(1)}, u32[]{:S(2)}) copy-start(bf16[128,256]{1,0:T(8,128)(2,1)S(1)} %reduce_sum.12.refs_2_) | copy-start | bytes 196612
  61.1 10.2 %copy-start.2 = (bf16[1024,512]{1,0:T(8,128)(2,1)}, bf16[1024,512]{1,0:T(8,128)(2,1)S(1)}, u32[]{:S(2)}) copy-start(bf16[1024,512]{1,0:T(8,128)(2,1)S(1)} %collective-permute-done.4.refs_1_) | copy-start | bytes 3145732
  61.1 1.6 %copy-start.1 = (bf16[1024,512]{1,0:T(8,128)(2,1)S(1)}, bf16[1024,512]{1,0:T(8,128)(2,1)}, u32[]{:S(2)}) copy-start(bf16[1024,512]{1,0:T(8,128)(2,1)} %get-tuple-element.44.refs_0_) | copy-start | bytes 3145732
  62.7 0.9 copy-start.3
  63.6 13.2 %copy-start.4 = (bf16[128,1024]{1,0:T(8,128)(2,1)S(1)}, bf16[128,1024]{1,0:T(8,128)(2,1)}, u32[]{:S(2)}) copy-start(bf16[128,1024]{1,0:T(8,128)(2,1)} %get-tuple-element.33.refs_2_) | copy-start | bytes 786436
  67.5 7.5 %collective-permute-start.13 = (bf16[128,256]{1,0:T(8,128)(2,1)S(1)}, bf16[128,256]{1,0:T(8,128)(2,1)S(1)}, u32[]{:S(2)}, u32[]{:S(2)}) collective-permute-start(bf16[128,256]{1,0:T(8,128)(2,1)S(1)} %reduce_sum.12.refs_2_), channel_id=1, source_target_pairs={{0,48},{16,0},{32,16},{48,32},{1,49},{17,1},{33,17},{49,33},{2,50}... | collective-permute-start | bytes 196616 | tf_op jit(solution)/shard_map/ppermute | solution.py:355
  70.1 5.9 %collective-permute-start.12 = (bf16[128,256]{1,0:T(8,128)(2,1)S(1)}, bf16[128,256]{1,0:T(8,128)(2,1)}, u32[]{:S(2)}, u32[]{:S(2)}) collective-permute-start(bf16[128,256]{1,0:T(8,128)(2,1)S(1)} %reduce_sum.12.refs_2_), channel_id=1, source_target_pairs={{0,32},{16,48},{32,0},{48,16},{1,33},{17,49},{33,1},{49,17},{2,34}... | collective-permute-start | bytes 196616 | tf_op jit(solution)/shard_map/ppermute | solution.py:355
  71.3 5.6 %collective-permute-start.11 = (bf16[128,256]{1,0:T(8,128)(2,1)S(1)}, bf16[128,256]{1,0:T(8,128)(2,1)}, u32[]{:S(2)}, u32[]{:S(2)}) collective-permute-start(bf16[128,256]{1,0:T(8,128)(2,1)S(1)} %reduce_sum.12.refs_2_), channel_id=1, source_target_pairs={{0,16},{16,32},{32,48},{48,0},{1,17},{17,33},{33,49},{49,1},{2,18}... | collective-permute-start | bytes 196616 | tf_op jit(solution)/shard_map/ppermute | solution.py:355
  71.3 29.0 %all-to-all-start.2 = ((bf16[4,256,1024]{2,1,0:T(8,128)(2,1)}), bf16[4,256,1024]{2,1,0:T(8,128)(2,1)S(1)}, u32[]{:S(2)}, u32[]{:S(2)}) async-start(bf16[4,256,1024]{2,1,0:T(8,128)(2,1)} %term_query.1), calls=%async_computation.2 | async-start | bytes 4194304 | tf_op jit(solution)/shard_map/all_to_all | solution.py:406
  74.9 2.0 %collective-permute-start.14 = (bf16[128,256]{1,0:T(8,128)(2,1)S(1)}, bf16[128,256]{1,0:T(8,128)(2,1)S(1)}, u32[]{:S(2)}, u32[]{:S(2)}) collective-permute-start(bf16[128,256]{1,0:T(8,128)(2,1)S(1)} %reduce_sum.12.refs_2_), channel_id=1, source_target_pairs={{0,8},{8,0},{1,9},{9,1},{2,10},{10,2},{3,11},{11,3},{4,12},{12,4},... | collective-permute-start | bytes 196616 | tf_op jit(solution)/shard_map/ppermute | solution.py:359
  75.0 3.3 %copy-start.12 = (bf16[128,256]{1,0:T(8,128)(2,1)}, bf16[128,256]{1,0:T(8,128)(2,1)S(1)}, u32[]{:S(2)}) copy-start(bf16[128,256]{1,0:T(8,128)(2,1)S(1)} %collective-permute-done.13.refs_5_) | copy-start | bytes 196612
  75.0 1.9 %collective-permute-start.17 = (bf16[128,256]{1,0:T(8,128)(2,1)S(1)}, bf16[128,256]{1,0:T(8,128)(2,1)S(1)}, u32[]{:S(2)}, u32[]{:S(2)}) collective-permute-start(bf16[128,256]{1,0:T(8,128)(2,1)S(1)} %collective-permute-done.13.refs_5_), channel_id=1, source_target_pairs={{0,8},{8,0},{1,9},{9,1},{2,10},{10,2},{3,11},{11,3},{4,12},{12,4},... | collective-permute-start | bytes 196616 | tf_op jit(solution)/shard_map/ppermute | solution.py:359
  75.9 1.5 %collective-permute-start.16 = (bf16[128,256]{1,0:T(8,128)(2,1)}, bf16[128,256]{1,0:T(8,128)(2,1)S(1)}, u32[]{:S(2)}, u32[]{:S(2)}) collective-permute-start(bf16[128,256]{1,0:T(8,128)(2,1)} %collective-permute-done.12.refs_4_), channel_id=1, source_target_pairs={{0,8},{8,0},{1,9},{9,1},{2,10},{10,2},{3,11},{11,3},{4,12},{12,4},... | collective-permute-start | bytes 196616 | tf_op jit(solution)/shard_map/ppermute | solution.py:359
  76.8 1.5 %collective-permute-start.15 = (bf16[128,256]{1,0:T(8,128)(2,1)}, bf16[128,256]{1,0:T(8,128)(2,1)S(1)}, u32[]{:S(2)}, u32[]{:S(2)}) collective-permute-start(bf16[128,256]{1,0:T(8,128)(2,1)} %collective-permute-done.11.refs_3_), channel_id=1, source_target_pairs={{0,8},{8,0},{1,9},{9,1},{2,10},{10,2},{3,11},{11,3},{4,12},{12,4},... | collective-permute-start | bytes 196616 | tf_op jit(solution)/shard_map/ppermute | solution.py:359
  76.9 1.4 %copy-start.13 = (bf16[128,256]{1,0:T(8,128)(2,1)}, bf16[128,256]{1,0:T(8,128)(2,1)S(1)}, u32[]{:S(2)}) copy-start(bf16[128,256]{1,0:T(8,128)(2,1)S(1)} %collective-permute-done.14.refs_6_) | copy-start | bytes 196612
  76.9 1.4 %copy-start.14 = (bf16[128,256]{1,0:T(8,128)(2,1)}, bf16[128,256]{1,0:T(8,128)(2,1)S(1)}, u32[]{:S(2)}) copy-start(bf16[128,256]{1,0:T(8,128)(2,1)S(1)} %collective-permute-done.17.refs_9_) | copy-start | bytes 196612
  77.4 0.9 copy-start.15
  78.3 0.6 copy-start.16
  82.0 16.6 %collective-permute-start.18 = (bf16[256,256]{1,0:T(8,128)(2,1)}, bf16[256,256]{1,0:T(8,128)(2,1)S(1)}, u32[]{:S(2)}, u32[]{:S(2)}) collective-permute-start(bf16[256,256]{1,0:T(8,128)(2,1)} %get-tuple-element.49), channel_id=1, source_target_pairs={{0,64},{64,4},{4,68},{68,0},{1,65},{65,5},{5,69},{69,1},{2,66},{66... | collective-permute-start | bytes 393224 | tf_op jit(solution)/shard_map/ppermute | solution.py:378
  83.0 15.5 %collective-permute-start.19 = (bf16[256,256]{1,0:T(8,128)(2,1)}, bf16[256,256]{1,0:T(8,128)(2,1)S(1)}, u32[]{:S(2)}, u32[]{:S(2)}) collective-permute-start(bf16[256,256]{1,0:T(8,128)(2,1)} %get-tuple-element.51), channel_id=1, source_target_pairs={{0,4},{64,68},{4,0},{68,64},{1,5},{65,69},{5,1},{69,65},{2,6},{66,... | collective-permute-start | bytes 393224 | tf_op jit(solution)/shard_map/ppermute | solution.py:378
  84.2 14.4 %copy-start.6 = (bf16[256,256]{1,0:T(8,128)(2,1)S(1)}, bf16[256,256]{1,0:T(8,128)(2,1)}, u32[]{:S(2)}) copy-start(bf16[256,256]{1,0:T(8,128)(2,1)} %get-tuple-element.47.refs_0_) | copy-start | bytes 393220
  84.2 14.4 %copy-start.8 = (s32[5]{0:T(128)S(1)}, s32[5]{0:T(128)}, u32[]{:S(2)}) copy-start(s32[5]{0:T(128)} %stack.23.where_ref) | copy-start | bytes 64
  84.2 14.4 %collective-permute-start.20 = (bf16[256,256]{1,0:T(8,128)(2,1)}, bf16[256,256]{1,0:T(8,128)(2,1)S(1)}, u32[]{:S(2)}, u32[]{:S(2)}) collective-permute-start(bf16[256,256]{1,0:T(8,128)(2,1)} %get-tuple-element.53), channel_id=1, source_target_pairs={{0,68},{64,0},{4,64},{68,4},{1,69},{65,1},{5,65},{69,5},{2,70},{66... | collective-permute-start | bytes 393224 | tf_op jit(solution)/shard_map/ppermute | solution.py:378
  101.3 12.3 %all-to-all-start.3 = ((bf16[4,64,1024]{2,1,0:T(8,128)(2,1)}), bf16[4,64,1024]{2,1,0:T(8,128)(2,1)S(1)}, u32[]{:S(2)}, u32[]{:S(2)}) async-start(bf16[4,64,1024]{2,1,0:T(8,128)(2,1)} %middle_z.1), calls=%async_computation.3 | async-start | bytes 1048576 | tf_op jit(solution)/shard_map/all_to_all | solution.py:414
  104.8 5.7 %collective-permute-start.22 = (bf16[64,256]{1,0:T(8,128)(2,1)}, bf16[64,256]{1,0:T(8,128)(2,1)S(1)}, u32[]{:S(2)}, u32[]{:S(2)}) collective-permute-start(bf16[64,256]{1,0:T(8,128)(2,1)} %get-tuple-element.58), channel_id=1, source_target_pairs={{0,2},{1,3},{2,0},{3,1},{4,6},{5,7},{6,4},{7,5},{8,10},{9,11},{10,... | collective-permute-start | bytes 98312 | tf_op jit(solution)/shard_map/ppermute | solution.py:382
  107.1 4.1 %collective-permute-start.23 = (bf16[64,256]{1,0:T(8,128)(2,1)}, bf16[64,256]{1,0:T(8,128)(2,1)S(1)}, u32[]{:S(2)}, u32[]{:S(2)}) collective-permute-start(bf16[64,256]{1,0:T(8,128)(2,1)} %get-tuple-element.59), channel_id=1, source_target_pairs={{0,3},{1,0},{2,1},{3,2},{4,7},{5,4},{6,5},{7,6},{8,11},{9,8},{10,9... | collective-permute-start | bytes 98312 | tf_op jit(solution)/shard_map/ppermute | solution.py:382
  108.3 5.3 %collective-permute-start.21 = (bf16[64,256]{1,0:T(8,128)(2,1)}, bf16[64,256]{1,0:T(8,128)(2,1)S(1)}, u32[]{:S(2)}, u32[]{:S(2)}) collective-permute-start(bf16[64,256]{1,0:T(8,128)(2,1)} %get-tuple-element.55), channel_id=1, source_target_pairs={{0,1},{1,2},{2,3},{3,0},{4,5},{5,6},{6,7},{7,4},{8,9},{9,10},{10,1... | collective-permute-start | bytes 98312 | tf_op jit(solution)/shard_map/ppermute | solution.py:382

commit v8 on v7

--- a/solution.py
+++ b/solution.py
@@ -10,7 +10,7 @@
 SPAN = 64
 LOG2E = 1.4426950408889634
 SEQ = ("zhi", "y")
-DEPTH = ("zlo", "zhi")
+OWN = ("zlo", "zhi", "y")
 
 
 def nt(a, b):
@@ -55,8 +55,9 @@
     for s in range(chips):
         chip = lax.rem(where_ref[0] + s, chips)
         for c in range(2):
+            core = where_ref[1] if c == 0 else 1 - where_ref[1]
             for z in range(2):
-                at = pl.multiple_of(z * (features // 2) + chip * 2 * width + c * width, width)
+                at = pl.multiple_of(z * (features // 2) + chip * 2 * width + core * width, width)
                 piece_ref[s, (2 * c + z) * width : (2 * c + z + 1) * width, :] = x_ref[:, pl.ds(at, width)].T
         stores.append(pltpu.make_async_copy(piece_ref.at[s], out_hbm[s], piece_sem.at[s]))
         stores[s].start()
@@ -118,30 +119,30 @@
     )(x, w)
 
 
-def halves_kernel(where_ref, *refs):
-    pieces, own_ref, send_ref = refs[:-2], refs[-2], refs[-1]
-    half, tokens = own_ref.shape[0], pieces[0].shape[1]
-    own = pl.multiple_of(where_ref[1] * half, half)
-    send = pl.multiple_of((1 - where_ref[1]) * half, half)
+def half_of(piece, at):
+    return pl.BlockSpec((piece.shape[0] // 2, piece.shape[1]), lambda i: (at, 0))
+
+
+def forward_kernel(*refs):
+    pieces, out_ref = refs[:-1], refs[-1]
+    tokens = pieces[0].shape[1]
     for i, piece in enumerate(pieces):
-        own_ref[:, i * tokens : (i + 1) * tokens] = piece[pl.ds(own, half), :]
-        send_ref[:, i * tokens : (i + 1) * tokens] = piece[pl.ds(send, half), :]
-
-
-def halves(where, pieces):
+        out_ref[:, i * tokens : (i + 1) * tokens] = piece[...]
+
+
+def forward(pieces):
     rows, tokens = pieces[0].shape
-    n = len(pieces)
-    shape = (rows // 2, n * tokens)
-    return pl.pallas_call(
-        halves_kernel,
+    out = pltpu.HBM((rows // 2, len(pieces) * tokens), jnp.bfloat16)
+    return pl.pallas_call(
+        forward_kernel,
         grid=(1,),
-        out_shape=(pltpu.HBM(shape, jnp.bfloat16),) * 2,
-        in_specs=[SMEM] + [VMEM] * n,
-        out_specs=(pl.BlockSpec(shape, lambda i: (0, 0)),) * 2,
+        out_shape=out,
+        in_specs=[half_of(piece, 1) for piece in pieces],
+        out_specs=pl.BlockSpec(out.shape, lambda i: (0, 0)),
         compiler_params=pltpu.CompilerParams(vmem_limit_bytes=60 * MIB),
         cost_estimate=SMALL,
-        name="halves",
-    )(where, *pieces)
+        name="forward",
+    )(*pieces)
 
 
 def attention_kernel(where_ref, order_ref, lens_ref, q_ref, do_ref, kv_ref, *refs):
@@ -221,133 +222,63 @@
     )(where, order, lens, query, grad, key_value)
 
 
-def term_query_kernel(*refs):
-    parts, pieces, out_ref = refs[:2], refs[2:-1], refs[-1]
-    step = pl.program_id(0)
-    width = out_ref.shape[2]
-    at = pl.multiple_of(step * width, width)
-    left = jnp.concatenate([part[...] for part in parts], axis=1)
+def term_kernel(count, other_ref, *refs):
+    parts, pieces, out_ref = refs[:count], refs[count:-1], refs[-1]
+    width = out_ref.shape[1]
+    at = pl.multiple_of(pl.program_id(0) * width, width)
+    left = jnp.concatenate([part[...] for part in parts] + [other_ref[...]], axis=1)
     right = jnp.concatenate([g[:, pl.ds(at, width)] for g in pieces], axis=0)
-    part = nn(left, right).astype(out_ref.dtype)
-    blocks = out_ref.shape[0]
-    rows = left.shape[0] // (blocks * blocks)
-    for i in range(blocks):
-        for y in range(blocks):
-            here = (i * blocks + y) * rows
-            out_ref[y, i * rows : (i + 1) * rows, :] = part[here : here + rows]
-
-
-def term_query(parts, pieces, blocks):
-    half = parts[0].shape[0]
+    out_ref[...] = nn(left, right).astype(out_ref.dtype)
+
+
+def term(parts, other, pieces, limit, name):
+    half = other.shape[0]
     width = pieces[0].shape[1]
     step = 2 * HD
     return pl.pallas_call(
-        term_query_kernel,
+        lambda *refs: term_kernel(len(parts), *refs),
         grid=(width // step,),
-        out_shape=pltpu.HBM((blocks, half // blocks, width), jnp.bfloat16),
-        in_specs=[VMEM] * (len(parts) + len(pieces)),
-        out_specs=pl.BlockSpec((blocks, half // blocks, step), lambda j: (0, 0, j)),
-        compiler_params=pltpu.CompilerParams(vmem_limit_bytes=20 * MIB),
-        cost_estimate=SMALL,
-        name="term_query",
-    )(*parts, *pieces)
-
-
-def ring_block(where_ref, s):
-    place = lax.rem(where_ref[3] + s, 4)
-    return 2 * lax.rem(place, 2) + place // 2
-
-
-def term_second_kernel(where_ref, *refs):
-    parts, pieces, outs = refs[:2], refs[2:-4], refs[-4:]
-    rows = outs[0].shape[0]
-    right = jnp.concatenate([g[...] for g in pieces], axis=0)
-    for s in range(4):
-        at = pl.multiple_of(ring_block(where_ref, s) * rows, rows)
-        left = jnp.concatenate([part[pl.ds(at, rows), :] for part in parts], axis=1)
-        outs[s][...] = nn(left, right).astype(outs[s].dtype)
-
-
-def term_second(where, parts, pieces):
-    half = parts[0].shape[0]
-    width = pieces[0].shape[1]
-    out = pltpu.HBM((half // 4, width), jnp.bfloat16)
-    return pl.pallas_call(
-        term_second_kernel,
-        grid=(1,),
-        out_shape=(out,) * 4,
-        in_specs=[SMEM] + [VMEM] * (len(parts) + len(pieces)),
-        out_specs=(pl.BlockSpec(out.shape, lambda i: (0, 0)),) * 4,
-        compiler_params=pltpu.CompilerParams(vmem_limit_bytes=60 * MIB),
-        cost_estimate=SMALL,
-        name="term_second",
-    )(where, *parts, *pieces)
-
-
-def middle_z_kernel(stack_ref, out_ref):
-    rows = out_ref.shape[1]
-    for i in range(out_ref.shape[0]):
-        parts = [stack_ref[j, i * rows : (i + 1) * rows, :].astype(jnp.float32) for j in range(stack_ref.shape[0])]
-        out_ref[i] = sum(parts).astype(out_ref.dtype)
-
-
-def middle_z(stack):
-    blocks, rows, width = stack.shape
-    out = pltpu.HBM((blocks, rows // blocks, width), jnp.bfloat16)
-    return pl.pallas_call(
-        middle_z_kernel,
-        grid=(1,),
-        out_shape=out,
+        out_shape=pltpu.HBM((half, width), jnp.bfloat16),
+        in_specs=[whole(other)] + [half_of(part, 0) for part in parts] + [VMEM] * len(pieces),
+        out_specs=pl.BlockSpec((half, step), lambda j: (0, j)),
+        compiler_params=pltpu.CompilerParams(vmem_limit_bytes=limit * MIB),
+        cost_estimate=SMALL,
+        name=name,
+    )(other, *parts, *pieces)
+
+
+def sum_kernel(stack_ref, out_ref):
+    out_ref[...] = sum(stack_ref[i].astype(jnp.float32) for i in range(stack_ref.shape[0]))
+
+
+def sum_query(stack):
+    return pl.pallas_call(
+        sum_kernel,
+        out_shape=jax.ShapeDtypeStruct(stack.shape[1:], jnp.float32),
         in_specs=[VMEM],
-        out_specs=pl.BlockSpec(out.shape, lambda i: (0, 0, 0)),
-        compiler_params=pltpu.CompilerParams(vmem_limit_bytes=14 * MIB),
-        cost_estimate=SMALL,
-        name="middle_z",
+        out_specs=VMEM,
+        compiler_params=pltpu.CompilerParams(vmem_limit_bytes=12 * MIB),
+        cost_estimate=SMALL,
+        name="sum_query",
     )(stack)
 
 
-def middle_y_kernel(where_ref, *refs):
-    parts, outs = refs[:-4], refs[-4:]
-    rows = outs[0].shape[0]
-    for s in range(4):
-        at = pl.multiple_of(lax.rem(where_ref[4] + s, 4) * rows, rows)
-        total = sum(part[pl.ds(at, rows), :].astype(jnp.float32) for part in parts)
-        outs[s][...] = total.astype(outs[s].dtype)
-
-
-def middle_y(where, parts):
-    rows, width = parts[0].shape
-    return pl.pallas_call(
-        middle_y_kernel,
-        grid=(1,),
-        out_shape=(jax.ShapeDtypeStruct((rows // 4, width), jnp.float32),) + (pltpu.HBM((rows // 4, width), jnp.bfloat16),) * 3,
-        in_specs=[SMEM] + [VMEM] * len(parts),
-        out_specs=(VMEM,) + (pl.BlockSpec((rows // 4, width), lambda i: (0, 0)),) * 3,
-        compiler_params=pltpu.CompilerParams(vmem_limit_bytes=14 * MIB),
-        cost_estimate=SMALL,
-        name="middle_y",
-    )(where, *parts)
-
-
-def final_kernel(stack_ref, *refs):
-    parts, out_ref = refs[:-1], refs[-1]
-    first = stack_ref.shape[2]
-    out_ref[:, :first] = sum(stack_ref[i].astype(jnp.float32) for i in range(stack_ref.shape[0]))
-    out_ref[:, first:] = sum(part[...].astype(jnp.float32) for part in parts)
-
-
-def final(stack, parts):
-    rows = stack.shape[1]
-    width = stack.shape[2] + parts[0].shape[1]
+def final_kernel(query_ref, stack_ref, out_ref):
+    first = query_ref.shape[1]
+    out_ref[:, :first] = query_ref[...]
+    out_ref[:, first:] = sum(stack_ref[i].astype(jnp.float32) for i in range(stack_ref.shape[0]))
+
+
+def final(query, stack):
     return pl.pallas_call(
         final_kernel,
-        out_shape=jax.ShapeDtypeStruct((rows, width), jnp.float32),
-        in_specs=[VMEM] * 5,
+        out_shape=jax.ShapeDtypeStruct((query.shape[0], query.shape[1] + stack.shape[2]), jnp.float32),
+        in_specs=[VMEM, VMEM],
         out_specs=VMEM,
         compiler_params=pltpu.CompilerParams(vmem_limit_bytes=8 * MIB),
         cost_estimate=SMALL,
         name="final",
-    )(stack, *parts)
+    )(query, stack)
 
 
 def shifted(value, s):
@@ -370,16 +301,9 @@
     return lax.optimization_barrier((value,) + others)[0]
 
 
-def ring_index(place):
-    return 2 * (place % 2) + place // 2
-
-
-def shifted_z(value, s):
-    return lax.ppermute(value, DEPTH, [(ring_index(i), ring_index((i + s) % 4)) for i in range(4)])
-
-
-def shifted_y(value, s):
-    return lax.ppermute(value, "y", [(i, (i + s) % 4) for i in range(4)])
+def to_owners(value):
+    owners = lax.axis_size("zlo") * lax.axis_size("zhi") * lax.axis_size("y")
+    return lax.all_to_all(value.reshape(owners, value.shape[0] // owners, value.shape[1]), OWN, 0, 0, tiled=True)
 
 
 def local(layer_input, w_qkv, d_out, span_order, doc_lengths):
@@ -387,10 +311,8 @@
     tokens = rows.shape[0]
     chips = lax.axis_size("x")
     seq = lax.axis_size("zhi") * lax.axis_size("y")
-    at_zlo, at_zhi, at_y = lax.axis_index("zlo"), lax.axis_index("zhi"), lax.axis_index("y")
-    where = jnp.stack(
-        [lax.axis_index("x"), lax.axis_index("core"), at_zhi * lax.axis_size("y") + at_y, at_zhi * 2 + at_zlo, at_y]
-    ).astype(jnp.int32)
+    place = lax.axis_index("zhi") * lax.axis_size("y") + lax.axis_index("y")
+    where = jnp.stack([lax.axis_index("x"), lax.axis_index("core"), place]).astype(jnp.int32)
 
     copies, *packed = first(where, rows, w_qkv, seq, chips)
     gathered = lax.all_to_all(copies, SEQ, 0, 0, tiled=True).reshape(seq * tokens, 2 * HD)
@@ -399,20 +321,17 @@
     d_query, terms = attention(where, span_order, doc_lengths, query, d_out[0], gathered)
     own_q, other_q = gather_chips(d_query)
     arrived = lax.all_to_all(after(terms, other_q[0]).reshape(seq, tokens, 2 * HD), SEQ, 0, 0, tiled=True)
-    x_own, x_send = halves(where, [after(piece, terms) for piece in pieces])
-    columns = [x_own, swapped(x_send)]
-
-    stacked = term_query(columns, own_q + other_q, lax.axis_size("y"))
-    group_y = lax.all_to_all(stacked, "y", 0, 0, tiled=True)
+    x_other = swapped(forward([after(piece, terms) for piece in pieces]))
+
+    term_query = term(pieces, x_other, own_q + other_q, 60, "term_query")
+    received_query = to_owners(term_query)
     owned = jnp.sum(arrived.astype(jnp.float32), axis=0).astype(jnp.bfloat16)
-    own_kv, other_kv = gather_chips(after(owned, stacked))
-    parts = term_second(where, columns, own_kv + other_kv)
-    d_qkv = after(jnp.concatenate([d_query, owned], axis=1), parts[0])
+    own_kv, other_kv = gather_chips(after(owned, term_query))
+    term_kv = term(pieces, x_other, own_kv + other_kv, 60, "term_kv")
+    d_qkv = after(jnp.concatenate([d_query, owned], axis=1), term_kv)
     d_rows = nt(d_qkv, w_qkv).astype(jnp.bfloat16)
-    group_z = [parts[0]] + [after(shifted_z(parts[s], s), d_rows) for s in range(1, 4)]
-    sums = middle_y(where, group_z)
-    second_z = lax.all_to_all(middle_z(after(group_y, sums[1])), DEPTH, 0, 0, tiled=True)
-    d_w = final(second_z, [sums[0]] + [shifted_y(sums[s], s) for s in range(1, 4)])
+    received_kv = to_owners(after(term_kv, received_query, d_rows))
+    d_w = final(sum_query(received_query), received_kv)
     return (d_rows[None], d_w)
 
 

time: 116 us -> 120 us (1.034); the launches traced: 114 us -> 120 us
  waiting for transfers between devices: 22 us -> 33.4 us
  starting transfers between devices: 41.7 us -> 37.5 us
  local copies, waits for them, and re-layouts: 3.9 us -> 2.32 us
    all_to_all x2, waiting for transfers between devices: 0.54 us -> 18.5 us  [to_owners(): lax.all_to_all(value.reshape(owners, value.shape[0] // owners, value.shap...]
    ppermute x6 -> x0, starting transfers between devices: 8.1 us -> none  [the longest x3 4.33 us: shifted_y(): return lax.ppermute(value, 'y', [(i, (i + s) % 4) for i in range(4)])]
    ppermute x6 -> x0, waiting for transfers between devices: 4.47 us -> none  [the longest x3 4.46 us: shifted_y(): return lax.ppermute(value, 'y', [(i, (i + s) % 4) for i in range(4)])]
    all_to_all x1, waiting for transfers between devices: 3.54 us -> 0.01 us  [local(): lax.all_to_all(after(terms, other_q[0]).reshape(seq, tokens, 2 * HD), SEQ...]
    ppermute x9, starting transfers between devices: 12.2 us -> 14.2 us  [shifted(): return lax.ppermute(value, 'x', [(i, (i + s) % n) for i in range(n)])]
    unnamed x34 -> x44, local copies, waits for them, and re-layouts: 3.22 us -> 2.32 us
    pallas_call x6 -> x5, Pallas kernels: 13.2 us -> 12.6 us  [the longest x2 9.18 us: term(): pl.pallas_call(lambda *refs: term_kernel(len(parts), *refs), grid=(width...]
  transfers between devices with their start and end apart: 28 -> 22, of which waited for: 14 -> 13; matrix products, arithmetic and copies ran while one was open for 11% -> 11% of each run, Pallas kernels for 16% -> 20%
where the time goes in v8:
time: 120 us
  starting transfers between devices  37.5 us (31%)
  waiting for transfers between devices  33.4 us (28%)
  Pallas kernels  32.4 us (27%)
  matrix products  12.5 us (10%)
  local copies, waits for them, and re-layouts  2.32 us (2%)
    all_to_all x2, waiting for transfers between devices, to_owners(): lax.all_to_all(value.reshape(owners, value.shape[0] // owners, value.shap...  18.5 us
    ppermute x9, starting transfers between devices, shifted(): return lax.ppermute(value, 'x', [(i, (i + s) % n) for i in range(n)])  14.2 us
    dot_general x1, matrix products, nt(): lax.dot_general(a, b, (((1,), (1,)), ((), ())), preferred_element_type=jn...  12.5 us
    pallas_call x2, Pallas kernels, term(): pl.pallas_call(lambda *refs: term_kernel(len(parts), *refs), grid=(width...  9.18 us
    ppermute x9, waiting for transfers between devices, shifted(): return lax.ppermute(value, 'x', [(i, (i + s) % n) for i in range(n)])  9.01 us
    all_to_all x2, starting transfers between devices, to_owners(): lax.all_to_all(value.reshape(owners, value.shape[0] // owners, value.shap...  8.2 us
    all_to_all x1, starting transfers between devices, local(): lax.all_to_all(copies, SEQ, 0, 0, tiled=True).reshape(seq * tokens, 2 * HD)  7.79 us
    pallas_call x1, Pallas kernels, project_query(): pl.pallas_call(query_kernel, grid=(HQ // 2,), out_shape=jax.ShapeDtypeStr...  7.42 us
  transfers between devices with their start and end apart: 22, of which 13 were waited for; matrix products, arithmetic and copies ran while one was open for 11% of the time, Pallas kernels for 20%

profile of v8, /device:TPU:0, one launch (start us, length us, event | category | flops | bytes accessed | tf_op | source)
XLA Modules:
  0.0 119.7 jit_solution(5865715489929024122)
XLA Ops:
  0.6 0.6 pad_add_fusion.where_ref
  1.2 5.5 %first.1 = (bf16[8,128,256]{2,1,0:T(8,128)(2,1)}, bf16[2048,128]{1,0:T(8,128)(2,1)}, bf16[2048,128]{1,0:T(8,128)(2,1)}, bf16[2048,128]{1,0:T(8,128)(2,1)}, bf16[2048,128]{1,0:T(8,128)(2,1)}) custom-call(s32[3]{0:T(128)} %pad_add_fusion.where_ref, bf16[128,8192]{1,0:T(8,128)(2,1)} %bitcast.12, bf16[8192,1280]{1,0:T(8,128)(2,1)} %w_ref.1), custom_call_target="tpu_custom_call" | custom-call | flops 1 | bytes 1 | tf_op jit(solution)/shard_map/first/pallas_call | solution.py:82
  6.8 1.6 %collective-permute-start.1 = (bf16[2048,128]{1,0:T(8,128)(2,1)}, bf16[2048,128]{1,0:T(8,128)(2,1)}, u32[]{:S(2)}, u32[]{:S(2)}) collective-permute-start(bf16[2048,128]{1,0:T(8,128)(2,1)} %get-tuple-element.25), channel_id=1, source_target_pairs={{0,16},{16,32},{32,48},{48,0},{1,17},{17,33},{33,49},{49,1},{2,18}... | collective-permute-start | bytes 1572872 | tf_op jit(solution)/shard_map/ppermute | solution.py:286
  8.4 2.7 %collective-permute-start.2 = (bf16[2048,128]{1,0:T(8,128)(2,1)}, bf16[2048,128]{1,0:T(8,128)(2,1)}, u32[]{:S(2)}, u32[]{:S(2)}) collective-permute-start(bf16[2048,128]{1,0:T(8,128)(2,1)} %get-tuple-element.27), channel_id=1, source_target_pairs={{0,32},{16,48},{32,0},{48,16},{1,33},{17,49},{33,1},{49,17},{2,34}... | collective-permute-start | bytes 1572872 | tf_op jit(solution)/shard_map/ppermute | solution.py:286
  11.1 1.4 %collective-permute-start.3 = (bf16[2048,128]{1,0:T(8,128)(2,1)}, bf16[2048,128]{1,0:T(8,128)(2,1)}, u32[]{:S(2)}, u32[]{:S(2)}) collective-permute-start(bf16[2048,128]{1,0:T(8,128)(2,1)} %get-tuple-element.29), channel_id=1, source_target_pairs={{0,48},{16,0},{32,16},{48,32},{1,49},{17,1},{33,17},{49,33},{2,50}... | collective-permute-start | bytes 1572872 | tf_op jit(solution)/shard_map/ppermute | solution.py:286
  12.6 7.8 %all-to-all-start = ((bf16[8,128,256]{2,1,0:T(8,128)(2,1)}), bf16[8,128,256]{2,1,0:T(8,128)(2,1)S(1)}, u32[]{:S(2)}, u32[]{:S(2)}) async-start(bf16[8,128,256]{2,1,0:T(8,128)(2,1)} %get-tuple-element.18), calls=%async_computation | async-start | bytes 1048576 | tf_op jit(solution)/shard_map/all_to_all | solution.py:318
  20.4 0.0 copy-start.1
  20.4 0.0 copy-start.3
  20.4 0.0 copy-start.4
  20.4 7.4 %project_query.1.q_ref = bf16[128,1024]{1,0:T(8,128)(2,1)S(1)} custom-call(bf16[128,8192]{1,0:T(8,128)(2,1)S(1)} %bitcast.13, bf16[8192,1280]{1,0:T(8,128)(2,1)} %w_ref.1), custom_call_target="tpu_custom_call" | custom-call | flops 1 | bytes 1 | tf_op jit(solution)/shard_map/project_query/pallas_call | solution.py:110
  27.8 3.3 %all-to-all-done = bf16[8,128,256]{2,1,0:T(8,128)(2,1)S(1)} async-done(((bf16[8,128,256]{2,1,0:T(8,128)(2,1)}), bf16[8,128,256]{2,1,0:T(8,128)(2,1)S(1)}, u32[]{:S(2)}, u32[]{:S(2)}) %all-to-all-start) | async-done | bytes 524320 | tf_op jit(solution)/shard_map/all_to_all | solution.py:318
  31.1 6.9 %attention.1 = (bf16[128,1024]{1,0:T(8,128)(2,1)}, bf16[1024,256]{1,0:T(8,128)(2,1)}) custom-call(s32[3]{0:T(128)S(1)} %copy-done.2, s32[1,16]{1,0:T(1,128)S(1)} %copy-done.3, s32[1,4]{1,0:T(1,128)S(1)} %copy-done.4, bf16[128,1024]{1,0:T(8,128)(2,1)S(1)} %project_query.1.q_ref, bf16[128,1024]{1,0:T(8,128)(2,1)S(1)} %bitcast.15, bf16[1024,256]{1,0:T(8,128)(2,1)S(1)} %bitcast.14), custom_call_target="tpu_custom_call" | custom-call | flops 1 | bytes 1 | tf_op jit(solution)/shard_map/attention/pallas_call | solution.py:205
  38.0 2.3 %forward.1 = bf16[1024,512]{1,0:T(8,128)(2,1)} custom-call(bf16[2048,128]{1,0:T(8,128)(2,1)} %get-tuple-element.24.refs_0_.refs_1_, bf16[2048,128]{1,0:T(8,128)(2,1)} %collective-permute-done.1.refs_1_.refs_2_, bf16[2048,128]{1,0:T(8,128)(2,1)} %collective-permute-done.2.refs_2_.refs_3_, bf16[2048,128]{1,0:T(8,128)(2,1)} %collective-permute-done.3.refs_3_.refs_4_), custom_call_target="tpu_custom_call" | custom-call | flops 1 | bytes 1 | tf_op jit(solution)/shard_map/forward/pallas_call | solution.py:136
  40.3 0.5 collective-permute-start
  40.8 0.6 collective-permute-start.5
  41.4 1.1 collective-permute-start.6
  42.6 1.5 %collective-permute-start.7 = (bf16[128,1024]{1,0:T(8,128)(2,1)}, bf16[128,1024]{1,0:T(8,128)(2,1)S(1)}, u32[]{:S(2)}, u32[]{:S(2)}) collective-permute-start(bf16[128,1024]{1,0:T(8,128)(2,1)} %get-tuple-element.20.refs_5_), channel_id=1, source_target_pairs={{0,48},{16,0},{32,16},{48,32},{1,49},{17,1},{33,17},{49,33},{2,50}... | collective-permute-start | bytes 786440 | tf_op jit(solution)/shard_map/ppermute | solution.py:286
  44.1 6.1 %all-to-all-start.1 = ((bf16[8,128,256]{2,1,0:T(8,128)(2,1)}), bf16[8,128,256]{2,1,0:T(8,128)(2,1)S(1)}, u32[]{:S(2)}, u32[]{:S(2)}) async-start(bf16[8,128,256]{2,1,0:T(8,128)(2,1)} %bitcast.18), calls=%async_computation.1 | async-start | bytes 1048576 | tf_op jit(solution)/shard_map/all_to_all | solution.py:323
  50.3 5.8 %collective-permute-done.5.refs_6_ = bf16[128,1024]{1,0:T(8,128)(2,1)S(1)} collective-permute-done((bf16[128,1024]{1,0:T(8,128)(2,1)}, bf16[128,1024]{1,0:T(8,128)(2,1)S(1)}, u32[]{:S(2)}, u32[]{:S(2)}) %collective-permute-start.5) | collective-permute-done | bytes 262176 | tf_op jit(solution)/shard_map/ppermute | solution.py:286
  56.1 0.5 collective-permute-start.9
  56.6 0.1 collective-permute-done.7.refs_8_
  56.7 0.2 collective-permute-start.10
  56.9 0.7 collective-permute-done.8.refs_10_
  57.6 0.4 collective-permute-done.9.refs_11_
  58.0 0.4 collective-permute-done.10.refs_12_
  58.4 0.3 copy-done.13
  58.7 0.4 copy-done.14
  59.1 1.0 copy-done.5
  60.1 6.1 %term_query.1 = bf16[1024,1024]{1,0:T(8,128)(2,1)} custom-call(bf16[1024,512]{1,0:T(8,128)(2,1)} %copy-done.5, bf16[2048,128]{1,0:T(8,128)(2,1)} %get-tuple-element.24.refs_0_.refs_1_, bf16[2048,128]{1,0:T(8,128)(2,1)} %collective-permute-done.1.refs_1_.refs_2_, bf16[2048,128]{1,0:T(8,128)(2,1)} %collective-permute-done.2.refs_2_.refs_3_, ...), custom_call_target="tpu_custom_call" | custom-call | flops 1 | bytes 1 | tf_op jit(solution)/shard_map/term_query/pallas_call | solution.py:238
  66.1 4.6 %all-to-all-start.2 = ((bf16[16,64,1024]{2,1,0:T(8,128)(2,1)}), bf16[16,64,1024]{2,1,0:T(8,128)(2,1)S(1)}, u32[]{:S(2)}, u32[]{:S(2)}) async-start(bf16[16,64,1024]{2,1,0:T(8,128)(2,1)} %bitcast.16), calls=%async_computation.2 | async-start | bytes 4194304 | tf_op jit(solution)/shard_map/all_to_all | solution.py:306
  70.8 0.1 reduce_sum.12.refs_5_
  70.9 1.5 %collective-permute-start.11 = (bf16[128,256]{1,0:T(8,128)(2,1)S(1)}, bf16[128,256]{1,0:T(8,128)(2,1)S(1)}, u32[]{:S(2)}, u32[]{:S(2)}) collective-permute-start(bf16[128,256]{1,0:T(8,128)(2,1)S(1)} %reduce_sum.12.refs_5_), channel_id=1, source_target_pairs={{0,16},{16,32},{32,48},{48,0},{1,17},{17,33},{33,49},{49,1},{2,18}... | collective-permute-start | bytes 196616 | tf_op jit(solution)/shard_map/ppermute | solution.py:286
  72.4 2.4 %collective-permute-start.12 = (bf16[128,256]{1,0:T(8,128)(2,1)S(1)}, bf16[128,256]{1,0:T(8,128)(2,1)S(1)}, u32[]{:S(2)}, u32[]{:S(2)}) collective-permute-start(bf16[128,256]{1,0:T(8,128)(2,1)S(1)} %reduce_sum.12.refs_5_), channel_id=1, source_target_pairs={{0,32},{16,48},{32,0},{48,16},{1,33},{17,49},{33,1},{49,17},{2,34}... | collective-permute-start | bytes 196616 | tf_op jit(solution)/shard_map/ppermute | solution.py:286
  74.8 1.2 collective-permute-start.13
  76.0 1.0 collective-permute-done.11.refs_6_
  77.0 1.2 collective-permute-done.12.refs_7_
  78.2 0.9 collective-permute-done.13.refs_8_
  79.1 0.0 copy-start.18
  79.2 0.3 collective-permute-done.16.refs_11_
  79.4 0.9 collective-permute-done.17.refs_12_
  80.4 0.6 copy-done.21
  81.0 3.1 %term_kv.1 = bf16[1024,256]{1,0:T(8,128)(2,1)} custom-call(bf16[1024,512]{1,0:T(8,128)(2,1)} %copy-done.5, bf16[2048,128]{1,0:T(8,128)(2,1)} %get-tuple-element.24.refs_0_.refs_1_, bf16[2048,128]{1,0:T(8,128)(2,1)} %collective-permute-done.1.refs_1_.refs_2_, bf16[2048,128]{1,0:T(8,128)(2,1)} %collective-permute-done.2.refs_2_.refs_3_, ...), custom_call_target="tpu_custom_call" | custom-call | flops 1 | bytes 1 | tf_op jit(solution)/shard_map/term_kv/pallas_call | solution.py:238
  84.1 12.5 %convolution_convert_fusion = bf16[128,8192]{1,0:T(8,128)(2,1)} fusion(bf16[128,1280]{1,0:T(8,128)(2,1)S(1)} %pad_maximum_fusion, bf16[8192,1280]{1,0:T(8,128)(2,1)} %w_ref.1), kind=kOutput, calls=%fused_computation | convolution fusion | flops 2685403136 | bytes 23396352 | tf_op jit(solution)/shard_map/dot_general | solution.py:17
  96.6 7.7 %all-to-all-done.2.stack_ref = bf16[16,64,1024]{2,1,0:T(8,128)(2,1)S(1)} async-done(((bf16[16,64,1024]{2,1,0:T(8,128)(2,1)}), bf16[16,64,1024]{2,1,0:T(8,128)(2,1)S(1)}, u32[]{:S(2)}, u32[]{:S(2)}) %all-to-all-start.2) | async-done | bytes 2097184 | tf_op jit(solution)/shard_map/all_to_all | solution.py:306
  104.4 3.6 %all-to-all-start.3 = ((bf16[16,64,256]{2,1,0:T(8,128)(2,1)}), bf16[16,64,256]{2,1,0:T(8,128)(2,1)S(1)}, u32[]{:S(2)}, u32[]{:S(2)}) async-start(bf16[16,64,256]{2,1,0:T(8,128)(2,1)} %bitcast.9), calls=%async_computation.3 | async-start | bytes 1048576 | tf_op jit(solution)/shard_map/all_to_all | solution.py:306
  107.9 0.3 sum_query.1.query_ref
  108.2 10.7 %all-to-all-done.3.stack_ref = bf16[16,64,256]{2,1,0:T(8,128)(2,1)S(1)} async-done(((bf16[16,64,256]{2,1,0:T(8,128)(2,1)}), bf16[16,64,256]{2,1,0:T(8,128)(2,1)S(1)}, u32[]{:S(2)}, u32[]{:S(2)}) %all-to-all-start.3) | async-done | bytes 524320 | tf_op jit(solution)/shard_map/all_to_all | solution.py:306
  118.9 0.8 final.1
  (52 shorter events, 0.1 us)
Async XLA Ops:
  1.2 19.1 %copy-start = (bf16[1,128,8192]{2,1,0:T(8,128)(2,1)S(1)}, bf16[1,128,8192]{2,1,0:T(8,128)(2,1)}, u32[]{:S(2)}) copy-start(bf16[1,128,8192]{2,1,0:T(8,128)(2,1)} %param.5) | copy-start | bytes 6291460
  6.8 31.2 %collective-permute-start.1 = (bf16[2048,128]{1,0:T(8,128)(2,1)}, bf16[2048,128]{1,0:T(8,128)(2,1)}, u32[]{:S(2)}, u32[]{:S(2)}) collective-permute-start(bf16[2048,128]{1,0:T(8,128)(2,1)} %get-tuple-element.25), channel_id=1, source_target_pairs={{0,16},{16,32},{32,48},{48,0},{1,17},{17,33},{33,49},{49,1},{2,18}... | collective-permute-start | bytes 1572872 | tf_op jit(solution)/shard_map/ppermute | solution.py:286
  8.4 29.6 %collective-permute-start.2 = (bf16[2048,128]{1,0:T(8,128)(2,1)}, bf16[2048,128]{1,0:T(8,128)(2,1)}, u32[]{:S(2)}, u32[]{:S(2)}) collective-permute-start(bf16[2048,128]{1,0:T(8,128)(2,1)} %get-tuple-element.27), channel_id=1, source_target_pairs={{0,32},{16,48},{32,0},{48,16},{1,33},{17,49},{33,1},{49,17},{2,34}... | collective-permute-start | bytes 1572872 | tf_op jit(solution)/shard_map/ppermute | solution.py:286
  11.1 26.9 %collective-permute-start.3 = (bf16[2048,128]{1,0:T(8,128)(2,1)}, bf16[2048,128]{1,0:T(8,128)(2,1)}, u32[]{:S(2)}, u32[]{:S(2)}) collective-permute-start(bf16[2048,128]{1,0:T(8,128)(2,1)} %get-tuple-element.29), channel_id=1, source_target_pairs={{0,48},{16,0},{32,16},{48,32},{1,49},{17,1},{33,17},{49,33},{2,50}... | collective-permute-start | bytes 1572872 | tf_op jit(solution)/shard_map/ppermute | solution.py:286
  12.6 18.5 %all-to-all-start = ((bf16[8,128,256]{2,1,0:T(8,128)(2,1)}), bf16[8,128,256]{2,1,0:T(8,128)(2,1)S(1)}, u32[]{:S(2)}, u32[]{:S(2)}) async-start(bf16[8,128,256]{2,1,0:T(8,128)(2,1)} %get-tuple-element.18), calls=%async_computation | async-start | bytes 1048576 | tf_op jit(solution)/shard_map/all_to_all | solution.py:318
  20.4 10.7 %copy-start.1 = (bf16[1,128,1024]{2,1,0:T(8,128)(2,1)S(1)}, bf16[1,128,1024]{2,1,0:T(8,128)(2,1)}, u32[]{:S(2)}) copy-start(bf16[1,128,1024]{2,1,0:T(8,128)(2,1)} %param.7) | copy-start | bytes 786436
  20.4 10.7 %copy-start.2 = (s32[3]{0:T(128)S(1)}, s32[3]{0:T(128)}, u32[]{:S(2)}) copy-start(s32[3]{0:T(128)} %pad_add_fusion.where_ref) | copy-start | bytes 40
  20.4 10.7 %copy-start.3 = (s32[1,16]{1,0:T(1,128)S(1)}, s32[1,16]{1,0:T(1,128)}, u32[]{:S(2)}) copy-start(s32[1,16]{1,0:T(1,128)} %order_ref.1) | copy-start | bytes 196
  20.4 10.7 %copy-start.4 = (s32[1,4]{1,0:T(1,128)S(1)}, s32[1,4]{1,0:T(1,128)}, u32[]{:S(2)}) copy-start(s32[1,4]{1,0:T(1,128)} %lens_ref.1) | copy-start | bytes 52
  40.3 18.1 %collective-permute-start.4 = (bf16[1024,512]{1,0:T(8,128)(2,1)}, bf16[1024,512]{1,0:T(8,128)(2,1)S(1)}, u32[]{:S(2)}, u32[]{:S(2)}) collective-permute-start(bf16[1024,512]{1,0:T(8,128)(2,1)} %forward.1), channel_id=1, source_target_pairs={{0,8},{8,0},{1,9},{9,1},{2,10},{10,2},{3,11},{11,3},{4,12},{12,4},... | collective-permute-start | bytes 3145736 | tf_op jit(solution)/shard_map/ppermute | solution.py:290
  40.3 3.8 %collective-permute-start = (bf16[128,1024]{1,0:T(8,128)(2,1)}, bf16[128,1024]{1,0:T(8,128)(2,1)S(1)}, u32[]{:S(2)}, u32[]{:S(2)}) collective-permute-start(bf16[128,1024]{1,0:T(8,128)(2,1)} %get-tuple-element.20.refs_5_), channel_id=1, source_target_pairs={{0,8},{8,0},{1,9},{9,1},{2,10},{10,2},{3,11},{11,3},{4,12},{12,4},... | collective-permute-start | bytes 786440 | tf_op jit(solution)/shard_map/ppermute | solution.py:290
  40.8 15.3 %collective-permute-start.5 = (bf16[128,1024]{1,0:T(8,128)(2,1)}, bf16[128,1024]{1,0:T(8,128)(2,1)S(1)}, u32[]{:S(2)}, u32[]{:S(2)}) collective-permute-start(bf16[128,1024]{1,0:T(8,128)(2,1)} %get-tuple-element.20.refs_5_), channel_id=1, source_target_pairs={{0,16},{16,32},{32,48},{48,0},{1,17},{17,33},{33,49},{49,1},{2,18}... | collective-permute-start | bytes 786440 | tf_op jit(solution)/shard_map/ppermute | solution.py:286
  41.4 14.7 %collective-permute-start.6 = (bf16[128,1024]{1,0:T(8,128)(2,1)}, bf16[128,1024]{1,0:T(8,128)(2,1)S(1)}, u32[]{:S(2)}, u32[]{:S(2)}) collective-permute-start(bf16[128,1024]{1,0:T(8,128)(2,1)} %get-tuple-element.20.refs_5_), channel_id=1, source_target_pairs={{0,32},{16,48},{32,0},{48,16},{1,33},{17,49},{33,1},{49,17},{2,34}... | collective-permute-start | bytes 786440 | tf_op jit(solution)/shard_map/ppermute | solution.py:286
  42.6 14.1 %collective-permute-start.7 = (bf16[128,1024]{1,0:T(8,128)(2,1)}, bf16[128,1024]{1,0:T(8,128)(2,1)S(1)}, u32[]{:S(2)}, u32[]{:S(2)}) collective-permute-start(bf16[128,1024]{1,0:T(8,128)(2,1)} %get-tuple-element.20.refs_5_), channel_id=1, source_target_pairs={{0,48},{16,0},{32,16},{48,32},{1,49},{17,1},{33,17},{49,33},{2,50}... | collective-permute-start | bytes 786440 | tf_op jit(solution)/shard_map/ppermute | solution.py:286
  44.1 14.3 %copy-start.8 = (bf16[128,1024]{1,0:T(8,128)(2,1)}, bf16[128,1024]{1,0:T(8,128)(2,1)S(1)}, u32[]{:S(2)}) copy-start(bf16[128,1024]{1,0:T(8,128)(2,1)S(1)} %collective-permute-done.refs_9_) | copy-start | bytes 786436
  44.1 22.0 %all-to-all-start.1 = ((bf16[8,128,256]{2,1,0:T(8,128)(2,1)}), bf16[8,128,256]{2,1,0:T(8,128)(2,1)S(1)}, u32[]{:S(2)}, u32[]{:S(2)}) async-start(bf16[8,128,256]{2,1,0:T(8,128)(2,1)} %bitcast.18), calls=%async_computation.1 | async-start | bytes 1048576 | tf_op jit(solution)/shard_map/all_to_all | solution.py:323
  56.1 2.3 %copy-start.9 = (bf16[128,1024]{1,0:T(8,128)(2,1)}, bf16[128,1024]{1,0:T(8,128)(2,1)S(1)}, u32[]{:S(2)}) copy-start(bf16[128,1024]{1,0:T(8,128)(2,1)S(1)} %collective-permute-done.5.refs_6_) | copy-start | bytes 786436
  56.1 1.5 %collective-permute-start.8 = (bf16[128,1024]{1,0:T(8,128)(2,1)S(1)}, bf16[128,1024]{1,0:T(8,128)(2,1)S(1)}, u32[]{:S(2)}, u32[]{:S(2)}) collective-permute-start(bf16[128,1024]{1,0:T(8,128)(2,1)S(1)} %collective-permute-done.5.refs_6_), channel_id=1, source_target_pairs={{0,8},{8,0},{1,9},{9,1},{2,10},{10,2},{3,11},{11,3},{4,12},{12,4},... | collective-permute-start | bytes 786440 | tf_op jit(solution)/shard_map/ppermute | solution.py:290
  56.1 2.3 %copy-start.10 = (bf16[128,1024]{1,0:T(8,128)(2,1)}, bf16[128,1024]{1,0:T(8,128)(2,1)S(1)}, u32[]{:S(2)}) copy-start(bf16[128,1024]{1,0:T(8,128)(2,1)S(1)} %collective-permute-done.6.refs_7_) | copy-start | bytes 786436
  56.1 1.9 %collective-permute-start.9 = (bf16[128,1024]{1,0:T(8,128)(2,1)S(1)}, bf16[128,1024]{1,0:T(8,128)(2,1)S(1)}, u32[]{:S(2)}, u32[]{:S(2)}) collective-permute-start(bf16[128,1024]{1,0:T(8,128)(2,1)S(1)} %collective-permute-done.6.refs_7_), channel_id=1, source_target_pairs={{0,8},{8,0},{1,9},{9,1},{2,10},{10,2},{3,11},{11,3},{4,12},{12,4},... | collective-permute-start | bytes 786440 | tf_op jit(solution)/shard_map/ppermute | solution.py:290
  56.7 1.7 %copy-start.11 = (bf16[128,1024]{1,0:T(8,128)(2,1)}, bf16[128,1024]{1,0:T(8,128)(2,1)S(1)}, u32[]{:S(2)}) copy-start(bf16[128,1024]{1,0:T(8,128)(2,1)S(1)} %collective-permute-done.7.refs_8_) | copy-start | bytes 786436
  56.7 1.7 %collective-permute-start.10 = (bf16[128,1024]{1,0:T(8,128)(2,1)S(1)}, bf16[128,1024]{1,0:T(8,128)(2,1)S(1)}, u32[]{:S(2)}, u32[]{:S(2)}) collective-permute-start(bf16[128,1024]{1,0:T(8,128)(2,1)S(1)} %collective-permute-done.7.refs_8_), channel_id=1, source_target_pairs={{0,8},{8,0},{1,9},{9,1},{2,10},{10,2},{3,11},{11,3},{4,12},{12,4},... | collective-permute-start | bytes 786440 | tf_op jit(solution)/shard_map/ppermute | solution.py:290
  57.6 0.8 copy-start.12
  58.0 0.7 copy-start.13
  58.4 0.7 copy-start.14
  59.1 1.0 copy-start.5
  66.1 12.9 %copy-start.6 = (bf16[128,1024]{1,0:T(8,128)(2,1)S(1)}, bf16[128,1024]{1,0:T(8,128)(2,1)}, u32[]{:S(2)}) copy-start(bf16[128,1024]{1,0:T(8,128)(2,1)} %get-tuple-element.20.refs_5_) | copy-start | bytes 786436
  66.1 38.2 %all-to-all-start.2 = ((bf16[16,64,1024]{2,1,0:T(8,128)(2,1)}), bf16[16,64,1024]{2,1,0:T(8,128)(2,1)S(1)}, u32[]{:S(2)}, u32[]{:S(2)}) async-start(bf16[16,64,1024]{2,1,0:T(8,128)(2,1)} %bitcast.16), calls=%async_computation.2 | async-start | bytes 4194304 | tf_op jit(solution)/shard_map/all_to_all | solution.py:306
  70.9 9.5 %copy-start.7 = (bf16[128,256]{1,0:T(8,128)(2,1)}, bf16[128,256]{1,0:T(8,128)(2,1)S(1)}, u32[]{:S(2)}) copy-start(bf16[128,256]{1,0:T(8,128)(2,1)S(1)} %reduce_sum.12.refs_5_) | copy-start | bytes 196612
  70.9 6.1 %collective-permute-start.11 = (bf16[128,256]{1,0:T(8,128)(2,1)S(1)}, bf16[128,256]{1,0:T(8,128)(2,1)S(1)}, u32[]{:S(2)}, u32[]{:S(2)}) collective-permute-start(bf16[128,256]{1,0:T(8,128)(2,1)S(1)} %reduce_sum.12.refs_5_), channel_id=1, source_target_pairs={{0,16},{16,32},{32,48},{48,0},{1,17},{17,33},{33,49},{49,1},{2,18}... | collective-permute-start | bytes 196616 | tf_op jit(solution)/shard_map/ppermute | solution.py:286
  72.4 5.8 %collective-permute-start.12 = (bf16[128,256]{1,0:T(8,128)(2,1)S(1)}, bf16[128,256]{1,0:T(8,128)(2,1)S(1)}, u32[]{:S(2)}, u32[]{:S(2)}) collective-permute-start(bf16[128,256]{1,0:T(8,128)(2,1)S(1)} %reduce_sum.12.refs_5_), channel_id=1, source_target_pairs={{0,32},{16,48},{32,0},{48,16},{1,33},{17,49},{33,1},{49,17},{2,34}... | collective-permute-start | bytes 196616 | tf_op jit(solution)/shard_map/ppermute | solution.py:286
  74.8 4.3 %collective-permute-start.13 = (bf16[128,256]{1,0:T(8,128)(2,1)S(1)}, bf16[128,256]{1,0:T(8,128)(2,1)S(1)}, u32[]{:S(2)}, u32[]{:S(2)}) collective-permute-start(bf16[128,256]{1,0:T(8,128)(2,1)S(1)} %reduce_sum.12.refs_5_), channel_id=1, source_target_pairs={{0,48},{16,0},{32,16},{48,32},{1,49},{17,1},{33,17},{49,33},{2,50}... | collective-permute-start | bytes 196616 | tf_op jit(solution)/shard_map/ppermute | solution.py:286
  76.0 3.1 %collective-permute-start.14 = (bf16[128,256]{1,0:T(8,128)(2,1)S(1)}, bf16[128,256]{1,0:T(8,128)(2,1)S(1)}, u32[]{:S(2)}, u32[]{:S(2)}) collective-permute-start(bf16[128,256]{1,0:T(8,128)(2,1)S(1)} %reduce_sum.12.refs_5_), channel_id=1, source_target_pairs={{0,8},{8,0},{1,9},{9,1},{2,10},{10,2},{3,11},{11,3},{4,12},{12,4},... | collective-permute-start | bytes 196616 | tf_op jit(solution)/shard_map/ppermute | solution.py:290
  77.0 3.3 %copy-start.15 = (bf16[128,256]{1,0:T(8,128)(2,1)}, bf16[128,256]{1,0:T(8,128)(2,1)S(1)}, u32[]{:S(2)}) copy-start(bf16[128,256]{1,0:T(8,128)(2,1)S(1)} %collective-permute-done.11.refs_6_) | copy-start | bytes 196612
  77.0 2.1 %collective-permute-start.15 = (bf16[128,256]{1,0:T(8,128)(2,1)S(1)}, bf16[128,256]{1,0:T(8,128)(2,1)S(1)}, u32[]{:S(2)}, u32[]{:S(2)}) collective-permute-start(bf16[128,256]{1,0:T(8,128)(2,1)S(1)} %collective-permute-done.11.refs_6_), channel_id=1, source_target_pairs={{0,8},{8,0},{1,9},{9,1},{2,10},{10,2},{3,11},{11,3},{4,12},{12,4},... | collective-permute-start | bytes 196616 | tf_op jit(solution)/shard_map/ppermute | solution.py:290
  78.2 2.1 %copy-start.16 = (bf16[128,256]{1,0:T(8,128)(2,1)}, bf16[128,256]{1,0:T(8,128)(2,1)S(1)}, u32[]{:S(2)}) copy-start(bf16[128,256]{1,0:T(8,128)(2,1)S(1)} %collective-permute-done.12.refs_7_) | copy-start | bytes 196612
  78.2 1.3 %collective-permute-start.16 = (bf16[128,256]{1,0:T(8,128)(2,1)S(1)}, bf16[128,256]{1,0:T(8,128)(2,1)S(1)}, u32[]{:S(2)}, u32[]{:S(2)}) collective-permute-start(bf16[128,256]{1,0:T(8,128)(2,1)S(1)} %collective-permute-done.12.refs_7_), channel_id=1, source_target_pairs={{0,8},{8,0},{1,9},{9,1},{2,10},{10,2},{3,11},{11,3},{4,12},{12,4},... | collective-permute-start | bytes 196616 | tf_op jit(solution)/shard_map/ppermute | solution.py:290
  79.1 1.3 %copy-start.17 = (bf16[128,256]{1,0:T(8,128)(2,1)}, bf16[128,256]{1,0:T(8,128)(2,1)S(1)}, u32[]{:S(2)}) copy-start(bf16[128,256]{1,0:T(8,128)(2,1)S(1)} %collective-permute-done.13.refs_8_) | copy-start | bytes 196612
  79.1 1.3 %collective-permute-start.17 = (bf16[128,256]{1,0:T(8,128)(2,1)S(1)}, bf16[128,256]{1,0:T(8,128)(2,1)S(1)}, u32[]{:S(2)}, u32[]{:S(2)}) collective-permute-start(bf16[128,256]{1,0:T(8,128)(2,1)S(1)} %collective-permute-done.13.refs_8_), channel_id=1, source_target_pairs={{0,8},{8,0},{1,9},{9,1},{2,10},{10,2},{3,11},{11,3},{4,12},{12,4},... | collective-permute-start | bytes 196616 | tf_op jit(solution)/shard_map/ppermute | solution.py:290
  79.1 1.2 %copy-start.18 = (bf16[128,256]{1,0:T(8,128)(2,1)}, bf16[128,256]{1,0:T(8,128)(2,1)S(1)}, u32[]{:S(2)}) copy-start(bf16[128,256]{1,0:T(8,128)(2,1)S(1)} %collective-permute-done.14.refs_9_) | copy-start | bytes 196612
  79.1 1.2 %copy-start.19 = (bf16[128,256]{1,0:T(8,128)(2,1)}, bf16[128,256]{1,0:T(8,128)(2,1)S(1)}, u32[]{:S(2)}) copy-start(bf16[128,256]{1,0:T(8,128)(2,1)S(1)} %collective-permute-done.15.refs_10_) | copy-start | bytes 196612
  79.4 0.9 copy-start.20
  80.4 0.6 copy-start.21
  104.4 14.6 %all-to-all-start.3 = ((bf16[16,64,256]{2,1,0:T(8,128)(2,1)}), bf16[16,64,256]{2,1,0:T(8,128)(2,1)S(1)}, u32[]{:S(2)}, u32[]{:S(2)}) async-start(bf16[16,64,256]{2,1,0:T(8,128)(2,1)} %bitcast.9), calls=%async_computation.3 | async-start | bytes 1048576 | tf_op jit(solution)/shard_map/all_to_all | solution.py:306

commit v9 on v8

--- a/solution.py
+++ b/solution.py
@@ -10,7 +10,7 @@
 SPAN = 64
 LOG2E = 1.4426950408889634
 SEQ = ("zhi", "y")
-OWN = ("zlo", "zhi", "y")
+DEPTH = ("zlo", "zhi")
 
 
 def nt(a, b):
@@ -222,63 +222,135 @@
     )(where, order, lens, query, grad, key_value)
 
 
-def term_kernel(count, other_ref, *refs):
-    parts, pieces, out_ref = refs[:count], refs[count:-1], refs[-1]
-    width = out_ref.shape[1]
-    at = pl.multiple_of(pl.program_id(0) * width, width)
+def product(parts, other_ref, pieces, at, width):
     left = jnp.concatenate([part[...] for part in parts] + [other_ref[...]], axis=1)
     right = jnp.concatenate([g[:, pl.ds(at, width)] for g in pieces], axis=0)
-    out_ref[...] = nn(left, right).astype(out_ref.dtype)
-
-
-def term(parts, other, pieces, limit, name):
+    return nn(left, right).astype(jnp.bfloat16)
+
+
+def term_query_kernel(count, other_ref, *refs):
+    parts, pieces, out_ref = refs[:count], refs[count:-1], refs[-1]
+    blocks, _, width = out_ref.shape
+    at = pl.multiple_of(pl.program_id(0) * width, width)
+    part = product(parts, other_ref, pieces, at, width)
+    rows = part.shape[0] // (blocks * blocks)
+    for i in range(blocks):
+        for y in range(blocks):
+            here = (i * blocks + y) * rows
+            out_ref[y, i * rows : (i + 1) * rows, :] = part[here : here + rows]
+
+
+def term_query(parts, other, pieces, blocks):
     half = other.shape[0]
     width = pieces[0].shape[1]
     step = 2 * HD
     return pl.pallas_call(
-        lambda *refs: term_kernel(len(parts), *refs),
+        lambda *refs: term_query_kernel(len(parts), *refs),
         grid=(width // step,),
-        out_shape=pltpu.HBM((half, width), jnp.bfloat16),
+        out_shape=pltpu.HBM((blocks, half // blocks, width), jnp.bfloat16),
         in_specs=[whole(other)] + [half_of(part, 0) for part in parts] + [VMEM] * len(pieces),
-        out_specs=pl.BlockSpec((half, step), lambda j: (0, j)),
-        compiler_params=pltpu.CompilerParams(vmem_limit_bytes=limit * MIB),
-        cost_estimate=SMALL,
-        name=name,
+        out_specs=pl.BlockSpec((blocks, half // blocks, step), lambda j: (0, 0, j)),
+        compiler_params=pltpu.CompilerParams(vmem_limit_bytes=60 * MIB),
+        cost_estimate=SMALL,
+        name="term_query",
     )(other, *parts, *pieces)
 
 
-def sum_kernel(stack_ref, out_ref):
+def term_kv_kernel(count, where_ref, other_ref, *refs):
+    parts, pieces, outs, full_ref = refs[:count], refs[count:-5], refs[-5:-1], refs[-1]
+    full_ref[...] = product(parts, other_ref, pieces, 0, full_ref.shape[1])
+    blocks = len(outs)
+    rows = full_ref.shape[0] // (blocks * blocks)
+    for s in range(blocks):
+        y = lax.rem(where_ref[3] + s, blocks)
+        for i in range(blocks):
+            at = pl.multiple_of((i * blocks + y) * rows, rows)
+            outs[s][i * rows : (i + 1) * rows, :] = full_ref[pl.ds(at, rows), :]
+
+
+def term_kv(where, parts, other, pieces, blocks):
+    half = other.shape[0]
+    width = pieces[0].shape[1]
+    out = pltpu.HBM((half // blocks, width), jnp.bfloat16)
+    return pl.pallas_call(
+        lambda *refs: term_kv_kernel(len(parts), *refs),
+        grid=(1,),
+        out_shape=(out,) * blocks,
+        in_specs=[SMEM, whole(other)] + [half_of(part, 0) for part in parts] + [VMEM] * len(pieces),
+        out_specs=(pl.BlockSpec(out.shape, lambda j: (0, 0)),) * blocks,
+        scratch_shapes=[pltpu.VMEM((half, width), jnp.bfloat16)],
+        compiler_params=pltpu.CompilerParams(vmem_limit_bytes=60 * MIB),
+        cost_estimate=SMALL,
+        name="term_kv",
+    )(where, other, *parts, *pieces)
+
+
+def middle_kernel(stack_ref, *refs):
+    parts, out_ref = refs[:-1], refs[-1]
+    first = stack_ref.shape[2]
+    blocks, rows, _ = out_ref.shape
+    for i in range(blocks):
+        here = slice(i * rows, (i + 1) * rows)
+        query = sum(stack_ref[j, here, :].astype(jnp.float32) for j in range(stack_ref.shape[0]))
+        out_ref[i, :, :first] = query.astype(out_ref.dtype)
+        out_ref[i, :, first:] = sum(part[here, :].astype(jnp.float32) for part in parts).astype(out_ref.dtype)
+
+
+def middle(stack, parts):
+    blocks, rows, width = stack.shape
+    out = pltpu.HBM((blocks, rows // blocks, width + parts[0].shape[1]), jnp.bfloat16)
+    return pl.pallas_call(
+        middle_kernel,
+        grid=(1,),
+        out_shape=out,
+        in_specs=[VMEM] * (1 + len(parts)),
+        out_specs=pl.BlockSpec(out.shape, lambda i: (0, 0, 0)),
+        compiler_params=pltpu.CompilerParams(vmem_limit_bytes=14 * MIB),
+        cost_estimate=SMALL,
+        name="middle",
+    )(stack, *parts)
+
+
+def final_kernel(stack_ref, out_ref):
     out_ref[...] = sum(stack_ref[i].astype(jnp.float32) for i in range(stack_ref.shape[0]))
 
 
-def sum_query(stack):
-    return pl.pallas_call(
-        sum_kernel,
+def final(stack):
+    return pl.pallas_call(
+        final_kernel,
         out_shape=jax.ShapeDtypeStruct(stack.shape[1:], jnp.float32),
         in_specs=[VMEM],
         out_specs=VMEM,
-        compiler_params=pltpu.CompilerParams(vmem_limit_bytes=12 * MIB),
-        cost_estimate=SMALL,
-        name="sum_query",
+        compiler_params=pltpu.CompilerParams(vmem_limit_bytes=8 * MIB),
+        cost_estimate=SMALL,
+        name="final",
     )(stack)
 
 
-def final_kernel(query_ref, stack_ref, out_ref):
-    first = query_ref.shape[1]
-    out_ref[:, :first] = query_ref[...]
-    out_ref[:, first:] = sum(stack_ref[i].astype(jnp.float32) for i in range(stack_ref.shape[0]))
-
-
-def final(query, stack):
-    return pl.pallas_call(
-        final_kernel,
-        out_shape=jax.ShapeDtypeStruct((query.shape[0], query.shape[1] + stack.shape[2]), jnp.float32),
-        in_specs=[VMEM, VMEM],
-        out_specs=VMEM,
-        compiler_params=pltpu.CompilerParams(vmem_limit_bytes=8 * MIB),
-        cost_estimate=SMALL,
-        name="final",
-    )(query, stack)
+def input_query_kernel(g_ref, w_ref, out_ref):
+    out_ref[...] = nt(g_ref[...], w_ref[...]).astype(out_ref.dtype)
+
+
+def input_last_kernel(g_ref, w_ref, part_ref, out_ref):
+    out_ref[...] = (part_ref[...].astype(jnp.float32) + nt(g_ref[...], w_ref[...])).astype(out_ref.dtype)
+
+
+def input_grad(grad, w, at, partial=()):
+    tokens, width = grad.shape
+    features = w.shape[0]
+    step = 2048
+    out = pltpu.HBM((tokens, features), jnp.bfloat16)
+    block = pl.BlockSpec((tokens, step), lambda i: (0, i))
+    return pl.pallas_call(
+        input_last_kernel if partial else input_query_kernel,
+        grid=(features // step,),
+        out_shape=out,
+        in_specs=[pl.BlockSpec((tokens, width), lambda i: (0, 0)), pl.BlockSpec((step, width), lambda i: (i, at))] + [block] * len(partial),
+        out_specs=block,
+        compiler_params=pltpu.CompilerParams(vmem_limit_bytes=60 * MIB),
+        cost_estimate=SMALL,
+        name="d_x_last" if partial else "d_x_query",
+    )(grad, w, *partial)
 
 
 def shifted(value, s):
@@ -301,9 +373,8 @@
     return lax.optimization_barrier((value,) + others)[0]
 
 
-def to_owners(value):
-    owners = lax.axis_size("zlo") * lax.axis_size("zhi") * lax.axis_size("y")
-    return lax.all_to_all(value.reshape(owners, value.shape[0] // owners, value.shape[1]), OWN, 0, 0, tiled=True)
+def shifted_y(value, s):
+    return lax.ppermute(value, "y", [(i, (i + s) % 4) for i in range(4)])
 
 
 def local(layer_input, w_qkv, d_out, span_order, doc_lengths):
@@ -312,26 +383,29 @@
     chips = lax.axis_size("x")
     seq = lax.axis_size("zhi") * lax.axis_size("y")
     place = lax.axis_index("zhi") * lax.axis_size("y") + lax.axis_index("y")
-    where = jnp.stack([lax.axis_index("x"), lax.axis_index("core"), place]).astype(jnp.int32)
+    where = jnp.stack([lax.axis_index("x"), lax.axis_index("core"), place, lax.axis_index("y")]).astype(jnp.int32)
 
     copies, *packed = first(where, rows, w_qkv, seq, chips)
     gathered = lax.all_to_all(copies, SEQ, 0, 0, tiled=True).reshape(seq * tokens, 2 * HD)
     pieces = [packed[0]] + [shifted(packed[s], s) for s in range(1, chips)]
     query = project_query(after(rows, copies), w_qkv)
     d_query, terms = attention(where, span_order, doc_lengths, query, d_out[0], gathered)
-    own_q, other_q = gather_chips(d_query)
+    own_q = [d_query] + [shifted(d_query, s) for s in range(1, chips)]
+    other_q = [swapped(d_query)]
     arrived = lax.all_to_all(after(terms, other_q[0]).reshape(seq, tokens, 2 * HD), SEQ, 0, 0, tiled=True)
     x_other = swapped(forward([after(piece, terms) for piece in pieces]))
-
-    term_query = term(pieces, x_other, own_q + other_q, 60, "term_query")
-    received_query = to_owners(term_query)
+    d_x_query = input_grad(after(d_query, terms,other_q[0]), w_qkv, 0)
+
+    other_q += [swapped(after(piece, d_x_query)) for piece in own_q[1:]]
+    places = lax.axis_size("y")
+    stacked = term_query(pieces, x_other, own_q + other_q, places)
+    group_query = lax.all_to_all(stacked, "y", 0, 0, tiled=True)
     owned = jnp.sum(arrived.astype(jnp.float32), axis=0).astype(jnp.bfloat16)
-    own_kv, other_kv = gather_chips(after(owned, term_query))
-    term_kv = term(pieces, x_other, own_kv + other_kv, 60, "term_kv")
-    d_qkv = after(jnp.concatenate([d_query, owned], axis=1), term_kv)
-    d_rows = nt(d_qkv, w_qkv).astype(jnp.bfloat16)
-    received_kv = to_owners(after(term_kv, received_query, d_rows))
-    d_w = final(sum_query(received_query), received_kv)
+    own_kv, other_kv = gather_chips(after(owned, stacked))
+    parts = term_kv(where, pieces, x_other, own_kv + other_kv, places)
+    d_rows = input_grad(after(owned, parts[0]), w_qkv, HQ // 2, (d_x_query,))
+    group_kv = [parts[0]] + [after(shifted_y(parts[s], s), d_rows) for s in range(1, places)]
+    d_w = final(lax.all_to_all(middle(group_query, group_kv), DEPTH, 0, 0, tiled=True))
     return (d_rows[None], d_w)
 
 

time: 120 us -> 125 us (1.042)
  Pallas kernels: 32.4 us -> 49.3 us
  waiting for transfers between devices: 33.4 us -> 17.2 us
  blocking collectives: 0 us -> 14.1 us
  matrix products: 12.5 us -> 0 us
  starting transfers between devices: 37.5 us -> 39.2 us
    all_to_all x2 -> x1, waiting for transfers between devices: 18.5 us -> 0.01 us  [local(): group_query = lax.all_to_all(stacked, 'y', 0, 0, tiled=True)]
    pallas_call x4 -> x6, Pallas kernels: 10.3 us -> 27.1 us  [the longest x2 16 us: input_grad(): pl.pallas_call(input_last_kernel if partial else input_query_kernel, grid...]
    all_to_all x0 -> x1, blocking collectives: none -> 14.1 us  [local(): lax.all_to_all(middle(group_query, group_kv), DEPTH, 0, 0, tiled=True)]
    dot_general x1 -> x0, matrix products: 12.5 us -> none  [nt(): lax.dot_general(a, b, (((1,), (1,)), ((), ())), preferred_element_type=jn...]
    ppermute x0 -> x3, waiting for transfers between devices: none -> 8.05 us  [shifted_y(): return lax.ppermute(value, 'y', [(i, (i + s) % 4) for i in range(4)])]
    ppermute x0 -> x3, starting transfers between devices: none -> 5.99 us  [shifted_y(): return lax.ppermute(value, 'y', [(i, (i + s) % 4) for i in range(4)])]
    ppermute x9, waiting for transfers between devices: 9.01 us -> 3.04 us  [shifted(): return lax.ppermute(value, 'x', [(i, (i + s) % n) for i in range(n)])]
    all_to_all x2 -> x1, starting transfers between devices: 8.2 us -> 4.79 us  [local(): group_query = lax.all_to_all(stacked, 'y', 0, 0, tiled=True)]
  transfers between devices with their start and end apart: 22 -> 24, of which waited for: 13 -> 11; matrix products, arithmetic and copies ran while one was open for 11% -> 0% of each run, Pallas kernels for 20% -> 32%
where the time goes in v9:
time: 125 us; the launch traced here: 124 us
  Pallas kernels  49.3 us (39%)
  starting transfers between devices  39.2 us (31%)
  waiting for transfers between devices  17.2 us (14%)
  blocking collectives  14.1 us (11%)
  local copies, waits for them, and re-layouts  2.55 us (2%)
    pallas_call x2, Pallas kernels, input_grad(): pl.pallas_call(input_last_kernel if partial else input_query_kernel, grid...  16 us
    all_to_all x1, blocking collectives, local(): lax.all_to_all(middle(group_query, group_kv), DEPTH, 0, 0, tiled=True)  14.1 us
    ppermute x9, starting transfers between devices, shifted(): return lax.ppermute(value, 'x', [(i, (i + s) % n) for i in range(n)])  12.6 us
    ppermute x3, waiting for transfers between devices, shifted_y(): return lax.ppermute(value, 'y', [(i, (i + s) % 4) for i in range(4)])  8.05 us
    all_to_all x1, starting transfers between devices, local(): lax.all_to_all(copies, SEQ, 0, 0, tiled=True).reshape(seq * tokens, 2 * HD)  7.78 us
    pallas_call x1, Pallas kernels, project_query(): pl.pallas_call(query_kernel, grid=(HQ // 2,), out_shape=jax.ShapeDtypeStr...  7.42 us
    pallas_call x1, Pallas kernels, attention(): pl.pallas_call(attention_kernel, out_shape=(pltpu.HBM((tokens, HQ * HD),...  6.85 us
    all_to_all x1, starting transfers between devices, local(): lax.all_to_all(after(terms, other_q[0]).reshape(seq, tokens, 2 * HD), SEQ...  6.1 us
  transfers between devices with their start and end apart: 24, of which 11 were waited for; matrix products, arithmetic and copies ran while one was open for 0% of the time, Pallas kernels for 32%

profile of v9, /device:TPU:0, one launch (start us, length us, event | category | flops | bytes accessed | tf_op | source)
XLA Modules:
  0.0 124.0 jit_solution(12419664808611829740)
XLA Ops:
  0.6 0.7 pad_add_fusion.where_ref.refs_0_
  1.3 5.5 %first.1 = (bf16[8,128,256]{2,1,0:T(8,128)(2,1)}, bf16[2048,128]{1,0:T(8,128)(2,1)}, bf16[2048,128]{1,0:T(8,128)(2,1)}, bf16[2048,128]{1,0:T(8,128)(2,1)}, bf16[2048,128]{1,0:T(8,128)(2,1)}) custom-call(s32[4]{0:T(128)} %pad_add_fusion.where_ref.refs_0_, bf16[128,8192]{1,0:T(8,128)(2,1)} %bitcast.9, bf16[8192,1280]{1,0:T(8,128)(2,1)} %w_ref.5), custom_call_target="tpu_custom_call" | custom-call | flops 1 | bytes 1 | tf_op jit(solution)/shard_map/first/pallas_call | solution.py:82
  6.8 1.6 %collective-permute-start.1 = (bf16[2048,128]{1,0:T(8,128)(2,1)}, bf16[2048,128]{1,0:T(8,128)(2,1)}, u32[]{:S(2)}, u32[]{:S(2)}) collective-permute-start(bf16[2048,128]{1,0:T(8,128)(2,1)} %get-tuple-element.35), channel_id=1, source_target_pairs={{0,16},{16,32},{32,48},{48,0},{1,17},{17,33},{33,49},{49,1},{2,18}... | collective-permute-start | bytes 1572872 | tf_op jit(solution)/shard_map/ppermute | solution.py:358
  8.5 2.7 %collective-permute-start.2 = (bf16[2048,128]{1,0:T(8,128)(2,1)}, bf16[2048,128]{1,0:T(8,128)(2,1)}, u32[]{:S(2)}, u32[]{:S(2)}) collective-permute-start(bf16[2048,128]{1,0:T(8,128)(2,1)} %get-tuple-element.37), channel_id=1, source_target_pairs={{0,32},{16,48},{32,0},{48,16},{1,33},{17,49},{33,1},{49,17},{2,34}... | collective-permute-start | bytes 1572872 | tf_op jit(solution)/shard_map/ppermute | solution.py:358
  11.2 1.4 %collective-permute-start.3 = (bf16[2048,128]{1,0:T(8,128)(2,1)}, bf16[2048,128]{1,0:T(8,128)(2,1)}, u32[]{:S(2)}, u32[]{:S(2)}) collective-permute-start(bf16[2048,128]{1,0:T(8,128)(2,1)} %get-tuple-element.39), channel_id=1, source_target_pairs={{0,48},{16,0},{32,16},{48,32},{1,49},{17,1},{33,17},{49,33},{2,50}... | collective-permute-start | bytes 1572872 | tf_op jit(solution)/shard_map/ppermute | solution.py:358
  12.7 7.8 %all-to-all-start = ((bf16[8,128,256]{2,1,0:T(8,128)(2,1)}), bf16[8,128,256]{2,1,0:T(8,128)(2,1)S(1)}, u32[]{:S(2)}, u32[]{:S(2)}) async-start(bf16[8,128,256]{2,1,0:T(8,128)(2,1)} %get-tuple-element.28), calls=%async_computation | async-start | bytes 1048576 | tf_op jit(solution)/shard_map/all_to_all | solution.py:389
  20.5 7.4 %project_query.1.q_ref = bf16[128,1024]{1,0:T(8,128)(2,1)S(1)} custom-call(bf16[128,8192]{1,0:T(8,128)(2,1)S(1)} %bitcast.10, bf16[8192,1280]{1,0:T(8,128)(2,1)} %w_ref.5), custom_call_target="tpu_custom_call" | custom-call | flops 1 | bytes 1 | tf_op jit(solution)/shard_map/project_query/pallas_call | solution.py:110
  27.9 3.3 %all-to-all-done = bf16[8,128,256]{2,1,0:T(8,128)(2,1)S(1)} async-done(((bf16[8,128,256]{2,1,0:T(8,128)(2,1)}), bf16[8,128,256]{2,1,0:T(8,128)(2,1)S(1)}, u32[]{:S(2)}, u32[]{:S(2)}) %all-to-all-start) | async-done | bytes 524320 | tf_op jit(solution)/shard_map/all_to_all | solution.py:389
  31.2 6.9 %attention.1 = (bf16[128,1024]{1,0:T(8,128)(2,1)}, bf16[1024,256]{1,0:T(8,128)(2,1)}) custom-call(s32[4]{0:T(128)S(1)} %copy-done.3, s32[1,16]{1,0:T(1,128)S(1)} %copy-done.4, s32[1,4]{1,0:T(1,128)S(1)} %copy-done.5, bf16[128,1024]{1,0:T(8,128)(2,1)S(1)} %project_query.1.q_ref, bf16[128,1024]{1,0:T(8,128)(2,1)S(1)} %bitcast.12, bf16[1024,256]{1,0:T(8,128)(2,1)S(1)} %bitcast.11), custom_call_target="tpu_custom_call" | custom-call | flops 1 | bytes 1 | tf_op jit(solution)/shard_map/attention/pallas_call | solution.py:205
  38.1 2.4 %forward.1 = bf16[1024,512]{1,0:T(8,128)(2,1)} custom-call(bf16[2048,128]{1,0:T(8,128)(2,1)} %get-tuple-element.34.refs_0_.refs_1_.refs_2_, bf16[2048,128]{1,0:T(8,128)(2,1)} %collective-permute-done.1.refs_1_.refs_2_.refs_3_, bf16[2048,128]{1,0:T(8,128)(2,1)} %collective-permute-done.2.refs_2_.refs_3_.refs_4_, ...), custom_call_target="tpu_custom_call" | custom-call | flops 1 | bytes 1 | tf_op jit(solution)/shard_map/forward/pallas_call | solution.py:136
  40.5 0.5 collective-permute-start
  41.0 0.6 collective-permute-start.5
  41.6 1.2 collective-permute-start.6
  42.7 1.5 %collective-permute-start.7 = (bf16[128,1024]{1,0:T(8,128)(2,1)S(1)}, bf16[128,1024]{1,0:T(8,128)(2,1)S(1)}, u32[]{:S(2)}, u32[]{:S(2)}) collective-permute-start(bf16[128,1024]{1,0:T(8,128)(2,1)S(1)} %copy-done.7), channel_id=1, source_target_pairs={{0,48},{16,0},{32,16},{48,32},{1,49},{17,1},{33,17},{49,33},{2,50}... | collective-permute-start | bytes 786440 | tf_op jit(solution)/shard_map/ppermute | solution.py:358
  44.2 6.1 %all-to-all-start.1 = ((bf16[8,128,256]{2,1,0:T(8,128)(2,1)}), bf16[8,128,256]{2,1,0:T(8,128)(2,1)S(1)}, u32[]{:S(2)}, u32[]{:S(2)}) async-start(bf16[8,128,256]{2,1,0:T(8,128)(2,1)} %bitcast.7), calls=%async_computation.1 | async-start | bytes 1048576 | tf_op jit(solution)/shard_map/all_to_all | solution.py:395
  50.3 10.1 %d_x_query.1.part_ref = bf16[128,8192]{1,0:T(8,128)(2,1)} custom-call(bf16[128,1024]{1,0:T(8,128)(2,1)} %get-tuple-element.41.g_ref.refs_5_, bf16[8192,1280]{1,0:T(8,128)(2,1)} %w_ref.5), custom_call_target="tpu_custom_call" | custom-call | flops 1 | bytes 1 | tf_op jit(solution)/shard_map/d_x_query/pallas_call | solution.py:344
  60.5 0.3 collective-permute-start.8
  60.8 0.5 collective-permute-start.9
  61.3 0.1 collective-permute-start.10
  61.4 0.9 collective-permute-done.8.refs_10_
  62.3 0.4 collective-permute-done.9.refs_11_
  62.7 0.4 collective-permute-done.10.refs_12_
  63.1 0.3 copy-done.14
  63.4 0.4 copy-done.15
  63.8 1.0 copy-done.6
  64.7 6.0 %term_query.1 = bf16[4,256,1024]{2,1,0:T(8,128)(2,1)} custom-call(bf16[1024,512]{1,0:T(8,128)(2,1)} %copy-done.6, bf16[2048,128]{1,0:T(8,128)(2,1)} %get-tuple-element.34.refs_0_.refs_1_.refs_2_, bf16[2048,128]{1,0:T(8,128)(2,1)} %collective-permute-done.1.refs_1_.refs_2_.refs_3_, bf16[2048,128]{1,0:T(8,128)(2,1)} %collective-permute-done.2.refs_2_.refs_3_.refs_4_, ...), custom_call_target="tpu_custom_call" | custom-call | flops 1 | bytes 1 | tf_op jit(solution)/shard_map/term_query/pallas_call | solution.py:247
  70.8 4.8 %all-to-all-start.2 = ((bf16[4,256,1024]{2,1,0:T(8,128)(2,1)}), bf16[4,256,1024]{2,1,0:T(8,128)(2,1)S(1)}, u32[]{:S(2)}, u32[]{:S(2)}) async-start(bf16[4,256,1024]{2,1,0:T(8,128)(2,1)} %term_query.1), calls=%async_computation.2 | async-start | bytes 4194304 | tf_op jit(solution)/shard_map/all_to_all | solution.py:402
  75.6 0.1 reduce_sum.12.refs_6_.g_ref
  75.7 0.5 collective-permute-start.11
  76.2 1.1 collective-permute-start.12
  77.3 1.9 %collective-permute-start.13 = (bf16[128,256]{1,0:T(8,128)(2,1)S(1)}, bf16[128,256]{1,0:T(8,128)(2,1)S(1)}, u32[]{:S(2)}, u32[]{:S(2)}) collective-permute-start(bf16[128,256]{1,0:T(8,128)(2,1)S(1)} %reduce_sum.12.refs_6_.g_ref), channel_id=1, source_target_pairs={{0,48},{16,0},{32,16},{48,32},{1,49},{17,1},{33,17},{49,33},{2,50}... | collective-permute-start | bytes 196616 | tf_op jit(solution)/shard_map/ppermute | solution.py:358
  79.2 3.0 %collective-permute-done.11.refs_7_ = bf16[128,256]{1,0:T(8,128)(2,1)S(1)} collective-permute-done((bf16[128,256]{1,0:T(8,128)(2,1)S(1)}, bf16[128,256]{1,0:T(8,128)(2,1)S(1)}, u32[]{:S(2)}, u32[]{:S(2)}) %collective-permute-start.11) | collective-permute-done | bytes 65568 | tf_op jit(solution)/shard_map/ppermute | solution.py:358
  82.2 0.5 collective-permute-start.16
  82.8 0.6 collective-permute-done.15.refs_11_
  83.5 0.2 collective-permute-done.16.refs_12_
  83.6 0.4 collective-permute-done.17.refs_13_
  84.1 0.2 copy-done.21
  84.2 0.6 copy-done.22
  84.9 3.1 %term_kv.1 = (bf16[256,256]{1,0:T(8,128)(2,1)}, bf16[256,256]{1,0:T(8,128)(2,1)}, bf16[256,256]{1,0:T(8,128)(2,1)}, bf16[256,256]{1,0:T(8,128)(2,1)}) custom-call(s32[4]{0:T(128)} %pad_add_fusion.where_ref.refs_0_, bf16[1024,512]{1,0:T(8,128)(2,1)} %copy-done.6, bf16[2048,128]{1,0:T(8,128)(2,1)} %get-tuple-element.34.refs_0_.refs_1_.refs_2_, ...), custom_call_target="tpu_custom_call" | custom-call | flops 1 | bytes 1 | tf_op jit(solution)/shard_map/term_kv/pallas_call | solution.py:275
  88.0 1.8 %collective-permute-start.18 = (bf16[256,256]{1,0:T(8,128)(2,1)}, bf16[256,256]{1,0:T(8,128)(2,1)S(1)}, u32[]{:S(2)}, u32[]{:S(2)}) collective-permute-start(bf16[256,256]{1,0:T(8,128)(2,1)} %get-tuple-element.48), channel_id=1, source_target_pairs={{0,1},{1,2},{2,3},{3,0},{4,5},{5,6},{6,7},{7,4},{8,9},{9,10},{10,1... | collective-permute-start | bytes 393224 | tf_op jit(solution)/shard_map/ppermute | solution.py:377
  89.9 2.7 %collective-permute-start.19 = (bf16[256,256]{1,0:T(8,128)(2,1)}, bf16[256,256]{1,0:T(8,128)(2,1)S(1)}, u32[]{:S(2)}, u32[]{:S(2)}) collective-permute-start(bf16[256,256]{1,0:T(8,128)(2,1)} %get-tuple-element.50), channel_id=1, source_target_pairs={{0,2},{1,3},{2,0},{3,1},{4,6},{5,7},{6,4},{7,5},{8,10},{9,11},{10,... | collective-permute-start | bytes 393224 | tf_op jit(solution)/shard_map/ppermute | solution.py:377
  92.5 1.5 %collective-permute-start.20 = (bf16[256,256]{1,0:T(8,128)(2,1)}, bf16[256,256]{1,0:T(8,128)(2,1)S(1)}, u32[]{:S(2)}, u32[]{:S(2)}) collective-permute-start(bf16[256,256]{1,0:T(8,128)(2,1)} %get-tuple-element.52), channel_id=1, source_target_pairs={{0,3},{1,0},{2,1},{3,2},{4,7},{5,4},{6,5},{7,6},{8,11},{9,8},{10,9... | collective-permute-start | bytes 393224 | tf_op jit(solution)/shard_map/ppermute | solution.py:377
  94.0 5.8 %d_x_last.1 = bf16[128,8192]{1,0:T(8,128)(2,1)} custom-call(bf16[128,256]{1,0:T(8,128)(2,1)} %copy-done.8, bf16[8192,1280]{1,0:T(8,128)(2,1)} %w_ref.5, bf16[128,8192]{1,0:T(8,128)(2,1)} %d_x_query.1.part_ref), custom_call_target="tpu_custom_call" | custom-call | flops 1 | bytes 1 | tf_op jit(solution)/shard_map/d_x_last/pallas_call | solution.py:344
  99.8 6.3 %collective-permute-done.18.refs_1_ = bf16[256,256]{1,0:T(8,128)(2,1)S(1)} collective-permute-done((bf16[256,256]{1,0:T(8,128)(2,1)}, bf16[256,256]{1,0:T(8,128)(2,1)S(1)}, u32[]{:S(2)}, u32[]{:S(2)}) %collective-permute-start.18) | collective-permute-done | bytes 131104 | tf_op jit(solution)/shard_map/ppermute | solution.py:377
  106.1 1.8 %collective-permute-done.19.refs_2_ = bf16[256,256]{1,0:T(8,128)(2,1)S(1)} collective-permute-done((bf16[256,256]{1,0:T(8,128)(2,1)}, bf16[256,256]{1,0:T(8,128)(2,1)S(1)}, u32[]{:S(2)}, u32[]{:S(2)}) %collective-permute-start.19) | collective-permute-done | bytes 131104 | tf_op jit(solution)/shard_map/ppermute | solution.py:377
  107.9 1.2 middle.1
  109.1 14.1 %all_to_all.20.stack_ref = bf16[4,64,1280]{2,1,0:T(8,128)(2,1)S(1)} all-to-all(bf16[4,64,1280]{2,1,0:T(8,128)(2,1)} %middle.1), channel_id=1, replica_groups=mesh['zlo'=2,'x'=4,'core'=2,'zhi'=2,'y'=4] {'zlo','zhi'}, dimensions={0} | all-to-all | bytes 1310720 | tf_op jit(solution)/shard_map/all_to_all | solution.py:408
  123.2 0.8 final.1
  (59 shorter events, 0.2 us)
Async XLA Ops:
  1.3 19.1 %copy-start = (bf16[1,128,8192]{2,1,0:T(8,128)(2,1)S(1)}, bf16[1,128,8192]{2,1,0:T(8,128)(2,1)}, u32[]{:S(2)}) copy-start(bf16[1,128,8192]{2,1,0:T(8,128)(2,1)} %param.5) | copy-start | bytes 6291460
  6.8 31.2 %collective-permute-start.1 = (bf16[2048,128]{1,0:T(8,128)(2,1)}, bf16[2048,128]{1,0:T(8,128)(2,1)}, u32[]{:S(2)}, u32[]{:S(2)}) collective-permute-start(bf16[2048,128]{1,0:T(8,128)(2,1)} %get-tuple-element.35), channel_id=1, source_target_pairs={{0,16},{16,32},{32,48},{48,0},{1,17},{17,33},{33,49},{49,1},{2,18}... | collective-permute-start | bytes 1572872 | tf_op jit(solution)/shard_map/ppermute | solution.py:358
  8.5 29.6 %collective-permute-start.2 = (bf16[2048,128]{1,0:T(8,128)(2,1)}, bf16[2048,128]{1,0:T(8,128)(2,1)}, u32[]{:S(2)}, u32[]{:S(2)}) collective-permute-start(bf16[2048,128]{1,0:T(8,128)(2,1)} %get-tuple-element.37), channel_id=1, source_target_pairs={{0,32},{16,48},{32,0},{48,16},{1,33},{17,49},{33,1},{49,17},{2,34}... | collective-permute-start | bytes 1572872 | tf_op jit(solution)/shard_map/ppermute | solution.py:358
  11.2 26.9 %collective-permute-start.3 = (bf16[2048,128]{1,0:T(8,128)(2,1)}, bf16[2048,128]{1,0:T(8,128)(2,1)}, u32[]{:S(2)}, u32[]{:S(2)}) collective-permute-start(bf16[2048,128]{1,0:T(8,128)(2,1)} %get-tuple-element.39), channel_id=1, source_target_pairs={{0,48},{16,0},{32,16},{48,32},{1,49},{17,1},{33,17},{49,33},{2,50}... | collective-permute-start | bytes 1572872 | tf_op jit(solution)/shard_map/ppermute | solution.py:358
  12.7 18.5 %all-to-all-start = ((bf16[8,128,256]{2,1,0:T(8,128)(2,1)}), bf16[8,128,256]{2,1,0:T(8,128)(2,1)S(1)}, u32[]{:S(2)}, u32[]{:S(2)}) async-start(bf16[8,128,256]{2,1,0:T(8,128)(2,1)} %get-tuple-element.28), calls=%async_computation | async-start | bytes 1048576 | tf_op jit(solution)/shard_map/all_to_all | solution.py:389
  20.4 10.7 %copy-start.1 = (bf16[1,128,1024]{2,1,0:T(8,128)(2,1)S(1)}, bf16[1,128,1024]{2,1,0:T(8,128)(2,1)}, u32[]{:S(2)}) copy-start(bf16[1,128,1024]{2,1,0:T(8,128)(2,1)} %param.7) | copy-start | bytes 786436
  20.5 10.7 %copy-start.3 = (s32[4]{0:T(128)S(1)}, s32[4]{0:T(128)}, u32[]{:S(2)}) copy-start(s32[4]{0:T(128)} %pad_add_fusion.where_ref.refs_0_) | copy-start | bytes 52
  20.5 10.7 %copy-start.4 = (s32[1,16]{1,0:T(1,128)S(1)}, s32[1,16]{1,0:T(1,128)}, u32[]{:S(2)}) copy-start(s32[1,16]{1,0:T(1,128)} %order_ref.1) | copy-start | bytes 196
  20.5 10.7 %copy-start.5 = (s32[1,4]{1,0:T(1,128)S(1)}, s32[1,4]{1,0:T(1,128)}, u32[]{:S(2)}) copy-start(s32[1,4]{1,0:T(1,128)} %lens_ref.1) | copy-start | bytes 52
  38.1 2.4 %copy-start.7 = (bf16[128,1024]{1,0:T(8,128)(2,1)S(1)}, bf16[128,1024]{1,0:T(8,128)(2,1)}, u32[]{:S(2)}) copy-start(bf16[128,1024]{1,0:T(8,128)(2,1)} %get-tuple-element.41.g_ref.refs_5_) | copy-start | bytes 786436
  40.5 22.6 %collective-permute-start.4 = (bf16[1024,512]{1,0:T(8,128)(2,1)}, bf16[1024,512]{1,0:T(8,128)(2,1)S(1)}, u32[]{:S(2)}, u32[]{:S(2)}) collective-permute-start(bf16[1024,512]{1,0:T(8,128)(2,1)} %forward.1), channel_id=1, source_target_pairs={{0,8},{8,0},{1,9},{9,1},{2,10},{10,2},{3,11},{11,3},{4,12},{12,4},... | collective-permute-start | bytes 3145736 | tf_op jit(solution)/shard_map/ppermute | solution.py:362
  40.5 3.8 %collective-permute-start = (bf16[128,1024]{1,0:T(8,128)(2,1)S(1)}, bf16[128,1024]{1,0:T(8,128)(2,1)S(1)}, u32[]{:S(2)}, u32[]{:S(2)}) collective-permute-start(bf16[128,1024]{1,0:T(8,128)(2,1)S(1)} %copy-done.7), channel_id=1, source_target_pairs={{0,8},{8,0},{1,9},{9,1},{2,10},{10,2},{3,11},{11,3},{4,12},{12,4},... | collective-permute-start | bytes 786440 | tf_op jit(solution)/shard_map/ppermute | solution.py:362
  41.0 19.5 %collective-permute-start.5 = (bf16[128,1024]{1,0:T(8,128)(2,1)S(1)}, bf16[128,1024]{1,0:T(8,128)(2,1)S(1)}, u32[]{:S(2)}, u32[]{:S(2)}) collective-permute-start(bf16[128,1024]{1,0:T(8,128)(2,1)S(1)} %copy-done.7), channel_id=1, source_target_pairs={{0,16},{16,32},{32,48},{48,0},{1,17},{17,33},{33,49},{49,1},{2,18}... | collective-permute-start | bytes 786440 | tf_op jit(solution)/shard_map/ppermute | solution.py:358
  41.6 19.2 %collective-permute-start.6 = (bf16[128,1024]{1,0:T(8,128)(2,1)S(1)}, bf16[128,1024]{1,0:T(8,128)(2,1)S(1)}, u32[]{:S(2)}, u32[]{:S(2)}) collective-permute-start(bf16[128,1024]{1,0:T(8,128)(2,1)S(1)} %copy-done.7), channel_id=1, source_target_pairs={{0,32},{16,48},{32,0},{48,16},{1,33},{17,49},{33,1},{49,17},{2,34}... | collective-permute-start | bytes 786440 | tf_op jit(solution)/shard_map/ppermute | solution.py:358
  42.7 18.6 %collective-permute-start.7 = (bf16[128,1024]{1,0:T(8,128)(2,1)S(1)}, bf16[128,1024]{1,0:T(8,128)(2,1)S(1)}, u32[]{:S(2)}, u32[]{:S(2)}) collective-permute-start(bf16[128,1024]{1,0:T(8,128)(2,1)S(1)} %copy-done.7), channel_id=1, source_target_pairs={{0,48},{16,0},{32,16},{48,32},{1,49},{17,1},{33,17},{49,33},{2,50}... | collective-permute-start | bytes 786440 | tf_op jit(solution)/shard_map/ppermute | solution.py:358
  44.2 16.3 %copy-start.9 = (bf16[128,1024]{1,0:T(8,128)(2,1)}, bf16[128,1024]{1,0:T(8,128)(2,1)S(1)}, u32[]{:S(2)}) copy-start(bf16[128,1024]{1,0:T(8,128)(2,1)S(1)} %collective-permute-done.refs_9_) | copy-start | bytes 786436
  44.2 26.5 %all-to-all-start.1 = ((bf16[8,128,256]{2,1,0:T(8,128)(2,1)}), bf16[8,128,256]{2,1,0:T(8,128)(2,1)S(1)}, u32[]{:S(2)}, u32[]{:S(2)}) async-start(bf16[8,128,256]{2,1,0:T(8,128)(2,1)} %bitcast.7), calls=%async_computation.1 | async-start | bytes 1048576 | tf_op jit(solution)/shard_map/all_to_all | solution.py:395
  60.5 2.6 %copy-start.10 = (bf16[128,1024]{1,0:T(8,128)(2,1)}, bf16[128,1024]{1,0:T(8,128)(2,1)S(1)}, u32[]{:S(2)}) copy-start(bf16[128,1024]{1,0:T(8,128)(2,1)S(1)} %collective-permute-done.5.refs_6_) | copy-start | bytes 786436
  60.5 1.8 %collective-permute-start.8 = (bf16[128,1024]{1,0:T(8,128)(2,1)S(1)}, bf16[128,1024]{1,0:T(8,128)(2,1)S(1)}, u32[]{:S(2)}, u32[]{:S(2)}) collective-permute-start(bf16[128,1024]{1,0:T(8,128)(2,1)S(1)} %collective-permute-done.5.refs_6_), channel_id=1, source_target_pairs={{0,8},{8,0},{1,9},{9,1},{2,10},{10,2},{3,11},{11,3},{4,12},{12,4},... | collective-permute-start | bytes 786440 | tf_op jit(solution)/shard_map/ppermute | solution.py:362
  60.8 2.3 %copy-start.11 = (bf16[128,1024]{1,0:T(8,128)(2,1)}, bf16[128,1024]{1,0:T(8,128)(2,1)S(1)}, u32[]{:S(2)}) copy-start(bf16[128,1024]{1,0:T(8,128)(2,1)S(1)} %collective-permute-done.6.refs_7_) | copy-start | bytes 786436
  60.8 1.9 %collective-permute-start.9 = (bf16[128,1024]{1,0:T(8,128)(2,1)S(1)}, bf16[128,1024]{1,0:T(8,128)(2,1)S(1)}, u32[]{:S(2)}, u32[]{:S(2)}) collective-permute-start(bf16[128,1024]{1,0:T(8,128)(2,1)S(1)} %collective-permute-done.6.refs_7_), channel_id=1, source_target_pairs={{0,8},{8,0},{1,9},{9,1},{2,10},{10,2},{3,11},{11,3},{4,12},{12,4},... | collective-permute-start | bytes 786440 | tf_op jit(solution)/shard_map/ppermute | solution.py:362
  61.3 1.8 %copy-start.12 = (bf16[128,1024]{1,0:T(8,128)(2,1)}, bf16[128,1024]{1,0:T(8,128)(2,1)S(1)}, u32[]{:S(2)}) copy-start(bf16[128,1024]{1,0:T(8,128)(2,1)S(1)} %collective-permute-done.7.refs_8_) | copy-start | bytes 786436
  61.3 1.8 %collective-permute-start.10 = (bf16[128,1024]{1,0:T(8,128)(2,1)S(1)}, bf16[128,1024]{1,0:T(8,128)(2,1)S(1)}, u32[]{:S(2)}, u32[]{:S(2)}) collective-permute-start(bf16[128,1024]{1,0:T(8,128)(2,1)S(1)} %collective-permute-done.7.refs_8_), channel_id=1, source_target_pairs={{0,8},{8,0},{1,9},{9,1},{2,10},{10,2},{3,11},{11,3},{4,12},{12,4},... | collective-permute-start | bytes 786440 | tf_op jit(solution)/shard_map/ppermute | solution.py:362
  62.3 0.8 copy-start.13
  62.7 0.7 copy-start.14
  63.0 0.7 copy-start.15
  63.8 1.0 copy-start.6
  70.8 37.1 %all-to-all-start.2 = ((bf16[4,256,1024]{2,1,0:T(8,128)(2,1)}), bf16[4,256,1024]{2,1,0:T(8,128)(2,1)S(1)}, u32[]{:S(2)}, u32[]{:S(2)}) async-start(bf16[4,256,1024]{2,1,0:T(8,128)(2,1)} %term_query.1), calls=%async_computation.2 | async-start | bytes 4194304 | tf_op jit(solution)/shard_map/all_to_all | solution.py:402
  75.6 8.4 %copy-start.8 = (bf16[128,256]{1,0:T(8,128)(2,1)}, bf16[128,256]{1,0:T(8,128)(2,1)S(1)}, u32[]{:S(2)}) copy-start(bf16[128,256]{1,0:T(8,128)(2,1)S(1)} %reduce_sum.12.refs_6_.g_ref) | copy-start | bytes 196612
  75.7 6.5 %collective-permute-start.11 = (bf16[128,256]{1,0:T(8,128)(2,1)S(1)}, bf16[128,256]{1,0:T(8,128)(2,1)S(1)}, u32[]{:S(2)}, u32[]{:S(2)}) collective-permute-start(bf16[128,256]{1,0:T(8,128)(2,1)S(1)} %reduce_sum.12.refs_6_.g_ref), channel_id=1, source_target_pairs={{0,16},{16,32},{32,48},{48,0},{1,17},{17,33},{33,49},{49,1},{2,18}... | collective-permute-start | bytes 196616 | tf_op jit(solution)/shard_map/ppermute | solution.py:358
  76.2 6.0 %collective-permute-start.12 = (bf16[128,256]{1,0:T(8,128)(2,1)S(1)}, bf16[128,256]{1,0:T(8,128)(2,1)S(1)}, u32[]{:S(2)}, u32[]{:S(2)}) collective-permute-start(bf16[128,256]{1,0:T(8,128)(2,1)S(1)} %reduce_sum.12.refs_6_.g_ref), channel_id=1, source_target_pairs={{0,32},{16,48},{32,0},{48,16},{1,33},{17,49},{33,1},{49,17},{2,34}... | collective-permute-start | bytes 196616 | tf_op jit(solution)/shard_map/ppermute | solution.py:358
  77.3 5.4 %collective-permute-start.13 = (bf16[128,256]{1,0:T(8,128)(2,1)S(1)}, bf16[128,256]{1,0:T(8,128)(2,1)S(1)}, u32[]{:S(2)}, u32[]{:S(2)}) collective-permute-start(bf16[128,256]{1,0:T(8,128)(2,1)S(1)} %reduce_sum.12.refs_6_.g_ref), channel_id=1, source_target_pairs={{0,48},{16,0},{32,16},{48,32},{1,49},{17,1},{33,17},{49,33},{2,50}... | collective-permute-start | bytes 196616 | tf_op jit(solution)/shard_map/ppermute | solution.py:358
  79.2 3.6 %collective-permute-start.14 = (bf16[128,256]{1,0:T(8,128)(2,1)S(1)}, bf16[128,256]{1,0:T(8,128)(2,1)S(1)}, u32[]{:S(2)}, u32[]{:S(2)}) collective-permute-start(bf16[128,256]{1,0:T(8,128)(2,1)S(1)} %reduce_sum.12.refs_6_.g_ref), channel_id=1, source_target_pairs={{0,8},{8,0},{1,9},{9,1},{2,10},{10,2},{3,11},{11,3},{4,12},{12,4},... | collective-permute-start | bytes 196616 | tf_op jit(solution)/shard_map/ppermute | solution.py:362
  82.2 1.8 %copy-start.16 = (bf16[128,256]{1,0:T(8,128)(2,1)}, bf16[128,256]{1,0:T(8,128)(2,1)S(1)}, u32[]{:S(2)}) copy-start(bf16[128,256]{1,0:T(8,128)(2,1)S(1)} %collective-permute-done.11.refs_7_) | copy-start | bytes 196612
  82.2 1.3 %collective-permute-start.15 = (bf16[128,256]{1,0:T(8,128)(2,1)S(1)}, bf16[128,256]{1,0:T(8,128)(2,1)S(1)}, u32[]{:S(2)}, u32[]{:S(2)}) collective-permute-start(bf16[128,256]{1,0:T(8,128)(2,1)S(1)} %collective-permute-done.11.refs_7_), channel_id=1, source_target_pairs={{0,8},{8,0},{1,9},{9,1},{2,10},{10,2},{3,11},{11,3},{4,12},{12,4},... | collective-permute-start | bytes 196616 | tf_op jit(solution)/shard_map/ppermute | solution.py:362
  82.2 1.8 %copy-start.17 = (bf16[128,256]{1,0:T(8,128)(2,1)}, bf16[128,256]{1,0:T(8,128)(2,1)S(1)}, u32[]{:S(2)}) copy-start(bf16[128,256]{1,0:T(8,128)(2,1)S(1)} %collective-permute-done.12.refs_8_) | copy-start | bytes 196612
  82.2 1.4 %collective-permute-start.16 = (bf16[128,256]{1,0:T(8,128)(2,1)S(1)}, bf16[128,256]{1,0:T(8,128)(2,1)S(1)}, u32[]{:S(2)}, u32[]{:S(2)}) collective-permute-start(bf16[128,256]{1,0:T(8,128)(2,1)S(1)} %collective-permute-done.12.refs_8_), channel_id=1, source_target_pairs={{0,8},{8,0},{1,9},{9,1},{2,10},{10,2},{3,11},{11,3},{4,12},{12,4},... | collective-permute-start | bytes 196616 | tf_op jit(solution)/shard_map/ppermute | solution.py:362
  82.8 1.3 %copy-start.18 = (bf16[128,256]{1,0:T(8,128)(2,1)}, bf16[128,256]{1,0:T(8,128)(2,1)S(1)}, u32[]{:S(2)}) copy-start(bf16[128,256]{1,0:T(8,128)(2,1)S(1)} %collective-permute-done.13.refs_9_) | copy-start | bytes 196612
  82.8 1.3 %collective-permute-start.17 = (bf16[128,256]{1,0:T(8,128)(2,1)S(1)}, bf16[128,256]{1,0:T(8,128)(2,1)S(1)}, u32[]{:S(2)}, u32[]{:S(2)}) collective-permute-start(bf16[128,256]{1,0:T(8,128)(2,1)S(1)} %collective-permute-done.13.refs_9_), channel_id=1, source_target_pairs={{0,8},{8,0},{1,9},{9,1},{2,10},{10,2},{3,11},{11,3},{4,12},{12,4},... | collective-permute-start | bytes 196616 | tf_op jit(solution)/shard_map/ppermute | solution.py:362
  82.8 1.2 copy-start.19
  83.5 0.6 copy-start.20
  83.6 0.6 copy-start.21
  84.2 0.6 copy-start.22
  88.0 18.1 %collective-permute-start.18 = (bf16[256,256]{1,0:T(8,128)(2,1)}, bf16[256,256]{1,0:T(8,128)(2,1)S(1)}, u32[]{:S(2)}, u32[]{:S(2)}) collective-permute-start(bf16[256,256]{1,0:T(8,128)(2,1)} %get-tuple-element.48), channel_id=1, source_target_pairs={{0,1},{1,2},{2,3},{3,0},{4,5},{5,6},{6,7},{7,4},{8,9},{9,10},{10,1... | collective-permute-start | bytes 393224 | tf_op jit(solution)/shard_map/ppermute | solution.py:377
  89.9 18.0 %collective-permute-start.19 = (bf16[256,256]{1,0:T(8,128)(2,1)}, bf16[256,256]{1,0:T(8,128)(2,1)S(1)}, u32[]{:S(2)}, u32[]{:S(2)}) collective-permute-start(bf16[256,256]{1,0:T(8,128)(2,1)} %get-tuple-element.50), channel_id=1, source_target_pairs={{0,2},{1,3},{2,0},{3,1},{4,6},{5,7},{6,4},{7,5},{8,10},{9,11},{10,... | collective-permute-start | bytes 393224 | tf_op jit(solution)/shard_map/ppermute | solution.py:377
  92.5 15.3 %collective-permute-start.20 = (bf16[256,256]{1,0:T(8,128)(2,1)}, bf16[256,256]{1,0:T(8,128)(2,1)S(1)}, u32[]{:S(2)}, u32[]{:S(2)}) collective-permute-start(bf16[256,256]{1,0:T(8,128)(2,1)} %get-tuple-element.52), channel_id=1, source_target_pairs={{0,3},{1,0},{2,1},{3,2},{4,7},{5,4},{6,5},{7,6},{8,11},{9,8},{10,9... | collective-permute-start | bytes 393224 | tf_op jit(solution)/shard_map/ppermute | solution.py:377
  94.0 13.9 %copy-start.2 = (bf16[256,256]{1,0:T(8,128)(2,1)S(1)}, bf16[256,256]{1,0:T(8,128)(2,1)}, u32[]{:S(2)}) copy-start(bf16[256,256]{1,0:T(8,128)(2,1)} %get-tuple-element.46.refs_0_) | copy-start | bytes 393220

commit v10 on v7

--- a/solution.py
+++ b/solution.py
@@ -9,6 +9,7 @@
 HQ = 8
 SPAN = 64
 LOG2E = 1.4426950408889634
+FIRST = 768
 SEQ = ("zhi", "y")
 DEPTH = ("zlo", "zhi")
 
@@ -222,7 +223,7 @@
 
 
 def term_query_kernel(*refs):
-    parts, pieces, out_ref = refs[:2], refs[2:-1], refs[-1]
+    parts, pieces, out_ref, done_ref = refs[:2], refs[2:-2], refs[-2], refs[-1]
     step = pl.program_id(0)
     width = out_ref.shape[2]
     at = pl.multiple_of(step * width, width)
@@ -231,22 +232,36 @@
     part = nn(left, right).astype(out_ref.dtype)
     blocks = out_ref.shape[0]
     rows = left.shape[0] // (blocks * blocks)
-    for i in range(blocks):
-        for y in range(blocks):
-            here = (i * blocks + y) * rows
-            out_ref[y, i * rows : (i + 1) * rows, :] = part[here : here + rows]
+
+    @pl.when(step < FIRST // (2 * HD))
+    def _():
+        for i in range(blocks):
+            for y in range(blocks):
+                here = (i * blocks + y) * rows
+                out_ref[y, i * rows : (i + 1) * rows, :] = part[here : here + rows]
+
+    @pl.when(step >= FIRST // (2 * HD))
+    def _():
+        done_ref[...] = part
 
 
 def term_query(parts, pieces, blocks):
     half = parts[0].shape[0]
     width = pieces[0].shape[1]
     step = 2 * HD
+    first = FIRST // step
     return pl.pallas_call(
         term_query_kernel,
         grid=(width // step,),
-        out_shape=pltpu.HBM((blocks, half // blocks, width), jnp.bfloat16),
+        out_shape=(
+            pltpu.HBM((blocks, half // blocks, FIRST), jnp.bfloat16),
+            pltpu.HBM((half, width - FIRST), jnp.bfloat16),
+        ),
         in_specs=[VMEM] * (len(parts) + len(pieces)),
-        out_specs=pl.BlockSpec((blocks, half // blocks, step), lambda j: (0, 0, j)),
+        out_specs=(
+            pl.BlockSpec((blocks, half // blocks, step), lambda j: (0, 0, jnp.minimum(j, first - 1))),
+            pl.BlockSpec((half, step), lambda j: (0, jnp.maximum(j - first, 0))),
+        ),
         compiler_params=pltpu.CompilerParams(vmem_limit_bytes=20 * MIB),
         cost_estimate=SMALL,
         name="term_query",
@@ -259,29 +274,31 @@
 
 
 def term_second_kernel(where_ref, *refs):
-    parts, pieces, outs = refs[:2], refs[2:-4], refs[-4:]
+    parts, done_ref, pieces, outs = refs[:2], refs[2], refs[3:-4], refs[-4:]
     rows = outs[0].shape[0]
+    done = done_ref.shape[1]
     right = jnp.concatenate([g[...] for g in pieces], axis=0)
     for s in range(4):
         at = pl.multiple_of(ring_block(where_ref, s) * rows, rows)
         left = jnp.concatenate([part[pl.ds(at, rows), :] for part in parts], axis=1)
-        outs[s][...] = nn(left, right).astype(outs[s].dtype)
-
-
-def term_second(where, parts, pieces):
+        outs[s][:, :done] = done_ref[pl.ds(at, rows), :]
+        outs[s][:, done:] = nn(left, right).astype(outs[s].dtype)
+
+
+def term_second(where, parts, done, pieces):
     half = parts[0].shape[0]
     width = pieces[0].shape[1]
-    out = pltpu.HBM((half // 4, width), jnp.bfloat16)
+    out = pltpu.HBM((half // 4, done.shape[1] + width), jnp.bfloat16)
     return pl.pallas_call(
         term_second_kernel,
         grid=(1,),
         out_shape=(out,) * 4,
-        in_specs=[SMEM] + [VMEM] * (len(parts) + len(pieces)),
+        in_specs=[SMEM] + [VMEM] * (1 + len(parts) + len(pieces)),
         out_specs=(pl.BlockSpec(out.shape, lambda i: (0, 0)),) * 4,
         compiler_params=pltpu.CompilerParams(vmem_limit_bytes=60 * MIB),
         cost_estimate=SMALL,
         name="term_second",
-    )(where, *parts, *pieces)
+    )(where, *parts, done, *pieces)
 
 
 def middle_z_kernel(stack_ref, out_ref):
@@ -331,14 +348,13 @@
 
 def final_kernel(stack_ref, *refs):
     parts, out_ref = refs[:-1], refs[-1]
-    first = stack_ref.shape[2]
-    out_ref[:, :first] = sum(stack_ref[i].astype(jnp.float32) for i in range(stack_ref.shape[0]))
-    out_ref[:, first:] = sum(part[...].astype(jnp.float32) for part in parts)
+    out_ref[:, :FIRST] = sum(stack_ref[i].astype(jnp.float32) for i in range(stack_ref.shape[0]))
+    out_ref[:, FIRST:] = sum(part[...].astype(jnp.float32) for part in parts)
 
 
 def final(stack, parts):
     rows = stack.shape[1]
-    width = stack.shape[2] + parts[0].shape[1]
+    width = FIRST + parts[0].shape[1]
     return pl.pallas_call(
         final_kernel,
         out_shape=jax.ShapeDtypeStruct((rows, width), jnp.float32),
@@ -348,6 +364,45 @@
         cost_estimate=SMALL,
         name="final",
     )(stack, *parts)
+
+
+def input_first_kernel(g_ref, w_ref, out_ref):
+    out_ref[...] = nt(g_ref[...], w_ref[...]).astype(out_ref.dtype)
+
+
+def input_last_kernel(g_ref, kv_ref, w_ref, w_kv_ref, part_ref, out_ref):
+    total = nt(g_ref[...], w_ref[...]) + nt(kv_ref[...], w_kv_ref[...])
+    out_ref[...] = (total + part_ref[...].astype(jnp.float32)).astype(out_ref.dtype)
+
+
+def input_grad(query, w, key_value=None, partial=None):
+    tokens, width = query.shape
+    features = w.shape[0]
+    half = width // 2
+    step = 2048
+    out = pl.BlockSpec((tokens, step), lambda i: (0, i))
+    if partial is None:
+        kernel, values = input_first_kernel, (query, w)
+        specs = [pl.BlockSpec((tokens, half), lambda i: (0, 0)), pl.BlockSpec((step, half), lambda i: (i, 0))]
+    else:
+        kernel, values = input_last_kernel, (query, key_value, w, w, partial)
+        specs = [
+            pl.BlockSpec((tokens, half), lambda i: (0, 1)),
+            pl.BlockSpec(key_value.shape, lambda i: (0, 0)),
+            pl.BlockSpec((step, half), lambda i: (i, 1)),
+            pl.BlockSpec((step, 2 * HD), lambda i: (i, HQ // 2)),
+            out,
+        ]
+    return pl.pallas_call(
+        kernel,
+        grid=(features // step,),
+        out_shape=pltpu.HBM((tokens, features), jnp.bfloat16),
+        in_specs=specs,
+        out_specs=out,
+        compiler_params=pltpu.CompilerParams(vmem_limit_bytes=60 * MIB),
+        cost_estimate=SMALL,
+        name="d_x_first" if partial is None else "d_x_last",
+    )(*values)
 
 
 def shifted(value, s):
@@ -397,21 +452,23 @@
     pieces = [packed[0]] + [shifted(packed[s], s) for s in range(1, chips)]
     query = project_query(after(rows, copies), w_qkv)
     d_query, terms = attention(where, span_order, doc_lengths, query, d_out[0], gathered)
-    own_q, other_q = gather_chips(d_query)
+    own_q = [d_query] + [shifted(d_query, s) for s in range(1, chips)]
+    other_q = [swapped(d_query)]
+    d_x_first = input_grad(after(d_query, terms, other_q[0]), w_qkv)
+    other_q += [swapped(after(piece, d_x_first)) for piece in own_q[1:]]
     arrived = lax.all_to_all(after(terms, other_q[0]).reshape(seq, tokens, 2 * HD), SEQ, 0, 0, tiled=True)
     x_own, x_send = halves(where, [after(piece, terms) for piece in pieces])
     columns = [x_own, swapped(x_send)]
 
-    stacked = term_query(columns, own_q + other_q, lax.axis_size("y"))
+    stacked, done = term_query(columns, own_q + other_q, lax.axis_size("y"))
     group_y = lax.all_to_all(stacked, "y", 0, 0, tiled=True)
     owned = jnp.sum(arrived.astype(jnp.float32), axis=0).astype(jnp.bfloat16)
-    own_kv, other_kv = gather_chips(after(owned, stacked))
-    parts = term_second(where, columns, own_kv + other_kv)
-    d_qkv = after(jnp.concatenate([d_query, owned], axis=1), parts[0])
-    d_rows = nt(d_qkv, w_qkv).astype(jnp.bfloat16)
+    own_kv, other_kv = gather_chips(after(owned, done))
+    parts = term_second(where, columns, done, own_kv + other_kv)
+    second_z = lax.all_to_all(middle_z(group_y), DEPTH, 0, 0, tiled=True)
+    d_rows = input_grad(d_query, w_qkv, after(owned, group_y), d_x_first)
     group_z = [parts[0]] + [after(shifted_z(parts[s], s), d_rows) for s in range(1, 4)]
     sums = middle_y(where, group_z)
-    second_z = lax.all_to_all(middle_z(after(group_y, sums[1])), DEPTH, 0, 0, tiled=True)
     d_w = final(second_z, [sums[0]] + [shifted_y(sums[s], s) for s in range(1, 4)])
     return (d_rows[None], d_w)
 

time: 116 us -> 116 us (level); the launches traced: 114 us -> 116 us
  Pallas kernels: 33 us -> 51 us
  matrix products: 12.8 us -> 0 us
  waiting for transfers between devices: 22 us -> 15.1 us
  starting transfers between devices: 41.7 us -> 46.4 us
  local copies, waits for them, and re-layouts: 3.9 us -> 1.38 us
    pallas_call x1 -> x3, Pallas kernels: 3.86 us -> 21.5 us  [the longest x2 16.2 us: input_grad(): pl.pallas_call(kernel, grid=(features // step,), out_shape=pltpu.HBM((tok...]
    dot_general x1 -> x0, matrix products: 12.8 us -> none  [nt(): lax.dot_general(a, b, (((1,), (1,)), ((), ())), preferred_element_type=jn...]
    all_to_all x1, waiting for transfers between devices: 3.54 us -> 0.01 us  [local(): lax.all_to_all(after(terms, other_q[0]).reshape(seq, tokens, 2 * HD), SEQ...]
    ppermute x9, waiting for transfers between devices: 8.72 us -> 5.91 us  [shifted(): return lax.ppermute(value, 'x', [(i, (i + s) % n) for i in range(n)])]
    unnamed x34, local copies, waits for them, and re-layouts: 3.22 us -> 0.7 us
    ppermute x3, starting transfers between devices: 3.77 us -> 5.6 us  [shifted_z(): lax.ppermute(value, DEPTH, [(ring_index(i), ring_index((i + s) % 4)) for...]
    ppermute x9, waiting for transfers between devices: 1.47 us -> 2.94 us  [swapped(): return lax.ppermute(value, 'core', [(0, 1), (1, 0)])]
    ppermute x3, waiting for transfers between devices: 4.46 us -> 3.02 us  [shifted_y(): return lax.ppermute(value, 'y', [(i, (i + s) % 4) for i in range(4)])]
  transfers between devices with their start and end apart: 28 -> 28, of which waited for: 14 -> 14; matrix products, arithmetic and copies ran while one was open for 11% -> 1% of each run, Pallas kernels for 16% -> 36%
where the time goes in v10:
time: 116 us
  Pallas kernels  51 us (44%)
  starting transfers between devices  46.4 us (40%)
  waiting for transfers between devices  15.1 us (13%)
  local copies, waits for them, and re-layouts  1.38 us (1%)
    pallas_call x2, Pallas kernels, input_grad(): pl.pallas_call(kernel, grid=(features // step,), out_shape=pltpu.HBM((tok...  16.2 us
    ppermute x9, starting transfers between devices, shifted(): return lax.ppermute(value, 'x', [(i, (i + s) % n) for i in range(n)])  12.3 us
    all_to_all x1, starting transfers between devices, local(): lax.all_to_all(copies, SEQ, 0, 0, tiled=True).reshape(seq * tokens, 2 * HD)  7.79 us
    pallas_call x1, Pallas kernels, project_query(): pl.pallas_call(query_kernel, grid=(HQ // 2,), out_shape=jax.ShapeDtypeStr...  7.42 us
    pallas_call x1, Pallas kernels, attention(): pl.pallas_call(attention_kernel, out_shape=(pltpu.HBM((tokens, HQ * HD),...  6.87 us
    ppermute x9, waiting for transfers between devices, shifted(): return lax.ppermute(value, 'x', [(i, (i + s) % n) for i in range(n)])  5.91 us
    ppermute x3, starting transfers between devices, shifted_z(): lax.ppermute(value, DEPTH, [(ring_index(i), ring_index((i + s) % 4)) for...  5.6 us
    ppermute x3, starting transfers between devices, shifted_y(): return lax.ppermute(value, 'y', [(i, (i + s) % 4) for i in range(4)])  5.56 us
  transfers between devices with their start and end apart: 28, of which 14 were waited for; matrix products, arithmetic and copies ran while one was open for 1% of the time, Pallas kernels for 36%

profile of v10, /device:TPU:0, one launch (start us, length us, event | category | flops | bytes accessed | tf_op | source)
XLA Modules:
  0.0 115.8 jit_solution(14341469854474547670)
XLA Ops:
  0.6 0.7 stack.23.where_ref
  1.3 5.5 %first.1 = (bf16[8,128,256]{2,1,0:T(8,128)(2,1)}, bf16[2048,128]{1,0:T(8,128)(2,1)}, bf16[2048,128]{1,0:T(8,128)(2,1)}, bf16[2048,128]{1,0:T(8,128)(2,1)}, bf16[2048,128]{1,0:T(8,128)(2,1)}) custom-call(s32[5]{0:T(128)} %stack.23.where_ref, bf16[128,8192]{1,0:T(8,128)(2,1)} %bitcast.10, bf16[8192,1280]{1,0:T(8,128)(2,1)} %w_kv_ref.1), custom_call_target="tpu_custom_call" | custom-call | flops 1 | bytes 1 | tf_op jit(solution)/shard_map/first/pallas_call | solution.py:82
  6.9 1.6 %collective-permute-start.1 = (bf16[2048,128]{1,0:T(8,128)(2,1)}, bf16[2048,128]{1,0:T(8,128)(2,1)}, u32[]{:S(2)}, u32[]{:S(2)}) collective-permute-start(bf16[2048,128]{1,0:T(8,128)(2,1)} %get-tuple-element.43), channel_id=1, source_target_pairs={{0,16},{16,32},{32,48},{48,0},{1,17},{17,33},{33,49},{49,1},{2,18}... | collective-permute-start | bytes 1572872 | tf_op jit(solution)/shard_map/ppermute | solution.py:410
  8.5 2.7 %collective-permute-start.2 = (bf16[2048,128]{1,0:T(8,128)(2,1)}, bf16[2048,128]{1,0:T(8,128)(2,1)}, u32[]{:S(2)}, u32[]{:S(2)}) collective-permute-start(bf16[2048,128]{1,0:T(8,128)(2,1)} %get-tuple-element.45), channel_id=1, source_target_pairs={{0,32},{16,48},{32,0},{48,16},{1,33},{17,49},{33,1},{49,17},{2,34}... | collective-permute-start | bytes 1572872 | tf_op jit(solution)/shard_map/ppermute | solution.py:410
  11.2 1.4 %collective-permute-start.3 = (bf16[2048,128]{1,0:T(8,128)(2,1)}, bf16[2048,128]{1,0:T(8,128)(2,1)}, u32[]{:S(2)}, u32[]{:S(2)}) collective-permute-start(bf16[2048,128]{1,0:T(8,128)(2,1)} %get-tuple-element.47), channel_id=1, source_target_pairs={{0,48},{16,0},{32,16},{48,32},{1,49},{17,1},{33,17},{49,33},{2,50}... | collective-permute-start | bytes 1572872 | tf_op jit(solution)/shard_map/ppermute | solution.py:410
  12.7 7.8 %all-to-all-start = ((bf16[8,128,256]{2,1,0:T(8,128)(2,1)}), bf16[8,128,256]{2,1,0:T(8,128)(2,1)S(1)}, u32[]{:S(2)}, u32[]{:S(2)}) async-start(bf16[8,128,256]{2,1,0:T(8,128)(2,1)} %get-tuple-element.36), calls=%async_computation | async-start | bytes 1048576 | tf_op jit(solution)/shard_map/all_to_all | solution.py:451
  20.5 7.4 %project_query.1.q_ref = bf16[128,1024]{1,0:T(8,128)(2,1)S(1)} custom-call(bf16[128,8192]{1,0:T(8,128)(2,1)S(1)} %bitcast.11, bf16[8192,1280]{1,0:T(8,128)(2,1)} %w_kv_ref.1), custom_call_target="tpu_custom_call" | custom-call | flops 1 | bytes 1 | tf_op jit(solution)/shard_map/project_query/pallas_call | solution.py:110
  27.9 3.3 %all-to-all-done = bf16[8,128,256]{2,1,0:T(8,128)(2,1)S(1)} async-done(((bf16[8,128,256]{2,1,0:T(8,128)(2,1)}), bf16[8,128,256]{2,1,0:T(8,128)(2,1)S(1)}, u32[]{:S(2)}, u32[]{:S(2)}) %all-to-all-start) | async-done | bytes 524320 | tf_op jit(solution)/shard_map/all_to_all | solution.py:451
  31.2 6.9 %attention.1 = (bf16[128,1024]{1,0:T(8,128)(2,1)}, bf16[1024,256]{1,0:T(8,128)(2,1)}) custom-call(s32[5]{0:T(128)S(1)} %copy-done.5, s32[1,16]{1,0:T(1,128)S(1)} %copy-done.7, s32[1,4]{1,0:T(1,128)S(1)} %copy-done.8, bf16[128,1024]{1,0:T(8,128)(2,1)S(1)} %project_query.1.q_ref, bf16[128,1024]{1,0:T(8,128)(2,1)S(1)} %bitcast.13, bf16[1024,256]{1,0:T(8,128)(2,1)S(1)} %bitcast.12), custom_call_target="tpu_custom_call" | custom-call | flops 1 | bytes 1 | tf_op jit(solution)/shard_map/attention/pallas_call | solution.py:205
  38.1 3.2 %halves.1 = (bf16[1024,512]{1,0:T(8,128)(2,1)}, bf16[1024,512]{1,0:T(8,128)(2,1)}) custom-call(s32[5]{0:T(128)} %stack.23.where_ref, bf16[2048,128]{1,0:T(8,128)(2,1)} %get-tuple-element.42.refs_0_, bf16[2048,128]{1,0:T(8,128)(2,1)} %collective-permute-done.1.refs_1_, bf16[2048,128]{1,0:T(8,128)(2,1)} %collective-permute-done.2.refs_2_, ...), custom_call_target="tpu_custom_call" | custom-call | flops 1 | bytes 1 | tf_op jit(solution)/shard_map/halves/pallas_call | solution.py:136
  41.3 0.5 collective-permute-start
  41.8 0.3 collective-permute-start.7
  42.1 2.4 %collective-permute-start.6 = (bf16[128,1024]{1,0:T(8,128)(2,1)}, bf16[128,1024]{1,0:T(8,128)(2,1)S(1)}, u32[]{:S(2)}, u32[]{:S(2)}) collective-permute-start(bf16[128,1024]{1,0:T(8,128)(2,1)} %get-tuple-element.51.g_ref.refs_2_), channel_id=1, source_target_pairs={{0,32},{16,48},{32,0},{48,16},{1,33},{17,49},{33,1},{49,17},{2,34}... | collective-permute-start | bytes 786440 | tf_op jit(solution)/shard_map/ppermute | solution.py:410
  44.6 5.5 %all-to-all-start.1 = ((bf16[8,128,256]{2,1,0:T(8,128)(2,1)}), bf16[8,128,256]{2,1,0:T(8,128)(2,1)}, u32[]{:S(2)}, u32[]{:S(2)}) async-start(bf16[8,128,256]{2,1,0:T(8,128)(2,1)} %bitcast.8), calls=%async_computation.1 | async-start | bytes 1048576 | tf_op jit(solution)/shard_map/all_to_all | solution.py:459
  50.0 6.9 %d_x_first.1.part_ref = bf16[128,8192]{1,0:T(8,128)(2,1)} custom-call(bf16[128,1024]{1,0:T(8,128)(2,1)} %get-tuple-element.51.g_ref.refs_2_, bf16[8192,1280]{1,0:T(8,128)(2,1)} %w_kv_ref.1), custom_call_target="tpu_custom_call" | custom-call | flops 1 | bytes 1 | tf_op jit(solution)/shard_map/d_x_first/pallas_call | solution.py:396
  56.9 0.4 collective-permute-done.5.refs_3_
  57.4 0.1 collective-permute-start.8
  57.5 0.4 collective-permute-start.9
  57.9 0.1 collective-permute-start.10
  58.0 0.9 collective-permute-done.8.refs_7_
  58.9 0.4 collective-permute-done.9.refs_8_
  59.3 0.4 collective-permute-done.10.refs_9_
  59.7 5.4 %term_query.1 = (bf16[4,256,768]{2,1,0:T(8,128)(2,1)}, bf16[1024,256]{1,0:T(8,128)(2,1)}) custom-call(bf16[1024,512]{1,0:T(8,128)(2,1)S(1)} %copy-done.1, bf16[1024,512]{1,0:T(8,128)(2,1)S(1)} %collective-permute-done.4.refs_1_, bf16[128,1024]{1,0:T(8,128)(2,1)} %get-tuple-element.51.g_ref.refs_2_, bf16[128,1024]{1,0:T(8,128)(2,1)S(1)} %collective-permute-done.5.refs_3_, ...), custom_call_target="tpu_custom_call" | custom-call | flops 1 | bytes 1 | tf_op jit(solution)/shard_map/term_query/pallas_call | solution.py:253
  65.1 4.5 %all-to-all-start.2 = ((bf16[4,256,768]{2,1,0:T(8,128)(2,1)}), bf16[4,256,768]{2,1,0:T(8,128)(2,1)S(1)}, u32[]{:S(2)}, u32[]{:S(2)}) async-start(bf16[4,256,768]{2,1,0:T(8,128)(2,1)} %get-tuple-element.55), calls=%async_computation.2 | async-start | bytes 3145728 | tf_op jit(solution)/shard_map/all_to_all | solution.py:464
  69.5 1.1 reduce_sum.12.kv_ref.refs_3_
  70.6 2.6 %collective-permute-start.13 = (bf16[128,256]{1,0:T(8,128)(2,1)S(1)}, bf16[128,256]{1,0:T(8,128)(2,1)S(1)}, u32[]{:S(2)}, u32[]{:S(2)}) collective-permute-start(bf16[128,256]{1,0:T(8,128)(2,1)S(1)} %reduce_sum.12.kv_ref.refs_3_), channel_id=1, source_target_pairs={{0,48},{16,0},{32,16},{48,32},{1,49},{17,1},{33,17},{49,33},{2,50}... | collective-permute-start | bytes 196616 | tf_op jit(solution)/shard_map/ppermute | solution.py:410
  73.3 1.2 %collective-permute-start.12 = (bf16[128,256]{1,0:T(8,128)(2,1)S(1)}, bf16[128,256]{1,0:T(8,128)(2,1)S(1)}, u32[]{:S(2)}, u32[]{:S(2)}) collective-permute-start(bf16[128,256]{1,0:T(8,128)(2,1)S(1)} %reduce_sum.12.kv_ref.refs_3_), channel_id=1, source_target_pairs={{0,32},{16,48},{32,0},{48,16},{1,33},{17,49},{33,1},{49,17},{2,34}... | collective-permute-start | bytes 196616 | tf_op jit(solution)/shard_map/ppermute | solution.py:410
  74.4 1.6 %collective-permute-done.13.refs_6_ = bf16[128,256]{1,0:T(8,128)(2,1)S(1)} collective-permute-done((bf16[128,256]{1,0:T(8,128)(2,1)S(1)}, bf16[128,256]{1,0:T(8,128)(2,1)S(1)}, u32[]{:S(2)}, u32[]{:S(2)}) %collective-permute-start.13) | collective-permute-done | bytes 65568 | tf_op jit(solution)/shard_map/ppermute | solution.py:410
  76.1 3.0 %collective-permute-done.12.refs_5_ = bf16[128,256]{1,0:T(8,128)(2,1)S(1)} collective-permute-done((bf16[128,256]{1,0:T(8,128)(2,1)S(1)}, bf16[128,256]{1,0:T(8,128)(2,1)S(1)}, u32[]{:S(2)}, u32[]{:S(2)}) %collective-permute-start.12) | collective-permute-done | bytes 65568 | tf_op jit(solution)/shard_map/ppermute | solution.py:410
  79.1 0.9 collective-permute-done.11.refs_4_
  80.0 0.3 collective-permute-done.16.refs_9_
  80.3 0.9 collective-permute-done.15.refs_8_
  81.2 0.6 copy-done.16
  81.9 3.4 %term_second.1 = (bf16[256,512]{1,0:T(8,128)(2,1)}, bf16[256,512]{1,0:T(8,128)(2,1)}, bf16[256,512]{1,0:T(8,128)(2,1)}, bf16[256,512]{1,0:T(8,128)(2,1)}) custom-call(s32[5]{0:T(128)} %stack.23.where_ref, bf16[1024,512]{1,0:T(8,128)(2,1)} %get-tuple-element.49.refs_0_, bf16[1024,512]{1,0:T(8,128)(2,1)} %copy-done.2, ...), custom_call_target="tpu_custom_call" | custom-call | flops 1 | bytes 1 | tf_op jit(solution)/shard_map/term_second/pallas_call | solution.py:292
  85.2 1.0 collective-permute-start.18
  86.2 3.6 %collective-permute-start.19 = (bf16[256,512]{1,0:T(8,128)(2,1)}, bf16[256,512]{1,0:T(8,128)(2,1)S(1)}, u32[]{:S(2)}, u32[]{:S(2)}) collective-permute-start(bf16[256,512]{1,0:T(8,128)(2,1)} %get-tuple-element.62), channel_id=1, source_target_pairs={{0,4},{64,68},{4,0},{68,64},{1,5},{65,69},{5,1},{69,65},{2,6},{66,... | collective-permute-start | bytes 786440 | tf_op jit(solution)/shard_map/ppermute | solution.py:433
  89.8 1.0 collective-permute-start.20
  90.8 1.0 middle_z.1
  91.8 4.1 %all-to-all-start.3 = ((bf16[4,64,768]{2,1,0:T(8,128)(2,1)}), bf16[4,64,768]{2,1,0:T(8,128)(2,1)S(1)}, u32[]{:S(2)}, u32[]{:S(2)}) async-start(bf16[4,64,768]{2,1,0:T(8,128)(2,1)} %middle_z.1), calls=%async_computation.3 | async-start | bytes 786432 | tf_op jit(solution)/shard_map/all_to_all | solution.py:468
  95.9 9.2 %d_x_last.1 = bf16[128,8192]{1,0:T(8,128)(2,1)} custom-call(bf16[128,1024]{1,0:T(8,128)(2,1)} %get-tuple-element.51.g_ref.refs_2_, bf16[128,256]{1,0:T(8,128)(2,1)} %copy-done.9, bf16[8192,1280]{1,0:T(8,128)(2,1)} %w_kv_ref.1, bf16[8192,1280]{1,0:T(8,128)(2,1)} %w_kv_ref.1, bf16[128,8192]{1,0:T(8,128)(2,1)} %d_x_first.1.part_ref), custom_call_target="tpu_custom_call" | custom-call | flops 1 | bytes 1 | tf_op jit(solution)/shard_map/d_x_last/pallas_call | solution.py:396
  105.2 1.3 %middle_y.1 = (f32[64,512]{1,0:T(8,128)S(1)}, bf16[64,512]{1,0:T(8,128)(2,1)}, bf16[64,512]{1,0:T(8,128)(2,1)}, bf16[64,512]{1,0:T(8,128)(2,1)}) custom-call(s32[5]{0:T(128)S(1)} %copy-done.6, bf16[256,512]{1,0:T(8,128)(2,1)S(1)} %copy-done.4, bf16[256,512]{1,0:T(8,128)(2,1)S(1)} %collective-permute-done.18.refs_1_, ...), custom_call_target="tpu_custom_call" | custom-call | flops 1 | bytes 1 | tf_op jit(solution)/shard_map/middle_y/pallas_call | solution.py:337
  106.4 1.4 %collective-permute-start.21 = (bf16[64,512]{1,0:T(8,128)(2,1)}, bf16[64,512]{1,0:T(8,128)(2,1)S(1)}, u32[]{:S(2)}, u32[]{:S(2)}) collective-permute-start(bf16[64,512]{1,0:T(8,128)(2,1)} %get-tuple-element.67), channel_id=1, source_target_pairs={{0,1},{1,2},{2,3},{3,0},{4,5},{5,6},{6,7},{7,4},{8,9},{9,10},{10,1... | collective-permute-start | bytes 196616 | tf_op jit(solution)/shard_map/ppermute | solution.py:437
  107.9 2.7 %collective-permute-start.22 = (bf16[64,512]{1,0:T(8,128)(2,1)}, bf16[64,512]{1,0:T(8,128)(2,1)S(1)}, u32[]{:S(2)}, u32[]{:S(2)}) collective-permute-start(bf16[64,512]{1,0:T(8,128)(2,1)} %get-tuple-element.68), channel_id=1, source_target_pairs={{0,2},{1,3},{2,0},{3,1},{4,6},{5,7},{6,4},{7,5},{8,10},{9,11},{10,... | collective-permute-start | bytes 196616 | tf_op jit(solution)/shard_map/ppermute | solution.py:437
  110.5 1.5 %collective-permute-start.23 = (bf16[64,512]{1,0:T(8,128)(2,1)}, bf16[64,512]{1,0:T(8,128)(2,1)S(1)}, u32[]{:S(2)}, u32[]{:S(2)}) collective-permute-start(bf16[64,512]{1,0:T(8,128)(2,1)} %get-tuple-element.69), channel_id=1, source_target_pairs={{0,3},{1,0},{2,1},{3,2},{4,7},{5,4},{6,5},{7,6},{8,11},{9,8},{10,9... | collective-permute-start | bytes 196616 | tf_op jit(solution)/shard_map/ppermute | solution.py:437
  112.0 0.7 collective-permute-done.21.refs_1_
  112.7 1.1 collective-permute-done.22.refs_2_
  113.8 1.2 %collective-permute-done.23.refs_3_ = bf16[64,512]{1,0:T(8,128)(2,1)S(1)} collective-permute-done((bf16[64,512]{1,0:T(8,128)(2,1)}, bf16[64,512]{1,0:T(8,128)(2,1)S(1)}, u32[]{:S(2)}, u32[]{:S(2)}) %collective-permute-start.23) | collective-permute-done | bytes 65568 | tf_op jit(solution)/shard_map/ppermute | solution.py:437
  115.0 0.8 final.1
  (55 shorter events, 0.2 us)
Async XLA Ops:
  1.3 19.1 %copy-start = (bf16[1,128,8192]{2,1,0:T(8,128)(2,1)S(1)}, bf16[1,128,8192]{2,1,0:T(8,128)(2,1)}, u32[]{:S(2)}) copy-start(bf16[1,128,8192]{2,1,0:T(8,128)(2,1)} %param.5) | copy-start | bytes 6291460
  6.9 31.2 %collective-permute-start.1 = (bf16[2048,128]{1,0:T(8,128)(2,1)}, bf16[2048,128]{1,0:T(8,128)(2,1)}, u32[]{:S(2)}, u32[]{:S(2)}) collective-permute-start(bf16[2048,128]{1,0:T(8,128)(2,1)} %get-tuple-element.43), channel_id=1, source_target_pairs={{0,16},{16,32},{32,48},{48,0},{1,17},{17,33},{33,49},{49,1},{2,18}... | collective-permute-start | bytes 1572872 | tf_op jit(solution)/shard_map/ppermute | solution.py:410
  8.5 29.6 %collective-permute-start.2 = (bf16[2048,128]{1,0:T(8,128)(2,1)}, bf16[2048,128]{1,0:T(8,128)(2,1)}, u32[]{:S(2)}, u32[]{:S(2)}) collective-permute-start(bf16[2048,128]{1,0:T(8,128)(2,1)} %get-tuple-element.45), channel_id=1, source_target_pairs={{0,32},{16,48},{32,0},{48,16},{1,33},{17,49},{33,1},{49,17},{2,34}... | collective-permute-start | bytes 1572872 | tf_op jit(solution)/shard_map/ppermute | solution.py:410
  11.2 26.9 %collective-permute-start.3 = (bf16[2048,128]{1,0:T(8,128)(2,1)}, bf16[2048,128]{1,0:T(8,128)(2,1)}, u32[]{:S(2)}, u32[]{:S(2)}) collective-permute-start(bf16[2048,128]{1,0:T(8,128)(2,1)} %get-tuple-element.47), channel_id=1, source_target_pairs={{0,48},{16,0},{32,16},{48,32},{1,49},{17,1},{33,17},{49,33},{2,50}... | collective-permute-start | bytes 1572872 | tf_op jit(solution)/shard_map/ppermute | solution.py:410
  12.7 18.5 %all-to-all-start = ((bf16[8,128,256]{2,1,0:T(8,128)(2,1)}), bf16[8,128,256]{2,1,0:T(8,128)(2,1)S(1)}, u32[]{:S(2)}, u32[]{:S(2)}) async-start(bf16[8,128,256]{2,1,0:T(8,128)(2,1)} %get-tuple-element.36), calls=%async_computation | async-start | bytes 1048576 | tf_op jit(solution)/shard_map/all_to_all | solution.py:451
  20.5 10.7 %copy-start.3 = (bf16[1,128,1024]{2,1,0:T(8,128)(2,1)S(1)}, bf16[1,128,1024]{2,1,0:T(8,128)(2,1)}, u32[]{:S(2)}) copy-start(bf16[1,128,1024]{2,1,0:T(8,128)(2,1)} %param.7) | copy-start | bytes 786436
  20.5 10.7 %copy-start.5 = (s32[5]{0:T(128)S(1)}, s32[5]{0:T(128)}, u32[]{:S(2)}) copy-start(s32[5]{0:T(128)} %stack.23.where_ref) | copy-start | bytes 64
  20.5 10.7 %copy-start.7 = (s32[1,16]{1,0:T(1,128)S(1)}, s32[1,16]{1,0:T(1,128)}, u32[]{:S(2)}) copy-start(s32[1,16]{1,0:T(1,128)} %order_ref.1) | copy-start | bytes 196
  20.5 10.7 %copy-start.8 = (s32[1,4]{1,0:T(1,128)S(1)}, s32[1,4]{1,0:T(1,128)}, u32[]{:S(2)}) copy-start(s32[1,4]{1,0:T(1,128)} %lens_ref.1) | copy-start | bytes 52
  41.3 18.4 %collective-permute-start.4 = (bf16[1024,512]{1,0:T(8,128)(2,1)}, bf16[1024,512]{1,0:T(8,128)(2,1)S(1)}, u32[]{:S(2)}, u32[]{:S(2)}) collective-permute-start(bf16[1024,512]{1,0:T(8,128)(2,1)} %get-tuple-element.50), channel_id=1, source_target_pairs={{0,8},{8,0},{1,9},{9,1},{2,10},{10,2},{3,11},{11,3},{4,12},{12,4},... | collective-permute-start | bytes 3145736 | tf_op jit(solution)/shard_map/ppermute | solution.py:414
  41.3 3.2 %collective-permute-start = (bf16[128,1024]{1,0:T(8,128)(2,1)}, bf16[128,1024]{1,0:T(8,128)(2,1)S(1)}, u32[]{:S(2)}, u32[]{:S(2)}) collective-permute-start(bf16[128,1024]{1,0:T(8,128)(2,1)} %get-tuple-element.51.g_ref.refs_2_), channel_id=1, source_target_pairs={{0,8},{8,0},{1,9},{9,1},{2,10},{10,2},{3,11},{11,3},{4,12},{12,4},... | collective-permute-start | bytes 786440 | tf_op jit(solution)/shard_map/ppermute | solution.py:414
  41.8 15.1 %collective-permute-start.7 = (bf16[128,1024]{1,0:T(8,128)(2,1)}, bf16[128,1024]{1,0:T(8,128)(2,1)S(1)}, u32[]{:S(2)}, u32[]{:S(2)}) collective-permute-start(bf16[128,1024]{1,0:T(8,128)(2,1)} %get-tuple-element.51.g_ref.refs_2_), channel_id=1, source_target_pairs={{0,48},{16,0},{32,16},{48,32},{1,49},{17,1},{33,17},{49,33},{2,50}... | collective-permute-start | bytes 786440 | tf_op jit(solution)/shard_map/ppermute | solution.py:410
  42.1 14.8 %collective-permute-start.6 = (bf16[128,1024]{1,0:T(8,128)(2,1)}, bf16[128,1024]{1,0:T(8,128)(2,1)S(1)}, u32[]{:S(2)}, u32[]{:S(2)}) collective-permute-start(bf16[128,1024]{1,0:T(8,128)(2,1)} %get-tuple-element.51.g_ref.refs_2_), channel_id=1, source_target_pairs={{0,32},{16,48},{32,0},{48,16},{1,33},{17,49},{33,1},{49,17},{2,34}... | collective-permute-start | bytes 786440 | tf_op jit(solution)/shard_map/ppermute | solution.py:410
  44.5 12.9 %collective-permute-start.5 = (bf16[128,1024]{1,0:T(8,128)(2,1)}, bf16[128,1024]{1,0:T(8,128)(2,1)S(1)}, u32[]{:S(2)}, u32[]{:S(2)}) collective-permute-start(bf16[128,1024]{1,0:T(8,128)(2,1)} %get-tuple-element.51.g_ref.refs_2_), channel_id=1, source_target_pairs={{0,16},{16,32},{32,48},{48,0},{1,17},{17,33},{33,49},{49,1},{2,18}... | collective-permute-start | bytes 786440 | tf_op jit(solution)/shard_map/ppermute | solution.py:410
  44.6 20.5 %all-to-all-start.1 = ((bf16[8,128,256]{2,1,0:T(8,128)(2,1)}), bf16[8,128,256]{2,1,0:T(8,128)(2,1)}, u32[]{:S(2)}, u32[]{:S(2)}) async-start(bf16[8,128,256]{2,1,0:T(8,128)(2,1)} %bitcast.8), calls=%async_computation.1 | async-start | bytes 1048576 | tf_op jit(solution)/shard_map/all_to_all | solution.py:459
  50.0 9.7 %copy-start.1 = (bf16[1024,512]{1,0:T(8,128)(2,1)S(1)}, bf16[1024,512]{1,0:T(8,128)(2,1)}, u32[]{:S(2)}) copy-start(bf16[1024,512]{1,0:T(8,128)(2,1)} %get-tuple-element.49.refs_0_) | copy-start | bytes 3145732
  57.4 1.5 %collective-permute-start.8 = (bf16[128,1024]{1,0:T(8,128)(2,1)S(1)}, bf16[128,1024]{1,0:T(8,128)(2,1)S(1)}, u32[]{:S(2)}, u32[]{:S(2)}) collective-permute-start(bf16[128,1024]{1,0:T(8,128)(2,1)S(1)} %collective-permute-done.5.refs_3_), channel_id=1, source_target_pairs={{0,8},{8,0},{1,9},{9,1},{2,10},{10,2},{3,11},{11,3},{4,12},{12,4},... | collective-permute-start | bytes 786440 | tf_op jit(solution)/shard_map/ppermute | solution.py:414
  57.5 1.8 %collective-permute-start.9 = (bf16[128,1024]{1,0:T(8,128)(2,1)S(1)}, bf16[128,1024]{1,0:T(8,128)(2,1)S(1)}, u32[]{:S(2)}, u32[]{:S(2)}) collective-permute-start(bf16[128,1024]{1,0:T(8,128)(2,1)S(1)} %collective-permute-done.6.refs_4_), channel_id=1, source_target_pairs={{0,8},{8,0},{1,9},{9,1},{2,10},{10,2},{3,11},{11,3},{4,12},{12,4},... | collective-permute-start | bytes 786440 | tf_op jit(solution)/shard_map/ppermute | solution.py:414
  57.9 1.8 %collective-permute-start.10 = (bf16[128,1024]{1,0:T(8,128)(2,1)S(1)}, bf16[128,1024]{1,0:T(8,128)(2,1)S(1)}, u32[]{:S(2)}, u32[]{:S(2)}) collective-permute-start(bf16[128,1024]{1,0:T(8,128)(2,1)S(1)} %collective-permute-done.7.refs_5_), channel_id=1, source_target_pairs={{0,8},{8,0},{1,9},{9,1},{2,10},{10,2},{3,11},{11,3},{4,12},{12,4},... | collective-permute-start | bytes 786440 | tf_op jit(solution)/shard_map/ppermute | solution.py:414
  59.7 5.4 %copy-start.2 = (bf16[1024,512]{1,0:T(8,128)(2,1)}, bf16[1024,512]{1,0:T(8,128)(2,1)S(1)}, u32[]{:S(2)}) copy-start(bf16[1024,512]{1,0:T(8,128)(2,1)S(1)} %collective-permute-done.4.refs_1_) | copy-start | bytes 3145732
  65.1 25.8 %all-to-all-start.2 = ((bf16[4,256,768]{2,1,0:T(8,128)(2,1)}), bf16[4,256,768]{2,1,0:T(8,128)(2,1)S(1)}, u32[]{:S(2)}, u32[]{:S(2)}) async-start(bf16[4,256,768]{2,1,0:T(8,128)(2,1)} %get-tuple-element.55), calls=%async_computation.2 | async-start | bytes 3145728 | tf_op jit(solution)/shard_map/all_to_all | solution.py:464
  70.6 10.5 %copy-start.9 = (bf16[128,256]{1,0:T(8,128)(2,1)}, bf16[128,256]{1,0:T(8,128)(2,1)S(1)}, u32[]{:S(2)}) copy-start(bf16[128,256]{1,0:T(8,128)(2,1)S(1)} %reduce_sum.12.kv_ref.refs_3_) | copy-start | bytes 196612
  70.6 5.4 %collective-permute-start.13 = (bf16[128,256]{1,0:T(8,128)(2,1)S(1)}, bf16[128,256]{1,0:T(8,128)(2,1)S(1)}, u32[]{:S(2)}, u32[]{:S(2)}) collective-permute-start(bf16[128,256]{1,0:T(8,128)(2,1)S(1)} %reduce_sum.12.kv_ref.refs_3_), channel_id=1, source_target_pairs={{0,48},{16,0},{32,16},{48,32},{1,49},{17,1},{33,17},{49,33},{2,50}... | collective-permute-start | bytes 196616 | tf_op jit(solution)/shard_map/ppermute | solution.py:410
  73.3 5.8 %collective-permute-start.12 = (bf16[128,256]{1,0:T(8,128)(2,1)S(1)}, bf16[128,256]{1,0:T(8,128)(2,1)S(1)}, u32[]{:S(2)}, u32[]{:S(2)}) collective-permute-start(bf16[128,256]{1,0:T(8,128)(2,1)S(1)} %reduce_sum.12.kv_ref.refs_3_), channel_id=1, source_target_pairs={{0,32},{16,48},{32,0},{48,16},{1,33},{17,49},{33,1},{49,17},{2,34}... | collective-permute-start | bytes 196616 | tf_op jit(solution)/shard_map/ppermute | solution.py:410
  74.4 5.5 %collective-permute-start.11 = (bf16[128,256]{1,0:T(8,128)(2,1)S(1)}, bf16[128,256]{1,0:T(8,128)(2,1)S(1)}, u32[]{:S(2)}, u32[]{:S(2)}) collective-permute-start(bf16[128,256]{1,0:T(8,128)(2,1)S(1)} %reduce_sum.12.kv_ref.refs_3_), channel_id=1, source_target_pairs={{0,16},{16,32},{32,48},{48,0},{1,17},{17,33},{33,49},{49,1},{2,18}... | collective-permute-start | bytes 196616 | tf_op jit(solution)/shard_map/ppermute | solution.py:410
  74.4 5.5 %collective-permute-start.14 = (bf16[128,256]{1,0:T(8,128)(2,1)S(1)}, bf16[128,256]{1,0:T(8,128)(2,1)S(1)}, u32[]{:S(2)}, u32[]{:S(2)}) collective-permute-start(bf16[128,256]{1,0:T(8,128)(2,1)S(1)} %reduce_sum.12.kv_ref.refs_3_), channel_id=1, source_target_pairs={{0,8},{8,0},{1,9},{9,1},{2,10},{10,2},{3,11},{11,3},{4,12},{12,4},... | collective-permute-start | bytes 196616 | tf_op jit(solution)/shard_map/ppermute | solution.py:414
  76.1 5.1 %copy-start.10 = (bf16[128,256]{1,0:T(8,128)(2,1)}, bf16[128,256]{1,0:T(8,128)(2,1)S(1)}, u32[]{:S(2)}) copy-start(bf16[128,256]{1,0:T(8,128)(2,1)S(1)} %collective-permute-done.13.refs_6_) | copy-start | bytes 196612
  76.1 3.9 %collective-permute-start.17 = (bf16[128,256]{1,0:T(8,128)(2,1)S(1)}, bf16[128,256]{1,0:T(8,128)(2,1)S(1)}, u32[]{:S(2)}, u32[]{:S(2)}) collective-permute-start(bf16[128,256]{1,0:T(8,128)(2,1)S(1)} %collective-permute-done.13.refs_6_), channel_id=1, source_target_pairs={{0,8},{8,0},{1,9},{9,1},{2,10},{10,2},{3,11},{11,3},{4,12},{12,4},... | collective-permute-start | bytes 196616 | tf_op jit(solution)/shard_map/ppermute | solution.py:414
  79.0 2.1 %copy-start.11 = (bf16[128,256]{1,0:T(8,128)(2,1)}, bf16[128,256]{1,0:T(8,128)(2,1)S(1)}, u32[]{:S(2)}) copy-start(bf16[128,256]{1,0:T(8,128)(2,1)S(1)} %collective-permute-done.12.refs_5_) | copy-start | bytes 196612
  79.0 1.3 %collective-permute-start.16 = (bf16[128,256]{1,0:T(8,128)(2,1)S(1)}, bf16[128,256]{1,0:T(8,128)(2,1)S(1)}, u32[]{:S(2)}, u32[]{:S(2)}) collective-permute-start(bf16[128,256]{1,0:T(8,128)(2,1)S(1)} %collective-permute-done.12.refs_5_), channel_id=1, source_target_pairs={{0,8},{8,0},{1,9},{9,1},{2,10},{10,2},{3,11},{11,3},{4,12},{12,4},... | collective-permute-start | bytes 196616 | tf_op jit(solution)/shard_map/ppermute | solution.py:414
  79.9 1.3 %copy-start.12 = (bf16[128,256]{1,0:T(8,128)(2,1)}, bf16[128,256]{1,0:T(8,128)(2,1)S(1)}, u32[]{:S(2)}) copy-start(bf16[128,256]{1,0:T(8,128)(2,1)S(1)} %collective-permute-done.11.refs_4_) | copy-start | bytes 196612
  79.9 1.3 %collective-permute-start.15 = (bf16[128,256]{1,0:T(8,128)(2,1)S(1)}, bf16[128,256]{1,0:T(8,128)(2,1)S(1)}, u32[]{:S(2)}, u32[]{:S(2)}) collective-permute-start(bf16[128,256]{1,0:T(8,128)(2,1)S(1)} %collective-permute-done.11.refs_4_), channel_id=1, source_target_pairs={{0,8},{8,0},{1,9},{9,1},{2,10},{10,2},{3,11},{11,3},{4,12},{12,4},... | collective-permute-start | bytes 196616 | tf_op jit(solution)/shard_map/ppermute | solution.py:414
  79.9 1.3 %copy-start.13 = (bf16[128,256]{1,0:T(8,128)(2,1)}, bf16[128,256]{1,0:T(8,128)(2,1)S(1)}, u32[]{:S(2)}) copy-start(bf16[128,256]{1,0:T(8,128)(2,1)S(1)} %collective-permute-done.14.refs_7_) | copy-start | bytes 196612
  79.9 1.3 %copy-start.14 = (bf16[128,256]{1,0:T(8,128)(2,1)}, bf16[128,256]{1,0:T(8,128)(2,1)S(1)}, u32[]{:S(2)}) copy-start(bf16[128,256]{1,0:T(8,128)(2,1)S(1)} %collective-permute-done.17.refs_10_) | copy-start | bytes 196612
  80.3 0.9 copy-start.15
  81.2 0.6 copy-start.16
  85.2 19.9 %collective-permute-start.18 = (bf16[256,512]{1,0:T(8,128)(2,1)}, bf16[256,512]{1,0:T(8,128)(2,1)S(1)}, u32[]{:S(2)}, u32[]{:S(2)}) collective-permute-start(bf16[256,512]{1,0:T(8,128)(2,1)} %get-tuple-element.60), channel_id=1, source_target_pairs={{0,64},{64,4},{4,68},{68,0},{1,65},{65,5},{5,69},{69,1},{2,66},{66... | collective-permute-start | bytes 786440 | tf_op jit(solution)/shard_map/ppermute | solution.py:433
  86.2 18.9 %collective-permute-start.19 = (bf16[256,512]{1,0:T(8,128)(2,1)}, bf16[256,512]{1,0:T(8,128)(2,1)S(1)}, u32[]{:S(2)}, u32[]{:S(2)}) collective-permute-start(bf16[256,512]{1,0:T(8,128)(2,1)} %get-tuple-element.62), channel_id=1, source_target_pairs={{0,4},{64,68},{4,0},{68,64},{1,5},{65,69},{5,1},{69,65},{2,6},{66,... | collective-permute-start | bytes 786440 | tf_op jit(solution)/shard_map/ppermute | solution.py:433
  89.8 15.3 %collective-permute-start.20 = (bf16[256,512]{1,0:T(8,128)(2,1)}, bf16[256,512]{1,0:T(8,128)(2,1)S(1)}, u32[]{:S(2)}, u32[]{:S(2)}) collective-permute-start(bf16[256,512]{1,0:T(8,128)(2,1)} %get-tuple-element.64), channel_id=1, source_target_pairs={{0,68},{64,0},{4,64},{68,4},{1,69},{65,1},{5,65},{69,5},{2,70},{66... | collective-permute-start | bytes 786440 | tf_op jit(solution)/shard_map/ppermute | solution.py:433
  91.8 23.2 %all-to-all-start.3 = ((bf16[4,64,768]{2,1,0:T(8,128)(2,1)}), bf16[4,64,768]{2,1,0:T(8,128)(2,1)S(1)}, u32[]{:S(2)}, u32[]{:S(2)}) async-start(bf16[4,64,768]{2,1,0:T(8,128)(2,1)} %middle_z.1), calls=%async_computation.3 | async-start | bytes 786432 | tf_op jit(solution)/shard_map/all_to_all | solution.py:468
  95.9 9.3 %copy-start.4 = (bf16[256,512]{1,0:T(8,128)(2,1)S(1)}, bf16[256,512]{1,0:T(8,128)(2,1)}, u32[]{:S(2)}) copy-start(bf16[256,512]{1,0:T(8,128)(2,1)} %get-tuple-element.59.refs_0_) | copy-start | bytes 786436
  95.9 9.3 %copy-start.6 = (s32[5]{0:T(128)S(1)}, s32[5]{0:T(128)}, u32[]{:S(2)}) copy-start(s32[5]{0:T(128)} %stack.23.where_ref) | copy-start | bytes 64
  106.4 6.3 %collective-permute-start.21 = (bf16[64,512]{1,0:T(8,128)(2,1)}, bf16[64,512]{1,0:T(8,128)(2,1)S(1)}, u32[]{:S(2)}, u32[]{:S(2)}) collective-permute-start(bf16[64,512]{1,0:T(8,128)(2,1)} %get-tuple-element.67), channel_id=1, source_target_pairs={{0,1},{1,2},{2,3},{3,0},{4,5},{5,6},{6,7},{7,4},{8,9},{9,10},{10,1... | collective-permute-start | bytes 196616 | tf_op jit(solution)/shard_map/ppermute | solution.py:437
  107.9 6.0 %collective-permute-start.22 = (bf16[64,512]{1,0:T(8,128)(2,1)}, bf16[64,512]{1,0:T(8,128)(2,1)S(1)}, u32[]{:S(2)}, u32[]{:S(2)}) collective-permute-start(bf16[64,512]{1,0:T(8,128)(2,1)} %get-tuple-element.68), channel_id=1, source_target_pairs={{0,2},{1,3},{2,0},{3,1},{4,6},{5,7},{6,4},{7,5},{8,10},{9,11},{10,... | collective-permute-start | bytes 196616 | tf_op jit(solution)/shard_map/ppermute | solution.py:437
  110.5 4.5 %collective-permute-start.23 = (bf16[64,512]{1,0:T(8,128)(2,1)}, bf16[64,512]{1,0:T(8,128)(2,1)S(1)}, u32[]{:S(2)}, u32[]{:S(2)}) collective-permute-start(bf16[64,512]{1,0:T(8,128)(2,1)} %get-tuple-element.69), channel_id=1, source_target_pairs={{0,3},{1,0},{2,1},{3,2},{4,7},{5,4},{6,5},{7,6},{8,11},{9,8},{10,9... | collective-permute-start | bytes 196616 | tf_op jit(solution)/shard_map/ppermute | solution.py:437

commit v11 on v9

--- a/solution.py
+++ b/solution.py
@@ -256,16 +256,18 @@
     )(other, *parts, *pieces)
 
 
+def ring_block(where_ref, s):
+    place = lax.rem(where_ref[3] + s, 4)
+    return 2 * lax.rem(place, 2) + place // 2
+
+
 def term_kv_kernel(count, where_ref, other_ref, *refs):
     parts, pieces, outs, full_ref = refs[:count], refs[count:-5], refs[-5:-1], refs[-1]
     full_ref[...] = product(parts, other_ref, pieces, 0, full_ref.shape[1])
-    blocks = len(outs)
-    rows = full_ref.shape[0] // (blocks * blocks)
-    for s in range(blocks):
-        y = lax.rem(where_ref[3] + s, blocks)
-        for i in range(blocks):
-            at = pl.multiple_of((i * blocks + y) * rows, rows)
-            outs[s][i * rows : (i + 1) * rows, :] = full_ref[pl.ds(at, rows), :]
+    rows = outs[0].shape[0]
+    for s in range(len(outs)):
+        at = pl.multiple_of(ring_block(where_ref, s) * rows, rows)
+        outs[s][...] = full_ref[pl.ds(at, rows), :]
 
 
 def term_kv(where, parts, other, pieces, blocks):
@@ -285,72 +287,109 @@
     )(where, other, *parts, *pieces)
 
 
-def middle_kernel(stack_ref, *refs):
+def middle_z_kernel(stack_ref, out_ref):
+    rows = out_ref.shape[1]
+    for i in range(out_ref.shape[0]):
+        parts = [stack_ref[j, i * rows : (i + 1) * rows, :].astype(jnp.float32) for j in range(stack_ref.shape[0])]
+        out_ref[i] = sum(parts).astype(out_ref.dtype)
+
+
+def middle_z(stack):
+    blocks, rows, width = stack.shape
+    out = pltpu.HBM((blocks, rows // blocks, width), jnp.bfloat16)
+    return pl.pallas_call(
+        middle_z_kernel,
+        grid=(1,),
+        out_shape=out,
+        in_specs=[VMEM],
+        out_specs=pl.BlockSpec(out.shape, lambda i: (0, 0, 0)),
+        compiler_params=pltpu.CompilerParams(vmem_limit_bytes=14 * MIB),
+        cost_estimate=SMALL,
+        name="middle_z",
+    )(stack)
+
+
+def middle_y_kernel(where_ref, *refs):
+    parts, outs = refs[:-4], refs[-4:]
+    rows = outs[0].shape[0]
+    for s in range(4):
+        at = pl.multiple_of(lax.rem(where_ref[4] + s, 4) * rows, rows)
+        total = sum(part[pl.ds(at, rows), :].astype(jnp.float32) for part in parts)
+        outs[s][...] = total.astype(outs[s].dtype)
+
+
+def middle_y(where, parts):
+    rows, width = parts[0].shape
+    return pl.pallas_call(
+        middle_y_kernel,
+        grid=(1,),
+        out_shape=(jax.ShapeDtypeStruct((rows // 4, width), jnp.float32),) + (pltpu.HBM((rows // 4, width), jnp.bfloat16),) * 3,
+        in_specs=[SMEM] + [VMEM] * len(parts),
+        out_specs=(VMEM,) + (pl.BlockSpec((rows // 4, width), lambda i: (0, 0)),) * 3,
+        compiler_params=pltpu.CompilerParams(vmem_limit_bytes=14 * MIB),
+        cost_estimate=SMALL,
+        name="middle_y",
+    )(where, *parts)
+
+
+def final_kernel(stack_ref, *refs):
     parts, out_ref = refs[:-1], refs[-1]
     first = stack_ref.shape[2]
-    blocks, rows, _ = out_ref.shape
-    for i in range(blocks):
-        here = slice(i * rows, (i + 1) * rows)
-        query = sum(stack_ref[j, here, :].astype(jnp.float32) for j in range(stack_ref.shape[0]))
-        out_ref[i, :, :first] = query.astype(out_ref.dtype)
-        out_ref[i, :, first:] = sum(part[here, :].astype(jnp.float32) for part in parts).astype(out_ref.dtype)
-
-
-def middle(stack, parts):
-    blocks, rows, width = stack.shape
-    out = pltpu.HBM((blocks, rows // blocks, width + parts[0].shape[1]), jnp.bfloat16)
-    return pl.pallas_call(
-        middle_kernel,
-        grid=(1,),
-        out_shape=out,
-        in_specs=[VMEM] * (1 + len(parts)),
-        out_specs=pl.BlockSpec(out.shape, lambda i: (0, 0, 0)),
-        compiler_params=pltpu.CompilerParams(vmem_limit_bytes=14 * MIB),
-        cost_estimate=SMALL,
-        name="middle",
-    )(stack, *parts)
-
-
-def final_kernel(stack_ref, out_ref):
-    out_ref[...] = sum(stack_ref[i].astype(jnp.float32) for i in range(stack_ref.shape[0]))
-
-
-def final(stack):
+    out_ref[:, :first] = sum(stack_ref[i].astype(jnp.float32) for i in range(stack_ref.shape[0]))
+    out_ref[:, first:] = sum(part[...].astype(jnp.float32) for part in parts)
+
+
+def final(stack, parts):
+    rows = stack.shape[1]
+    width = stack.shape[2] + parts[0].shape[1]
     return pl.pallas_call(
         final_kernel,
-        out_shape=jax.ShapeDtypeStruct(stack.shape[1:], jnp.float32),
-        in_specs=[VMEM],
+        out_shape=jax.ShapeDtypeStruct((rows, width), jnp.float32),
+        in_specs=[VMEM] * 5,
         out_specs=VMEM,
         compiler_params=pltpu.CompilerParams(vmem_limit_bytes=8 * MIB),
         cost_estimate=SMALL,
         name="final",
-    )(stack)
-
-
-def input_query_kernel(g_ref, w_ref, out_ref):
+    )(stack, *parts)
+
+
+def input_first_kernel(g_ref, w_ref, out_ref):
     out_ref[...] = nt(g_ref[...], w_ref[...]).astype(out_ref.dtype)
 
 
-def input_last_kernel(g_ref, w_ref, part_ref, out_ref):
-    out_ref[...] = (part_ref[...].astype(jnp.float32) + nt(g_ref[...], w_ref[...])).astype(out_ref.dtype)
-
-
-def input_grad(grad, w, at, partial=()):
-    tokens, width = grad.shape
+def input_last_kernel(g_ref, kv_ref, w_ref, w_kv_ref, part_ref, out_ref):
+    total = nt(g_ref[...], w_ref[...]) + nt(kv_ref[...], w_kv_ref[...])
+    out_ref[...] = (total + part_ref[...].astype(jnp.float32)).astype(out_ref.dtype)
+
+
+def input_grad(query, w, key_value=None, partial=None):
+    tokens, width = query.shape
     features = w.shape[0]
+    half = width // 2
     step = 2048
-    out = pltpu.HBM((tokens, features), jnp.bfloat16)
-    block = pl.BlockSpec((tokens, step), lambda i: (0, i))
-    return pl.pallas_call(
-        input_last_kernel if partial else input_query_kernel,
+    out = pl.BlockSpec((tokens, step), lambda i: (0, i))
+    if partial is None:
+        kernel, values = input_first_kernel, (query, w)
+        specs = [pl.BlockSpec((tokens, half), lambda i: (0, 0)), pl.BlockSpec((step, half), lambda i: (i, 0))]
+    else:
+        kernel, values = input_last_kernel, (query, key_value, w, w, partial)
+        specs = [
+            pl.BlockSpec((tokens, half), lambda i: (0, 1)),
+            pl.BlockSpec(key_value.shape, lambda i: (0, 0)),
+            pl.BlockSpec((step, half), lambda i: (i, 1)),
+            pl.BlockSpec((step, 2 * HD), lambda i: (i, HQ // 2)),
+            out,
+        ]
+    return pl.pallas_call(
+        kernel,
         grid=(features // step,),
-        out_shape=out,
-        in_specs=[pl.BlockSpec((tokens, width), lambda i: (0, 0)), pl.BlockSpec((step, width), lambda i: (i, at))] + [block] * len(partial),
-        out_specs=block,
+        out_shape=pltpu.HBM((tokens, features), jnp.bfloat16),
+        in_specs=specs,
+        out_specs=out,
         compiler_params=pltpu.CompilerParams(vmem_limit_bytes=60 * MIB),
         cost_estimate=SMALL,
-        name="d_x_last" if partial else "d_x_query",
-    )(grad, w, *partial)
+        name="d_x_first" if partial is None else "d_x_last",
+    )(*values)
 
 
 def shifted(value, s):
@@ -371,6 +410,14 @@
     if not others:
         return value
     return lax.optimization_barrier((value,) + others)[0]
+
+
+def ring_index(place):
+    return 2 * (place % 2) + place // 2
+
+
+def shifted_z(value, s):
+    return lax.ppermute(value, DEPTH, [(ring_index(i), ring_index((i + s) % 4)) for i in range(4)])
 
 
 def shifted_y(value, s):
@@ -383,7 +430,8 @@
     chips = lax.axis_size("x")
     seq = lax.axis_size("zhi") * lax.axis_size("y")
     place = lax.axis_index("zhi") * lax.axis_size("y") + lax.axis_index("y")
-    where = jnp.stack([lax.axis_index("x"), lax.axis_index("core"), place, lax.axis_index("y")]).astype(jnp.int32)
+    ring = lax.axis_index("zhi") * 2 + lax.axis_index("zlo")
+    where = jnp.stack([lax.axis_index("x"), lax.axis_index("core"), place, ring, lax.axis_index("y")]).astype(jnp.int32)
 
     copies, *packed = first(where, rows, w_qkv, seq, chips)
     gathered = lax.all_to_all(copies, SEQ, 0, 0, tiled=True).reshape(seq * tokens, 2 * HD)
@@ -392,20 +440,22 @@
     d_query, terms = attention(where, span_order, doc_lengths, query, d_out[0], gathered)
     own_q = [d_query] + [shifted(d_query, s) for s in range(1, chips)]
     other_q = [swapped(d_query)]
+    d_x_first = input_grad(after(d_query, terms, other_q[0]), w_qkv)
+    other_q += [swapped(after(piece, d_x_first)) for piece in own_q[1:]]
     arrived = lax.all_to_all(after(terms, other_q[0]).reshape(seq, tokens, 2 * HD), SEQ, 0, 0, tiled=True)
     x_other = swapped(forward([after(piece, terms) for piece in pieces]))
-    d_x_query = input_grad(after(d_query, terms,other_q[0]), w_qkv, 0)
-
-    other_q += [swapped(after(piece, d_x_query)) for piece in own_q[1:]]
+
     places = lax.axis_size("y")
     stacked = term_query(pieces, x_other, own_q + other_q, places)
-    group_query = lax.all_to_all(stacked, "y", 0, 0, tiled=True)
+    group_y = lax.all_to_all(stacked, "y", 0, 0, tiled=True)
     owned = jnp.sum(arrived.astype(jnp.float32), axis=0).astype(jnp.bfloat16)
     own_kv, other_kv = gather_chips(after(owned, stacked))
     parts = term_kv(where, pieces, x_other, own_kv + other_kv, places)
-    d_rows = input_grad(after(owned, parts[0]), w_qkv, HQ // 2, (d_x_query,))
-    group_kv = [parts[0]] + [after(shifted_y(parts[s], s), d_rows) for s in range(1, places)]
-    d_w = final(lax.all_to_all(middle(group_query, group_kv), DEPTH, 0, 0, tiled=True))
+    d_rows = input_grad(d_query, w_qkv, after(owned, parts[0]), d_x_first)
+    group_z = [parts[0]] + [after(shifted_z(parts[s], s), d_rows) for s in range(1, places)]
+    sums = middle_y(where, group_z)
+    second_z = lax.all_to_all(middle_z(after(group_y, sums[1])), DEPTH, 0, 0, tiled=True)
+    d_w = final(second_z, [sums[0]] + [shifted_y(sums[s], s) for s in range(1, places)])
     return (d_rows[None], d_w)
 
 

time: 125 us -> 116 us (0.928)
  blocking collectives: 14.1 us -> 0 us
  starting transfers between devices: 39.2 us -> 48.3 us
  waiting for transfers between devices: 17.2 us -> 12 us
    all_to_all x1 -> x0, blocking collectives: 14.1 us -> none  [local(): lax.all_to_all(middle(group_query, group_kv), DEPTH, 0, 0, tiled=True)]
    ppermute x0 -> x3, starting transfers between devices: none -> 5.6 us  [shifted_z(): lax.ppermute(value, DEPTH, [(ring_index(i), ring_index((i + s) % 4)) for...]
    ppermute x3, waiting for transfers between devices: 8.05 us -> 2.46 us  [shifted_y(): return lax.ppermute(value, 'y', [(i, (i + s) % 4) for i in range(4)])]
    all_to_all x1 -> x2, starting transfers between devices: 4.79 us -> 8.26 us  [the longest x1 4.79 us: local(): group_y = lax.all_to_all(stacked, 'y', 0, 0, tiled=True)]
    pallas_call x4 -> x5, Pallas kernels: 17.9 us -> 19.2 us  [the longest x2 16.1 us: input_grad(): pl.pallas_call(kernel, grid=(features // step,), out_shape=pltpu.HBM((tok...]
    unnamed x46 -> x54, local copies, waits for them, and re-layouts: 2.55 us -> 2.57 us
  transfers between devices with their start and end apart: 24 -> 28, of which waited for: 11 -> 12; matrix products, arithmetic and copies ran while one was open for 0% -> 0% of each run, Pallas kernels for 32% -> 35%
where the time goes in v11:
time: 116 us; the launch traced here: 115 us
  Pallas kernels  50.5 us (44%)
  starting transfers between devices  48.3 us (42%)
  waiting for transfers between devices  12 us (10%)
  local copies, waits for them, and re-layouts  3.19 us (3%)
    pallas_call x2, Pallas kernels, input_grad(): pl.pallas_call(kernel, grid=(features // step,), out_shape=pltpu.HBM((tok...  16.1 us
    ppermute x9, starting transfers between devices, shifted(): return lax.ppermute(value, 'x', [(i, (i + s) % n) for i in range(n)])  12.6 us
    all_to_all x1, starting transfers between devices, local(): lax.all_to_all(copies, SEQ, 0, 0, tiled=True).reshape(seq * tokens, 2 * HD)  7.78 us
    pallas_call x1, Pallas kernels, project_query(): pl.pallas_call(query_kernel, grid=(HQ // 2,), out_shape=jax.ShapeDtypeStr...  7.42 us
    pallas_call x1, Pallas kernels, attention(): pl.pallas_call(attention_kernel, out_shape=(pltpu.HBM((tokens, HQ * HD),...  6.86 us
    all_to_all x1, starting transfers between devices, local(): lax.all_to_all(after(terms, other_q[0]).reshape(seq, tokens, 2 * HD), SEQ...  6.09 us
    ppermute x3, starting transfers between devices, shifted_y(): return lax.ppermute(value, 'y', [(i, (i + s) % 4) for i in range(4)])  6.06 us
    pallas_call x1, Pallas kernels, term_query(): pl.pallas_call(lambda *refs: term_query_kernel(len(parts), *refs), grid=(...  6.05 us
  transfers between devices with their start and end apart: 28, of which 12 were waited for; matrix products, arithmetic and copies ran while one was open for 0% of the time, Pallas kernels for 35%

profile of v11, /device:TPU:0, one launch (start us, length us, event | category | flops | bytes accessed | tf_op | source)
XLA Modules:
  0.0 115.1 jit_solution(12034981343142859808)
XLA Ops:
  0.6 0.6 stack.23.where_ref.refs_0_
  1.3 5.5 %first.1 = (bf16[8,128,256]{2,1,0:T(8,128)(2,1)}, bf16[2048,128]{1,0:T(8,128)(2,1)}, bf16[2048,128]{1,0:T(8,128)(2,1)}, bf16[2048,128]{1,0:T(8,128)(2,1)}, bf16[2048,128]{1,0:T(8,128)(2,1)}) custom-call(s32[5]{0:T(128)} %stack.23.where_ref.refs_0_, bf16[128,8192]{1,0:T(8,128)(2,1)} %bitcast.10, bf16[8192,1280]{1,0:T(8,128)(2,1)} %w_kv_ref.1), custom_call_target="tpu_custom_call" | custom-call | flops 1 | bytes 1 | tf_op jit(solution)/shard_map/first/pallas_call | solution.py:82
  6.8 1.6 %collective-permute-start.1 = (bf16[2048,128]{1,0:T(8,128)(2,1)}, bf16[2048,128]{1,0:T(8,128)(2,1)}, u32[]{:S(2)}, u32[]{:S(2)}) collective-permute-start(bf16[2048,128]{1,0:T(8,128)(2,1)} %get-tuple-element.40), channel_id=1, source_target_pairs={{0,16},{16,32},{32,48},{48,0},{1,17},{17,33},{33,49},{49,1},{2,18}... | collective-permute-start | bytes 1572872 | tf_op jit(solution)/shard_map/ppermute | solution.py:397
  8.4 2.7 %collective-permute-start.2 = (bf16[2048,128]{1,0:T(8,128)(2,1)}, bf16[2048,128]{1,0:T(8,128)(2,1)}, u32[]{:S(2)}, u32[]{:S(2)}) collective-permute-start(bf16[2048,128]{1,0:T(8,128)(2,1)} %get-tuple-element.42), channel_id=1, source_target_pairs={{0,32},{16,48},{32,0},{48,16},{1,33},{17,49},{33,1},{49,17},{2,34}... | collective-permute-start | bytes 1572872 | tf_op jit(solution)/shard_map/ppermute | solution.py:397
  11.2 1.4 %collective-permute-start.3 = (bf16[2048,128]{1,0:T(8,128)(2,1)}, bf16[2048,128]{1,0:T(8,128)(2,1)}, u32[]{:S(2)}, u32[]{:S(2)}) collective-permute-start(bf16[2048,128]{1,0:T(8,128)(2,1)} %get-tuple-element.44), channel_id=1, source_target_pairs={{0,48},{16,0},{32,16},{48,32},{1,49},{17,1},{33,17},{49,33},{2,50}... | collective-permute-start | bytes 1572872 | tf_op jit(solution)/shard_map/ppermute | solution.py:397
  12.6 7.8 %all-to-all-start = ((bf16[8,128,256]{2,1,0:T(8,128)(2,1)}), bf16[8,128,256]{2,1,0:T(8,128)(2,1)S(1)}, u32[]{:S(2)}, u32[]{:S(2)}) async-start(bf16[8,128,256]{2,1,0:T(8,128)(2,1)} %get-tuple-element.33), calls=%async_computation | async-start | bytes 1048576 | tf_op jit(solution)/shard_map/all_to_all | solution.py:437
  20.4 7.4 %project_query.1.q_ref = bf16[128,1024]{1,0:T(8,128)(2,1)S(1)} custom-call(bf16[128,8192]{1,0:T(8,128)(2,1)S(1)} %bitcast.11, bf16[8192,1280]{1,0:T(8,128)(2,1)} %w_kv_ref.1), custom_call_target="tpu_custom_call" | custom-call | flops 1 | bytes 1 | tf_op jit(solution)/shard_map/project_query/pallas_call | solution.py:110
  27.9 3.3 %all-to-all-done = bf16[8,128,256]{2,1,0:T(8,128)(2,1)S(1)} async-done(((bf16[8,128,256]{2,1,0:T(8,128)(2,1)}), bf16[8,128,256]{2,1,0:T(8,128)(2,1)S(1)}, u32[]{:S(2)}, u32[]{:S(2)}) %all-to-all-start) | async-done | bytes 524320 | tf_op jit(solution)/shard_map/all_to_all | solution.py:437
  31.2 6.9 %attention.1 = (bf16[128,1024]{1,0:T(8,128)(2,1)}, bf16[1024,256]{1,0:T(8,128)(2,1)}) custom-call(s32[5]{0:T(128)S(1)} %copy-done.3, s32[1,16]{1,0:T(1,128)S(1)} %copy-done.5, s32[1,4]{1,0:T(1,128)S(1)} %copy-done.6, bf16[128,1024]{1,0:T(8,128)(2,1)S(1)} %project_query.1.q_ref, bf16[128,1024]{1,0:T(8,128)(2,1)S(1)} %bitcast.13, bf16[1024,256]{1,0:T(8,128)(2,1)S(1)} %bitcast.12), custom_call_target="tpu_custom_call" | custom-call | flops 1 | bytes 1 | tf_op jit(solution)/shard_map/attention/pallas_call | solution.py:205
  38.0 2.4 %forward.1 = bf16[1024,512]{1,0:T(8,128)(2,1)} custom-call(bf16[2048,128]{1,0:T(8,128)(2,1)} %get-tuple-element.39.refs_0_.refs_1_.refs_2_, bf16[2048,128]{1,0:T(8,128)(2,1)} %collective-permute-done.1.refs_1_.refs_2_.refs_3_, bf16[2048,128]{1,0:T(8,128)(2,1)} %collective-permute-done.2.refs_2_.refs_3_.refs_4_, ...), custom_call_target="tpu_custom_call" | custom-call | flops 1 | bytes 1 | tf_op jit(solution)/shard_map/forward/pallas_call | solution.py:136
  40.4 0.5 collective-permute-start
  40.9 0.6 collective-permute-start.5
  41.5 1.2 %collective-permute-start.6 = (bf16[128,1024]{1,0:T(8,128)(2,1)S(1)}, bf16[128,1024]{1,0:T(8,128)(2,1)S(1)}, u32[]{:S(2)}, u32[]{:S(2)}) collective-permute-start(bf16[128,1024]{1,0:T(8,128)(2,1)S(1)} %copy-done.8), channel_id=1, source_target_pairs={{0,32},{16,48},{32,0},{48,16},{1,33},{17,49},{33,1},{49,17},{2,34}... | collective-permute-start | bytes 786440 | tf_op jit(solution)/shard_map/ppermute | solution.py:397
  42.7 1.5 %collective-permute-start.7 = (bf16[128,1024]{1,0:T(8,128)(2,1)S(1)}, bf16[128,1024]{1,0:T(8,128)(2,1)S(1)}, u32[]{:S(2)}, u32[]{:S(2)}) collective-permute-start(bf16[128,1024]{1,0:T(8,128)(2,1)S(1)} %copy-done.8), channel_id=1, source_target_pairs={{0,48},{16,0},{32,16},{48,32},{1,49},{17,1},{33,17},{49,33},{2,50}... | collective-permute-start | bytes 786440 | tf_op jit(solution)/shard_map/ppermute | solution.py:397
  44.2 6.1 %all-to-all-start.1 = ((bf16[8,128,256]{2,1,0:T(8,128)(2,1)}), bf16[8,128,256]{2,1,0:T(8,128)(2,1)S(1)}, u32[]{:S(2)}, u32[]{:S(2)}) async-start(bf16[8,128,256]{2,1,0:T(8,128)(2,1)} %bitcast.8), calls=%async_computation.1 | async-start | bytes 1048576 | tf_op jit(solution)/shard_map/all_to_all | solution.py:445
  50.3 6.8 %d_x_first.1.part_ref = bf16[128,8192]{1,0:T(8,128)(2,1)} custom-call(bf16[128,1024]{1,0:T(8,128)(2,1)} %get-tuple-element.46.g_ref.refs_5_, bf16[8192,1280]{1,0:T(8,128)(2,1)} %w_kv_ref.1), custom_call_target="tpu_custom_call" | custom-call | flops 1 | bytes 1 | tf_op jit(solution)/shard_map/d_x_first/pallas_call | solution.py:383
  57.3 0.5 collective-permute-start.9
  58.0 0.7 collective-permute-done.8.refs_10_
  58.8 0.4 collective-permute-done.9.refs_11_
  59.1 0.4 collective-permute-done.10.refs_12_
  59.5 0.3 copy-done.15
  59.8 0.4 copy-done.16
  60.2 1.0 copy-done.7
  61.2 6.1 %term_query.1 = bf16[4,256,1024]{2,1,0:T(8,128)(2,1)} custom-call(bf16[1024,512]{1,0:T(8,128)(2,1)} %copy-done.7, bf16[2048,128]{1,0:T(8,128)(2,1)} %get-tuple-element.39.refs_0_.refs_1_.refs_2_, bf16[2048,128]{1,0:T(8,128)(2,1)} %collective-permute-done.1.refs_1_.refs_2_.refs_3_, bf16[2048,128]{1,0:T(8,128)(2,1)} %collective-permute-done.2.refs_2_.refs_3_.refs_4_, ...), custom_call_target="tpu_custom_call" | custom-call | flops 1 | bytes 1 | tf_op jit(solution)/shard_map/term_query/pallas_call | solution.py:247
  67.3 4.8 %all-to-all-start.2 = ((bf16[4,256,1024]{2,1,0:T(8,128)(2,1)}), bf16[4,256,1024]{2,1,0:T(8,128)(2,1)S(1)}, u32[]{:S(2)}, u32[]{:S(2)}) async-start(bf16[4,256,1024]{2,1,0:T(8,128)(2,1)} %term_query.1), calls=%async_computation.2 | async-start | bytes 4194304 | tf_op jit(solution)/shard_map/all_to_all | solution.py:450
  72.1 0.5 collective-permute-start.11
  72.7 1.1 collective-permute-start.12
  73.8 1.9 %collective-permute-start.13 = (bf16[128,256]{1,0:T(8,128)(2,1)S(1)}, bf16[128,256]{1,0:T(8,128)(2,1)S(1)}, u32[]{:S(2)}, u32[]{:S(2)}) collective-permute-start(bf16[128,256]{1,0:T(8,128)(2,1)S(1)} %reduce_sum.12.refs_6_.kv_ref), channel_id=1, source_target_pairs={{0,48},{16,0},{32,16},{48,32},{1,49},{17,1},{33,17},{49,33},{2,50}... | collective-permute-start | bytes 196616 | tf_op jit(solution)/shard_map/ppermute | solution.py:397
  75.7 3.0 %collective-permute-done.11.refs_7_ = bf16[128,256]{1,0:T(8,128)(2,1)S(1)} collective-permute-done((bf16[128,256]{1,0:T(8,128)(2,1)S(1)}, bf16[128,256]{1,0:T(8,128)(2,1)S(1)}, u32[]{:S(2)}, u32[]{:S(2)}) %collective-permute-start.11) | collective-permute-done | bytes 65568 | tf_op jit(solution)/shard_map/ppermute | solution.py:397
  78.7 0.5 collective-permute-start.16
  79.3 0.6 collective-permute-done.15.refs_11_
  80.1 0.4 collective-permute-done.17.refs_13_
  80.7 0.7 copy-done.23
  81.4 3.1 %term_kv.1 = (bf16[256,256]{1,0:T(8,128)(2,1)}, bf16[256,256]{1,0:T(8,128)(2,1)}, bf16[256,256]{1,0:T(8,128)(2,1)}, bf16[256,256]{1,0:T(8,128)(2,1)}) custom-call(s32[5]{0:T(128)} %stack.23.where_ref.refs_0_, bf16[1024,512]{1,0:T(8,128)(2,1)} %copy-done.7, bf16[2048,128]{1,0:T(8,128)(2,1)} %get-tuple-element.39.refs_0_.refs_1_.refs_2_, ...), custom_call_target="tpu_custom_call" | custom-call | flops 1 | bytes 1 | tf_op jit(solution)/shard_map/term_kv/pallas_call | solution.py:277
  84.5 1.0 collective-permute-start.18
  85.5 3.6 %collective-permute-start.19 = (bf16[256,256]{1,0:T(8,128)(2,1)}, bf16[256,256]{1,0:T(8,128)(2,1)S(1)}, u32[]{:S(2)}, u32[]{:S(2)}) collective-permute-start(bf16[256,256]{1,0:T(8,128)(2,1)} %get-tuple-element.55), channel_id=1, source_target_pairs={{0,4},{64,68},{4,0},{68,64},{1,5},{65,69},{5,1},{69,65},{2,6},{66,... | collective-permute-start | bytes 393224 | tf_op jit(solution)/shard_map/ppermute | solution.py:420
  89.1 1.0 collective-permute-start.20
  90.1 9.2 %d_x_last.1 = bf16[128,8192]{1,0:T(8,128)(2,1)} custom-call(bf16[128,1024]{1,0:T(8,128)(2,1)} %get-tuple-element.46.g_ref.refs_5_, bf16[128,256]{1,0:T(8,128)(2,1)} %copy-done.9, bf16[8192,1280]{1,0:T(8,128)(2,1)} %w_kv_ref.1, bf16[8192,1280]{1,0:T(8,128)(2,1)} %w_kv_ref.1, bf16[128,8192]{1,0:T(8,128)(2,1)} %d_x_first.1.part_ref), custom_call_target="tpu_custom_call" | custom-call | flops 1 | bytes 1 | tf_op jit(solution)/shard_map/d_x_last/pallas_call | solution.py:383
  99.4 1.2 %middle_y.1 = (f32[64,256]{1,0:T(8,128)S(1)}, bf16[64,256]{1,0:T(8,128)(2,1)}, bf16[64,256]{1,0:T(8,128)(2,1)}, bf16[64,256]{1,0:T(8,128)(2,1)}) custom-call(s32[5]{0:T(128)S(1)} %copy-done.4, bf16[256,256]{1,0:T(8,128)(2,1)S(1)} %copy-done.2, bf16[256,256]{1,0:T(8,128)(2,1)S(1)} %collective-permute-done.18.refs_1_, ...), custom_call_target="tpu_custom_call" | custom-call | flops 1 | bytes 1 | tf_op jit(solution)/shard_map/middle_y/pallas_call | solution.py:323
  100.6 1.1 middle_z.1
  101.7 3.5 %all-to-all-start.3 = ((bf16[4,64,1024]{2,1,0:T(8,128)(2,1)}), bf16[4,64,1024]{2,1,0:T(8,128)(2,1)S(1)}, u32[]{:S(2)}, u32[]{:S(2)}) async-start(bf16[4,64,1024]{2,1,0:T(8,128)(2,1)} %middle_z.1), calls=%async_computation.3 | async-start | bytes 1048576 | tf_op jit(solution)/shard_map/all_to_all | solution.py:457
  105.2 1.9 %collective-permute-start.21 = (bf16[64,256]{1,0:T(8,128)(2,1)S(1)}, bf16[64,256]{1,0:T(8,128)(2,1)S(1)}, u32[]{:S(2)}, u32[]{:S(2)}) collective-permute-start(bf16[64,256]{1,0:T(8,128)(2,1)S(1)} %copy-done.26), channel_id=1, source_target_pairs={{0,1},{1,2},{2,3},{3,0},{4,5},{5,6},{6,7},{7,4},{8,9},{9,10},{10,1... | collective-permute-start | bytes 98312 | tf_op jit(solution)/shard_map/ppermute | solution.py:424
  107.1 2.7 %collective-permute-start.22 = (bf16[64,256]{1,0:T(8,128)(2,1)S(1)}, bf16[64,256]{1,0:T(8,128)(2,1)S(1)}, u32[]{:S(2)}, u32[]{:S(2)}) collective-permute-start(bf16[64,256]{1,0:T(8,128)(2,1)S(1)} %copy-done.25), channel_id=1, source_target_pairs={{0,2},{1,3},{2,0},{3,1},{4,6},{5,7},{6,4},{7,5},{8,10},{9,11},{10,... | collective-permute-start | bytes 98312 | tf_op jit(solution)/shard_map/ppermute | solution.py:424
  109.8 1.5 %collective-permute-start.23 = (bf16[64,256]{1,0:T(8,128)(2,1)S(1)}, bf16[64,256]{1,0:T(8,128)(2,1)S(1)}, u32[]{:S(2)}, u32[]{:S(2)}) collective-permute-start(bf16[64,256]{1,0:T(8,128)(2,1)S(1)} %copy-done.24), channel_id=1, source_target_pairs={{0,3},{1,0},{2,1},{3,2},{4,7},{5,4},{6,5},{7,6},{8,11},{9,8},{10,9... | collective-permute-start | bytes 98312 | tf_op jit(solution)/shard_map/ppermute | solution.py:424
  111.2 1.3 %collective-permute-done.22.refs_2_ = bf16[64,256]{1,0:T(8,128)(2,1)S(1)} collective-permute-done((bf16[64,256]{1,0:T(8,128)(2,1)S(1)}, bf16[64,256]{1,0:T(8,128)(2,1)S(1)}, u32[]{:S(2)}, u32[]{:S(2)}) %collective-permute-start.22) | collective-permute-done | bytes 32800 | tf_op jit(solution)/shard_map/ppermute | solution.py:424
  112.5 1.2 %collective-permute-done.23.refs_3_ = bf16[64,256]{1,0:T(8,128)(2,1)S(1)} collective-permute-done((bf16[64,256]{1,0:T(8,128)(2,1)S(1)}, bf16[64,256]{1,0:T(8,128)(2,1)S(1)}, u32[]{:S(2)}, u32[]{:S(2)}) %collective-permute-start.23) | collective-permute-done | bytes 32800 | tf_op jit(solution)/shard_map/ppermute | solution.py:424
  113.7 0.6 all-to-all-done.3.stack_ref
  114.3 0.8 final.1
  (75 shorter events, 1.0 us)
Async XLA Ops:
  1.3 19.1 %copy-start = (bf16[1,128,8192]{2,1,0:T(8,128)(2,1)S(1)}, bf16[1,128,8192]{2,1,0:T(8,128)(2,1)}, u32[]{:S(2)}) copy-start(bf16[1,128,8192]{2,1,0:T(8,128)(2,1)} %param.5) | copy-start | bytes 6291460
  6.8 31.2 %collective-permute-start.1 = (bf16[2048,128]{1,0:T(8,128)(2,1)}, bf16[2048,128]{1,0:T(8,128)(2,1)}, u32[]{:S(2)}, u32[]{:S(2)}) collective-permute-start(bf16[2048,128]{1,0:T(8,128)(2,1)} %get-tuple-element.40), channel_id=1, source_target_pairs={{0,16},{16,32},{32,48},{48,0},{1,17},{17,33},{33,49},{49,1},{2,18}... | collective-permute-start | bytes 1572872 | tf_op jit(solution)/shard_map/ppermute | solution.py:397
  8.4 29.6 %collective-permute-start.2 = (bf16[2048,128]{1,0:T(8,128)(2,1)}, bf16[2048,128]{1,0:T(8,128)(2,1)}, u32[]{:S(2)}, u32[]{:S(2)}) collective-permute-start(bf16[2048,128]{1,0:T(8,128)(2,1)} %get-tuple-element.42), channel_id=1, source_target_pairs={{0,32},{16,48},{32,0},{48,16},{1,33},{17,49},{33,1},{49,17},{2,34}... | collective-permute-start | bytes 1572872 | tf_op jit(solution)/shard_map/ppermute | solution.py:397
  11.2 26.9 %collective-permute-start.3 = (bf16[2048,128]{1,0:T(8,128)(2,1)}, bf16[2048,128]{1,0:T(8,128)(2,1)}, u32[]{:S(2)}, u32[]{:S(2)}) collective-permute-start(bf16[2048,128]{1,0:T(8,128)(2,1)} %get-tuple-element.44), channel_id=1, source_target_pairs={{0,48},{16,0},{32,16},{48,32},{1,49},{17,1},{33,17},{49,33},{2,50}... | collective-permute-start | bytes 1572872 | tf_op jit(solution)/shard_map/ppermute | solution.py:397
  12.6 18.5 %all-to-all-start = ((bf16[8,128,256]{2,1,0:T(8,128)(2,1)}), bf16[8,128,256]{2,1,0:T(8,128)(2,1)S(1)}, u32[]{:S(2)}, u32[]{:S(2)}) async-start(bf16[8,128,256]{2,1,0:T(8,128)(2,1)} %get-tuple-element.33), calls=%async_computation | async-start | bytes 1048576 | tf_op jit(solution)/shard_map/all_to_all | solution.py:437
  20.4 10.7 %copy-start.1 = (bf16[1,128,1024]{2,1,0:T(8,128)(2,1)S(1)}, bf16[1,128,1024]{2,1,0:T(8,128)(2,1)}, u32[]{:S(2)}) copy-start(bf16[1,128,1024]{2,1,0:T(8,128)(2,1)} %param.7) | copy-start | bytes 786436
  20.4 10.7 %copy-start.3 = (s32[5]{0:T(128)S(1)}, s32[5]{0:T(128)}, u32[]{:S(2)}) copy-start(s32[5]{0:T(128)} %stack.23.where_ref.refs_0_) | copy-start | bytes 64
  20.4 10.7 %copy-start.5 = (s32[1,16]{1,0:T(1,128)S(1)}, s32[1,16]{1,0:T(1,128)}, u32[]{:S(2)}) copy-start(s32[1,16]{1,0:T(1,128)} %order_ref.1) | copy-start | bytes 196
  20.4 10.7 %copy-start.6 = (s32[1,4]{1,0:T(1,128)S(1)}, s32[1,4]{1,0:T(1,128)}, u32[]{:S(2)}) copy-start(s32[1,4]{1,0:T(1,128)} %lens_ref.1) | copy-start | bytes 52
  38.0 2.4 %copy-start.8 = (bf16[128,1024]{1,0:T(8,128)(2,1)S(1)}, bf16[128,1024]{1,0:T(8,128)(2,1)}, u32[]{:S(2)}) copy-start(bf16[128,1024]{1,0:T(8,128)(2,1)} %get-tuple-element.46.g_ref.refs_5_) | copy-start | bytes 786436
  40.4 19.1 %collective-permute-start.4 = (bf16[1024,512]{1,0:T(8,128)(2,1)}, bf16[1024,512]{1,0:T(8,128)(2,1)S(1)}, u32[]{:S(2)}, u32[]{:S(2)}) collective-permute-start(bf16[1024,512]{1,0:T(8,128)(2,1)} %forward.1), channel_id=1, source_target_pairs={{0,8},{8,0},{1,9},{9,1},{2,10},{10,2},{3,11},{11,3},{4,12},{12,4},... | collective-permute-start | bytes 3145736 | tf_op jit(solution)/shard_map/ppermute | solution.py:401
  40.4 3.8 %collective-permute-start = (bf16[128,1024]{1,0:T(8,128)(2,1)S(1)}, bf16[128,1024]{1,0:T(8,128)(2,1)S(1)}, u32[]{:S(2)}, u32[]{:S(2)}) collective-permute-start(bf16[128,1024]{1,0:T(8,128)(2,1)S(1)} %copy-done.8), channel_id=1, source_target_pairs={{0,8},{8,0},{1,9},{9,1},{2,10},{10,2},{3,11},{11,3},{4,12},{12,4},... | collective-permute-start | bytes 786440 | tf_op jit(solution)/shard_map/ppermute | solution.py:401
  40.9 16.2 %collective-permute-start.5 = (bf16[128,1024]{1,0:T(8,128)(2,1)S(1)}, bf16[128,1024]{1,0:T(8,128)(2,1)S(1)}, u32[]{:S(2)}, u32[]{:S(2)}) collective-permute-start(bf16[128,1024]{1,0:T(8,128)(2,1)S(1)} %copy-done.8), channel_id=1, source_target_pairs={{0,16},{16,32},{32,48},{48,0},{1,17},{17,33},{33,49},{49,1},{2,18}... | collective-permute-start | bytes 786440 | tf_op jit(solution)/shard_map/ppermute | solution.py:397
  41.5 15.7 %collective-permute-start.6 = (bf16[128,1024]{1,0:T(8,128)(2,1)S(1)}, bf16[128,1024]{1,0:T(8,128)(2,1)S(1)}, u32[]{:S(2)}, u32[]{:S(2)}) collective-permute-start(bf16[128,1024]{1,0:T(8,128)(2,1)S(1)} %copy-done.8), channel_id=1, source_target_pairs={{0,32},{16,48},{32,0},{48,16},{1,33},{17,49},{33,1},{49,17},{2,34}... | collective-permute-start | bytes 786440 | tf_op jit(solution)/shard_map/ppermute | solution.py:397
  42.7 15.1 %collective-permute-start.7 = (bf16[128,1024]{1,0:T(8,128)(2,1)S(1)}, bf16[128,1024]{1,0:T(8,128)(2,1)S(1)}, u32[]{:S(2)}, u32[]{:S(2)}) collective-permute-start(bf16[128,1024]{1,0:T(8,128)(2,1)S(1)} %copy-done.8), channel_id=1, source_target_pairs={{0,48},{16,0},{32,16},{48,32},{1,49},{17,1},{33,17},{49,33},{2,50}... | collective-permute-start | bytes 786440 | tf_op jit(solution)/shard_map/ppermute | solution.py:397
  44.2 12.9 %copy-start.10 = (bf16[128,1024]{1,0:T(8,128)(2,1)}, bf16[128,1024]{1,0:T(8,128)(2,1)S(1)}, u32[]{:S(2)}) copy-start(bf16[128,1024]{1,0:T(8,128)(2,1)S(1)} %collective-permute-done.refs_9_) | copy-start | bytes 786436
  44.2 23.0 %all-to-all-start.1 = ((bf16[8,128,256]{2,1,0:T(8,128)(2,1)}), bf16[8,128,256]{2,1,0:T(8,128)(2,1)S(1)}, u32[]{:S(2)}, u32[]{:S(2)}) async-start(bf16[8,128,256]{2,1,0:T(8,128)(2,1)} %bitcast.8), calls=%async_computation.1 | async-start | bytes 1048576 | tf_op jit(solution)/shard_map/all_to_all | solution.py:445
  57.1 2.4 %copy-start.11 = (bf16[128,1024]{1,0:T(8,128)(2,1)}, bf16[128,1024]{1,0:T(8,128)(2,1)S(1)}, u32[]{:S(2)}) copy-start(bf16[128,1024]{1,0:T(8,128)(2,1)S(1)} %collective-permute-done.5.refs_6_) | copy-start | bytes 786436
  57.1 1.6 %collective-permute-start.8 = (bf16[128,1024]{1,0:T(8,128)(2,1)S(1)}, bf16[128,1024]{1,0:T(8,128)(2,1)S(1)}, u32[]{:S(2)}, u32[]{:S(2)}) collective-permute-start(bf16[128,1024]{1,0:T(8,128)(2,1)S(1)} %collective-permute-done.5.refs_6_), channel_id=1, source_target_pairs={{0,8},{8,0},{1,9},{9,1},{2,10},{10,2},{3,11},{11,3},{4,12},{12,4},... | collective-permute-start | bytes 786440 | tf_op jit(solution)/shard_map/ppermute | solution.py:401
  57.2 2.3 %copy-start.12 = (bf16[128,1024]{1,0:T(8,128)(2,1)}, bf16[128,1024]{1,0:T(8,128)(2,1)S(1)}, u32[]{:S(2)}) copy-start(bf16[128,1024]{1,0:T(8,128)(2,1)S(1)} %collective-permute-done.6.refs_7_) | copy-start | bytes 786436
  57.3 1.9 %collective-permute-start.9 = (bf16[128,1024]{1,0:T(8,128)(2,1)S(1)}, bf16[128,1024]{1,0:T(8,128)(2,1)S(1)}, u32[]{:S(2)}, u32[]{:S(2)}) collective-permute-start(bf16[128,1024]{1,0:T(8,128)(2,1)S(1)} %collective-permute-done.6.refs_7_), channel_id=1, source_target_pairs={{0,8},{8,0},{1,9},{9,1},{2,10},{10,2},{3,11},{11,3},{4,12},{12,4},... | collective-permute-start | bytes 786440 | tf_op jit(solution)/shard_map/ppermute | solution.py:401
  57.7 1.8 %copy-start.13 = (bf16[128,1024]{1,0:T(8,128)(2,1)}, bf16[128,1024]{1,0:T(8,128)(2,1)S(1)}, u32[]{:S(2)}) copy-start(bf16[128,1024]{1,0:T(8,128)(2,1)S(1)} %collective-permute-done.7.refs_8_) | copy-start | bytes 786436
  57.7 1.8 %collective-permute-start.10 = (bf16[128,1024]{1,0:T(8,128)(2,1)S(1)}, bf16[128,1024]{1,0:T(8,128)(2,1)S(1)}, u32[]{:S(2)}, u32[]{:S(2)}) collective-permute-start(bf16[128,1024]{1,0:T(8,128)(2,1)S(1)} %collective-permute-done.7.refs_8_), channel_id=1, source_target_pairs={{0,8},{8,0},{1,9},{9,1},{2,10},{10,2},{3,11},{11,3},{4,12},{12,4},... | collective-permute-start | bytes 786440 | tf_op jit(solution)/shard_map/ppermute | solution.py:401
  67.3 33.3 %all-to-all-start.2 = ((bf16[4,256,1024]{2,1,0:T(8,128)(2,1)}), bf16[4,256,1024]{2,1,0:T(8,128)(2,1)S(1)}, u32[]{:S(2)}, u32[]{:S(2)}) async-start(bf16[4,256,1024]{2,1,0:T(8,128)(2,1)} %term_query.1), calls=%async_computation.2 | async-start | bytes 4194304 | tf_op jit(solution)/shard_map/all_to_all | solution.py:450
  72.1 8.4 %copy-start.9 = (bf16[128,256]{1,0:T(8,128)(2,1)}, bf16[128,256]{1,0:T(8,128)(2,1)S(1)}, u32[]{:S(2)}) copy-start(bf16[128,256]{1,0:T(8,128)(2,1)S(1)} %reduce_sum.12.refs_6_.kv_ref) | copy-start | bytes 196612
  72.1 6.5 %collective-permute-start.11 = (bf16[128,256]{1,0:T(8,128)(2,1)S(1)}, bf16[128,256]{1,0:T(8,128)(2,1)S(1)}, u32[]{:S(2)}, u32[]{:S(2)}) collective-permute-start(bf16[128,256]{1,0:T(8,128)(2,1)S(1)} %reduce_sum.12.refs_6_.kv_ref), channel_id=1, source_target_pairs={{0,16},{16,32},{32,48},{48,0},{1,17},{17,33},{33,49},{49,1},{2,18}... | collective-permute-start | bytes 196616 | tf_op jit(solution)/shard_map/ppermute | solution.py:397
  72.7 6.0 %collective-permute-start.12 = (bf16[128,256]{1,0:T(8,128)(2,1)S(1)}, bf16[128,256]{1,0:T(8,128)(2,1)S(1)}, u32[]{:S(2)}, u32[]{:S(2)}) collective-permute-start(bf16[128,256]{1,0:T(8,128)(2,1)S(1)} %reduce_sum.12.refs_6_.kv_ref), channel_id=1, source_target_pairs={{0,32},{16,48},{32,0},{48,16},{1,33},{17,49},{33,1},{49,17},{2,34}... | collective-permute-start | bytes 196616 | tf_op jit(solution)/shard_map/ppermute | solution.py:397
  73.8 5.4 %collective-permute-start.13 = (bf16[128,256]{1,0:T(8,128)(2,1)S(1)}, bf16[128,256]{1,0:T(8,128)(2,1)S(1)}, u32[]{:S(2)}, u32[]{:S(2)}) collective-permute-start(bf16[128,256]{1,0:T(8,128)(2,1)S(1)} %reduce_sum.12.refs_6_.kv_ref), channel_id=1, source_target_pairs={{0,48},{16,0},{32,16},{48,32},{1,49},{17,1},{33,17},{49,33},{2,50}... | collective-permute-start | bytes 196616 | tf_op jit(solution)/shard_map/ppermute | solution.py:397
  75.7 3.6 %collective-permute-start.14 = (bf16[128,256]{1,0:T(8,128)(2,1)S(1)}, bf16[128,256]{1,0:T(8,128)(2,1)S(1)}, u32[]{:S(2)}, u32[]{:S(2)}) collective-permute-start(bf16[128,256]{1,0:T(8,128)(2,1)S(1)} %reduce_sum.12.refs_6_.kv_ref), channel_id=1, source_target_pairs={{0,8},{8,0},{1,9},{9,1},{2,10},{10,2},{3,11},{11,3},{4,12},{12,4},... | collective-permute-start | bytes 196616 | tf_op jit(solution)/shard_map/ppermute | solution.py:401
  78.7 1.8 %copy-start.17 = (bf16[128,256]{1,0:T(8,128)(2,1)}, bf16[128,256]{1,0:T(8,128)(2,1)S(1)}, u32[]{:S(2)}) copy-start(bf16[128,256]{1,0:T(8,128)(2,1)S(1)} %collective-permute-done.11.refs_7_) | copy-start | bytes 196612
  78.7 1.3 %collective-permute-start.15 = (bf16[128,256]{1,0:T(8,128)(2,1)S(1)}, bf16[128,256]{1,0:T(8,128)(2,1)S(1)}, u32[]{:S(2)}, u32[]{:S(2)}) collective-permute-start(bf16[128,256]{1,0:T(8,128)(2,1)S(1)} %collective-permute-done.11.refs_7_), channel_id=1, source_target_pairs={{0,8},{8,0},{1,9},{9,1},{2,10},{10,2},{3,11},{11,3},{4,12},{12,4},... | collective-permute-start | bytes 196616 | tf_op jit(solution)/shard_map/ppermute | solution.py:401
  78.7 1.8 %copy-start.18 = (bf16[128,256]{1,0:T(8,128)(2,1)}, bf16[128,256]{1,0:T(8,128)(2,1)S(1)}, u32[]{:S(2)}) copy-start(bf16[128,256]{1,0:T(8,128)(2,1)S(1)} %collective-permute-done.12.refs_8_) | copy-start | bytes 196612
  78.7 1.4 %collective-permute-start.16 = (bf16[128,256]{1,0:T(8,128)(2,1)S(1)}, bf16[128,256]{1,0:T(8,128)(2,1)S(1)}, u32[]{:S(2)}, u32[]{:S(2)}) collective-permute-start(bf16[128,256]{1,0:T(8,128)(2,1)S(1)} %collective-permute-done.12.refs_8_), channel_id=1, source_target_pairs={{0,8},{8,0},{1,9},{9,1},{2,10},{10,2},{3,11},{11,3},{4,12},{12,4},... | collective-permute-start | bytes 196616 | tf_op jit(solution)/shard_map/ppermute | solution.py:401
  79.2 1.3 %copy-start.19 = (bf16[128,256]{1,0:T(8,128)(2,1)}, bf16[128,256]{1,0:T(8,128)(2,1)S(1)}, u32[]{:S(2)}) copy-start(bf16[128,256]{1,0:T(8,128)(2,1)S(1)} %collective-permute-done.13.refs_9_) | copy-start | bytes 196612
  79.2 1.3 %collective-permute-start.17 = (bf16[128,256]{1,0:T(8,128)(2,1)S(1)}, bf16[128,256]{1,0:T(8,128)(2,1)S(1)}, u32[]{:S(2)}, u32[]{:S(2)}) collective-permute-start(bf16[128,256]{1,0:T(8,128)(2,1)S(1)} %collective-permute-done.13.refs_9_), channel_id=1, source_target_pairs={{0,8},{8,0},{1,9},{9,1},{2,10},{10,2},{3,11},{11,3},{4,12},{12,4},... | collective-permute-start | bytes 196616 | tf_op jit(solution)/shard_map/ppermute | solution.py:401
  79.3 1.2 %copy-start.20 = (bf16[128,256]{1,0:T(8,128)(2,1)}, bf16[128,256]{1,0:T(8,128)(2,1)S(1)}, u32[]{:S(2)}) copy-start(bf16[128,256]{1,0:T(8,128)(2,1)S(1)} %collective-permute-done.14.refs_10_) | copy-start | bytes 196612
  84.5 14.8 %collective-permute-start.18 = (bf16[256,256]{1,0:T(8,128)(2,1)}, bf16[256,256]{1,0:T(8,128)(2,1)S(1)}, u32[]{:S(2)}, u32[]{:S(2)}) collective-permute-start(bf16[256,256]{1,0:T(8,128)(2,1)} %get-tuple-element.53), channel_id=1, source_target_pairs={{0,64},{64,4},{4,68},{68,0},{1,65},{65,5},{5,69},{69,1},{2,66},{66... | collective-permute-start | bytes 393224 | tf_op jit(solution)/shard_map/ppermute | solution.py:420
  85.5 13.8 %collective-permute-start.19 = (bf16[256,256]{1,0:T(8,128)(2,1)}, bf16[256,256]{1,0:T(8,128)(2,1)S(1)}, u32[]{:S(2)}, u32[]{:S(2)}) collective-permute-start(bf16[256,256]{1,0:T(8,128)(2,1)} %get-tuple-element.55), channel_id=1, source_target_pairs={{0,4},{64,68},{4,0},{68,64},{1,5},{65,69},{5,1},{69,65},{2,6},{66,... | collective-permute-start | bytes 393224 | tf_op jit(solution)/shard_map/ppermute | solution.py:420
  89.1 10.3 %collective-permute-start.20 = (bf16[256,256]{1,0:T(8,128)(2,1)}, bf16[256,256]{1,0:T(8,128)(2,1)S(1)}, u32[]{:S(2)}, u32[]{:S(2)}) collective-permute-start(bf16[256,256]{1,0:T(8,128)(2,1)} %get-tuple-element.57), channel_id=1, source_target_pairs={{0,68},{64,0},{4,64},{68,4},{1,69},{65,1},{5,65},{69,5},{2,70},{66... | collective-permute-start | bytes 393224 | tf_op jit(solution)/shard_map/ppermute | solution.py:420
  90.1 9.3 %copy-start.2 = (bf16[256,256]{1,0:T(8,128)(2,1)S(1)}, bf16[256,256]{1,0:T(8,128)(2,1)}, u32[]{:S(2)}) copy-start(bf16[256,256]{1,0:T(8,128)(2,1)} %get-tuple-element.51.refs_0_) | copy-start | bytes 393220
  90.1 9.3 %copy-start.4 = (s32[5]{0:T(128)S(1)}, s32[5]{0:T(128)}, u32[]{:S(2)}) copy-start(s32[5]{0:T(128)} %stack.23.where_ref.refs_0_) | copy-start | bytes 64
  100.6 4.6 %copy-start.26 = (bf16[64,256]{1,0:T(8,128)(2,1)S(1)}, bf16[64,256]{1,0:T(8,128)(2,1)}, u32[]{:S(2)}) copy-start(bf16[64,256]{1,0:T(8,128)(2,1)} %get-tuple-element.59) | copy-start | bytes 98308
  100.6 6.5 %copy-start.25 = (bf16[64,256]{1,0:T(8,128)(2,1)S(1)}, bf16[64,256]{1,0:T(8,128)(2,1)}, u32[]{:S(2)}) copy-start(bf16[64,256]{1,0:T(8,128)(2,1)} %get-tuple-element.62) | copy-start | bytes 98308
  100.6 9.2 %copy-start.24 = (bf16[64,256]{1,0:T(8,128)(2,1)S(1)}, bf16[64,256]{1,0:T(8,128)(2,1)}, u32[]{:S(2)}) copy-start(bf16[64,256]{1,0:T(8,128)(2,1)} %get-tuple-element.63) | copy-start | bytes 98308
  101.7 12.6 %all-to-all-start.3 = ((bf16[4,64,1024]{2,1,0:T(8,128)(2,1)}), bf16[4,64,1024]{2,1,0:T(8,128)(2,1)S(1)}, u32[]{:S(2)}, u32[]{:S(2)}) async-start(bf16[4,64,1024]{2,1,0:T(8,128)(2,1)} %middle_z.1), calls=%async_computation.3 | async-start | bytes 1048576 | tf_op jit(solution)/shard_map/all_to_all | solution.py:457
  105.2 6.1 %collective-permute-start.21 = (bf16[64,256]{1,0:T(8,128)(2,1)S(1)}, bf16[64,256]{1,0:T(8,128)(2,1)S(1)}, u32[]{:S(2)}, u32[]{:S(2)}) collective-permute-start(bf16[64,256]{1,0:T(8,128)(2,1)S(1)} %copy-done.26), channel_id=1, source_target_pairs={{0,1},{1,2},{2,3},{3,0},{4,5},{5,6},{6,7},{7,4},{8,9},{9,10},{10,1... | collective-permute-start | bytes 98312 | tf_op jit(solution)/shard_map/ppermute | solution.py:424
  107.1 5.4 %collective-permute-start.22 = (bf16[64,256]{1,0:T(8,128)(2,1)S(1)}, bf16[64,256]{1,0:T(8,128)(2,1)S(1)}, u32[]{:S(2)}, u32[]{:S(2)}) collective-permute-start(bf16[64,256]{1,0:T(8,128)(2,1)S(1)} %copy-done.25), channel_id=1, source_target_pairs={{0,2},{1,3},{2,0},{3,1},{4,6},{5,7},{6,4},{7,5},{8,10},{9,11},{10,... | collective-permute-start | bytes 98312 | tf_op jit(solution)/shard_map/ppermute | solution.py:424
  109.8 3.9 %collective-permute-start.23 = (bf16[64,256]{1,0:T(8,128)(2,1)S(1)}, bf16[64,256]{1,0:T(8,128)(2,1)S(1)}, u32[]{:S(2)}, u32[]{:S(2)}) collective-permute-start(bf16[64,256]{1,0:T(8,128)(2,1)S(1)} %copy-done.24), channel_id=1, source_target_pairs={{0,3},{1,0},{2,1},{3,2},{4,7},{5,4},{6,5},{7,6},{8,11},{9,8},{10,9... | collective-permute-start | bytes 98312 | tf_op jit(solution)/shard_map/ppermute | solution.py:424
  (7 other events, 5.1 us)

commit v12 on v11

--- a/solution.py
+++ b/solution.py
@@ -250,7 +250,7 @@
         out_shape=pltpu.HBM((blocks, half // blocks, width), jnp.bfloat16),
         in_specs=[whole(other)] + [half_of(part, 0) for part in parts] + [VMEM] * len(pieces),
         out_specs=pl.BlockSpec((blocks, half // blocks, step), lambda j: (0, 0, j)),
-        compiler_params=pltpu.CompilerParams(vmem_limit_bytes=60 * MIB),
+        compiler_params=pltpu.CompilerParams(vmem_limit_bytes=20 * MIB),
         cost_estimate=SMALL,
         name="term_query",
     )(other, *parts, *pieces)

time: 116 us -> 116 us (level)
  starting transfers between devices: 48.3 us -> 46.6 us
    ppermute x9, starting transfers between devices: 12.6 us -> 14.7 us  [shifted(): return lax.ppermute(value, 'x', [(i, (i + s) % n) for i in range(n)])]
    all_to_all x1, starting transfers between devices: 6.09 us -> 4.14 us  [local(): lax.all_to_all(after(terms, other_q[0]).reshape(seq, tokens, 2 * HD), SEQ...]
    unnamed x54 -> x48, local copies, waits for them, and re-layouts: 2.57 us -> 2.61 us
  transfers between devices with their start and end apart: 28 -> 28, of which waited for: 12 -> 14; matrix products, arithmetic and copies ran while one was open for 0% -> 1% of each run, Pallas kernels for 35% -> 35%
where the time goes in v12:
time: 116 us; the launch traced here: 114 us
  Pallas kernels  50.3 us (43%)
  starting transfers between devices  46.6 us (40%)
  waiting for transfers between devices  12.2 us (11%)
  local copies, waits for them, and re-layouts  3.27 us (3%)
    pallas_call x2, Pallas kernels, input_grad(): pl.pallas_call(kernel, grid=(features // step,), out_shape=pltpu.HBM((tok...  16.2 us
    ppermute x9, starting transfers between devices, shifted(): return lax.ppermute(value, 'x', [(i, (i + s) % n) for i in range(n)])  14.7 us
    all_to_all x1, starting transfers between devices, local(): lax.all_to_all(copies, SEQ, 0, 0, tiled=True).reshape(seq * tokens, 2 * HD)  7.78 us
    pallas_call x1, Pallas kernels, project_query(): pl.pallas_call(query_kernel, grid=(HQ // 2,), out_shape=jax.ShapeDtypeStr...  7.4 us
    pallas_call x1, Pallas kernels, attention(): pl.pallas_call(attention_kernel, out_shape=(pltpu.HBM((tokens, HQ * HD),...  7.36 us
    ppermute x3, starting transfers between devices, shifted_y(): return lax.ppermute(value, 'y', [(i, (i + s) % 4) for i in range(4)])  6.19 us
    pallas_call x1, Pallas kernels, first(): pl.pallas_call(first_kernel, out_shape=(pltpu.HBM((copies, tokens, width)...  5.53 us
    ppermute x3, starting transfers between devices, shifted_z(): lax.ppermute(value, DEPTH, [(ring_index(i), ring_index((i + s) % 4)) for...  5.32 us
  transfers between devices with their start and end apart: 28, of which 14 were waited for; matrix products, arithmetic and copies ran while one was open for 1% of the time, Pallas kernels for 35%

profile of v12, /device:TPU:0, one launch (start us, length us, event | category | flops | bytes accessed | tf_op | source)
XLA Modules:
  0.0 114.4 jit_solution(3746906439260916885)
XLA Ops:
  0.6 0.7 stack.23.where_ref.refs_0_
  1.3 5.5 %first.1 = (bf16[8,128,256]{2,1,0:T(8,128)(2,1)}, bf16[2048,128]{1,0:T(8,128)(2,1)}, bf16[2048,128]{1,0:T(8,128)(2,1)}, bf16[2048,128]{1,0:T(8,128)(2,1)}, bf16[2048,128]{1,0:T(8,128)(2,1)}) custom-call(s32[5]{0:T(128)} %stack.23.where_ref.refs_0_, bf16[128,8192]{1,0:T(8,128)(2,1)} %bitcast.10, bf16[8192,1280]{1,0:T(8,128)(2,1)} %w_kv_ref.1), custom_call_target="tpu_custom_call" | custom-call | flops 1 | bytes 1 | tf_op jit(solution)/shard_map/first/pallas_call | solution.py:82
  6.8 1.6 %collective-permute-start.1 = (bf16[2048,128]{1,0:T(8,128)(2,1)}, bf16[2048,128]{1,0:T(8,128)(2,1)S(1)}, u32[]{:S(2)}, u32[]{:S(2)}) collective-permute-start(bf16[2048,128]{1,0:T(8,128)(2,1)} %get-tuple-element.40), channel_id=1, source_target_pairs={{0,16},{16,32},{32,48},{48,0},{1,17},{17,33},{33,49},{49,1},{2,18}... | collective-permute-start | bytes 1572872 | tf_op jit(solution)/shard_map/ppermute | solution.py:397
  8.5 2.7 %collective-permute-start.2 = (bf16[2048,128]{1,0:T(8,128)(2,1)}, bf16[2048,128]{1,0:T(8,128)(2,1)S(1)}, u32[]{:S(2)}, u32[]{:S(2)}) collective-permute-start(bf16[2048,128]{1,0:T(8,128)(2,1)} %get-tuple-element.42), channel_id=1, source_target_pairs={{0,32},{16,48},{32,0},{48,16},{1,33},{17,49},{33,1},{49,17},{2,34}... | collective-permute-start | bytes 1572872 | tf_op jit(solution)/shard_map/ppermute | solution.py:397
  11.2 1.4 %collective-permute-start.3 = (bf16[2048,128]{1,0:T(8,128)(2,1)}, bf16[2048,128]{1,0:T(8,128)(2,1)}, u32[]{:S(2)}, u32[]{:S(2)}) collective-permute-start(bf16[2048,128]{1,0:T(8,128)(2,1)} %get-tuple-element.44), channel_id=1, source_target_pairs={{0,48},{16,0},{32,16},{48,32},{1,49},{17,1},{33,17},{49,33},{2,50}... | collective-permute-start | bytes 1572872 | tf_op jit(solution)/shard_map/ppermute | solution.py:397
  12.6 7.8 %all-to-all-start = ((bf16[8,128,256]{2,1,0:T(8,128)(2,1)}), bf16[8,128,256]{2,1,0:T(8,128)(2,1)}, u32[]{:S(2)}, u32[]{:S(2)}) async-start(bf16[8,128,256]{2,1,0:T(8,128)(2,1)} %get-tuple-element.33), calls=%async_computation | async-start | bytes 1048576 | tf_op jit(solution)/shard_map/all_to_all | solution.py:437
  20.5 7.4 %project_query.1.q_ref = bf16[128,1024]{1,0:T(8,128)(2,1)S(1)} custom-call(bf16[128,8192]{1,0:T(8,128)(2,1)S(1)} %bitcast.11, bf16[8192,1280]{1,0:T(8,128)(2,1)} %w_kv_ref.1), custom_call_target="tpu_custom_call" | custom-call | flops 1 | bytes 1 | tf_op jit(solution)/shard_map/project_query/pallas_call | solution.py:110
  27.9 3.4 %all-to-all-done = bf16[8,128,256]{2,1,0:T(8,128)(2,1)} async-done(((bf16[8,128,256]{2,1,0:T(8,128)(2,1)}), bf16[8,128,256]{2,1,0:T(8,128)(2,1)}, u32[]{:S(2)}, u32[]{:S(2)}) %all-to-all-start) | async-done | bytes 524320 | tf_op jit(solution)/shard_map/all_to_all | solution.py:437
  31.3 0.9 copy-done.7
  32.3 7.4 %attention.1 = (bf16[128,1024]{1,0:T(8,128)(2,1)}, bf16[1024,256]{1,0:T(8,128)(2,1)}) custom-call(s32[5]{0:T(128)S(1)} %copy-done.9, s32[1,16]{1,0:T(1,128)S(1)} %copy-done.11, s32[1,4]{1,0:T(1,128)S(1)} %copy-done.12, bf16[128,1024]{1,0:T(8,128)(2,1)S(1)} %project_query.1.q_ref, bf16[128,1024]{1,0:T(8,128)(2,1)S(1)} %bitcast.12, ...), custom_call_target="tpu_custom_call" | custom-call | flops 1 | bytes 1 | tf_op jit(solution)/shard_map/attention/pallas_call | solution.py:205
  39.6 0.8 copy-done.2
  40.6 2.3 %forward.1 = bf16[1024,512]{1,0:T(8,128)(2,1)} custom-call(bf16[2048,128]{1,0:T(8,128)(2,1)} %get-tuple-element.39.refs_0_.refs_1_.refs_2_, bf16[2048,128]{1,0:T(8,128)(2,1)} %copy-done.2, bf16[2048,128]{1,0:T(8,128)(2,1)} %copy-done.4, bf16[2048,128]{1,0:T(8,128)(2,1)} %collective-permute-done.3.refs_3_.refs_4_.refs_5_), custom_call_target="tpu_custom_call" | custom-call | flops 1 | bytes 1 | tf_op jit(solution)/shard_map/forward/pallas_call | solution.py:136
  42.9 0.5 collective-permute-start
  43.5 0.6 collective-permute-start.5
  44.0 1.2 %collective-permute-start.6 = (bf16[128,1024]{1,0:T(8,128)(2,1)}, bf16[128,1024]{1,0:T(8,128)(2,1)S(1)}, u32[]{:S(2)}, u32[]{:S(2)}) collective-permute-start(bf16[128,1024]{1,0:T(8,128)(2,1)} %get-tuple-element.46.g_ref.refs_5_), channel_id=1, source_target_pairs={{0,32},{16,48},{32,0},{48,16},{1,33},{17,49},{33,1},{49,17},{2,34}... | collective-permute-start | bytes 786440 | tf_op jit(solution)/shard_map/ppermute | solution.py:397
  45.2 1.5 %collective-permute-start.7 = (bf16[128,1024]{1,0:T(8,128)(2,1)}, bf16[128,1024]{1,0:T(8,128)(2,1)S(1)}, u32[]{:S(2)}, u32[]{:S(2)}) collective-permute-start(bf16[128,1024]{1,0:T(8,128)(2,1)} %get-tuple-element.46.g_ref.refs_5_), channel_id=1, source_target_pairs={{0,48},{16,0},{32,16},{48,32},{1,49},{17,1},{33,17},{49,33},{2,50}... | collective-permute-start | bytes 786440 | tf_op jit(solution)/shard_map/ppermute | solution.py:397
  46.7 4.1 %all-to-all-start.1 = ((bf16[8,128,256]{2,1,0:T(8,128)(2,1)}), bf16[8,128,256]{2,1,0:T(8,128)(2,1)}, u32[]{:S(2)}, u32[]{:S(2)}) async-start(bf16[8,128,256]{2,1,0:T(8,128)(2,1)} %bitcast.8), calls=%async_computation.1 | async-start | bytes 1048576 | tf_op jit(solution)/shard_map/all_to_all | solution.py:445
  50.9 7.0 %d_x_first.1.part_ref = bf16[128,8192]{1,0:T(8,128)(2,1)} custom-call(bf16[128,1024]{1,0:T(8,128)(2,1)} %get-tuple-element.46.g_ref.refs_5_, bf16[8192,1280]{1,0:T(8,128)(2,1)} %w_kv_ref.1), custom_call_target="tpu_custom_call" | custom-call | flops 1 | bytes 1 | tf_op jit(solution)/shard_map/d_x_first/pallas_call | solution.py:383
  57.9 0.9 collective-permute-done.5.refs_6_
  58.7 0.5 collective-permute-start.9
  59.5 0.8 collective-permute-done.8.refs_10_
  61.0 5.3 %term_query.1 = bf16[4,256,1024]{2,1,0:T(8,128)(2,1)} custom-call(bf16[1024,512]{1,0:T(8,128)(2,1)S(1)} %collective-permute-done.4.refs_0_.refs_1_, bf16[2048,128]{1,0:T(8,128)(2,1)S(1)} %copy-done.1, bf16[2048,128]{1,0:T(8,128)(2,1)S(1)} %copy-done.3, bf16[2048,128]{1,0:T(8,128)(2,1)S(1)} %copy-done.5, ...), custom_call_target="tpu_custom_call" | custom-call | flops 1 | bytes 1 | tf_op jit(solution)/shard_map/term_query/pallas_call | solution.py:247
  66.3 3.8 %all-to-all-start.2 = ((bf16[4,256,1024]{2,1,0:T(8,128)(2,1)}), bf16[4,256,1024]{2,1,0:T(8,128)(2,1)S(1)}, u32[]{:S(2)}, u32[]{:S(2)}) async-start(bf16[4,256,1024]{2,1,0:T(8,128)(2,1)} %term_query.1), calls=%async_computation.2 | async-start | bytes 4194304 | tf_op jit(solution)/shard_map/all_to_all | solution.py:450
  70.1 1.1 reduce_sum.12.refs_6_.kv_ref
  71.3 0.9 collective-permute-start.11
  72.2 2.7 %collective-permute-start.12 = (bf16[128,256]{1,0:T(8,128)(2,1)S(1)}, bf16[128,256]{1,0:T(8,128)(2,1)S(1)}, u32[]{:S(2)}, u32[]{:S(2)}) collective-permute-start(bf16[128,256]{1,0:T(8,128)(2,1)S(1)} %reduce_sum.12.refs_6_.kv_ref), channel_id=1, source_target_pairs={{0,32},{16,48},{32,0},{48,16},{1,33},{17,49},{33,1},{49,17},{2,34}... | collective-permute-start | bytes 196616 | tf_op jit(solution)/shard_map/ppermute | solution.py:397
  74.8 2.0 %collective-permute-start.13 = (bf16[128,256]{1,0:T(8,128)(2,1)S(1)}, bf16[128,256]{1,0:T(8,128)(2,1)S(1)}, u32[]{:S(2)}, u32[]{:S(2)}) collective-permute-start(bf16[128,256]{1,0:T(8,128)(2,1)S(1)} %reduce_sum.12.refs_6_.kv_ref), channel_id=1, source_target_pairs={{0,48},{16,0},{32,16},{48,32},{1,49},{17,1},{33,17},{49,33},{2,50}... | collective-permute-start | bytes 196616 | tf_op jit(solution)/shard_map/ppermute | solution.py:397
  76.9 0.6 collective-permute-done.11.refs_7_
  77.5 0.9 collective-permute-done.12.refs_8_
  78.4 0.8 collective-permute-done.13.refs_9_
  79.2 0.5 collective-permute-done.16.refs_12_
  79.6 0.8 collective-permute-done.17.refs_13_
  80.4 0.6 copy-done.20
  81.0 3.1 %term_kv.1 = (bf16[256,256]{1,0:T(8,128)(2,1)}, bf16[256,256]{1,0:T(8,128)(2,1)}, bf16[256,256]{1,0:T(8,128)(2,1)}, bf16[256,256]{1,0:T(8,128)(2,1)}) custom-call(s32[5]{0:T(128)} %stack.23.where_ref.refs_0_, bf16[1024,512]{1,0:T(8,128)(2,1)} %copy-done.6, bf16[2048,128]{1,0:T(8,128)(2,1)} %get-tuple-element.39.refs_0_.refs_1_.refs_2_, ...), custom_call_target="tpu_custom_call" | custom-call | flops 1 | bytes 1 | tf_op jit(solution)/shard_map/term_kv/pallas_call | solution.py:277
  84.2 1.0 collective-permute-start.18
  85.2 3.3 %collective-permute-start.19 = (bf16[256,256]{1,0:T(8,128)(2,1)}, bf16[256,256]{1,0:T(8,128)(2,1)S(1)}, u32[]{:S(2)}, u32[]{:S(2)}) collective-permute-start(bf16[256,256]{1,0:T(8,128)(2,1)} %get-tuple-element.55), channel_id=1, source_target_pairs={{0,4},{64,68},{4,0},{68,64},{1,5},{65,69},{5,1},{69,65},{2,6},{66,... | collective-permute-start | bytes 393224 | tf_op jit(solution)/shard_map/ppermute | solution.py:420
  88.5 1.0 collective-permute-start.20
  89.5 9.2 %d_x_last.1 = bf16[128,8192]{1,0:T(8,128)(2,1)} custom-call(bf16[128,1024]{1,0:T(8,128)(2,1)} %get-tuple-element.46.g_ref.refs_5_, bf16[128,256]{1,0:T(8,128)(2,1)} %copy-done.13, bf16[8192,1280]{1,0:T(8,128)(2,1)} %w_kv_ref.1, bf16[8192,1280]{1,0:T(8,128)(2,1)} %w_kv_ref.1, bf16[128,8192]{1,0:T(8,128)(2,1)} %d_x_first.1.part_ref), custom_call_target="tpu_custom_call" | custom-call | flops 1 | bytes 1 | tf_op jit(solution)/shard_map/d_x_last/pallas_call | solution.py:383
  98.8 1.2 %middle_y.1 = (f32[64,256]{1,0:T(8,128)S(1)}, bf16[64,256]{1,0:T(8,128)(2,1)}, bf16[64,256]{1,0:T(8,128)(2,1)}, bf16[64,256]{1,0:T(8,128)(2,1)}) custom-call(s32[5]{0:T(128)S(1)} %copy-done.10, bf16[256,256]{1,0:T(8,128)(2,1)S(1)} %copy-done.8, bf16[256,256]{1,0:T(8,128)(2,1)S(1)} %collective-permute-done.18.refs_1_, ...), custom_call_target="tpu_custom_call" | custom-call | flops 1 | bytes 1 | tf_op jit(solution)/shard_map/middle_y/pallas_call | solution.py:323
  100.0 1.1 middle_z.1
  101.0 3.5 %all-to-all-start.3 = ((bf16[4,64,1024]{2,1,0:T(8,128)(2,1)}), bf16[4,64,1024]{2,1,0:T(8,128)(2,1)S(1)}, u32[]{:S(2)}, u32[]{:S(2)}) async-start(bf16[4,64,1024]{2,1,0:T(8,128)(2,1)} %middle_z.1), calls=%async_computation.3 | async-start | bytes 1048576 | tf_op jit(solution)/shard_map/all_to_all | solution.py:457
  104.5 2.1 %collective-permute-start.21 = (bf16[64,256]{1,0:T(8,128)(2,1)S(1)}, bf16[64,256]{1,0:T(8,128)(2,1)S(1)}, u32[]{:S(2)}, u32[]{:S(2)}) collective-permute-start(bf16[64,256]{1,0:T(8,128)(2,1)S(1)} %copy-done.23), channel_id=1, source_target_pairs={{0,1},{1,2},{2,3},{3,0},{4,5},{5,6},{6,7},{7,4},{8,9},{9,10},{10,1... | collective-permute-start | bytes 98312 | tf_op jit(solution)/shard_map/ppermute | solution.py:424
  106.6 2.7 %collective-permute-start.22 = (bf16[64,256]{1,0:T(8,128)(2,1)S(1)}, bf16[64,256]{1,0:T(8,128)(2,1)S(1)}, u32[]{:S(2)}, u32[]{:S(2)}) collective-permute-start(bf16[64,256]{1,0:T(8,128)(2,1)S(1)} %copy-done.22), channel_id=1, source_target_pairs={{0,2},{1,3},{2,0},{3,1},{4,6},{5,7},{6,4},{7,5},{8,10},{9,11},{10,... | collective-permute-start | bytes 98312 | tf_op jit(solution)/shard_map/ppermute | solution.py:424
  109.3 1.5 %collective-permute-start.23 = (bf16[64,256]{1,0:T(8,128)(2,1)S(1)}, bf16[64,256]{1,0:T(8,128)(2,1)S(1)}, u32[]{:S(2)}, u32[]{:S(2)}) collective-permute-start(bf16[64,256]{1,0:T(8,128)(2,1)S(1)} %copy-done.21), channel_id=1, source_target_pairs={{0,3},{1,0},{2,1},{3,2},{4,7},{5,4},{6,5},{7,6},{8,11},{9,8},{10,9... | collective-permute-start | bytes 98312 | tf_op jit(solution)/shard_map/ppermute | solution.py:424
  110.7 1.3 %collective-permute-done.22.refs_2_ = bf16[64,256]{1,0:T(8,128)(2,1)S(1)} collective-permute-done((bf16[64,256]{1,0:T(8,128)(2,1)S(1)}, bf16[64,256]{1,0:T(8,128)(2,1)S(1)}, u32[]{:S(2)}, u32[]{:S(2)}) %collective-permute-start.22) | collective-permute-done | bytes 32800 | tf_op jit(solution)/shard_map/ppermute | solution.py:424
  112.0 1.2 %collective-permute-done.23.refs_3_ = bf16[64,256]{1,0:T(8,128)(2,1)S(1)} collective-permute-done((bf16[64,256]{1,0:T(8,128)(2,1)S(1)}, bf16[64,256]{1,0:T(8,128)(2,1)S(1)}, u32[]{:S(2)}, u32[]{:S(2)}) %collective-permute-start.23) | collective-permute-done | bytes 32800 | tf_op jit(solution)/shard_map/ppermute | solution.py:424
  113.2 0.4 all-to-all-done.3.stack_ref
  113.6 0.8 final.1
  (69 shorter events, 1.3 us)
Async XLA Ops:
  1.3 19.1 %copy-start = (bf16[1,128,8192]{2,1,0:T(8,128)(2,1)S(1)}, bf16[1,128,8192]{2,1,0:T(8,128)(2,1)}, u32[]{:S(2)}) copy-start(bf16[1,128,8192]{2,1,0:T(8,128)(2,1)} %param.5) | copy-start | bytes 6291460
  6.8 32.8 %collective-permute-start.1 = (bf16[2048,128]{1,0:T(8,128)(2,1)}, bf16[2048,128]{1,0:T(8,128)(2,1)S(1)}, u32[]{:S(2)}, u32[]{:S(2)}) collective-permute-start(bf16[2048,128]{1,0:T(8,128)(2,1)} %get-tuple-element.40), channel_id=1, source_target_pairs={{0,16},{16,32},{32,48},{48,0},{1,17},{17,33},{33,49},{49,1},{2,18}... | collective-permute-start | bytes 1572872 | tf_op jit(solution)/shard_map/ppermute | solution.py:397
  8.5 31.1 %collective-permute-start.2 = (bf16[2048,128]{1,0:T(8,128)(2,1)}, bf16[2048,128]{1,0:T(8,128)(2,1)S(1)}, u32[]{:S(2)}, u32[]{:S(2)}) collective-permute-start(bf16[2048,128]{1,0:T(8,128)(2,1)} %get-tuple-element.42), channel_id=1, source_target_pairs={{0,32},{16,48},{32,0},{48,16},{1,33},{17,49},{33,1},{49,17},{2,34}... | collective-permute-start | bytes 1572872 | tf_op jit(solution)/shard_map/ppermute | solution.py:397
  11.2 28.4 %collective-permute-start.3 = (bf16[2048,128]{1,0:T(8,128)(2,1)}, bf16[2048,128]{1,0:T(8,128)(2,1)}, u32[]{:S(2)}, u32[]{:S(2)}) collective-permute-start(bf16[2048,128]{1,0:T(8,128)(2,1)} %get-tuple-element.44), channel_id=1, source_target_pairs={{0,48},{16,0},{32,16},{48,32},{1,49},{17,1},{33,17},{49,33},{2,50}... | collective-permute-start | bytes 1572872 | tf_op jit(solution)/shard_map/ppermute | solution.py:397
  12.6 18.6 %all-to-all-start = ((bf16[8,128,256]{2,1,0:T(8,128)(2,1)}), bf16[8,128,256]{2,1,0:T(8,128)(2,1)}, u32[]{:S(2)}, u32[]{:S(2)}) async-start(bf16[8,128,256]{2,1,0:T(8,128)(2,1)} %get-tuple-element.33), calls=%async_computation | async-start | bytes 1048576 | tf_op jit(solution)/shard_map/all_to_all | solution.py:437
  20.4 10.8 %copy-start.9 = (s32[5]{0:T(128)S(1)}, s32[5]{0:T(128)}, u32[]{:S(2)}) copy-start(s32[5]{0:T(128)} %stack.23.where_ref.refs_0_) | copy-start | bytes 64
  20.4 10.8 %copy-start.11 = (s32[1,16]{1,0:T(1,128)S(1)}, s32[1,16]{1,0:T(1,128)}, u32[]{:S(2)}) copy-start(s32[1,16]{1,0:T(1,128)} %order_ref.1) | copy-start | bytes 196
  20.5 10.8 %copy-start.12 = (s32[1,4]{1,0:T(1,128)S(1)}, s32[1,4]{1,0:T(1,128)}, u32[]{:S(2)}) copy-start(s32[1,4]{1,0:T(1,128)} %lens_ref.1) | copy-start | bytes 52
  39.6 1.0 copy-start.4
  42.9 18.1 %collective-permute-start.4 = (bf16[1024,512]{1,0:T(8,128)(2,1)}, bf16[1024,512]{1,0:T(8,128)(2,1)S(1)}, u32[]{:S(2)}, u32[]{:S(2)}) collective-permute-start(bf16[1024,512]{1,0:T(8,128)(2,1)} %forward.1), channel_id=1, source_target_pairs={{0,8},{8,0},{1,9},{9,1},{2,10},{10,2},{3,11},{11,3},{4,12},{12,4},... | collective-permute-start | bytes 3145736 | tf_op jit(solution)/shard_map/ppermute | solution.py:401
  42.9 3.8 %collective-permute-start = (bf16[128,1024]{1,0:T(8,128)(2,1)}, bf16[128,1024]{1,0:T(8,128)(2,1)S(1)}, u32[]{:S(2)}, u32[]{:S(2)}) collective-permute-start(bf16[128,1024]{1,0:T(8,128)(2,1)} %get-tuple-element.46.g_ref.refs_5_), channel_id=1, source_target_pairs={{0,8},{8,0},{1,9},{9,1},{2,10},{10,2},{3,11},{11,3},{4,12},{12,4},... | collective-permute-start | bytes 786440 | tf_op jit(solution)/shard_map/ppermute | solution.py:401
  43.5 15.3 %collective-permute-start.5 = (bf16[128,1024]{1,0:T(8,128)(2,1)}, bf16[128,1024]{1,0:T(8,128)(2,1)S(1)}, u32[]{:S(2)}, u32[]{:S(2)}) collective-permute-start(bf16[128,1024]{1,0:T(8,128)(2,1)} %get-tuple-element.46.g_ref.refs_5_), channel_id=1, source_target_pairs={{0,16},{16,32},{32,48},{48,0},{1,17},{17,33},{33,49},{49,1},{2,18}... | collective-permute-start | bytes 786440 | tf_op jit(solution)/shard_map/ppermute | solution.py:397
  44.0 14.7 %collective-permute-start.6 = (bf16[128,1024]{1,0:T(8,128)(2,1)}, bf16[128,1024]{1,0:T(8,128)(2,1)S(1)}, u32[]{:S(2)}, u32[]{:S(2)}) collective-permute-start(bf16[128,1024]{1,0:T(8,128)(2,1)} %get-tuple-element.46.g_ref.refs_5_), channel_id=1, source_target_pairs={{0,32},{16,48},{32,0},{48,16},{1,33},{17,49},{33,1},{49,17},{2,34}... | collective-permute-start | bytes 786440 | tf_op jit(solution)/shard_map/ppermute | solution.py:397
  45.2 14.1 %collective-permute-start.7 = (bf16[128,1024]{1,0:T(8,128)(2,1)}, bf16[128,1024]{1,0:T(8,128)(2,1)S(1)}, u32[]{:S(2)}, u32[]{:S(2)}) collective-permute-start(bf16[128,1024]{1,0:T(8,128)(2,1)} %get-tuple-element.46.g_ref.refs_5_), channel_id=1, source_target_pairs={{0,48},{16,0},{32,16},{48,32},{1,49},{17,1},{33,17},{49,33},{2,50}... | collective-permute-start | bytes 786440 | tf_op jit(solution)/shard_map/ppermute | solution.py:397
  46.7 19.6 %all-to-all-start.1 = ((bf16[8,128,256]{2,1,0:T(8,128)(2,1)}), bf16[8,128,256]{2,1,0:T(8,128)(2,1)}, u32[]{:S(2)}, u32[]{:S(2)}) async-start(bf16[8,128,256]{2,1,0:T(8,128)(2,1)} %bitcast.8), calls=%async_computation.1 | async-start | bytes 1048576 | tf_op jit(solution)/shard_map/all_to_all | solution.py:445
  50.9 10.1 %copy-start.1 = (bf16[2048,128]{1,0:T(8,128)(2,1)S(1)}, bf16[2048,128]{1,0:T(8,128)(2,1)}, u32[]{:S(2)}) copy-start(bf16[2048,128]{1,0:T(8,128)(2,1)} %get-tuple-element.39.refs_0_.refs_1_.refs_2_) | copy-start | bytes 1572868
  50.9 10.1 %copy-start.3 = (bf16[2048,128]{1,0:T(8,128)(2,1)S(1)}, bf16[2048,128]{1,0:T(8,128)(2,1)}, u32[]{:S(2)}) copy-start(bf16[2048,128]{1,0:T(8,128)(2,1)} %copy-done.2) | copy-start | bytes 1572868
  50.9 10.1 %copy-start.5 = (bf16[2048,128]{1,0:T(8,128)(2,1)S(1)}, bf16[2048,128]{1,0:T(8,128)(2,1)}, u32[]{:S(2)}) copy-start(bf16[2048,128]{1,0:T(8,128)(2,1)} %copy-done.4) | copy-start | bytes 1572868
  58.7 1.5 %collective-permute-start.8 = (bf16[128,1024]{1,0:T(8,128)(2,1)S(1)}, bf16[128,1024]{1,0:T(8,128)(2,1)S(1)}, u32[]{:S(2)}, u32[]{:S(2)}) collective-permute-start(bf16[128,1024]{1,0:T(8,128)(2,1)S(1)} %collective-permute-done.5.refs_6_), channel_id=1, source_target_pairs={{0,8},{8,0},{1,9},{9,1},{2,10},{10,2},{3,11},{11,3},{4,12},{12,4},... | collective-permute-start | bytes 786440 | tf_op jit(solution)/shard_map/ppermute | solution.py:401
  58.7 1.9 %collective-permute-start.9 = (bf16[128,1024]{1,0:T(8,128)(2,1)S(1)}, bf16[128,1024]{1,0:T(8,128)(2,1)S(1)}, u32[]{:S(2)}, u32[]{:S(2)}) collective-permute-start(bf16[128,1024]{1,0:T(8,128)(2,1)S(1)} %collective-permute-done.6.refs_7_), channel_id=1, source_target_pairs={{0,8},{8,0},{1,9},{9,1},{2,10},{10,2},{3,11},{11,3},{4,12},{12,4},... | collective-permute-start | bytes 786440 | tf_op jit(solution)/shard_map/ppermute | solution.py:401
  59.3 1.7 %collective-permute-start.10 = (bf16[128,1024]{1,0:T(8,128)(2,1)S(1)}, bf16[128,1024]{1,0:T(8,128)(2,1)S(1)}, u32[]{:S(2)}, u32[]{:S(2)}) collective-permute-start(bf16[128,1024]{1,0:T(8,128)(2,1)S(1)} %collective-permute-done.7.refs_8_), channel_id=1, source_target_pairs={{0,8},{8,0},{1,9},{9,1},{2,10},{10,2},{3,11},{11,3},{4,12},{12,4},... | collective-permute-start | bytes 786440 | tf_op jit(solution)/shard_map/ppermute | solution.py:401
  61.0 5.3 %copy-start.6 = (bf16[1024,512]{1,0:T(8,128)(2,1)}, bf16[1024,512]{1,0:T(8,128)(2,1)S(1)}, u32[]{:S(2)}) copy-start(bf16[1024,512]{1,0:T(8,128)(2,1)S(1)} %collective-permute-done.4.refs_0_.refs_1_) | copy-start | bytes 3145732
  66.3 33.6 %all-to-all-start.2 = ((bf16[4,256,1024]{2,1,0:T(8,128)(2,1)}), bf16[4,256,1024]{2,1,0:T(8,128)(2,1)S(1)}, u32[]{:S(2)}, u32[]{:S(2)}) async-start(bf16[4,256,1024]{2,1,0:T(8,128)(2,1)} %term_query.1), calls=%async_computation.2 | async-start | bytes 4194304 | tf_op jit(solution)/shard_map/all_to_all | solution.py:450
  71.3 9.1 %copy-start.13 = (bf16[128,256]{1,0:T(8,128)(2,1)}, bf16[128,256]{1,0:T(8,128)(2,1)S(1)}, u32[]{:S(2)}) copy-start(bf16[128,256]{1,0:T(8,128)(2,1)S(1)} %reduce_sum.12.refs_6_.kv_ref) | copy-start | bytes 196612
  71.3 6.2 %collective-permute-start.11 = (bf16[128,256]{1,0:T(8,128)(2,1)S(1)}, bf16[128,256]{1,0:T(8,128)(2,1)S(1)}, u32[]{:S(2)}, u32[]{:S(2)}) collective-permute-start(bf16[128,256]{1,0:T(8,128)(2,1)S(1)} %reduce_sum.12.refs_6_.kv_ref), channel_id=1, source_target_pairs={{0,16},{16,32},{32,48},{48,0},{1,17},{17,33},{33,49},{49,1},{2,18}... | collective-permute-start | bytes 196616 | tf_op jit(solution)/shard_map/ppermute | solution.py:397
  72.2 6.2 %collective-permute-start.12 = (bf16[128,256]{1,0:T(8,128)(2,1)S(1)}, bf16[128,256]{1,0:T(8,128)(2,1)S(1)}, u32[]{:S(2)}, u32[]{:S(2)}) collective-permute-start(bf16[128,256]{1,0:T(8,128)(2,1)S(1)} %reduce_sum.12.refs_6_.kv_ref), channel_id=1, source_target_pairs={{0,32},{16,48},{32,0},{48,16},{1,33},{17,49},{33,1},{49,17},{2,34}... | collective-permute-start | bytes 196616 | tf_op jit(solution)/shard_map/ppermute | solution.py:397
  74.8 4.3 %collective-permute-start.13 = (bf16[128,256]{1,0:T(8,128)(2,1)S(1)}, bf16[128,256]{1,0:T(8,128)(2,1)S(1)}, u32[]{:S(2)}, u32[]{:S(2)}) collective-permute-start(bf16[128,256]{1,0:T(8,128)(2,1)S(1)} %reduce_sum.12.refs_6_.kv_ref), channel_id=1, source_target_pairs={{0,48},{16,0},{32,16},{48,32},{1,49},{17,1},{33,17},{49,33},{2,50}... | collective-permute-start | bytes 196616 | tf_op jit(solution)/shard_map/ppermute | solution.py:397
  76.9 2.3 %collective-permute-start.14 = (bf16[128,256]{1,0:T(8,128)(2,1)S(1)}, bf16[128,256]{1,0:T(8,128)(2,1)S(1)}, u32[]{:S(2)}, u32[]{:S(2)}) collective-permute-start(bf16[128,256]{1,0:T(8,128)(2,1)S(1)} %reduce_sum.12.refs_6_.kv_ref), channel_id=1, source_target_pairs={{0,8},{8,0},{1,9},{9,1},{2,10},{10,2},{3,11},{11,3},{4,12},{12,4},... | collective-permute-start | bytes 196616 | tf_op jit(solution)/shard_map/ppermute | solution.py:401
  77.5 2.9 %copy-start.14 = (bf16[128,256]{1,0:T(8,128)(2,1)}, bf16[128,256]{1,0:T(8,128)(2,1)S(1)}, u32[]{:S(2)}) copy-start(bf16[128,256]{1,0:T(8,128)(2,1)S(1)} %collective-permute-done.11.refs_7_) | copy-start | bytes 196612
  77.5 1.7 %collective-permute-start.15 = (bf16[128,256]{1,0:T(8,128)(2,1)S(1)}, bf16[128,256]{1,0:T(8,128)(2,1)S(1)}, u32[]{:S(2)}, u32[]{:S(2)}) collective-permute-start(bf16[128,256]{1,0:T(8,128)(2,1)S(1)} %collective-permute-done.11.refs_7_), channel_id=1, source_target_pairs={{0,8},{8,0},{1,9},{9,1},{2,10},{10,2},{3,11},{11,3},{4,12},{12,4},... | collective-permute-start | bytes 196616 | tf_op jit(solution)/shard_map/ppermute | solution.py:401
  78.3 2.0 %copy-start.15 = (bf16[128,256]{1,0:T(8,128)(2,1)}, bf16[128,256]{1,0:T(8,128)(2,1)S(1)}, u32[]{:S(2)}) copy-start(bf16[128,256]{1,0:T(8,128)(2,1)S(1)} %collective-permute-done.12.refs_8_) | copy-start | bytes 196612
  78.4 1.3 %collective-permute-start.16 = (bf16[128,256]{1,0:T(8,128)(2,1)S(1)}, bf16[128,256]{1,0:T(8,128)(2,1)S(1)}, u32[]{:S(2)}, u32[]{:S(2)}) collective-permute-start(bf16[128,256]{1,0:T(8,128)(2,1)S(1)} %collective-permute-done.12.refs_8_), channel_id=1, source_target_pairs={{0,8},{8,0},{1,9},{9,1},{2,10},{10,2},{3,11},{11,3},{4,12},{12,4},... | collective-permute-start | bytes 196616 | tf_op jit(solution)/shard_map/ppermute | solution.py:401
  79.1 1.3 %copy-start.16 = (bf16[128,256]{1,0:T(8,128)(2,1)}, bf16[128,256]{1,0:T(8,128)(2,1)S(1)}, u32[]{:S(2)}) copy-start(bf16[128,256]{1,0:T(8,128)(2,1)S(1)} %collective-permute-done.13.refs_9_) | copy-start | bytes 196612
  79.1 1.3 %collective-permute-start.17 = (bf16[128,256]{1,0:T(8,128)(2,1)S(1)}, bf16[128,256]{1,0:T(8,128)(2,1)S(1)}, u32[]{:S(2)}, u32[]{:S(2)}) collective-permute-start(bf16[128,256]{1,0:T(8,128)(2,1)S(1)} %collective-permute-done.13.refs_9_), channel_id=1, source_target_pairs={{0,8},{8,0},{1,9},{9,1},{2,10},{10,2},{3,11},{11,3},{4,12},{12,4},... | collective-permute-start | bytes 196616 | tf_op jit(solution)/shard_map/ppermute | solution.py:401
  79.1 1.3 %copy-start.17 = (bf16[128,256]{1,0:T(8,128)(2,1)}, bf16[128,256]{1,0:T(8,128)(2,1)S(1)}, u32[]{:S(2)}) copy-start(bf16[128,256]{1,0:T(8,128)(2,1)S(1)} %collective-permute-done.14.refs_10_) | copy-start | bytes 196612
  79.1 1.3 %copy-start.18 = (bf16[128,256]{1,0:T(8,128)(2,1)}, bf16[128,256]{1,0:T(8,128)(2,1)S(1)}, u32[]{:S(2)}) copy-start(bf16[128,256]{1,0:T(8,128)(2,1)S(1)} %collective-permute-done.15.refs_11_) | copy-start | bytes 196612
  84.2 14.6 %collective-permute-start.18 = (bf16[256,256]{1,0:T(8,128)(2,1)}, bf16[256,256]{1,0:T(8,128)(2,1)S(1)}, u32[]{:S(2)}, u32[]{:S(2)}) collective-permute-start(bf16[256,256]{1,0:T(8,128)(2,1)} %get-tuple-element.53), channel_id=1, source_target_pairs={{0,64},{64,4},{4,68},{68,0},{1,65},{65,5},{5,69},{69,1},{2,66},{66... | collective-permute-start | bytes 393224 | tf_op jit(solution)/shard_map/ppermute | solution.py:420
  85.2 13.5 %collective-permute-start.19 = (bf16[256,256]{1,0:T(8,128)(2,1)}, bf16[256,256]{1,0:T(8,128)(2,1)S(1)}, u32[]{:S(2)}, u32[]{:S(2)}) collective-permute-start(bf16[256,256]{1,0:T(8,128)(2,1)} %get-tuple-element.55), channel_id=1, source_target_pairs={{0,4},{64,68},{4,0},{68,64},{1,5},{65,69},{5,1},{69,65},{2,6},{66,... | collective-permute-start | bytes 393224 | tf_op jit(solution)/shard_map/ppermute | solution.py:420
  88.5 10.3 %collective-permute-start.20 = (bf16[256,256]{1,0:T(8,128)(2,1)}, bf16[256,256]{1,0:T(8,128)(2,1)S(1)}, u32[]{:S(2)}, u32[]{:S(2)}) collective-permute-start(bf16[256,256]{1,0:T(8,128)(2,1)} %get-tuple-element.57), channel_id=1, source_target_pairs={{0,68},{64,0},{4,64},{68,4},{1,69},{65,1},{5,65},{69,5},{2,70},{66... | collective-permute-start | bytes 393224 | tf_op jit(solution)/shard_map/ppermute | solution.py:420
  89.5 9.3 %copy-start.8 = (bf16[256,256]{1,0:T(8,128)(2,1)S(1)}, bf16[256,256]{1,0:T(8,128)(2,1)}, u32[]{:S(2)}) copy-start(bf16[256,256]{1,0:T(8,128)(2,1)} %get-tuple-element.51.refs_0_) | copy-start | bytes 393220
  89.5 9.3 %copy-start.10 = (s32[5]{0:T(128)S(1)}, s32[5]{0:T(128)}, u32[]{:S(2)}) copy-start(s32[5]{0:T(128)} %stack.23.where_ref.refs_0_) | copy-start | bytes 64
  100.0 4.6 %copy-start.23 = (bf16[64,256]{1,0:T(8,128)(2,1)S(1)}, bf16[64,256]{1,0:T(8,128)(2,1)}, u32[]{:S(2)}) copy-start(bf16[64,256]{1,0:T(8,128)(2,1)} %get-tuple-element.59) | copy-start | bytes 98308
  100.0 6.6 %copy-start.22 = (bf16[64,256]{1,0:T(8,128)(2,1)S(1)}, bf16[64,256]{1,0:T(8,128)(2,1)}, u32[]{:S(2)}) copy-start(bf16[64,256]{1,0:T(8,128)(2,1)} %get-tuple-element.62) | copy-start | bytes 98308
  100.0 9.3 %copy-start.21 = (bf16[64,256]{1,0:T(8,128)(2,1)S(1)}, bf16[64,256]{1,0:T(8,128)(2,1)}, u32[]{:S(2)}) copy-start(bf16[64,256]{1,0:T(8,128)(2,1)} %get-tuple-element.63) | copy-start | bytes 98308
  101.0 12.6 %all-to-all-start.3 = ((bf16[4,64,1024]{2,1,0:T(8,128)(2,1)}), bf16[4,64,1024]{2,1,0:T(8,128)(2,1)S(1)}, u32[]{:S(2)}, u32[]{:S(2)}) async-start(bf16[4,64,1024]{2,1,0:T(8,128)(2,1)} %middle_z.1), calls=%async_computation.3 | async-start | bytes 1048576 | tf_op jit(solution)/shard_map/all_to_all | solution.py:457
  104.5 6.2 %collective-permute-start.21 = (bf16[64,256]{1,0:T(8,128)(2,1)S(1)}, bf16[64,256]{1,0:T(8,128)(2,1)S(1)}, u32[]{:S(2)}, u32[]{:S(2)}) collective-permute-start(bf16[64,256]{1,0:T(8,128)(2,1)S(1)} %copy-done.23), channel_id=1, source_target_pairs={{0,1},{1,2},{2,3},{3,0},{4,5},{5,6},{6,7},{7,4},{8,9},{9,10},{10,1... | collective-permute-start | bytes 98312 | tf_op jit(solution)/shard_map/ppermute | solution.py:424
  106.6 5.4 %collective-permute-start.22 = (bf16[64,256]{1,0:T(8,128)(2,1)S(1)}, bf16[64,256]{1,0:T(8,128)(2,1)S(1)}, u32[]{:S(2)}, u32[]{:S(2)}) collective-permute-start(bf16[64,256]{1,0:T(8,128)(2,1)S(1)} %copy-done.22), channel_id=1, source_target_pairs={{0,2},{1,3},{2,0},{3,1},{4,6},{5,7},{6,4},{7,5},{8,10},{9,11},{10,... | collective-permute-start | bytes 98312 | tf_op jit(solution)/shard_map/ppermute | solution.py:424
  109.3 3.9 %collective-permute-start.23 = (bf16[64,256]{1,0:T(8,128)(2,1)S(1)}, bf16[64,256]{1,0:T(8,128)(2,1)S(1)}, u32[]{:S(2)}, u32[]{:S(2)}) collective-permute-start(bf16[64,256]{1,0:T(8,128)(2,1)S(1)} %copy-done.21), channel_id=1, source_target_pairs={{0,3},{1,0},{2,1},{3,2},{4,7},{5,4},{6,5},{7,6},{8,11},{9,8},{10,9... | collective-permute-start | bytes 98312 | tf_op jit(solution)/shard_map/ppermute | solution.py:424
  (4 other events, 3.2 us)
